TPU v7x, 256 devices: a whole 4x4x8 slice. The times are simulated.
256 devices in a mesh: dp: 4 (over z_hi, core), ctx: 16 (over z_lo, y), tp: 4 (over x).
Axes of the slice: x: 4, y: 4, z: 8 (z_hi: 2, z_lo: 4; z = z_hi * 4 + z_lo), core: 2. Of those that a mesh axis runs over, the one named last changes fastest.
Arguments:
- hidden_in: bfloat16 [4, 3584, 8192], P('dp', 'ctx', 'tp'), may hold values from -6 to 6
- queries: bfloat16 [4, 3584, 4096], P('dp', 'ctx', 'tp'), may hold values from -6 to 6
- keys_in: bfloat16 [4, 3584, 512], P('dp', 'ctx', 'tp'), may hold values from -6 to 6
- values_in: bfloat16 [4, 3584, 512], P('dp', 'ctx', 'tp'), may hold values from -6 to 6
- out_grad: bfloat16 [4, 3584, 4096], P('dp', 'ctx', 'tp'), may hold values from -6 to 6
- doc_lengths: int32 [4, 6], P('dp'), may hold values from 1 to 1194, 3584 in all within a row
- pair_perm: int32 [16], replicated, may hold values from 0 to 15, each once
Outputs:
- grad_queries: bfloat16 [4, 3584, 4096], P('dp', 'ctx', 'tp')
- grad_keys: bfloat16 [4, 3584, 512], P('dp', 'ctx', 'tp')
- grad_values: bfloat16 [4, 3584, 512], P('dp', 'ctx', 'tp')
- grad_kv_weight: float32 [1024, 8192], P(('dp', 'ctx'), 'tp')
Inputs may be any that keep to these rules, and one draw needn't show every extreme that they name: `doc_lengths`: each row is a permutation of the documents' lengths summing to 3584, the largest exactly 1194. `pair_perm`: a permutation of the indices of ctx.
All inputs are finite; a program needn't handle non-finite values.
Results may differ from a plain program's by a relative error of at most 0.019.
Values may be sent and summed in bfloat16 or wider, within the bound.
No kernel may reach another device: no remote copies, remote signals or barrier semaphores. Data moves between devices by JAX's collectives and lax.ppermute only.
A program may use at most 64 MiB of HBM per device.

v0:
```python
import jax
import jax.numpy as jnp
from jax import lax
from jax.sharding import PartitionSpec as P

QH = 32
KVH = 4
DH = 128


def token_positions(row_ids, pair_perm, half_rows, ctx_count):
    ctx_rank = row_ids // (2 * half_rows)
    within = row_ids % (2 * half_rows)
    all_ranks = jnp.arange(ctx_count, dtype=jnp.int32)
    chosen = jnp.sum(
        jnp.where(ctx_rank[:, None] == all_ranks[None, :], pair_perm[None, :], 0), axis=1
    )
    first_pos = chosen * half_rows + within
    second_pos = (2 * ctx_count - 1 - chosen) * half_rows + within - half_rows
    return jnp.where(within < half_rows, first_pos, second_pos)


def document_of(positions, lengths_row):
    doc_ends = jnp.cumsum(lengths_row)
    return jnp.sum((positions[:, None] >= doc_ends[None, :]).astype(jnp.int32), axis=1)


def block_length(row_total, shard_rows):
    shards = row_total // shard_rows
    best = 1
    for factor in range(1, shards + 1):
        if shards % factor == 0 and factor * shard_rows <= max(1024, shard_rows):
            best = factor
    return best * shard_rows


def per_device(hidden_in, queries, keys_in, values_in, out_grad, doc_lengths, pair_perm):
    row_count = queries.shape[1]
    half_rows = row_count // 2
    ctx_count = lax.axis_size("ctx")
    ctx_rank = lax.axis_index("ctx")
    kv_local = keys_in.shape[2] // DH
    group_size = QH // KVH
    score_scale = DH ** (-0.5)
    seq_len = row_count * ctx_count
    query_blk = queries[0].reshape(row_count, kv_local, group_size, DH)
    grad_out = out_grad[0].reshape(row_count, kv_local, group_size, DH)
    own_lengths = doc_lengths[0]
    query_pos = token_positions(
        ctx_rank * row_count + jnp.arange(row_count, dtype=jnp.int32),
        pair_perm,
        half_rows,
        ctx_count,
    )
    query_doc = document_of(query_pos, own_lengths)

    def key_mask(first_row, span):
        key_pos = token_positions(
            first_row + jnp.arange(span, dtype=jnp.int32), pair_perm, half_rows, ctx_count
        )
        key_doc = document_of(key_pos, own_lengths)
        return (key_pos[None, :] <= query_pos[:, None]) & (key_doc[None, :] == query_doc[:, None])

    def guarded(update, status):
        result = update(status)
        return result

    forward_init = (
        jnp.zeros((kv_local, group_size, row_count), jnp.float32),
        jnp.zeros((row_count, kv_local, group_size, DH), jnp.float32),
    )
    backward_init = (
        jnp.zeros((row_count, kv_local, group_size, DH), jnp.float32),
        jnp.zeros((seq_len, kv_local * DH), jnp.float32),
        jnp.zeros((seq_len, kv_local * DH), jnp.float32),
    )
    key_part = lax.all_gather(keys_in[0], "ctx", axis=0, tiled=True)
    value_part = lax.all_gather(values_in[0], "ctx", axis=0, tiled=True)
    span = block_length(key_part.shape[0], row_count)

    def forward_one_block(index, status):
        offset = index * span
        key_blk = lax.dynamic_slice_in_dim(key_part, offset, span, 0).reshape(span, kv_local, DH)
        value_blk = lax.dynamic_slice_in_dim(value_part, offset, span, 0).reshape(
            span, kv_local, DH
        )
        allowed = key_mask(offset, span)

        def update(inner):
            summed, numerator = inner
            scores = (
                jnp.einsum("qgrd,kgd->grqk", query_blk, key_blk, preferred_element_type=jnp.float32)
                * score_scale
            )
            weights = jnp.where(allowed[None, None], jnp.exp(scores), 0.0)
            summed = summed + jnp.sum(weights, axis=3)
            numerator = numerator + jnp.einsum(
                "grqk,kgd->qgrd",
                weights.astype(jnp.bfloat16),
                value_blk,
                preferred_element_type=jnp.float32,
            )
            return (summed, numerator)

        return guarded(update, status)

    forward_stats = lax.fori_loop(0, key_part.shape[0] // span, forward_one_block, forward_init)
    summed, numerator = forward_stats
    attn_out = (numerator / summed.transpose(2, 0, 1)[..., None]).astype(jnp.bfloat16)
    log_sum = jnp.log(summed)
    delta_row = jnp.sum(
        grad_out.astype(jnp.float32) * attn_out.astype(jnp.float32), axis=3
    ).transpose(1, 2, 0)
    backward_key_part = lax.all_gather(keys_in[0], "ctx", axis=0, tiled=True)
    backward_value_part = lax.all_gather(values_in[0], "ctx", axis=0, tiled=True)
    backward_span = block_length(backward_key_part.shape[0], row_count)

    def backward_one_block(index, status):
        offset = index * backward_span
        key_blk = lax.dynamic_slice_in_dim(backward_key_part, offset, backward_span, 0).reshape(
            backward_span, kv_local, DH
        )
        value_blk = lax.dynamic_slice_in_dim(backward_value_part, offset, backward_span, 0).reshape(
            backward_span, kv_local, DH
        )
        allowed = key_mask(offset, backward_span)

        def update(inner):
            query_acc, key_buffer, value_buffer = inner
            scores = (
                jnp.einsum("qgrd,kgd->grqk", query_blk, key_blk, preferred_element_type=jnp.float32)
                * score_scale
            )
            probabilities = jnp.where(
                allowed[None, None], jnp.exp(scores - log_sum[..., None]), 0.0
            )
            value_term = jnp.einsum(
                "grqk,qgrd->kgd",
                probabilities.astype(jnp.bfloat16),
                grad_out,
                preferred_element_type=jnp.float32,
            )
            grad_probs = jnp.einsum(
                "qgrd,kgd->grqk", grad_out, value_blk, preferred_element_type=jnp.float32
            )
            grad_scores = (probabilities * (grad_probs - delta_row[..., None])).astype(jnp.bfloat16)
            query_acc = query_acc + jnp.einsum(
                "grqk,kgd->qgrd", grad_scores, key_blk, preferred_element_type=jnp.float32
            )
            key_term = (
                jnp.einsum(
                    "grqk,qgrd->kgd", grad_scores, query_blk, preferred_element_type=jnp.float32
                )
                * score_scale
            )
            old_keys = lax.dynamic_slice_in_dim(key_buffer, offset, backward_span, 0)
            key_buffer = lax.dynamic_update_slice_in_dim(
                key_buffer, old_keys + key_term.reshape(backward_span, kv_local * DH), offset, 0
            )
            old_values = lax.dynamic_slice_in_dim(value_buffer, offset, backward_span, 0)
            value_buffer = lax.dynamic_update_slice_in_dim(
                value_buffer,
                old_values + value_term.reshape(backward_span, kv_local * DH),
                offset,
                0,
            )
            return (query_acc, key_buffer, value_buffer)

        return guarded(update, status)

    gradients = lax.fori_loop(
        0, backward_key_part.shape[0] // backward_span, backward_one_block, backward_init
    )
    query_acc, key_buffer, value_buffer = gradients
    key_sum, value_sum = (
        lax.psum_scatter(
            key_buffer.astype(jnp.bfloat16), "ctx", scatter_dimension=0, tiled=True
        ).astype(jnp.float32),
        lax.psum_scatter(
            value_buffer.astype(jnp.bfloat16), "ctx", scatter_dimension=0, tiled=True
        ).astype(jnp.float32),
    )
    grad_keys = key_sum.astype(jnp.bfloat16)
    grad_values = value_sum.astype(jnp.bfloat16)
    grad_queries = (
        (query_acc * score_scale)
        .reshape(row_count, kv_local * group_size * DH)
        .astype(jnp.bfloat16)
    )
    all_keys, all_values = (
        lax.all_gather(grad_keys, "tp", axis=1, tiled=True),
        lax.all_gather(grad_values, "tp", axis=1, tiled=True),
    )
    stacked = jnp.concatenate([all_keys, all_values], axis=1)
    features = hidden_in[0]
    grad_weight = lax.psum_scatter(
        lax.dot_general(
            stacked, features, (((0,), (0,)), ((), ())), preferred_element_type=jnp.float32
        ),
        ("dp", "ctx"),
        scatter_dimension=0,
        tiled=True,
    )
    return (grad_queries[None], grad_keys[None], grad_values[None], grad_weight)


def solution(mesh):
    in_specs = (
        P("dp", "ctx", "tp"),
        P("dp", "ctx", "tp"),
        P("dp", "ctx", "tp"),
        P("dp", "ctx", "tp"),
        P("dp", "ctx", "tp"),
        P("dp", None),
        P(),
    )
    out_specs = (
        P("dp", "ctx", "tp"),
        P("dp", "ctx", "tp"),
        P("dp", "ctx", "tp"),
        P(("dp", "ctx"), "tp"),
    )
    return jax.shard_map(
        per_device, mesh=mesh, in_specs=in_specs, out_specs=out_specs, check_vma=False
    )
```

profile of v0, /device:TPU:1, one launch (start us, length us, event | category | flops | bytes accessed | tf_op | source)
XLA Modules:
  0.0 686.9 jit_solution(2631558619947895929)
XLA Ops:
  7.3 0.9 broadcast_in_dim.212
  8.2 0.8 reduce-window.10
  9.0 0.7 select_reduce_fusion.2
  9.8 1.1 copy.32
  10.9 1.1 copy.33
  12.0 0.8 copy-done.1
  12.8 0.8 copy.29
  13.6 45.0 %all-gather = bf16[1,3584,128]{2,1,0:T(8,128)(2,1)} all-gather(bf16[1,224,128]{2,1,0:T(8,128)(2,1)} %param.13), channel_id=2, replica_groups=mesh['dp'=4,'ctx'=16,'tp'=4] {'ctx'}, dimensions={1}, use_global_device_ids=true | all-gather | bytes 974848 | tf_op jit(solution)/shard_map/all_gather | solution.py:114
  58.6 38.6 %all-gather.1 = bf16[1,3584,128]{2,1,0:T(8,128)(2,1)} all-gather(bf16[1,224,128]{2,1,0:T(8,128)(2,1)} %param.14), channel_id=3, replica_groups=mesh['dp'=4,'ctx'=16,'tp'=4] {'ctx'}, dimensions={1}, use_global_device_ids=true | all-gather | bytes 974848 | tf_op jit(solution)/shard_map/all_gather | solution.py:115
  97.2 25.0 %while.38 = (s32[]{:T(128)}, f32[1,8,224]{2,1,0:T(8,128)S(1)}, f32[224,1,8,128]{3,0,2,1:T(8,128)S(1)}, s32[16]{0:T(128)}, s32[224]{0:T(256)S(1)}, /*index=5*/s32...) while((s32[]{:T(128)}, f32[1,8,224]{2,1,0:T(8,128)S(1)}, ...), condition=%wide.region_8.9_spmd.clone, body=%wide.region_4.8_spmd.clone.sunk | while | flops 832858880 | bytes 16262702 | solution.py:107
  97.3 0.7 select_reduce_fusion.5
  98.1 0.2 compare_and_fusion.4
  98.4 2.7 fusion.107
  101.1 2.4 fusion.108
  103.5 0.7 select_reduce_fusion.5
  104.4 0.2 compare_and_fusion.4
  104.6 2.7 fusion.107
  107.3 2.4 fusion.108
  109.8 0.7 select_reduce_fusion.5
  110.9 2.7 fusion.107
  113.6 2.4 fusion.108
  116.0 0.7 select_reduce_fusion.5
  116.9 0.2 compare_and_fusion.4
  117.1 2.7 fusion.107
  119.8 2.4 fusion.108
  122.4 1.9 multiply_reduce_fusion
  124.3 1.4 broadcast.748.clone
  125.7 1.4 broadcast.748
  127.0 61.1 %while.39 = (s32[]{:T(128)}, f32[224,1,8,128]{3,0,2,1:T(8,128)S(1)}, f32[3584,128]{1,0:T(8,128)}, f32[3584,128]{1,0:T(8,128)}, bf16[3584,128]{1,0:T(8,128)(2,1)}...) while((s32[]{:T(128)}, ...), condition=%wide.region_13.14_spmd.clone, body=%wide.region_10.13_spmd.clone.sunk | while | flops 2072749056 | bytes 37587572 | solution.py:171
  127.1 0.8 select_reduce_fusion.6
  128.0 0.2 compare_and_fusion.5
  128.2 1.9 fusion.119
  130.1 3.8 fusion.123
  133.9 3.3 fusion.120
  137.2 2.3 fusion.121
  139.5 2.8 fusion.122
  142.3 0.8 select_reduce_fusion.6
  143.5 1.9 fusion.119
  145.4 3.8 fusion.123
  149.2 3.3 fusion.120
  152.5 2.3 fusion.121
  154.7 2.8 fusion.122
  157.6 0.8 select_reduce_fusion.6
  158.5 0.2 compare_and_fusion.5
  158.7 1.9 fusion.119
  160.7 3.8 fusion.123
  164.5 3.3 fusion.120
  167.8 2.3 fusion.121
  170.0 2.8 fusion.122
  172.9 0.8 select_reduce_fusion.6
  174.0 1.9 fusion.119
  176.0 3.8 fusion.123
  179.8 3.3 fusion.120
  183.0 2.3 fusion.121
  185.3 2.9 fusion.122
  188.2 2.5 convert_element_type.100
  190.8 2.5 convert_element_type.99
  193.4 84.3 %reduce-scatter.6.cloned.1.call-done = bf16[224,128]{1,0:T(8,128)(2,1)} async-done(((bf16[3584,128]{1,0:T(8,128)(2,1)}), bf16[224,128]{1,0:T(8,128)(2,1)}) %reduce-scatter.6.cloned.1.call-update) | async-done | bytes 57360 | tf_op jit(solution)/shard_map/reduce_scatter | solution.py:179
  277.7 10.3 %all_gather.17 = bf16[224,512]{1,0:T(8,128)(2,1)S(1)} all-gather(bf16[224,128]{1,0:T(8,128)(2,1)} %reduce-scatter.6.cloned.1.call-done), channel_id=1, replica_groups=mesh['dp'=4,'ctx'=16,'tp'=4] {'tp'}, dimensions={1}, use_global_device_ids=true | all-gather | bytes 286720 | tf_op jit(solution)/shard_map/all_gather | solution.py:192
  287.9 74.3 %reduce-scatter.4.cloned.1.call-done = bf16[224,128]{1,0:T(8,128)(2,1)} async-done(((bf16[3584,128]{1,0:T(8,128)(2,1)}), bf16[224,128]{1,0:T(8,128)(2,1)}) %reduce-scatter.4.cloned.1.call-update) | async-done | bytes 57360 | tf_op jit(solution)/shard_map/reduce_scatter | solution.py:176
  362.3 10.3 %all_gather.16 = bf16[224,512]{1,0:T(8,128)(2,1)S(1)} all-gather(bf16[224,128]{1,0:T(8,128)(2,1)} %reduce-scatter.4.cloned.1.call-done), channel_id=1, replica_groups=mesh['dp'=4,'ctx'=16,'tp'=4] {'tp'}, dimensions={1}, use_global_device_ids=true | all-gather | bytes 286720 | tf_op jit(solution)/shard_map/all_gather | solution.py:191
  372.6 4.5 fusion.75
  377.4 1.0 convert_element_type.98
  378.3 302.1 %reduce-scatter.8.cloned.1.call-done = f32[16,2048]{1,0:T(8,128)} async-done(((f32[1024,2048]{1,0:T(8,128)}), f32[16,2048]{1,0:T(8,128)}) %reduce-scatter.8.cloned.1.call-update) | async-done | bytes 131088 | tf_op jit(solution)/shard_map/reduce_scatter | solution.py:196
  (60 shorter events, 2.5 us)
Async XLA Ops:
  7.2 365.4 %copy-start = (bf16[1,224,2048]{2,1,0:T(8,128)(2,1)S(1)}, bf16[1,224,2048]{2,1,0:T(8,128)(2,1)}, u32[]{:S(2)}) copy-start(bf16[1,224,2048]{2,1,0:T(8,128)(2,1)} %param.11) | copy-start | bytes 2752516
  7.2 270.5 %reduce-scatter.6.cloned.1.call-start = ((), (), s32[]{:S(2)}) async-start(), calls=%async_computation.4 | async-start | bytes 974848 | tf_op jit(solution)/shard_map/reduce_scatter | solution.py:179
  12.0 0.8 copy-start.1
  127.0 3.1 copy-start.2
  142.3 3.1 copy-start.2
  157.6 3.1 copy-start.2
  172.9 3.1 copy-start.2
  190.7 171.6 %reduce-scatter.4.cloned.1.call-start = ((), (), s32[]{:S(2)}) async-start(), calls=%async_computation.3 | async-start | bytes 974848 | tf_op jit(solution)/shard_map/reduce_scatter | solution.py:176
  193.3 487.1 %reduce-scatter.8.cloned.1.call-start = ((), (), s32[]{:S(2)}) async-start(), calls=%async_computation.5 | async-start | bytes 8519680 | tf_op jit(solution)/shard_map/reduce_scatter | solution.py:196
Sparse Core Ops, SparseCore 0:
  190.8 86.7 reduce-scatter.5
  280.9 81.3 reduce-scatter.3
  377.2 303.1 reduce-scatter.7
where the time goes:
time: 688 us; the launch traced here: 687 us
  waiting for transfers between devices  461 us (67%)
  blocking collectives  104 us (15%)
  matrix products  81.3 us (12%)
  other arithmetic  18.5 us (3%)
  between operations  13.9 us (2%)
  local copies, waits for them, and re-layouts  7.91 us (1%)
    reduce_scatter x1, waiting for transfers between devices, per_device(): lax.psum_scatter(lax.dot_general(stacked, features, (((0,), (0,)), ((), (...  302 us
    reduce_scatter x1, waiting for transfers between devices, per_device(): lax.psum_scatter(value_buffer.astype(jnp.bfloat16), 'ctx', scatter_dimens...  84.3 us
    reduce_scatter x1, waiting for transfers between devices, per_device(): lax.psum_scatter(key_buffer.astype(jnp.bfloat16), 'ctx', scatter_dimensio...  74.3 us
    all_gather x1, blocking collectives, per_device(): backward_key_part = lax.all_gather(keys_in[0], 'ctx', axis=0, tiled=True)  45 us
    all_gather x1, blocking collectives, per_device(): lax.all_gather(values_in[0], 'ctx', axis=0, tiled=True)  38.6 us
    dot_general x8, matrix products, update(): jnp.einsum('qgrd,kgd->grqk', query_blk, key_blk, preferred_element_type=j...  18.5 us
    dot_general x4, matrix products, update(): jnp.einsum('grqk,qgrd->kgd', probabilities.astype(jnp.bfloat16), grad_out...  15.1 us
  transfers between devices with their start and end apart: 3, of which 3 were waited for; matrix products, arithmetic and copies ran while one was open for 1% of the time, Pallas kernels for 0%

commit v1 on v0

v1 whole, which is shorter than its diff:
```python
import functools

import jax
import jax.numpy as jnp
import numpy as np
from jax import lax
from jax.experimental import pallas as pl
from jax.experimental.pallas import tpu as pltpu
from jax.sharding import Mesh, PartitionSpec as P

DH = 128
HEADS = 8
HALF = 112
ROWS = 2 * HALF
LANES = HEADS * HALF
RANKS = 16
BLOCKS = 2 * RANKS
SEQ = ROWS * RANKS
DOCS = 6
MAX_DOC = 1194
SPAN = 256
STEPS = -(-(MAX_DOC - 1 + HALF) // SPAN)
PAD = SPAN
SCALE = DH**-0.5
LOG2E = 1.4426950408889634
MASKED = -1e30
CARDINAL = ("zh", "co", "zl", "y", "x")
SIZES = (2, 2, 4, 4, 4)
BF = jnp.bfloat16
F32 = jnp.float32


def dot(a, b, ca, cb):
    return lax.dot_general(a, b, (((ca,), (cb,)), ((), ())), preferred_element_type=F32)


def fold(x, op):
    return op(x.reshape(x.shape[0] // 8, 8, x.shape[1]), axis=0)


def attention_kernel(
    len_ref, perm_ref, where_ref, q_ref, do_ref, kv0, kv1, kv2, kv3, dq_ref, dkv_ref,
    kbuf, vbuf, dkacc, dvacc, s_scr, dp_scr, qs, dos,
):
    rank = where_ref[0]
    my_y = where_ref[1]
    kbuf[0:PAD, :] = jnp.zeros((PAD, DH), BF)
    vbuf[0:PAD, :] = jnp.zeros((PAD, DH), BF)
    for shift, ref in enumerate((kv0, kv1, kv2, kv3)):
        src_y = lax.rem(my_y + 4 - shift, 4)
        for zl in range(4):
            pair = perm_ref[zl * 4 + src_y]
            for half, block in enumerate((pair, BLOCKS - 1 - pair)):
                to = pl.ds(pl.multiple_of(PAD + block * HALF, 16), HALF)
                kbuf[to, :] = ref[zl, half * HALF : (half + 1) * HALF, 0:DH]
                vbuf[to, :] = ref[zl, half * HALF : (half + 1) * HALF, DH : 2 * DH]
    dkacc[...] = jnp.zeros_like(dkacc)
    dvacc[...] = jnp.zeros_like(dvacc)

    ends = []
    total = jnp.int32(0)
    for d in range(DOCS - 1):
        total = total + len_ref[d]
        ends.append(total)

    lane = lax.broadcasted_iota(jnp.int32, (1, LANES), 1)
    within = lane
    for h in range(1, HEADS):
        within = jnp.where(lane >= h * HALF, lane - h * HALF, within)

    def one_block(half, carry):
        pair = perm_ref[rank]
        block = jnp.where(half == 0, pair, BLOCKS - 1 - pair)
        row0 = pl.multiple_of(half * HALF, 16)
        for h in range(HEADS):
            qs[h * HALF : (h + 1) * HALF, :] = q_ref[pl.ds(row0, HALF), h * DH : (h + 1) * DH]
            dos[h * HALF : (h + 1) * HALF, :] = do_ref[pl.ds(row0, HALF), h * DH : (h + 1) * DH]
        first = block * HALF
        pos = within + first
        low = jnp.zeros_like(pos)
        low0 = jnp.int32(0)
        for end in ends:
            low = jnp.where(pos >= end, end, low)
            low0 = jnp.where(first >= end, end, low0)
        stop = first + HALF
        count = lax.div(stop - low0 + (SPAN - 1), SPAN)
        start = stop - count * SPAN

        def keys_at(t):
            return pl.ds(pl.multiple_of(PAD + start + t * SPAN, 16), SPAN)

        def kept_at(t):
            return pl.ds(pl.multiple_of(t * SPAN, SPAN), SPAN)

        def score(t, top):
            s = dot(kbuf[keys_at(t), :], qs[...], 1, 1)
            key = lax.broadcasted_iota(jnp.int32, (SPAN, LANES), 0) + (start + t * SPAN)
            s = jnp.where((key >= low) & (key <= pos), s * (SCALE * LOG2E), MASKED)
            s_scr[kept_at(t), :] = s
            return jnp.maximum(top, fold(s, jnp.max))

        top = lax.fori_loop(0, count, score, jnp.full((8, LANES), MASKED, F32))
        top = jnp.max(top, axis=0, keepdims=True)

        def weigh(t, sums):
            mass, moment = sums
            e = jnp.exp2(s_scr[kept_at(t), :] - top)
            dp = dot(vbuf[keys_at(t), :], dos[...], 1, 1)
            s_scr[kept_at(t), :] = e
            dp_scr[kept_at(t), :] = dp
            return mass + fold(e, jnp.sum), moment + fold(e * dp, jnp.sum)

        zero = jnp.zeros((8, LANES), F32)
        mass, moment = lax.fori_loop(0, count, weigh, (zero, zero))
        inverse = 1.0 / jnp.sum(mass, axis=0, keepdims=True)
        delta = jnp.sum(moment, axis=0, keepdims=True) * inverse

        def spread(t, dqt):
            p = s_scr[kept_at(t), :] * inverse
            g = (p * (dp_scr[kept_at(t), :] - delta)).astype(BF)
            at = keys_at(t)
            dvacc[at, :] += dot(p.astype(BF), dos[...], 1, 0)
            dkacc[at, :] += dot(g, qs[...], 1, 0)
            return dqt + dot(kbuf[at, :], g, 0, 0)

        dqt = lax.fori_loop(0, count, spread, jnp.zeros((DH, LANES), F32))
        dq = (dqt * SCALE).T.astype(BF)
        for h in range(HEADS):
            dq_ref[pl.ds(row0, HALF), h * DH : (h + 1) * DH] = dq[h * HALF : (h + 1) * HALF, :]
        return carry

    lax.fori_loop(0, 2, one_block, 0)

    for y in range(4):
        for zl in range(4):
            pair = perm_ref[zl * 4 + y]
            for half, block in enumerate((pair, BLOCKS - 1 - pair)):
                at = pl.ds(pl.multiple_of(PAD + block * HALF, 16), HALF)
                rows = slice(half * HALF, (half + 1) * HALF)
                dkv_ref[y, zl, rows, 0:DH] = (dkacc[at, :] * SCALE).astype(BF)
                dkv_ref[y, zl, rows, DH : 2 * DH] = dvacc[at, :].astype(BF)


def attention(lengths, perm, where, q, do, kvs):
    smem = pl.BlockSpec(memory_space=pltpu.SMEM)
    vmem = pl.BlockSpec(memory_space=pltpu.VMEM)
    return pl.pallas_call(
        attention_kernel,
        out_shape=(
            jax.ShapeDtypeStruct((ROWS, HEADS * DH), BF),
            jax.ShapeDtypeStruct((4, 4, ROWS, 2 * DH), BF),
        ),
        in_specs=[smem] * 3 + [vmem] * 6,
        out_specs=(vmem, vmem),
        scratch_shapes=[
            pltpu.VMEM((PAD + SEQ, DH), BF),
            pltpu.VMEM((PAD + SEQ, DH), BF),
            pltpu.VMEM((PAD + SEQ, DH), F32),
            pltpu.VMEM((PAD + SEQ, DH), F32),
            pltpu.VMEM((STEPS * SPAN, LANES), F32),
            pltpu.VMEM((STEPS * SPAN, LANES), F32),
            pltpu.VMEM((LANES, DH), BF),
            pltpu.VMEM((LANES, DH), BF),
        ],
        compiler_params=pltpu.CompilerParams(vmem_limit_bytes=44 * 2**20),
        cost_estimate=pl.CostEstimate(
            flops=6 * 10**9, bytes_accessed=6 * 10**6, transcendentals=3 * 10**6
        ),
    )(lengths, perm, where, q, do, *kvs)


def ring(shift):
    return [(i, (i + shift) % 4) for i in range(4)]


def total(x):
    return jnp.sum(x.astype(F32), axis=0)


def per_device(hidden_in, queries, keys_in, values_in, out_grad, doc_lengths, pair_perm):
    zl, y = lax.axis_index("zl"), lax.axis_index("y")
    where = jnp.stack([zl * 4 + y, y]).astype(jnp.int32)

    own = jnp.concatenate([keys_in[0], values_in[0]], axis=1)
    column = lax.all_gather(own, "zl", axis=0, tiled=False)
    kvs = [column] + [lax.ppermute(column, "y", ring(j)) for j in (1, 2, 3)]
    dq, dkv = attention(doc_lengths[0], pair_perm, where, queries[0], out_grad[0], kvs)

    part = total(lax.all_to_all(dkv, "y", 0, 0)).astype(BF)
    grads = total(lax.all_to_all(part, "zl", 0, 0)).astype(BF)

    core = lax.axis_index("co")
    swap = [(0, 1), (1, 0)]
    hidden = hidden_in[0].reshape(ROWS, 2, -1)
    mine = lax.dynamic_index_in_dim(hidden, core, 1, False)
    theirs = lax.ppermute(lax.dynamic_index_in_dim(hidden, 1 - core, 1, False), "co", swap)
    features = jnp.concatenate([mine, theirs], axis=0)
    stacked = lax.all_gather(grads, "x", axis=1, tiled=False)
    stacked = stacked.reshape(ROWS, 4, 2, DH).transpose(0, 2, 1, 3).reshape(ROWS, 8 * DH)
    both = jnp.concatenate([stacked, lax.ppermute(stacked, "co", swap)], axis=0)
    w = dot(both, features, 0, 0).astype(BF)
    cols = w.shape[1]
    w = w.reshape(2, 2, 4, 4, 16, cols).transpose(3, 2, 0, 1, 4, 5)
    w = total(lax.all_to_all(w, "y", 0, 0)).astype(BF)
    w = total(lax.all_to_all(w, "zl", 0, 0)).astype(BF)
    w = total(lax.all_to_all(w, "zh", 0, 0))
    keep = lax.dynamic_index_in_dim(w, core, 0, False)
    got = lax.ppermute(lax.dynamic_index_in_dim(w, 1 - core, 0, False), "co", swap)
    pair = jnp.stack([keep, got])
    first = lax.dynamic_index_in_dim(pair, core, 0, False)
    second = lax.dynamic_index_in_dim(pair, 1 - core, 0, False)
    grad_weight = jnp.concatenate([first, second], axis=1)
    return dq[None], grads[None, :, :DH], grads[None, :, DH:], grad_weight


def solution(mesh):
    fine = Mesh(mesh.devices.reshape(SIZES), CARDINAL)
    dp, ctx, tp = ("zh", "co"), ("zl", "y"), "x"
    tokens = P(dp, ctx, tp)
    return jax.shard_map(
        per_device,
        mesh=fine,
        in_specs=(tokens,) * 5 + (P(dp, None), P()),
        out_specs=(tokens,) * 3 + (P(dp + ctx, tp),),
        check_vma=False,
    )
```

time: 688 us -> 182 us (0.26)
  waiting for transfers between devices: 461 us -> 32.6 us
  matrix products: 81.3 us -> 2.31 us
  starting transfers between devices: 0.12 us -> 17.8 us
  other arithmetic: 18.5 us -> 3.4 us
  between operations: 13.9 us -> 0.74 us
  blocking collectives: 104 us -> 111 us
    reduce_scatter x3 -> x0, waiting for transfers between devices: 461 us -> none  [the longest x1 302 us: per_device(): lax.psum_scatter(lax.dot_general(stacked, features, (((0,), (0,)), ((), (...]
    all_to_all x0 -> x4, blocking collectives: none -> 85.3 us  [the longest x1 28.6 us: per_device(): w = total(lax.all_to_all(w, 'y', 0, 0)).astype(BF)]
    dot_general x29 -> x1, matrix products: 81.3 us -> 2.31 us  [dot(): lax.dot_general(a, b, (((ca,), (cb,)), ((), ())), preferred_element_type=...]
    all_gather x4 -> x2, blocking collectives: 104 us -> 26.2 us  [the longest x1 15.4 us: per_device(): column = lax.all_gather(own, 'zl', axis=0, tiled=False)]
    ppermute x0 -> x6, waiting for transfers between devices: none -> 24.2 us  [the longest x3 22.7 us: per_device(): kvs = [column] + [lax.ppermute(column, 'y', ring(j)) for j in (1, 2, 3)]]
    ppermute x0 -> x6, starting transfers between devices: none -> 11.8 us  [the longest x1 3.96 us: per_device(): both = jnp.concatenate([stacked, lax.ppermute(stacked, 'co', swap)], axis=0)]
    all_to_all x0 -> x1, waiting for transfers between devices: none -> 8.4 us  [per_device(): grads = total(lax.all_to_all(part, 'zl', 0, 0)).astype(BF)]
    reduce_sum x19 -> x5, other arithmetic: 9.49 us -> 1.77 us  [total(): return jnp.sum(x.astype(F32), axis=0)]
  transfers between devices with their start and end apart: 3 -> 7, of which waited for: 3 -> 6; matrix products, arithmetic and copies ran while one was open for 1% -> 2% of each run, Pallas kernels for 0% -> 0%
where the time goes in v1:
time: 182 us; the launch traced here: 183 us
  blocking collectives  111 us (61%)
  waiting for transfers between devices  32.6 us (18%)
  starting transfers between devices  17.8 us (10%)
  local copies, waits for them, and re-layouts  8.01 us (4%)
  Pallas kernels  6.43 us (4%)
  other arithmetic  3.4 us (2%)
  matrix products  2.31 us (1%)
    all_to_all x1, blocking collectives, per_device(): w = total(lax.all_to_all(w, 'y', 0, 0)).astype(BF)  28.6 us
    all_to_all x1, blocking collectives, per_device(): part = total(lax.all_to_all(dkv, 'y', 0, 0)).astype(BF)  27.4 us
    ppermute x3, waiting for transfers between devices, per_device(): kvs = [column] + [lax.ppermute(column, 'y', ring(j)) for j in (1, 2, 3)]  22.7 us
    all_to_all x1, blocking collectives, per_device(): w = total(lax.all_to_all(w, 'zl', 0, 0)).astype(BF)  16.2 us
    all_gather x1, blocking collectives, per_device(): column = lax.all_gather(own, 'zl', axis=0, tiled=False)  15.4 us
    all_to_all x1, blocking collectives, per_device(): w = total(lax.all_to_all(w, 'zh', 0, 0))  13.2 us
    all_gather x1, blocking collectives, per_device(): stacked = lax.all_gather(grads, 'x', axis=1, tiled=False)  10.8 us
    all_to_all x1, waiting for transfers between devices, per_device(): grads = total(lax.all_to_all(part, 'zl', 0, 0)).astype(BF)  8.4 us
  transfers between devices with their start and end apart: 7, of which 6 were waited for; matrix products, arithmetic and copies ran while one was open for 2% of the time, Pallas kernels for 0%

profile of v1, /device:TPU:1, one launch (start us, length us, event | category | flops | bytes accessed | tf_op | source)
XLA Modules:
  0.0 182.7 jit_solution(8040171712539819766)
XLA Ops:
  0.6 0.9 pad_maximum_fusion.1
  1.5 15.4 %all-gather = bf16[896,256]{1,0:T(8,128)(2,1)S(1)} all-gather(bf16[224,256]{1,0:T(8,128)(2,1)S(1)} %pad_maximum_fusion.1), channel_id=2, replica_groups=mesh['zh'=2,'co'=2,'zl'=4,'y'=4,'x'=4] {'zl'}, dimensions={0}, use_global_device_ids=true | all-gather | bytes 573440 | tf_op jit(solution)/shard_map/all_gather | solution.py:185
  16.9 2.7 %collective-permute-start.2 = (bf16[4,224,256]{2,1,0:T(8,128)(2,1)S(1)}, bf16[4,224,256]{2,1,0:T(8,128)(2,1)S(1)}, u32[]{:S(2)}, u32[]{:S(2)}) collective-permute-start(bf16[4,224,256]{2,1,0:T(8,128)(2,1)S(1)} %bitcast.33), channel_id=1, source_target_pairs={{0,12},{4,0},{8,4},{12,8},{1,13},{5,1},{9,5},{13,9},{2,14},{6,2},{... | collective-permute-start | bytes 1376264 | tf_op jit(solution)/shard_map/ppermute | solution.py:186
  19.7 0.3 collective-permute-start.1
  20.0 0.7 collective-permute-start
  20.7 0.1 pad_add_fusion.where_ref
  20.8 7.3 %collective-permute-done.2.kv3 = bf16[4,224,256]{2,1,0:T(8,128)(2,1)S(1)} collective-permute-done((bf16[4,224,256]{2,1,0:T(8,128)(2,1)S(1)}, bf16[4,224,256]{2,1,0:T(8,128)(2,1)S(1)}, u32[]{:S(2)}, u32[]{:S(2)}) %collective-permute-start.2) | collective-permute-done | bytes 458784 | tf_op jit(solution)/shard_map/ppermute | solution.py:186
  28.1 2.5 %collective-permute-done.1.kv2 = bf16[4,224,256]{2,1,0:T(8,128)(2,1)S(1)} collective-permute-done((bf16[4,224,256]{2,1,0:T(8,128)(2,1)S(1)}, bf16[4,224,256]{2,1,0:T(8,128)(2,1)S(1)}, u32[]{:S(2)}, u32[]{:S(2)}) %collective-permute-start.1) | collective-permute-done | bytes 458784 | tf_op jit(solution)/shard_map/ppermute | solution.py:186
  30.5 12.9 %collective-permute-done.kv1 = bf16[4,224,256]{2,1,0:T(8,128)(2,1)S(1)} collective-permute-done((bf16[4,224,256]{2,1,0:T(8,128)(2,1)S(1)}, bf16[4,224,256]{2,1,0:T(8,128)(2,1)S(1)}, u32[]{:S(2)}, u32[]{:S(2)}) %collective-permute-start) | collective-permute-done | bytes 458784 | tf_op jit(solution)/shard_map/ppermute | solution.py:186
  43.4 0.0 copy-start
  43.4 1.0 copy-done
  44.5 0.0 copy-start.1
  44.5 1.0 copy-done.1
  45.5 0.0 copy-start.2
  45.5 0.7 copy-done.2
  46.1 0.0 copy-start.3
  46.1 0.7 copy-done.3
  46.8 6.4 %shard_map.102 = (bf16[224,1024]{1,0:T(8,128)(2,1)}, bf16[4,4,224,256]{3,2,1,0:T(8,128)(2,1)S(1)}) custom-call(s32[6]{0:T(128)S(1)} %bitcast.39, s32[16]{0:T(128)S(1)} %copy-done.3, s32[2]{0:T(128)S(1)} %pad_add_fusion.where_ref, bf16[224,1024]{1,0:T(8,128)(2,1)S(1)} %bitcast.37, bf16[224,1024]{1,0:T(8,128)(2,1)S(1)} %bitcast.38, ...), custom_call_target="tpu_custom_call" | custom-call | flops 6000000000 | bytes 6000000 | tf_op jit(solution)/shard_map/pallas_call | solution.py:147
  53.2 27.4 %all_to_all.25 = bf16[4,4,224,256]{3,2,1,0:T(8,128)(2,1)S(1)} all-to-all(bf16[4,4,224,256]{3,2,1,0:T(8,128)(2,1)S(1)} %get-tuple-element.7), channel_id=1, replica_groups=mesh['zh'=2,'co'=2,'zl'=4,'y'=4,'x'=4] {'y'}, dimensions={0} | all-to-all | bytes 3670016 | tf_op jit(solution)/shard_map/all_to_all | solution.py:189
  80.6 0.0 copy-start.4
  80.6 1.2 reduce_sum.57
  81.7 5.9 %all-to-all-start.1 = ((bf16[4,224,256]{2,1,0:T(8,128)(2,1)}), bf16[4,224,256]{2,1,0:T(8,128)(2,1)S(1)}, u32[]{:S(2)}, u32[]{:S(2)}) async-start(bf16[4,224,256]{2,1,0:T(8,128)(2,1)} %reduce_sum.57), calls=%async_computation.1 | async-start | bytes 917504 | tf_op jit(solution)/shard_map/all_to_all | solution.py:190
  87.7 0.0 copy-done.4
  87.7 0.7 reshape_squeeze.3
  88.3 1.9 %constant_dynamic-slice_fusion.2 = (bf16[224,1,1024]{2,1,0:T(2,128)(2,1)S(1)}, bf16[224,1,1024]{2,1,0:T(2,128)(2,1)S(1)}) fusion(bf16[224,2,1024]{2,1,0:T(2,128)(2,1)S(1)} %reshape_squeeze.3, s32[]{:T(128)S(6)} %select_n.12, s32[]{:T(128)S(6)} %select_n.13), kind=kLoop, calls=%fused_computation.27 | loop fusion | bytes 1835016 | tf_op jit(solution)/shard_map/jit(dynamic_index_in_dim)/dynamic_slice | solution.py:195
  90.3 0.1 copy.32
  90.4 1.5 collective-permute-start.4
  91.9 8.4 %all-to-all-done.1 = bf16[4,224,256]{2,1,0:T(8,128)(2,1)S(1)} async-done(((bf16[4,224,256]{2,1,0:T(8,128)(2,1)}), bf16[4,224,256]{2,1,0:T(8,128)(2,1)S(1)}, u32[]{:S(2)}, u32[]{:S(2)}) %all-to-all-start.1) | async-done | bytes 458784 | tf_op jit(solution)/shard_map/all_to_all | solution.py:190
  100.3 0.1 reduce_sum.58
  100.3 10.8 %all-gather.1 = bf16[224,1024]{1,0:T(8,128)(2,1)S(1)} all-gather(bf16[224,256]{1,0:T(8,128)(2,1)S(1)} %reduce_sum.58), channel_id=3, replica_groups=mesh['zh'=2,'co'=2,'zl'=4,'y'=4,'x'=4] {'x'}, dimensions={1}, use_global_device_ids=true | all-gather | bytes 573440 | tf_op jit(solution)/shard_map/all_gather | solution.py:198
  111.1 0.3 reshape.17
  111.4 0.2 copy.34
  111.6 0.3 reshape.18
  111.9 4.0 %collective-permute-start.3 = (bf16[224,1024]{1,0:T(8,128)(2,1)S(1)}, bf16[224,1024]{1,0:T(8,128)(2,1)S(1)}, u32[]{:S(2)}, u32[]{:S(2)}) collective-permute-start(bf16[224,1024]{1,0:T(8,128)(2,1)S(1)} %reshape.18), channel_id=1, source_target_pairs={{0,64},{64,0},{1,65},{65,1},{2,66},{66,2},{3,67},{67,3},{4,68},{68... | collective-permute-start | bytes 1376264 | tf_op jit(solution)/shard_map/ppermute | solution.py:200
  115.9 0.1 copy.33
  116.0 0.0 collective-permute-done.4
  116.0 1.3 collective-permute-done.3
  117.3 2.3 %convolution_convert_fusion = bf16[1024,1024]{1,0:T(8,128)(2,1)S(1)} fusion(bf16[224,1024]{1,0:T(8,128)(2,1)S(1)} %collective-permute-done.3, bf16[224,1024]{1,0:T(8,128)(2,1)S(1)} %reshape.18, bf16[224,1024]{1,0:T(8,128)(2,1)} %collective-permute-done.4, bf16[224,1024]{1,0:T(8,128)(2,1)S(1)} %bitcast.44), kind=kOutput, calls=%fused_computation.1 | convolution fusion | flops 944242688 | bytes 3932160 | tf_op jit(solution)/shard_map/dot_general | solution.py:34
  119.6 0.3 copy.31
  119.9 28.6 %all_to_all.26 = bf16[4,4,2,2,16,1024]{5,4,1,3,2,0:T(8,128)(2,1)S(1)} all-to-all(bf16[4,4,2,2,16,1024]{5,4,1,3,2,0:T(8,128)(2,1)S(1)} %bitcast.40), channel_id=1, replica_groups=mesh['zh'=2,'co'=2,'zl'=4,'y'=4,'x'=4] {'y'}, dimensions={0} | all-to-all | bytes 4194304 | tf_op jit(solution)/shard_map/all_to_all | solution.py:204
  148.5 0.4 reduce_sum.59
  149.0 16.2 %all_to_all.27 = bf16[4,2,2,16,1024]{4,3,2,1,0:T(8,128)(2,1)S(1)} all-to-all(bf16[4,2,2,16,1024]{4,3,2,1,0:T(8,128)(2,1)S(1)} %copy.23), channel_id=1, replica_groups=mesh['zh'=2,'co'=2,'zl'=4,'y'=4,'x'=4] {'zl'}, dimensions={0} | all-to-all | bytes 1048576 | tf_op jit(solution)/shard_map/all_to_all | solution.py:205
  165.2 0.1 reduce_sum.60
  165.3 13.2 %all_to_all.28 = bf16[2,2,16,1024]{3,2,1,0:T(8,128)(2,1)S(1)} all-to-all(bf16[2,2,16,1024]{3,2,1,0:T(8,128)(2,1)S(1)} %reduce_sum.60), channel_id=1, replica_groups=mesh['zh'=2,'co'=2,'zl'=4,'y'=4,'x'=4] {'zh'}, dimensions={0} | all-to-all | bytes 262144 | tf_op jit(solution)/shard_map/all_to_all | solution.py:206
  178.5 2.7 %collective-permute-start.5 = (f32[16,1024]{1,0:T(8,128)S(1)}, f32[16,1024]{1,0:T(8,128)S(1)}, u32[]{:S(2)}, u32[]{:S(2)}) collective-permute-start(f32[16,1024]{1,0:T(8,128)S(1)} %get-tuple-element.12), channel_id=1, source_target_pairs={{0,64},{64,0},{1,65},{65,1},{2,66},{66,2},{3,67},{67,3},{4,68},{68... | collective-permute-start | bytes 196616 | tf_op jit(solution)/shard_map/ppermute | solution.py:208
  181.1 0.6 slice_bitcast_fusion
  181.8 0.3 collective-permute-done.5
  182.1 0.7 pad_maximum_fusion
  (4 shorter events, 0.1 us)
Async XLA Ops:
  16.9 11.2 %collective-permute-start.2 = (bf16[4,224,256]{2,1,0:T(8,128)(2,1)S(1)}, bf16[4,224,256]{2,1,0:T(8,128)(2,1)S(1)}, u32[]{:S(2)}, u32[]{:S(2)}) collective-permute-start(bf16[4,224,256]{2,1,0:T(8,128)(2,1)S(1)} %bitcast.33), channel_id=1, source_target_pairs={{0,12},{4,0},{8,4},{12,8},{1,13},{5,1},{9,5},{13,9},{2,14},{6,2},{... | collective-permute-start | bytes 1376264 | tf_op jit(solution)/shard_map/ppermute | solution.py:186
  19.7 10.9 %collective-permute-start.1 = (bf16[4,224,256]{2,1,0:T(8,128)(2,1)S(1)}, bf16[4,224,256]{2,1,0:T(8,128)(2,1)S(1)}, u32[]{:S(2)}, u32[]{:S(2)}) collective-permute-start(bf16[4,224,256]{2,1,0:T(8,128)(2,1)S(1)} %bitcast.34), channel_id=1, source_target_pairs={{0,8},{4,12},{8,0},{12,4},{1,9},{5,13},{9,1},{13,5},{2,10},{6,14},... | collective-permute-start | bytes 1376264 | tf_op jit(solution)/shard_map/ppermute | solution.py:186
  20.0 23.4 %collective-permute-start = (bf16[4,224,256]{2,1,0:T(8,128)(2,1)S(1)}, bf16[4,224,256]{2,1,0:T(8,128)(2,1)S(1)}, u32[]{:S(2)}, u32[]{:S(2)}) collective-permute-start(bf16[4,224,256]{2,1,0:T(8,128)(2,1)S(1)} %bitcast.35), channel_id=1, source_target_pairs={{0,4},{4,8},{8,12},{12,0},{1,5},{5,9},{9,13},{13,1},{2,6},{6,10},{... | collective-permute-start | bytes 1376264 | tf_op jit(solution)/shard_map/ppermute | solution.py:186
  43.4 1.0 copy-start
  44.5 1.0 copy-start.1
  45.5 0.7 copy-start.2
  46.1 0.7 copy-start.3
  80.6 7.1 %copy-start.4 = (bf16[1,224,2048]{2,1,0:T(8,128)(2,1)S(1)}, bf16[1,224,2048]{2,1,0:T(8,128)(2,1)}, u32[]{:S(2)}) copy-start(bf16[1,224,2048]{2,1,0:T(8,128)(2,1)} %param.7) | copy-start | bytes 2752516
  81.7 18.5 %all-to-all-start.1 = ((bf16[4,224,256]{2,1,0:T(8,128)(2,1)}), bf16[4,224,256]{2,1,0:T(8,128)(2,1)S(1)}, u32[]{:S(2)}, u32[]{:S(2)}) async-start(bf16[4,224,256]{2,1,0:T(8,128)(2,1)} %reduce_sum.57), calls=%async_computation.1 | async-start | bytes 917504 | tf_op jit(solution)/shard_map/all_to_all | solution.py:190
  90.4 25.6 %collective-permute-start.4 = (bf16[224,1024]{1,0:T(8,128)(2,1)S(1)}, bf16[224,1024]{1,0:T(8,128)(2,1)}, u32[]{:S(2)}, u32[]{:S(2)}) collective-permute-start(bf16[224,1024]{1,0:T(8,128)(2,1)S(1)} %bitcast.43), channel_id=1, source_target_pairs={{0,64},{64,0},{1,65},{65,1},{2,66},{66,2},{3,67},{67,3},{4,68},{68... | collective-permute-start | bytes 1376264 | tf_op jit(solution)/shard_map/ppermute | solution.py:196
  111.9 5.4 %collective-permute-start.3 = (bf16[224,1024]{1,0:T(8,128)(2,1)S(1)}, bf16[224,1024]{1,0:T(8,128)(2,1)S(1)}, u32[]{:S(2)}, u32[]{:S(2)}) collective-permute-start(bf16[224,1024]{1,0:T(8,128)(2,1)S(1)} %reshape.18), channel_id=1, source_target_pairs={{0,64},{64,0},{1,65},{65,1},{2,66},{66,2},{3,67},{67,3},{4,68},{68... | collective-permute-start | bytes 1376264 | tf_op jit(solution)/shard_map/ppermute | solution.py:200
  178.5 3.6 %collective-permute-start.5 = (f32[16,1024]{1,0:T(8,128)S(1)}, f32[16,1024]{1,0:T(8,128)S(1)}, u32[]{:S(2)}, u32[]{:S(2)}) collective-permute-start(f32[16,1024]{1,0:T(8,128)S(1)} %get-tuple-element.12), channel_id=1, source_target_pairs={{0,64},{64,0},{1,65},{65,1},{2,66},{66,2},{3,67},{67,3},{4,68},{68... | collective-permute-start | bytes 196616 | tf_op jit(solution)/shard_map/ppermute | solution.py:208

commit v2 on v1

--- a/solution.py
+++ b/solution.py
@@ -39,28 +39,46 @@
 
 
 def attention_kernel(
-    len_ref, perm_ref, where_ref, q_ref, do_ref, kv0, kv1, kv2, kv3, dq_ref, dkv_ref,
-    kbuf, vbuf, dkacc, dvacc, s_scr, dp_scr, qs, dos,
+    facts, q_hbm, do_hbm, kv0, kv1, kv2, kv3, dq_ref, out0, out1, out2, out3,
+    q_ref, do_ref, sems, kbuf, vbuf, dkacc, dvacc, s_scr, dp_scr, qs, dos,
 ):
-    rank = where_ref[0]
-    my_y = where_ref[1]
+    loads = [
+        pltpu.make_async_copy(q_hbm, q_ref, sems.at[0]),
+        pltpu.make_async_copy(do_hbm, do_ref, sems.at[1]),
+    ]
+    for load in loads:
+        load.start()
+
+    def len_of(d):
+        return facts[d]
+
+    def pair_of(rank):
+        return facts[DOCS + rank]
+
+    my_zl = facts[DOCS + RANKS]
+    my_y = facts[DOCS + RANKS + 1]
+
+    def place(pair, half):
+        block = pair if half == 0 else BLOCKS - 1 - pair
+        return pl.ds(pl.multiple_of(PAD + block * HALF, 16), HALF)
+
     kbuf[0:PAD, :] = jnp.zeros((PAD, DH), BF)
     vbuf[0:PAD, :] = jnp.zeros((PAD, DH), BF)
     for shift, ref in enumerate((kv0, kv1, kv2, kv3)):
         src_y = lax.rem(my_y + 4 - shift, 4)
-        for zl in range(4):
-            pair = perm_ref[zl * 4 + src_y]
-            for half, block in enumerate((pair, BLOCKS - 1 - pair)):
-                to = pl.ds(pl.multiple_of(PAD + block * HALF, 16), HALF)
-                kbuf[to, :] = ref[zl, half * HALF : (half + 1) * HALF, 0:DH]
-                vbuf[to, :] = ref[zl, half * HALF : (half + 1) * HALF, DH : 2 * DH]
+        for a in range(4):
+            pair = pair_of(lax.rem(my_zl + 4 - a, 4) * 4 + src_y)
+            for half in range(2):
+                rows = slice(half * HALF, (half + 1) * HALF)
+                kbuf[place(pair, half), :] = ref[a, rows, 0:DH]
+                vbuf[place(pair, half), :] = ref[a, rows, DH : 2 * DH]
     dkacc[...] = jnp.zeros_like(dkacc)
     dvacc[...] = jnp.zeros_like(dvacc)
 
     ends = []
     total = jnp.int32(0)
     for d in range(DOCS - 1):
-        total = total + len_ref[d]
+        total = total + len_of(d)
         ends.append(total)
 
     lane = lax.broadcasted_iota(jnp.int32, (1, LANES), 1)
@@ -68,8 +86,11 @@
     for h in range(1, HEADS):
         within = jnp.where(lane >= h * HALF, lane - h * HALF, within)
 
+    for load in loads:
+        load.wait()
+
     def one_block(half, carry):
-        pair = perm_ref[rank]
+        pair = pair_of(my_zl * 4 + my_y)
         block = jnp.where(half == 0, pair, BLOCKS - 1 - pair)
         row0 = pl.multiple_of(half * HALF, 16)
         for h in range(HEADS):
@@ -131,28 +152,30 @@
 
     lax.fori_loop(0, 2, one_block, 0)
 
-    for y in range(4):
-        for zl in range(4):
-            pair = perm_ref[zl * 4 + y]
-            for half, block in enumerate((pair, BLOCKS - 1 - pair)):
-                at = pl.ds(pl.multiple_of(PAD + block * HALF, 16), HALF)
+    for shift, ref in enumerate((out0, out1, out2, out3)):
+        y = lax.rem(my_y + shift, 4)
+        for a in range(4):
+            pair = pair_of(lax.rem(my_zl + a, 4) * 4 + y)
+            for half in range(2):
+                at = place(pair, half)
                 rows = slice(half * HALF, (half + 1) * HALF)
-                dkv_ref[y, zl, rows, 0:DH] = (dkacc[at, :] * SCALE).astype(BF)
-                dkv_ref[y, zl, rows, DH : 2 * DH] = dvacc[at, :].astype(BF)
-
-
-def attention(lengths, perm, where, q, do, kvs):
-    smem = pl.BlockSpec(memory_space=pltpu.SMEM)
+                ref[a, rows, 0:DH] = (dkacc[at, :] * SCALE).astype(BF)
+                ref[a, rows, DH : 2 * DH] = dvacc[at, :].astype(BF)
+
+
+def attention(facts, q, do, kvs):
     vmem = pl.BlockSpec(memory_space=pltpu.VMEM)
+    hbm = pl.BlockSpec(memory_space=pltpu.HBM)
     return pl.pallas_call(
         attention_kernel,
-        out_shape=(
-            jax.ShapeDtypeStruct((ROWS, HEADS * DH), BF),
-            jax.ShapeDtypeStruct((4, 4, ROWS, 2 * DH), BF),
-        ),
-        in_specs=[smem] * 3 + [vmem] * 6,
-        out_specs=(vmem, vmem),
+        out_shape=(jax.ShapeDtypeStruct((ROWS, HEADS * DH), BF),)
+        + (jax.ShapeDtypeStruct((4, ROWS, 2 * DH), BF),) * 4,
+        in_specs=[pl.BlockSpec(memory_space=pltpu.SMEM), hbm, hbm] + [vmem] * 4,
+        out_specs=(vmem,) * 5,
         scratch_shapes=[
+            pltpu.VMEM((ROWS, HEADS * DH), BF),
+            pltpu.VMEM((ROWS, HEADS * DH), BF),
+            pltpu.SemaphoreType.DMA((2,)),
             pltpu.VMEM((PAD + SEQ, DH), BF),
             pltpu.VMEM((PAD + SEQ, DH), BF),
             pltpu.VMEM((PAD + SEQ, DH), F32),
@@ -162,54 +185,82 @@
             pltpu.VMEM((LANES, DH), BF),
             pltpu.VMEM((LANES, DH), BF),
         ],
-        compiler_params=pltpu.CompilerParams(vmem_limit_bytes=44 * 2**20),
+        compiler_params=pltpu.CompilerParams(vmem_limit_bytes=40 * 2**20),
         cost_estimate=pl.CostEstimate(
             flops=6 * 10**9, bytes_accessed=6 * 10**6, transcendentals=3 * 10**6
         ),
-    )(lengths, perm, where, q, do, *kvs)
+    )(facts, q, do, *kvs)
 
 
 def ring(shift):
     return [(i, (i + shift) % 4) for i in range(4)]
 
 
-def total(x):
-    return jnp.sum(x.astype(F32), axis=0)
+def add_up(*xs):
+    return functools.reduce(lambda a, b: a + b, [x.astype(F32) for x in xs])
+
+
+def owner(v):
+    pairs = []
+    for index in np.ndindex(*SIZES):
+        zh, co, zl, y, x = index
+        target = (zh, x >> 1, (x & 1) * 2 + (zl & 1), (zl >> 1) * 2 + (v ^ co), y)
+        pairs.append(tuple(int(np.ravel_multi_index(i, SIZES)) for i in (index, target)))
+    return pairs
+
+
+def hidden_for_weight(hidden, core, y, x):
+    width = hidden.shape[1] // 2
+    run = width // 4
+    mine = lax.dynamic_slice_in_dim(hidden, core * width, width, 1)
+    theirs = lax.ppermute(
+        lax.dynamic_slice_in_dim(hidden, (1 - core) * width, width, 1), "co", [(0, 1), (1, 0)]
+    )
+    both = jnp.concatenate([mine, theirs], axis=0)
+    runs = []
+    for j in range(4):
+        chunk = lax.dynamic_slice_in_dim(both, lax.rem(x + j, 4) * run, run, 1)
+        runs.append(chunk if j == 0 else lax.ppermute(chunk, "x", ring(j)))
+    runs = jnp.stack(runs)
+    tokens = []
+    for s in range(4):
+        block = lax.dynamic_index_in_dim(runs, lax.rem(x - y - s + 8, 4), 0, False)
+        tokens.append(block if s == 0 else lax.ppermute(block, "y", ring(s)))
+    return lax.all_gather(jnp.concatenate(tokens, axis=0), "x", axis=0, tiled=False)
 
 
 def per_device(hidden_in, queries, keys_in, values_in, out_grad, doc_lengths, pair_perm):
-    zl, y = lax.axis_index("zl"), lax.axis_index("y")
-    where = jnp.stack([zl * 4 + y, y]).astype(jnp.int32)
-
-    own = jnp.concatenate([keys_in[0], values_in[0]], axis=1)
-    column = lax.all_gather(own, "zl", axis=0, tiled=False)
-    kvs = [column] + [lax.ppermute(column, "y", ring(j)) for j in (1, 2, 3)]
-    dq, dkv = attention(doc_lengths[0], pair_perm, where, queries[0], out_grad[0], kvs)
-
-    part = total(lax.all_to_all(dkv, "y", 0, 0)).astype(BF)
-    grads = total(lax.all_to_all(part, "zl", 0, 0)).astype(BF)
-
+    zl, y, x = (lax.axis_index(a) for a in ("zl", "y", "x"))
     core = lax.axis_index("co")
     swap = [(0, 1), (1, 0)]
-    hidden = hidden_in[0].reshape(ROWS, 2, -1)
-    mine = lax.dynamic_index_in_dim(hidden, core, 1, False)
-    theirs = lax.ppermute(lax.dynamic_index_in_dim(hidden, 1 - core, 1, False), "co", swap)
-    features = jnp.concatenate([mine, theirs], axis=0)
-    stacked = lax.all_gather(grads, "x", axis=1, tiled=False)
-    stacked = stacked.reshape(ROWS, 4, 2, DH).transpose(0, 2, 1, 3).reshape(ROWS, 8 * DH)
-    both = jnp.concatenate([stacked, lax.ppermute(stacked, "co", swap)], axis=0)
-    w = dot(both, features, 0, 0).astype(BF)
-    cols = w.shape[1]
-    w = w.reshape(2, 2, 4, 4, 16, cols).transpose(3, 2, 0, 1, 4, 5)
-    w = total(lax.all_to_all(w, "y", 0, 0)).astype(BF)
-    w = total(lax.all_to_all(w, "zl", 0, 0)).astype(BF)
-    w = total(lax.all_to_all(w, "zh", 0, 0))
-    keep = lax.dynamic_index_in_dim(w, core, 0, False)
-    got = lax.ppermute(lax.dynamic_index_in_dim(w, 1 - core, 0, False), "co", swap)
-    pair = jnp.stack([keep, got])
-    first = lax.dynamic_index_in_dim(pair, core, 0, False)
-    second = lax.dynamic_index_in_dim(pair, 1 - core, 0, False)
-    grad_weight = jnp.concatenate([first, second], axis=1)
+    facts = jnp.concatenate([doc_lengths[0], pair_perm, jnp.stack([zl, y]).astype(jnp.int32)])
+
+    own = jnp.concatenate([keys_in[0], values_in[0]], axis=1)
+    column = jnp.stack([own] + [lax.ppermute(own, "zl", ring(a)) for a in (1, 2, 3)])
+    kvs = [column] + [lax.ppermute(column, "y", ring(s)) for s in (1, 2, 3)]
+    hidden = hidden_for_weight(hidden_in[0], core, y, x)
+    dq, *dkv = attention(facts, queries[0], out_grad[0], kvs)
+
+    got = [dkv[0]] + [lax.ppermute(dkv[s], "y", ring(s)) for s in (1, 2, 3)]
+    parts = [add_up(*[g[a] for g in got]) for a in range(4)]
+    parts = [parts[0]] + [lax.ppermute(parts[a].astype(BF), "zl", ring(a)) for a in (1, 2, 3)]
+    grads = add_up(*parts).astype(BF)
+
+    rows = jnp.stack([grads] + [lax.ppermute(grads, "y", ring(s)) for s in (1, 2, 3)])
+    rows = jnp.stack([rows, lax.ppermute(rows, "co", swap)], axis=1)
+    rows = rows.reshape(8 * ROWS, 2 * DH)
+    w = lax.dot_general(rows, hidden, (((0,), (1,)), ((), ())), preferred_element_type=F32)
+    w = w.astype(BF).reshape(2, 2, 2, 32, -1).transpose(0, 2, 1, 3, 4).reshape(8, 32, -1)
+    w = lax.all_to_all(w, ("zh", "zl"), 0, 0)
+    w = jnp.sum(w.astype(F32), axis=0)
+    blocks = []
+    for v in range(2):
+        block = lax.dynamic_slice_in_dim(w, lax.rem(core + v, 2) * 16, 16, 0)
+        blocks.append(lax.ppermute(block, CARDINAL, owner(v)))
+    even = lax.rem(y, 2) == 0
+    left = jnp.where(even, blocks[0], blocks[1])
+    right = jnp.where(even, blocks[1], blocks[0])
+    grad_weight = jnp.concatenate([left, right], axis=1)
     return dq[None], grads[None, :, :DH], grads[None, :, DH:], grad_weight
 
 

time: 182 us -> 193 us (1.060)
  the two profiles are of different devices: /device:TPU:1 before, /device:TPU:25 now
where the time goes in v2:
time: 193 us; the launch traced here: 192 us
  waiting for transfers between devices  119 us (62%)
  starting transfers between devices  39.8 us (21%)
  between operations  14.2 us (7%)
  Pallas kernels  9.35 us (5%)
  local copies, waits for them, and re-layouts  3.64 us (2%)
  matrix products  3.17 us (2%)
  other arithmetic  2.59 us (1%)
    ppermute x3, waiting for transfers between devices, per_device(): kvs = [column] + [lax.ppermute(column, 'y', ring(s)) for s in (1, 2, 3)]  22.5 us
    ppermute x3, waiting for transfers between devices, per_device(): got = [dkv[0]] + [lax.ppermute(dkv[s], 'y', ring(s)) for s in (1, 2, 3)]  20.8 us
    all_to_all x1, waiting for transfers between devices, per_device(): w = lax.all_to_all(w, ('zh', 'zl'), 0, 0)  18 us
    ppermute x3, waiting for transfers between devices, hidden_for_weight(): runs.append(chunk if j == 0 else lax.ppermute(chunk, 'x', ring(j)))  12.8 us
    ppermute x3, waiting for transfers between devices, hidden_for_weight(): tokens.append(block if s == 0 else lax.ppermute(block, 'y', ring(s)))  10.2 us
    pallas_call x1, Pallas kernels, attention(): pl.pallas_call(attention_kernel, out_shape=(jax.ShapeDtypeStruct((ROWS, H...  9.35 us
    ppermute x3, waiting for transfers between devices, per_device(): lax.ppermute(own, 'zl', ring(a))  9.15 us
    ppermute x3, waiting for transfers between devices, per_device(): lax.ppermute(parts[a].astype(BF), 'zl', ring(a))  9.12 us
  transfers between devices with their start and end apart: 27, of which 20 were waited for; matrix products, arithmetic and copies ran while one was open for 1% of the time, Pallas kernels for 5%

profile of v2, /device:TPU:25, one launch (start us, length us, event | category | flops | bytes accessed | tf_op | source)
XLA Modules:
  0.0 191.9 jit_solution(16846100268587076054)
XLA Ops:
  7.2 0.0 all-gather.3.cloned.1.call-start
  7.2 1.2 dynamic-slice_bitcast_fusion
  8.4 0.8 collective-permute-start.16
  9.2 1.4 collective-permute-done.16
  10.6 0.1 fusion.2
  10.8 2.6 %collective-permute-start.19 = (bf16[448,256]{1,0:T(8,128)(2,1)S(1)}, bf16[448,256]{1,0:T(8,128)(2,1)S(1)}, u32[]{:S(2)}, u32[]{:S(2)}) collective-permute-start(bf16[448,256]{1,0:T(8,128)(2,1)S(1)} %get-tuple-element.24), channel_id=1, source_target_pairs={{0,3},{1,0},{2,1},{3,2},{4,7},{5,4},{6,5},{7,6},{8,11},{9,8},{10,9... | collective-permute-start | bytes 688136 | tf_op jit(solution)/shard_map/ppermute | solution.py:223
  13.3 0.5 collective-permute-start.18
  13.8 0.6 collective-permute-start.17
  14.5 8.3 %collective-permute-done.19 = bf16[448,256]{1,0:T(8,128)(2,1)S(1)} collective-permute-done((bf16[448,256]{1,0:T(8,128)(2,1)S(1)}, bf16[448,256]{1,0:T(8,128)(2,1)S(1)}, u32[]{:S(2)}, u32[]{:S(2)}) %collective-permute-start.19) | collective-permute-done | bytes 229408 | tf_op jit(solution)/shard_map/ppermute | solution.py:223
  22.7 4.6 %collective-permute-done.17 = bf16[448,256]{1,0:T(8,128)(2,1)S(1)} collective-permute-done((bf16[448,256]{1,0:T(8,128)(2,1)S(1)}, bf16[448,256]{1,0:T(8,128)(2,1)S(1)}, u32[]{:S(2)}, u32[]{:S(2)}) %collective-permute-start.17) | collective-permute-done | bytes 229408 | tf_op jit(solution)/shard_map/ppermute | solution.py:223
  27.3 0.1 pad_maximum_fusion.1
  27.4 0.1 dynamic-slice_bitcast_fusion.5
  27.5 0.5 collective-permute-start.22
  28.0 0.7 collective-permute-start.21
  28.7 1.9 collective-permute-start.20
  30.6 9.8 %collective-permute-done.22 = bf16[448,256]{1,0:T(8,128)(2,1)S(1)} collective-permute-done((bf16[448,256]{1,0:T(8,128)(2,1)S(1)}, bf16[448,256]{1,0:T(8,128)(2,1)S(1)}, u32[]{:S(2)}, u32[]{:S(2)}) %collective-permute-start.22) | collective-permute-done | bytes 229408 | tf_op jit(solution)/shard_map/ppermute | solution.py:228
  40.4 0.4 collective-permute-done.20
  40.8 1.0 pad_maximum_fusion.2
  41.9 4.4 %collective-permute-start.2 = (bf16[224,256]{1,0:T(8,128)(2,1)S(1)}, bf16[224,256]{1,0:T(8,128)(2,1)S(1)}, u32[]{:S(2)}, u32[]{:S(2)}) collective-permute-start(bf16[224,256]{1,0:T(8,128)(2,1)S(1)} %get-tuple-element.36), channel_id=1, source_target_pairs={{0,48},{16,0},{32,16},{48,32},{1,49},{17,1},{33,17},{49,33},{2,50}... | collective-permute-start | bytes 344072 | tf_op jit(solution)/shard_map/ppermute | solution.py:239
  46.3 0.4 collective-permute-start
  46.7 1.4 collective-permute-done.2
  48.1 7.7 %collective-permute-done.1 = bf16[224,256]{1,0:T(8,128)(2,1)S(1)} collective-permute-done((bf16[224,256]{1,0:T(8,128)(2,1)S(1)}, bf16[224,256]{1,0:T(8,128)(2,1)S(1)}, u32[]{:S(2)}, u32[]{:S(2)}) %collective-permute-start.1) | collective-permute-done | bytes 114720 | tf_op jit(solution)/shard_map/ppermute | solution.py:239
  55.8 0.1 pad_maximum_fusion.3.kv0
  55.9 4.1 %collective-permute-start.3 = (bf16[4,224,256]{2,1,0:T(8,128)(2,1)S(1)}, bf16[4,224,256]{2,1,0:T(8,128)(2,1)S(1)}, u32[]{:S(2)}, u32[]{:S(2)}) collective-permute-start(bf16[4,224,256]{2,1,0:T(8,128)(2,1)S(1)} %pad_maximum_fusion.3.kv0), channel_id=1, source_target_pairs={{0,4},{4,8},{8,12},{12,0},{1,5},{5,9},{9,13},{13,1},{2,6},{6,10},{... | collective-permute-start | bytes 1376264 | tf_op jit(solution)/shard_map/ppermute | solution.py:240
  59.9 0.7 collective-permute-start.5
  60.6 0.1 pad_add_fusion.facts
  60.7 17.8 %collective-permute-done.3.kv1 = bf16[4,224,256]{2,1,0:T(8,128)(2,1)S(1)} collective-permute-done((bf16[4,224,256]{2,1,0:T(8,128)(2,1)S(1)}, bf16[4,224,256]{2,1,0:T(8,128)(2,1)S(1)}, u32[]{:S(2)}, u32[]{:S(2)}) %collective-permute-start.3) | collective-permute-done | bytes 458784 | tf_op jit(solution)/shard_map/ppermute | solution.py:240
  78.5 4.7 %collective-permute-done.5.kv3 = bf16[4,224,256]{2,1,0:T(8,128)(2,1)S(1)} collective-permute-done((bf16[4,224,256]{2,1,0:T(8,128)(2,1)S(1)}, bf16[4,224,256]{2,1,0:T(8,128)(2,1)S(1)}, u32[]{:S(2)}, u32[]{:S(2)}) %collective-permute-start.5) | collective-permute-done | bytes 458784 | tf_op jit(solution)/shard_map/ppermute | solution.py:240
  83.2 9.4 %shard_map.102 = (bf16[224,1024]{1,0:T(8,128)(2,1)}, bf16[4,224,256]{2,1,0:T(8,128)(2,1)S(1)}, bf16[4,224,256]{2,1,0:T(8,128)(2,1)S(1)}, bf16[4,224,256]{2,1,0:T(8,128)(2,1)S(1)}, bf16[4,224,256]{2,1,0:T(8,128)(2,1)S(1)}) custom-call(s32[24]{0:T(128)S(1)} %pad_add_fusion.facts, bf16[224,1024]{1,0:T(8,128)(2,1)S(1)} %bitcast.63, ...), custom_call_target="tpu_custom_call" | custom-call | flops 6000000000 | bytes 6000000 | tf_op jit(solution)/shard_map/pallas_call | solution.py:169
  92.5 0.1 collective-permute-start.8
  92.6 2.9 %collective-permute-start.7 = (bf16[4,224,256]{2,1,0:T(8,128)(2,1)S(1)}, bf16[4,224,256]{2,1,0:T(8,128)(2,1)S(1)}, u32[]{:S(2)}, u32[]{:S(2)}) collective-permute-start(bf16[4,224,256]{2,1,0:T(8,128)(2,1)S(1)} %get-tuple-element.12), channel_id=1, source_target_pairs={{0,8},{4,12},{8,0},{12,4},{1,9},{5,13},{9,1},{13,5},{2,10},{6,14},... | collective-permute-start | bytes 1376264 | tf_op jit(solution)/shard_map/ppermute | solution.py:244
  95.5 9.6 %collective-permute-done.8 = bf16[4,224,256]{2,1,0:T(8,128)(2,1)S(1)} collective-permute-done((bf16[4,224,256]{2,1,0:T(8,128)(2,1)S(1)}, bf16[4,224,256]{2,1,0:T(8,128)(2,1)S(1)}, u32[]{:S(2)}, u32[]{:S(2)}) %collective-permute-start.8) | collective-permute-done | bytes 458784 | tf_op jit(solution)/shard_map/ppermute | solution.py:244
  105.1 11.2 %collective-permute-done.7 = bf16[4,224,256]{2,1,0:T(8,128)(2,1)S(1)} collective-permute-done((bf16[4,224,256]{2,1,0:T(8,128)(2,1)S(1)}, bf16[4,224,256]{2,1,0:T(8,128)(2,1)S(1)}, u32[]{:S(2)}, u32[]{:S(2)}) %collective-permute-start.7) | collective-permute-done | bytes 458784 | tf_op jit(solution)/shard_map/ppermute | solution.py:244
  116.3 0.2 fusion.8
  116.5 0.1 collective-permute-start.11
  116.6 0.2 collective-permute-start.10
  116.7 1.4 collective-permute-start.9
  118.1 2.3 %collective-permute-done.11 = bf16[224,256]{1,0:T(8,128)(2,1)S(1)} collective-permute-done((bf16[224,256]{1,0:T(8,128)(2,1)S(1)}, bf16[224,256]{1,0:T(8,128)(2,1)S(1)}, u32[]{:S(2)}, u32[]{:S(2)}) %collective-permute-start.11) | collective-permute-done | bytes 114720 | tf_op jit(solution)/shard_map/ppermute | solution.py:246
  120.4 6.8 %collective-permute-done.10 = bf16[224,256]{1,0:T(8,128)(2,1)S(1)} collective-permute-done((bf16[224,256]{1,0:T(8,128)(2,1)S(1)}, bf16[224,256]{1,0:T(8,128)(2,1)S(1)}, u32[]{:S(2)}, u32[]{:S(2)}) %collective-permute-start.10) | collective-permute-done | bytes 114720 | tf_op jit(solution)/shard_map/ppermute | solution.py:246
  127.2 0.1 fusion.7
  127.3 1.0 collective-permute-start.14
  128.3 2.4 %collective-permute-start.13 = (bf16[224,256]{1,0:T(8,128)(2,1)S(1)}, bf16[224,256]{1,0:T(8,128)(2,1)S(1)}, u32[]{:S(2)}, u32[]{:S(2)}) collective-permute-start(bf16[224,256]{1,0:T(8,128)(2,1)S(1)} %fusion.7), channel_id=1, source_target_pairs={{0,8},{4,12},{8,0},{12,4},{1,9},{5,13},{9,1},{13,5},{2,10},{6,14},... | collective-permute-start | bytes 344072 | tf_op jit(solution)/shard_map/ppermute | solution.py:249
  130.7 0.1 collective-permute-start.12
  130.8 1.5 collective-permute-done.14
  132.3 2.4 %collective-permute-done.13 = bf16[224,256]{1,0:T(8,128)(2,1)S(1)} collective-permute-done((bf16[224,256]{1,0:T(8,128)(2,1)S(1)}, bf16[224,256]{1,0:T(8,128)(2,1)S(1)}, u32[]{:S(2)}, u32[]{:S(2)}) %collective-permute-start.13) | collective-permute-done | bytes 114720 | tf_op jit(solution)/shard_map/ppermute | solution.py:249
  134.6 0.8 collective-permute-done.12
  135.4 0.1 fusion.12
  135.5 2.1 %collective-permute-start.15 = (bf16[4,224,256]{2,1,0:T(8,128)(2,1)S(1)}, bf16[4,224,256]{2,1,0:T(8,128)(2,1)S(1)}, u32[]{:S(2)}, u32[]{:S(2)}) collective-permute-start(bf16[4,224,256]{2,1,0:T(8,128)(2,1)S(1)} %get-tuple-element.28), channel_id=1, source_target_pairs={{0,64},{64,0},{1,65},{65,1},{2,66},{66,2},{3,67},{67,3},{4,68},{68... | collective-permute-start | bytes 1376264 | tf_op jit(solution)/shard_map/ppermute | solution.py:250
  137.6 1.4 collective-permute-done.15
  139.1 0.1 pad_maximum_fusion
  139.2 0.1 copy.11
  139.3 3.2 %convolution_convert_fusion = bf16[256,4,256]{2,0,1:T(8,128)(2,1)S(1)} fusion(bf16[1792,256,1]{1,0,2:T(8,128)(2,1)S(1)} %bitcast.67, bf16[4,1792,256]{2,1,0:T(8,128)(2,1)} %bitcast.81), kind=kOutput, calls=%fused_computation | convolution fusion | flops 939786240 | bytes 5111808 | tf_op jit(solution)/shard_map/dot_general | solution.py:252
  142.5 0.4 copy.13
  142.9 0.4 reshape.51
  143.2 0.8 copy.14
  144.1 8.2 %all-to-all-start = ((bf16[8,32,1024]{2,1,0:T(8,128)(2,1)}), bf16[8,32,1024]{2,1,0:T(8,128)(2,1)S(1)}, u32[]{:S(2)}, u32[]{:S(2)}) async-start(bf16[8,32,1024]{2,1,0:T(8,128)(2,1)} %bitcast.38), calls=%async_computation | async-start | bytes 1048576 | tf_op jit(solution)/shard_map/all_to_all | solution.py:254
  152.2 18.0 %all-to-all-done = bf16[8,32,1024]{2,1,0:T(8,128)(2,1)S(1)} async-done(((bf16[8,32,1024]{2,1,0:T(8,128)(2,1)}), bf16[8,32,1024]{2,1,0:T(8,128)(2,1)S(1)}, u32[]{:S(2)}, u32[]{:S(2)}) %all-to-all-start) | async-done | bytes 524320 | tf_op jit(solution)/shard_map/all_to_all | solution.py:254
  170.2 0.1 convert_reduce_fusion
  170.3 2.2 %collective-permute-start.23 = (f32[16,1024]{1,0:T(8,128)S(1)}, f32[16,1024]{1,0:T(8,128)S(1)}, u32[]{:S(2)}, u32[]{:S(2)}) collective-permute-start(f32[16,1024]{1,0:T(8,128)S(1)} %get-tuple-element.31), channel_id=1, source_target_pairs={{0,0},{1,32},{2,64},{3,96},{4,1},{5,33},{6,65},{7,97},{8,2},{9,34}... | collective-permute-start | bytes 196616 | tf_op jit(solution)/shard_map/ppermute | solution.py:259
  172.5 2.2 %collective-permute-start.24 = (f32[16,1024]{1,0:T(8,128)S(1)}, f32[16,1024]{1,0:T(8,128)S(1)}, u32[]{:S(2)}, u32[]{:S(2)}) collective-permute-start(f32[16,1024]{1,0:T(8,128)S(1)} %get-tuple-element.32), channel_id=1, source_target_pairs={{0,4},{1,36},{2,68},{3,100},{4,5},{5,37},{6,69},{7,101},{8,6},{9,3... | collective-permute-start | bytes 196616 | tf_op jit(solution)/shard_map/ppermute | solution.py:259
  174.7 0.6 slice_bitcast_fusion
  175.3 7.4 %collective-permute-done.23 = f32[16,1024]{1,0:T(8,128)S(1)} collective-permute-done((f32[16,1024]{1,0:T(8,128)S(1)}, f32[16,1024]{1,0:T(8,128)S(1)}, u32[]{:S(2)}, u32[]{:S(2)}) %collective-permute-start.23) | collective-permute-done | bytes 65568 | tf_op jit(solution)/shard_map/ppermute | solution.py:259
  182.7 1.7 collective-permute-done.24
  184.4 0.7 pad_maximum_fusion.5
  (26 shorter events, 0.1 us)
Async XLA Ops:
  7.2 132.1 %all-gather.3.cloned.1.call-start = ((), (), s32[]{:S(2)}) async-start(), calls=%async_computation.1 | async-start | bytes 4587520 | tf_op jit(solution)/shard_map/all_gather | solution.py:229
  8.4 2.2 %collective-permute-start.16 = (bf16[224,1024]{1,0:T(8,128)(2,1)S(1)}, bf16[224,1024]{1,0:T(8,128)(2,1)S(1)}, u32[]{:S(2)}, u32[]{:S(2)}) collective-permute-start(bf16[224,1024]{1,0:T(8,128)(2,1)S(1)} %get-tuple-element.25), channel_id=1, source_target_pairs={{0,64},{64,0},{1,65},{65,1},{2,66},{66,2},{3,67},{67,3},{4,68},{68... | collective-permute-start | bytes 1376264 | tf_op jit(solution)/shard_map/ppermute | solution.py:216
  10.8 11.9 %collective-permute-start.19 = (bf16[448,256]{1,0:T(8,128)(2,1)S(1)}, bf16[448,256]{1,0:T(8,128)(2,1)S(1)}, u32[]{:S(2)}, u32[]{:S(2)}) collective-permute-start(bf16[448,256]{1,0:T(8,128)(2,1)S(1)} %get-tuple-element.24), channel_id=1, source_target_pairs={{0,3},{1,0},{2,1},{3,2},{4,7},{5,4},{6,5},{7,6},{8,11},{9,8},{10,9... | collective-permute-start | bytes 688136 | tf_op jit(solution)/shard_map/ppermute | solution.py:223
  13.3 9.4 %collective-permute-start.18 = (bf16[448,256]{1,0:T(8,128)(2,1)S(1)}, bf16[448,256]{1,0:T(8,128)(2,1)S(1)}, u32[]{:S(2)}, u32[]{:S(2)}) collective-permute-start(bf16[448,256]{1,0:T(8,128)(2,1)S(1)} %get-tuple-element.23), channel_id=1, source_target_pairs={{0,2},{1,3},{2,0},{3,1},{4,6},{5,7},{6,4},{7,5},{8,10},{9,11},{10,... | collective-permute-start | bytes 688136 | tf_op jit(solution)/shard_map/ppermute | solution.py:223
  13.8 13.4 %collective-permute-start.17 = (bf16[448,256]{1,0:T(8,128)(2,1)S(1)}, bf16[448,256]{1,0:T(8,128)(2,1)S(1)}, u32[]{:S(2)}, u32[]{:S(2)}) collective-permute-start(bf16[448,256]{1,0:T(8,128)(2,1)S(1)} %get-tuple-element.22), channel_id=1, source_target_pairs={{0,1},{1,2},{2,3},{3,0},{4,5},{5,6},{6,7},{7,4},{8,9},{9,10},{10,1... | collective-permute-start | bytes 688136 | tf_op jit(solution)/shard_map/ppermute | solution.py:223
  27.5 14.3 %copy-start.2 = (bf16[1,224,128]{2,1,0:T(8,128)(2,1)S(1)}, bf16[1,224,128]{2,1,0:T(8,128)(2,1)}, u32[]{:S(2)}) copy-start(bf16[1,224,128]{2,1,0:T(8,128)(2,1)} %param.10) | copy-start | bytes 172036
  27.5 14.3 %copy-start.3 = (bf16[1,224,128]{2,1,0:T(8,128)(2,1)S(1)}, bf16[1,224,128]{2,1,0:T(8,128)(2,1)}, u32[]{:S(2)}) copy-start(bf16[1,224,128]{2,1,0:T(8,128)(2,1)} %param.9) | copy-start | bytes 172036
  27.5 12.9 %collective-permute-start.22 = (bf16[448,256]{1,0:T(8,128)(2,1)S(1)}, bf16[448,256]{1,0:T(8,128)(2,1)S(1)}, u32[]{:S(2)}, u32[]{:S(2)}) collective-permute-start(bf16[448,256]{1,0:T(8,128)(2,1)S(1)} %get-tuple-element.18), channel_id=1, source_target_pairs={{0,12},{4,0},{8,4},{12,8},{1,13},{5,1},{9,5},{13,9},{2,14},{6,2},{... | collective-permute-start | bytes 688136 | tf_op jit(solution)/shard_map/ppermute | solution.py:228
  28.0 12.3 %collective-permute-start.21 = (bf16[448,256]{1,0:T(8,128)(2,1)S(1)}, bf16[448,256]{1,0:T(8,128)(2,1)S(1)}, u32[]{:S(2)}, u32[]{:S(2)}) collective-permute-start(bf16[448,256]{1,0:T(8,128)(2,1)S(1)} %get-tuple-element.19), channel_id=1, source_target_pairs={{0,8},{4,12},{8,0},{12,4},{1,9},{5,13},{9,1},{13,5},{2,10},{6,14},... | collective-permute-start | bytes 688136 | tf_op jit(solution)/shard_map/ppermute | solution.py:228
  28.7 12.1 %collective-permute-start.20 = (bf16[448,256]{1,0:T(8,128)(2,1)S(1)}, bf16[448,256]{1,0:T(8,128)(2,1)S(1)}, u32[]{:S(2)}, u32[]{:S(2)}) collective-permute-start(bf16[448,256]{1,0:T(8,128)(2,1)S(1)} %get-tuple-element.20), channel_id=1, source_target_pairs={{0,4},{4,8},{8,12},{12,0},{1,5},{5,9},{9,13},{13,1},{2,6},{6,10},{... | collective-permute-start | bytes 688136 | tf_op jit(solution)/shard_map/ppermute | solution.py:228
  40.8 19.8 %copy-start.4 = (s32[16]{0:T(128)S(1)}, s32[16]{0:T(128)}, u32[]{:S(2)}) copy-start(s32[16]{0:T(128)} %param.13) | copy-start | bytes 196
  40.8 19.8 %copy-start.5 = (s32[1,6]{1,0:T(1,128)S(1)}, s32[1,6]{1,0:T(1,128)}, u32[]{:S(2)}) copy-start(s32[1,6]{1,0:T(1,128)} %param.12) | copy-start | bytes 76
  40.8 42.4 %copy-start = (bf16[1,224,1024]{2,1,0:T(8,128)(2,1)S(1)}, bf16[1,224,1024]{2,1,0:T(8,128)(2,1)}, u32[]{:S(2)}) copy-start(bf16[1,224,1024]{2,1,0:T(8,128)(2,1)} %param.8) | copy-start | bytes 1376260
  40.8 42.4 %copy-start.1 = (bf16[1,224,1024]{2,1,0:T(8,128)(2,1)S(1)}, bf16[1,224,1024]{2,1,0:T(8,128)(2,1)}, u32[]{:S(2)}) copy-start(bf16[1,224,1024]{2,1,0:T(8,128)(2,1)} %param.11) | copy-start | bytes 1376260
  41.9 6.2 %collective-permute-start.2 = (bf16[224,256]{1,0:T(8,128)(2,1)S(1)}, bf16[224,256]{1,0:T(8,128)(2,1)S(1)}, u32[]{:S(2)}, u32[]{:S(2)}) collective-permute-start(bf16[224,256]{1,0:T(8,128)(2,1)S(1)} %get-tuple-element.36), channel_id=1, source_target_pairs={{0,48},{16,0},{32,16},{48,32},{1,49},{17,1},{33,17},{49,33},{2,50}... | collective-permute-start | bytes 344072 | tf_op jit(solution)/shard_map/ppermute | solution.py:239
  46.3 9.5 %collective-permute-start.1 = (bf16[224,256]{1,0:T(8,128)(2,1)S(1)}, bf16[224,256]{1,0:T(8,128)(2,1)S(1)}, u32[]{:S(2)}, u32[]{:S(2)}) collective-permute-start(bf16[224,256]{1,0:T(8,128)(2,1)S(1)} %get-tuple-element.36), channel_id=1, source_target_pairs={{0,32},{16,48},{32,0},{48,16},{1,33},{17,49},{33,1},{49,17},{2,34}... | collective-permute-start | bytes 344072 | tf_op jit(solution)/shard_map/ppermute | solution.py:239
  46.3 9.5 %collective-permute-start = (bf16[224,256]{1,0:T(8,128)(2,1)S(1)}, bf16[224,256]{1,0:T(8,128)(2,1)S(1)}, u32[]{:S(2)}, u32[]{:S(2)}) collective-permute-start(bf16[224,256]{1,0:T(8,128)(2,1)S(1)} %get-tuple-element.36), channel_id=1, source_target_pairs={{0,16},{16,32},{32,48},{48,0},{1,17},{17,33},{33,49},{49,1},{2,18}... | collective-permute-start | bytes 344072 | tf_op jit(solution)/shard_map/ppermute | solution.py:239
  55.9 22.6 %collective-permute-start.3 = (bf16[4,224,256]{2,1,0:T(8,128)(2,1)S(1)}, bf16[4,224,256]{2,1,0:T(8,128)(2,1)S(1)}, u32[]{:S(2)}, u32[]{:S(2)}) collective-permute-start(bf16[4,224,256]{2,1,0:T(8,128)(2,1)S(1)} %pad_maximum_fusion.3.kv0), channel_id=1, source_target_pairs={{0,4},{4,8},{8,12},{12,0},{1,5},{5,9},{9,13},{13,1},{2,6},{6,10},{... | collective-permute-start | bytes 1376264 | tf_op jit(solution)/shard_map/ppermute | solution.py:240
  59.9 18.6 %collective-permute-start.4 = (bf16[4,224,256]{2,1,0:T(8,128)(2,1)S(1)}, bf16[4,224,256]{2,1,0:T(8,128)(2,1)S(1)}, u32[]{:S(2)}, u32[]{:S(2)}) collective-permute-start(bf16[4,224,256]{2,1,0:T(8,128)(2,1)S(1)} %pad_maximum_fusion.3.kv0), channel_id=1, source_target_pairs={{0,8},{4,12},{8,0},{12,4},{1,9},{5,13},{9,1},{13,5},{2,10},{6,14},... | collective-permute-start | bytes 1376264 | tf_op jit(solution)/shard_map/ppermute | solution.py:240
  59.9 23.2 %collective-permute-start.5 = (bf16[4,224,256]{2,1,0:T(8,128)(2,1)S(1)}, bf16[4,224,256]{2,1,0:T(8,128)(2,1)S(1)}, u32[]{:S(2)}, u32[]{:S(2)}) collective-permute-start(bf16[4,224,256]{2,1,0:T(8,128)(2,1)S(1)} %pad_maximum_fusion.3.kv0), channel_id=1, source_target_pairs={{0,12},{4,0},{8,4},{12,8},{1,13},{5,1},{9,5},{13,9},{2,14},{6,2},{... | collective-permute-start | bytes 1376264 | tf_op jit(solution)/shard_map/ppermute | solution.py:240
  92.5 12.6 %collective-permute-start.8 = (bf16[4,224,256]{2,1,0:T(8,128)(2,1)S(1)}, bf16[4,224,256]{2,1,0:T(8,128)(2,1)S(1)}, u32[]{:S(2)}, u32[]{:S(2)}) collective-permute-start(bf16[4,224,256]{2,1,0:T(8,128)(2,1)S(1)} %get-tuple-element.13), channel_id=1, source_target_pairs={{0,12},{4,0},{8,4},{12,8},{1,13},{5,1},{9,5},{13,9},{2,14},{6,2},{... | collective-permute-start | bytes 1376264 | tf_op jit(solution)/shard_map/ppermute | solution.py:244
  92.6 23.7 %collective-permute-start.7 = (bf16[4,224,256]{2,1,0:T(8,128)(2,1)S(1)}, bf16[4,224,256]{2,1,0:T(8,128)(2,1)S(1)}, u32[]{:S(2)}, u32[]{:S(2)}) collective-permute-start(bf16[4,224,256]{2,1,0:T(8,128)(2,1)S(1)} %get-tuple-element.12), channel_id=1, source_target_pairs={{0,8},{4,12},{8,0},{12,4},{1,9},{5,13},{9,1},{13,5},{2,10},{6,14},... | collective-permute-start | bytes 1376264 | tf_op jit(solution)/shard_map/ppermute | solution.py:244
  95.5 20.8 %collective-permute-start.6 = (bf16[4,224,256]{2,1,0:T(8,128)(2,1)S(1)}, bf16[4,224,256]{2,1,0:T(8,128)(2,1)S(1)}, u32[]{:S(2)}, u32[]{:S(2)}) collective-permute-start(bf16[4,224,256]{2,1,0:T(8,128)(2,1)S(1)} %get-tuple-element.11), channel_id=1, source_target_pairs={{0,4},{4,8},{8,12},{12,0},{1,5},{5,9},{9,13},{13,1},{2,6},{6,10},{... | collective-permute-start | bytes 1376264 | tf_op jit(solution)/shard_map/ppermute | solution.py:244
  116.5 4.0 %collective-permute-start.11 = (bf16[224,256]{1,0:T(8,128)(2,1)S(1)}, bf16[224,256]{1,0:T(8,128)(2,1)S(1)}, u32[]{:S(2)}, u32[]{:S(2)}) collective-permute-start(bf16[224,256]{1,0:T(8,128)(2,1)S(1)} %get-tuple-element.15), channel_id=1, source_target_pairs={{0,48},{16,0},{32,16},{48,32},{1,49},{17,1},{33,17},{49,33},{2,50}... | collective-permute-start | bytes 344072 | tf_op jit(solution)/shard_map/ppermute | solution.py:246
  116.6 10.7 %collective-permute-start.10 = (bf16[224,256]{1,0:T(8,128)(2,1)S(1)}, bf16[224,256]{1,0:T(8,128)(2,1)S(1)}, u32[]{:S(2)}, u32[]{:S(2)}) collective-permute-start(bf16[224,256]{1,0:T(8,128)(2,1)S(1)} %get-tuple-element.16), channel_id=1, source_target_pairs={{0,32},{16,48},{32,0},{48,16},{1,33},{17,49},{33,1},{49,17},{2,34}... | collective-permute-start | bytes 344072 | tf_op jit(solution)/shard_map/ppermute | solution.py:246
  116.7 10.5 %collective-permute-start.9 = (bf16[224,256]{1,0:T(8,128)(2,1)S(1)}, bf16[224,256]{1,0:T(8,128)(2,1)S(1)}, u32[]{:S(2)}, u32[]{:S(2)}) collective-permute-start(bf16[224,256]{1,0:T(8,128)(2,1)S(1)} %get-tuple-element.14), channel_id=1, source_target_pairs={{0,16},{16,32},{32,48},{48,0},{1,17},{17,33},{33,49},{49,1},{2,18}... | collective-permute-start | bytes 344072 | tf_op jit(solution)/shard_map/ppermute | solution.py:246
  127.3 4.9 %collective-permute-start.14 = (bf16[224,256]{1,0:T(8,128)(2,1)S(1)}, bf16[224,256]{1,0:T(8,128)(2,1)S(1)}, u32[]{:S(2)}, u32[]{:S(2)}) collective-permute-start(bf16[224,256]{1,0:T(8,128)(2,1)S(1)} %fusion.7), channel_id=1, source_target_pairs={{0,12},{4,0},{8,4},{12,8},{1,13},{5,1},{9,5},{13,9},{2,14},{6,2},{... | collective-permute-start | bytes 344072 | tf_op jit(solution)/shard_map/ppermute | solution.py:249
  128.3 6.3 %collective-permute-start.13 = (bf16[224,256]{1,0:T(8,128)(2,1)S(1)}, bf16[224,256]{1,0:T(8,128)(2,1)S(1)}, u32[]{:S(2)}, u32[]{:S(2)}) collective-permute-start(bf16[224,256]{1,0:T(8,128)(2,1)S(1)} %fusion.7), channel_id=1, source_target_pairs={{0,8},{4,12},{8,0},{12,4},{1,9},{5,13},{9,1},{13,5},{2,10},{6,14},... | collective-permute-start | bytes 344072 | tf_op jit(solution)/shard_map/ppermute | solution.py:249
  130.7 4.7 %collective-permute-start.12 = (bf16[224,256]{1,0:T(8,128)(2,1)S(1)}, bf16[224,256]{1,0:T(8,128)(2,1)S(1)}, u32[]{:S(2)}, u32[]{:S(2)}) collective-permute-start(bf16[224,256]{1,0:T(8,128)(2,1)S(1)} %fusion.7), channel_id=1, source_target_pairs={{0,4},{4,8},{8,12},{12,0},{1,5},{5,9},{9,13},{13,1},{2,6},{6,10},{... | collective-permute-start | bytes 344072 | tf_op jit(solution)/shard_map/ppermute | solution.py:249
  135.5 3.6 %collective-permute-start.15 = (bf16[4,224,256]{2,1,0:T(8,128)(2,1)S(1)}, bf16[4,224,256]{2,1,0:T(8,128)(2,1)S(1)}, u32[]{:S(2)}, u32[]{:S(2)}) collective-permute-start(bf16[4,224,256]{2,1,0:T(8,128)(2,1)S(1)} %get-tuple-element.28), channel_id=1, source_target_pairs={{0,64},{64,0},{1,65},{65,1},{2,66},{66,2},{3,67},{67,3},{4,68},{68... | collective-permute-start | bytes 1376264 | tf_op jit(solution)/shard_map/ppermute | solution.py:250
  144.1 26.1 %all-to-all-start = ((bf16[8,32,1024]{2,1,0:T(8,128)(2,1)}), bf16[8,32,1024]{2,1,0:T(8,128)(2,1)S(1)}, u32[]{:S(2)}, u32[]{:S(2)}) async-start(bf16[8,32,1024]{2,1,0:T(8,128)(2,1)} %bitcast.38), calls=%async_computation | async-start | bytes 1048576 | tf_op jit(solution)/shard_map/all_to_all | solution.py:254
  170.3 12.4 %collective-permute-start.23 = (f32[16,1024]{1,0:T(8,128)S(1)}, f32[16,1024]{1,0:T(8,128)S(1)}, u32[]{:S(2)}, u32[]{:S(2)}) collective-permute-start(f32[16,1024]{1,0:T(8,128)S(1)} %get-tuple-element.31), channel_id=1, source_target_pairs={{0,0},{1,32},{2,64},{3,96},{4,1},{5,33},{6,65},{7,97},{8,2},{9,34}... | collective-permute-start | bytes 196616 | tf_op jit(solution)/shard_map/ppermute | solution.py:259
  172.5 11.9 %collective-permute-start.24 = (f32[16,1024]{1,0:T(8,128)S(1)}, f32[16,1024]{1,0:T(8,128)S(1)}, u32[]{:S(2)}, u32[]{:S(2)}) collective-permute-start(f32[16,1024]{1,0:T(8,128)S(1)} %get-tuple-element.32), channel_id=1, source_target_pairs={{0,4},{1,36},{2,68},{3,100},{4,5},{5,37},{6,69},{7,101},{8,6},{9,3... | collective-permute-start | bytes 196616 | tf_op jit(solution)/shard_map/ppermute | solution.py:259
Sparse Core Ops, SparseCore 0:
  41.9 47.6 all-gather.2

commit v3 on v2

--- a/solution.py
+++ b/solution.py
@@ -204,41 +204,71 @@
     pairs = []
     for index in np.ndindex(*SIZES):
         zh, co, zl, y, x = index
-        target = (zh, x >> 1, (x & 1) * 2 + (zl & 1), (zl >> 1) * 2 + (v ^ co), y)
+        target = (zh, x >> 1, (x & 1) * 2 + (v ^ co), y, zl)
         pairs.append(tuple(int(np.ravel_multi_index(i, SIZES)) for i in (index, target)))
     return pairs
 
 
-def hidden_for_weight(hidden, core, y, x):
-    width = hidden.shape[1] // 2
-    run = width // 4
-    mine = lax.dynamic_slice_in_dim(hidden, core * width, width, 1)
-    theirs = lax.ppermute(
-        lax.dynamic_slice_in_dim(hidden, (1 - core) * width, width, 1), "co", [(0, 1), (1, 0)]
-    )
-    both = jnp.concatenate([mine, theirs], axis=0)
+def product_kernel(facts, hidden, *refs):
+    rows, outs, acc = refs[:-5], refs[-5:-1], refs[-1]
+    my_y = facts[DOCS + RANKS + 1]
+    for run in range(4):
+        total = None
+        for i, piece in enumerate(rows):
+            tokens = hidden[run, i * ROWS * 4 : (i + 1) * ROWS * 4, :]
+            part = dot(piece[...].reshape(4 * ROWS, 2 * DH), tokens, 0, 0)
+            total = part if total is None else total + part
+        acc[...] = total
+        for shift, out in enumerate(outs):
+            y = lax.rem(my_y + shift, 4)
+            for block in range(4):
+                at = pl.ds(pl.multiple_of(block * 64 + y * 16, 16), 16)
+                out[block, :, run * 256 : (run + 1) * 256] = acc[at, :].astype(BF)
+
+
+def weight_product(facts, hidden, rows):
+    vmem = pl.BlockSpec(memory_space=pltpu.VMEM)
+    return pl.pallas_call(
+        product_kernel,
+        out_shape=(jax.ShapeDtypeStruct((4, 16, 1024), BF),) * 4,
+        in_specs=[pl.BlockSpec(memory_space=pltpu.SMEM)] + [vmem] * (1 + len(rows)),
+        out_specs=(vmem,) * 4,
+        scratch_shapes=[pltpu.VMEM((2 * DH, 256), F32)],
+        compiler_params=pltpu.CompilerParams(vmem_limit_bytes=24 * 2**20),
+        cost_estimate=pl.CostEstimate(flops=10**9, bytes_accessed=6 * 10**6, transcendentals=0),
+    )(facts, hidden, *rows)
+
+
+def per_device(hidden_in, queries, keys_in, values_in, out_grad, doc_lengths, pair_perm):
+    zl, y, x = (lax.axis_index(a) for a in ("zl", "y", "x"))
+    zh, core = lax.axis_index("zh"), lax.axis_index("co")
+    swap = [(0, 1), (1, 0)]
+    facts = jnp.concatenate([doc_lengths[0], pair_perm, jnp.stack([zl, y]).astype(jnp.int32)])
+
+    own = jnp.concatenate([keys_in[0], values_in[0]], axis=1)
+    column = [own] + [lax.ppermute(own, "zl", ring(a)) for a in (1, 2, 3)]
+    halves = hidden_in[0].reshape(ROWS, 2, 4, -1)
     runs = []
     for j in range(4):
-        chunk = lax.dynamic_slice_in_dim(both, lax.rem(x + j, 4) * run, run, 1)
-        runs.append(chunk if j == 0 else lax.ppermute(chunk, "x", ring(j)))
-    runs = jnp.stack(runs)
+        run = lax.dynamic_index_in_dim(halves, lax.rem(x + j, 4), 2, False)
+        run = run.transpose(1, 0, 2)
+        runs.append(run if j == 0 else lax.ppermute(run, "x", ring(j)))
+    column, runs = lax.optimization_barrier((column, runs))
+
+    column, runs = jnp.stack(column), jnp.stack(runs)
+    kvs = [column] + [lax.ppermute(column, "y", ring(s)) for s in (1, 2, 3)]
     tokens = []
     for s in range(4):
-        block = lax.dynamic_index_in_dim(runs, lax.rem(x - y - s + 8, 4), 0, False)
-        tokens.append(block if s == 0 else lax.ppermute(block, "y", ring(s)))
-    return lax.all_gather(jnp.concatenate(tokens, axis=0), "x", axis=0, tiled=False)
-
-
-def per_device(hidden_in, queries, keys_in, values_in, out_grad, doc_lengths, pair_perm):
-    zl, y, x = (lax.axis_index(a) for a in ("zl", "y", "x"))
-    core = lax.axis_index("co")
-    swap = [(0, 1), (1, 0)]
-    facts = jnp.concatenate([doc_lengths[0], pair_perm, jnp.stack([zl, y]).astype(jnp.int32)])
-
-    own = jnp.concatenate([keys_in[0], values_in[0]], axis=1)
-    column = jnp.stack([own] + [lax.ppermute(own, "zl", ring(a)) for a in (1, 2, 3)])
-    kvs = [column] + [lax.ppermute(column, "y", ring(s)) for s in (1, 2, 3)]
-    hidden = hidden_for_weight(hidden_in[0], core, y, x)
+        block = lax.dynamic_index_in_dim(runs, lax.rem(x - zl - s + 8, 4), 0, False)
+        tokens.append(block if s == 0 else lax.ppermute(block, "zl", ring(s)))
+    kvs, tokens = lax.optimization_barrier((kvs, tokens))
+
+    tokens = jnp.stack(tokens)
+    mine = lax.dynamic_index_in_dim(tokens, core, 1, False)
+    theirs = lax.ppermute(lax.dynamic_index_in_dim(tokens, 1 - core, 1, False), "co", swap)
+    hidden = jnp.concatenate([mine.reshape(4 * ROWS, -1), theirs.reshape(4 * ROWS, -1)], axis=0)
+    hidden = lax.all_gather(hidden, "x", axis=0, tiled=False)
+
     dq, *dkv = attention(facts, queries[0], out_grad[0], kvs)
 
     got = [dkv[0]] + [lax.ppermute(dkv[s], "y", ring(s)) for s in (1, 2, 3)]
@@ -246,18 +276,19 @@
     parts = [parts[0]] + [lax.ppermute(parts[a].astype(BF), "zl", ring(a)) for a in (1, 2, 3)]
     grads = add_up(*parts).astype(BF)
 
-    rows = jnp.stack([grads] + [lax.ppermute(grads, "y", ring(s)) for s in (1, 2, 3)])
-    rows = jnp.stack([rows, lax.ppermute(rows, "co", swap)], axis=1)
-    rows = rows.reshape(8 * ROWS, 2 * DH)
-    w = lax.dot_general(rows, hidden, (((0,), (1,)), ((), ())), preferred_element_type=F32)
-    w = w.astype(BF).reshape(2, 2, 2, 32, -1).transpose(0, 2, 1, 3, 4).reshape(8, 32, -1)
-    w = lax.all_to_all(w, ("zh", "zl"), 0, 0)
-    w = jnp.sum(w.astype(F32), axis=0)
+    rows = jnp.stack([grads] + [lax.ppermute(grads, "zl", ring(s)) for s in (1, 2, 3)])
+    rows = (rows, lax.ppermute(rows, "co", swap))
+    shares = weight_product(facts, hidden, rows)
+    shares = [shares[0]] + [lax.ppermute(shares[s], "y", ring(s)) for s in (1, 2, 3)]
+    share = add_up(*shares).reshape(2, 2, 16, -1)
+    kept = lax.dynamic_index_in_dim(share, zh, 0, False)
+    sent = lax.dynamic_index_in_dim(share, 1 - zh, 0, False).astype(BF)
+    share = kept + lax.ppermute(sent, "zh", swap).astype(F32)
     blocks = []
     for v in range(2):
-        block = lax.dynamic_slice_in_dim(w, lax.rem(core + v, 2) * 16, 16, 0)
+        block = lax.dynamic_index_in_dim(share, lax.rem(core + v, 2), 0, False)
         blocks.append(lax.ppermute(block, CARDINAL, owner(v)))
-    even = lax.rem(y, 2) == 0
+    even = lax.rem(zl, 2) == 0
     left = jnp.where(even, blocks[0], blocks[1])
     right = jnp.where(even, blocks[1], blocks[0])
     grad_weight = jnp.concatenate([left, right], axis=1)

time: 193 us -> 166 us (0.86)
  the two profiles are of different devices: /device:TPU:25 before, /device:TPU:1 now
where the time goes in v3:
time: 166 us; the launch traced here: 164 us
  waiting for transfers between devices  77.2 us (47%)
  starting transfers between devices  49 us (30%)
  between operations  14.3 us (9%)
  Pallas kernels  12.6 us (8%)
  local copies, waits for them, and re-layouts  7.38 us (4%)
  other arithmetic  3.32 us (2%)
    ppermute x3, waiting for transfers between devices, per_device(): got = [dkv[0]] + [lax.ppermute(dkv[s], 'y', ring(s)) for s in (1, 2, 3)]  22.6 us
    pallas_call x1, Pallas kernels, attention(): pl.pallas_call(attention_kernel, out_shape=(jax.ShapeDtypeStruct((ROWS, H...  10.6 us
    ppermute x3, waiting for transfers between devices, per_device(): tokens.append(block if s == 0 else lax.ppermute(block, 'zl', ring(s)))  10.4 us
    ppermute x1, starting transfers between devices, per_device(): share = kept + lax.ppermute(sent, 'zh', swap).astype(F32)  9.13 us
    ppermute x3, waiting for transfers between devices, per_device(): lax.ppermute(grads, 'zl', ring(s))  9.01 us
    ppermute x3, waiting for transfers between devices, per_device(): lax.ppermute(parts[a].astype(BF), 'zl', ring(a))  8.86 us
    ppermute x3, waiting for transfers between devices, per_device(): lax.ppermute(shares[s], 'y', ring(s))  7.79 us
    ppermute x3, starting transfers between devices, per_device(): column = [own] + [lax.ppermute(own, 'zl', ring(a)) for a in (1, 2, 3)]  6.26 us
  transfers between devices with their start and end apart: 30, of which 19 were waited for; matrix products, arithmetic and copies ran while one was open for 3% of the time, Pallas kernels for 6%

profile of v3, /device:TPU:1, one launch (start us, length us, event | category | flops | bytes accessed | tf_op | source)
XLA Modules:
  0.0 163.8 jit_solution(3980823990251021632)
XLA Ops:
  7.2 0.9 pad_maximum_fusion.6
  8.1 2.5 %collective-permute-start = (bf16[224,256]{1,0:T(8,128)(2,1)S(1)}, bf16[224,256]{1,0:T(8,128)(2,1)S(1)}, u32[]{:S(2)}, u32[]{:S(2)}) collective-permute-start(bf16[224,256]{1,0:T(8,128)(2,1)S(1)} %pad_maximum_fusion.6), channel_id=1, source_target_pairs={{0,16},{16,32},{32,48},{48,0},{1,17},{17,33},{33,49},{49,1},{2,18}... | collective-permute-start | bytes 344072 | tf_op jit(solution)/shard_map/ppermute | solution.py:249
  10.6 2.5 %reshape_squeeze.3 = bf16[224,2,4,256]{3,2,1,0:T(4,128)(2,1)S(1)} reshape(bf16[1,224,2048]{2,1,0:T(8,128)(2,1)} %param.7) | data formatting | bytes 1835008 | tf_op jit(solution)/shard_map/reshape;squeeze | solution.py:250
  13.1 1.9 %constant_dynamic-slice_fusion.1 = (bf16[224,2,1,256]{3,2,1,0:T(2,128)(2,1)S(1)}, bf16[224,2,1,256]{3,2,1,0:T(2,128)(2,1)S(1)}, bf16[224,2,1,256]{3,2,1,0:T(2,128)(2,1)S(1)}, bf16[224,2,1,256]{3,2,1,0:T(2,128)(2,1)S(1)}) fusion(bf16[224,2,4,256]{3,2,1,0:T(4,128)(2,1)S(1)} %reshape_squeeze.3, s32[]{:T(128)S(6)} %select_n.62, s32[]{:T(128)S(6)} %select_n.61, ...), kind=kLoop, calls=%fused_computation.37 | loop fusion | bytes 1835024 | tf_op jit(solution)/shard_map/jit(dynamic_index_in_dim)/dynamic_slice | solution.py:253
  15.1 1.3 collective-permute-start.3
  16.4 2.5 %collective-permute-start.4 = (bf16[2,224,256]{2,1,0:T(8,128)(2,1)S(1)}, bf16[2,224,256]{2,1,0:T(8,128)(2,1)S(1)}, u32[]{:S(2)}, u32[]{:S(2)}) collective-permute-start(bf16[2,224,256]{2,1,0:T(8,128)(2,1)S(1)} %bitcast.102), channel_id=1, source_target_pairs={{0,2},{1,3},{2,0},{3,1},{4,6},{5,7},{6,4},{7,5},{8,10},{9,11},{10,... | collective-permute-start | bytes 688136 | tf_op jit(solution)/shard_map/ppermute | solution.py:255
  19.0 1.2 collective-permute-start.5
  20.2 3.0 %collective-permute-start.1 = (bf16[224,256]{1,0:T(8,128)(2,1)S(1)}, bf16[224,256]{1,0:T(8,128)(2,1)S(1)}, u32[]{:S(2)}, u32[]{:S(2)}) collective-permute-start(bf16[224,256]{1,0:T(8,128)(2,1)S(1)} %pad_maximum_fusion.6), channel_id=1, source_target_pairs={{0,32},{16,48},{32,0},{48,16},{1,33},{17,49},{33,1},{49,17},{2,34}... | collective-permute-start | bytes 344072 | tf_op jit(solution)/shard_map/ppermute | solution.py:249
  23.2 0.7 collective-permute-start.2
  24.0 3.2 %collective-permute-done.1 = bf16[224,256]{1,0:T(8,128)(2,1)S(1)} collective-permute-done((bf16[224,256]{1,0:T(8,128)(2,1)S(1)}, bf16[224,256]{1,0:T(8,128)(2,1)S(1)}, u32[]{:S(2)}, u32[]{:S(2)}) %collective-permute-start.1) | collective-permute-done | bytes 114720 | tf_op jit(solution)/shard_map/ppermute | solution.py:249
  27.2 0.9 collective-permute-done.2
  28.1 0.3 collective-permute-done.4
  28.4 0.1 pad_maximum_fusion
  28.5 0.1 dynamic-slice_bitcast_fusion.1
  28.6 2.9 %collective-permute-start.9 = (bf16[2,224,256]{2,1,0:T(8,128)(2,1)S(1)}, bf16[2,224,256]{2,1,0:T(8,128)(2,1)S(1)}, u32[]{:S(2)}, u32[]{:S(2)}) collective-permute-start(bf16[2,224,256]{2,1,0:T(8,128)(2,1)S(1)} %get-tuple-element.61), channel_id=1, source_target_pairs={{0,16},{16,32},{32,48},{48,0},{1,17},{17,33},{33,49},{49,1},{2,18}... | collective-permute-start | bytes 688136 | tf_op jit(solution)/shard_map/ppermute | solution.py:263
  31.6 1.4 collective-permute-start.6
  32.9 2.6 %collective-permute-start.7 = (bf16[4,224,256]{2,1,0:T(8,128)(2,1)S(1)}, bf16[4,224,256]{2,1,0:T(8,128)(2,1)S(1)}, u32[]{:S(2)}, u32[]{:S(2)}) collective-permute-start(bf16[4,224,256]{2,1,0:T(8,128)(2,1)S(1)} %pad_maximum_fusion.3.kv0), channel_id=1, source_target_pairs={{0,8},{4,12},{8,0},{12,4},{1,9},{5,13},{9,1},{13,5},{2,10},{6,14},... | collective-permute-start | bytes 1376264 | tf_op jit(solution)/shard_map/ppermute | solution.py:259
  35.5 1.1 collective-permute-start.8
  36.6 0.6 collective-permute-start.10
  37.2 2.0 %collective-permute-start.11 = (bf16[2,224,256]{2,1,0:T(8,128)(2,1)S(1)}, bf16[2,224,256]{2,1,0:T(8,128)(2,1)S(1)}, u32[]{:S(2)}, u32[]{:S(2)}) collective-permute-start(bf16[2,224,256]{2,1,0:T(8,128)(2,1)S(1)} %get-tuple-element.59), channel_id=1, source_target_pairs={{0,48},{16,0},{32,16},{48,32},{1,49},{17,1},{33,17},{49,33},{2,50}... | collective-permute-start | bytes 688136 | tf_op jit(solution)/shard_map/ppermute | solution.py:263
  39.2 10.4 %collective-permute-done.10 = bf16[2,224,256]{2,1,0:T(8,128)(2,1)S(1)} collective-permute-done((bf16[2,224,256]{2,1,0:T(8,128)(2,1)S(1)}, bf16[2,224,256]{2,1,0:T(8,128)(2,1)S(1)}, u32[]{:S(2)}, u32[]{:S(2)}) %collective-permute-start.10) | collective-permute-done | bytes 229408 | tf_op jit(solution)/shard_map/ppermute | solution.py:263
  49.6 4.7 %collective-permute-done.7.kv2 = bf16[4,224,256]{2,1,0:T(8,128)(2,1)S(1)} collective-permute-done((bf16[4,224,256]{2,1,0:T(8,128)(2,1)S(1)}, bf16[4,224,256]{2,1,0:T(8,128)(2,1)S(1)}, u32[]{:S(2)}, u32[]{:S(2)}) %collective-permute-start.7) | collective-permute-done | bytes 458784 | tf_op jit(solution)/shard_map/ppermute | solution.py:259
  54.4 0.5 collective-permute-done.8.kv3
  54.8 0.1 pad_maximum_fusion.1
  54.9 0.1 constant_dynamic-slice_fusion
  55.1 2.1 %collective-permute-start.18 = (bf16[4,224,256]{2,1,0:T(8,128)(2,1)S(1)}, bf16[4,224,256]{2,1,0:T(8,128)(2,1)S(1)}, u32[]{:S(2)}, u32[]{:S(2)}) collective-permute-start(bf16[4,224,256]{2,1,0:T(8,128)(2,1)S(1)} %get-tuple-element.58), channel_id=1, source_target_pairs={{0,64},{64,0},{1,65},{65,1},{2,66},{66,2},{3,67},{67,3},{4,68},{68... | collective-permute-start | bytes 1376264 | tf_op jit(solution)/shard_map/ppermute | solution.py:268
  57.2 1.4 collective-permute-done.18
  58.6 1.0 pad_maximum_fusion.2
  59.7 0.1 pad_add_fusion.facts
  59.7 10.6 %shard_map.102 = (bf16[224,1024]{1,0:T(8,128)(2,1)}, bf16[4,224,256]{2,1,0:T(8,128)(2,1)S(1)}, bf16[4,224,256]{2,1,0:T(8,128)(2,1)S(1)}, bf16[4,224,256]{2,1,0:T(8,128)(2,1)S(1)}, bf16[4,224,256]{2,1,0:T(8,128)(2,1)S(1)}) custom-call(s32[24]{0:T(128)S(1)} %pad_add_fusion.facts, bf16[224,1024]{1,0:T(8,128)(2,1)S(1)} %bitcast.85, ...), custom_call_target="tpu_custom_call" | custom-call | flops 6000000000 | bytes 6000000 | tf_op jit(solution)/shard_map/pallas_call | solution.py:169
  70.3 1.9 %collective-permute-start.14 = (bf16[4,224,256]{2,1,0:T(8,128)(2,1)S(1)}, bf16[4,224,256]{2,1,0:T(8,128)(2,1)S(1)}, u32[]{:S(2)}, u32[]{:S(2)}) collective-permute-start(bf16[4,224,256]{2,1,0:T(8,128)(2,1)S(1)} %get-tuple-element.45), channel_id=1, source_target_pairs={{0,12},{4,0},{8,4},{12,8},{1,13},{5,1},{9,5},{13,9},{2,14},{6,2},{... | collective-permute-start | bytes 1376264 | tf_op jit(solution)/shard_map/ppermute | solution.py:274
  72.2 0.9 collective-permute-start.13
  73.1 0.5 collective-permute-start.12
  73.5 18.0 %collective-permute-done.14 = bf16[4,224,256]{2,1,0:T(8,128)(2,1)S(1)} collective-permute-done((bf16[4,224,256]{2,1,0:T(8,128)(2,1)S(1)}, bf16[4,224,256]{2,1,0:T(8,128)(2,1)S(1)}, u32[]{:S(2)}, u32[]{:S(2)}) %collective-permute-start.14) | collective-permute-done | bytes 458784 | tf_op jit(solution)/shard_map/ppermute | solution.py:274
  91.5 4.6 %collective-permute-done.12 = bf16[4,224,256]{2,1,0:T(8,128)(2,1)S(1)} collective-permute-done((bf16[4,224,256]{2,1,0:T(8,128)(2,1)S(1)}, bf16[4,224,256]{2,1,0:T(8,128)(2,1)S(1)}, u32[]{:S(2)}, u32[]{:S(2)}) %collective-permute-start.12) | collective-permute-done | bytes 458784 | tf_op jit(solution)/shard_map/ppermute | solution.py:274
  96.1 0.2 fusion.3
  96.3 0.1 collective-permute-start.17
  96.4 0.1 collective-permute-start.16
  96.5 1.4 collective-permute-start.15
  97.9 4.1 %collective-permute-done.17 = bf16[224,256]{1,0:T(8,128)(2,1)S(1)} collective-permute-done((bf16[224,256]{1,0:T(8,128)(2,1)S(1)}, bf16[224,256]{1,0:T(8,128)(2,1)S(1)}, u32[]{:S(2)}, u32[]{:S(2)}) %collective-permute-start.17) | collective-permute-done | bytes 114720 | tf_op jit(solution)/shard_map/ppermute | solution.py:276
  102.0 4.7 %collective-permute-done.16 = bf16[224,256]{1,0:T(8,128)(2,1)S(1)} collective-permute-done((bf16[224,256]{1,0:T(8,128)(2,1)S(1)}, bf16[224,256]{1,0:T(8,128)(2,1)S(1)}, u32[]{:S(2)}, u32[]{:S(2)}) %collective-permute-start.16) | collective-permute-done | bytes 114720 | tf_op jit(solution)/shard_map/ppermute | solution.py:276
  106.7 0.1 fusion.2
  106.8 1.7 %collective-permute-start.21 = (bf16[224,256]{1,0:T(8,128)(2,1)S(1)}, bf16[224,256]{1,0:T(8,128)(2,1)S(1)}, u32[]{:S(2)}, u32[]{:S(2)}) collective-permute-start(bf16[224,256]{1,0:T(8,128)(2,1)S(1)} %fusion.2), channel_id=1, source_target_pairs={{0,48},{16,0},{32,16},{48,32},{1,49},{17,1},{33,17},{49,33},{2,50}... | collective-permute-start | bytes 344072 | tf_op jit(solution)/shard_map/ppermute | solution.py:279
  108.5 1.5 collective-permute-start.20
  110.0 1.4 collective-permute-start.19
  111.4 9.0 %collective-permute-done.20 = bf16[224,256]{1,0:T(8,128)(2,1)S(1)} collective-permute-done((bf16[224,256]{1,0:T(8,128)(2,1)S(1)}, bf16[224,256]{1,0:T(8,128)(2,1)S(1)}, u32[]{:S(2)}, u32[]{:S(2)}) %collective-permute-start.20) | collective-permute-done | bytes 114720 | tf_op jit(solution)/shard_map/ppermute | solution.py:279
  120.5 1.1 collective-permute-start.22
  121.6 1.4 collective-permute-done.22.refs_1_
  123.0 2.0 %copy-done = bf16[7168,256]{1,0:T(8,128)(2,1)S(1)} copy-done((bf16[7168,256]{1,0:T(8,128)(2,1)S(1)}, bf16[7168,256]{1,0:T(8,128)(2,1)}, u32[]{:S(2)}) %copy-start) | copy-done | bytes 3670040
  125.1 2.0 %shard_map.103 = (bf16[4,16,1024]{2,1,0:T(8,128)(2,1)S(1)}, bf16[4,16,1024]{2,1,0:T(8,128)(2,1)S(1)}, bf16[4,16,1024]{2,1,0:T(8,128)(2,1)S(1)}, bf16[4,16,1024]{2,1,0:T(8,128)(2,1)S(1)}) custom-call(s32[24]{0:T(128)S(1)} %pad_add_fusion.facts, bf16[4,1792,256]{2,1,0:T(8,128)(2,1)S(1)} %bitcast.84, bf16[4,224,256]{2,1,0:T(8,128)(2,1)S(1)} %pad_maximum_fusion.4.refs_0_, ...), custom_call_target="tpu_custom_call" | custom-call | flops 1000000000 | bytes 6000000 | tf_op jit(solution)/shard_map/pallas_call | solution.py:231
  127.1 0.4 collective-permute-start.25
  127.4 1.5 collective-permute-start.24
  128.9 0.3 collective-permute-start.23
  129.2 2.8 %collective-permute-done.25 = bf16[4,16,1024]{2,1,0:T(8,128)(2,1)S(1)} collective-permute-done((bf16[4,16,1024]{2,1,0:T(8,128)(2,1)S(1)}, bf16[4,16,1024]{2,1,0:T(8,128)(2,1)S(1)}, u32[]{:S(2)}, u32[]{:S(2)}) %collective-permute-start.25) | collective-permute-done | bytes 131104 | tf_op jit(solution)/shard_map/ppermute | solution.py:282
  132.1 1.3 collective-permute-done.24
  133.4 3.6 %collective-permute-done.23 = bf16[4,16,1024]{2,1,0:T(8,128)(2,1)S(1)} collective-permute-done((bf16[4,16,1024]{2,1,0:T(8,128)(2,1)S(1)}, bf16[4,16,1024]{2,1,0:T(8,128)(2,1)S(1)}, u32[]{:S(2)}, u32[]{:S(2)}) %collective-permute-start.23) | collective-permute-done | bytes 131104 | tf_op jit(solution)/shard_map/ppermute | solution.py:282
  137.1 9.1 %collective-permute-start.26 = (bf16[2,16,1024]{2,1,0:T(8,128)(2,1)S(1)}, bf16[2,16,1024]{2,1,0:T(8,128)(2,1)S(1)}, u32[]{:S(2)}, u32[]{:S(2)}) collective-permute-start(bf16[2,16,1024]{2,1,0:T(8,128)(2,1)S(1)} %fusion.6), channel_id=1, source_target_pairs={{0,128},{128,0},{1,129},{129,1},{2,130},{130,2},{3,131},{131,3},{4... | collective-permute-start | bytes 196616 | tf_op jit(solution)/shard_map/ppermute | solution.py:286
  146.2 2.0 %collective-permute-done.26 = bf16[2,16,1024]{2,1,0:T(8,128)(2,1)S(1)} collective-permute-done((bf16[2,16,1024]{2,1,0:T(8,128)(2,1)S(1)}, bf16[2,16,1024]{2,1,0:T(8,128)(2,1)S(1)}, u32[]{:S(2)}, u32[]{:S(2)}) %collective-permute-start.26) | collective-permute-done | bytes 65568 | tf_op jit(solution)/shard_map/ppermute | solution.py:286
  148.3 3.2 %collective-permute-start.27 = (f32[16,1024]{1,0:T(8,128)S(1)}, f32[16,1024]{1,0:T(8,128)S(1)}, u32[]{:S(2)}, u32[]{:S(2)}) collective-permute-start(f32[16,1024]{1,0:T(8,128)S(1)} %get-tuple-element.69), channel_id=1, source_target_pairs={{0,0},{1,32},{2,64},{3,96},{4,4},{5,36},{6,68},{7,100},{8,8},{9,40... | collective-permute-start | bytes 196616 | tf_op jit(solution)/shard_map/ppermute | solution.py:290
  151.5 0.1 collective-permute-start.28
  151.6 0.6 slice_bitcast_fusion
  152.3 3.1 %collective-permute-done.27 = f32[16,1024]{1,0:T(8,128)S(1)} collective-permute-done((f32[16,1024]{1,0:T(8,128)S(1)}, f32[16,1024]{1,0:T(8,128)S(1)}, u32[]{:S(2)}, u32[]{:S(2)}) %collective-permute-start.27) | collective-permute-done | bytes 65568 | tf_op jit(solution)/shard_map/ppermute | solution.py:290
  155.4 0.8 collective-permute-done.28
  156.2 0.7 pad_maximum_fusion.5
  (33 shorter events, 0.5 us)
Async XLA Ops:
  7.2 115.9 %all-gather.3.cloned.1.call-start = ((), (), s32[]{:S(2)}) async-start(), calls=%async_computation | async-start | bytes 4587520 | tf_op jit(solution)/shard_map/all_gather | solution.py:270
  8.1 15.1 %collective-permute-start = (bf16[224,256]{1,0:T(8,128)(2,1)S(1)}, bf16[224,256]{1,0:T(8,128)(2,1)S(1)}, u32[]{:S(2)}, u32[]{:S(2)}) collective-permute-start(bf16[224,256]{1,0:T(8,128)(2,1)S(1)} %pad_maximum_fusion.6), channel_id=1, source_target_pairs={{0,16},{16,32},{32,48},{48,0},{1,17},{17,33},{33,49},{49,1},{2,18}... | collective-permute-start | bytes 344072 | tf_op jit(solution)/shard_map/ppermute | solution.py:249
  15.1 13.1 %collective-permute-start.3 = (bf16[2,224,256]{2,1,0:T(8,128)(2,1)S(1)}, bf16[2,224,256]{2,1,0:T(8,128)(2,1)S(1)}, u32[]{:S(2)}, u32[]{:S(2)}) collective-permute-start(bf16[2,224,256]{2,1,0:T(8,128)(2,1)S(1)} %bitcast.101), channel_id=1, source_target_pairs={{0,1},{1,2},{2,3},{3,0},{4,5},{5,6},{6,7},{7,4},{8,9},{9,10},{10,1... | collective-permute-start | bytes 688136 | tf_op jit(solution)/shard_map/ppermute | solution.py:255
  16.4 12.0 %collective-permute-start.4 = (bf16[2,224,256]{2,1,0:T(8,128)(2,1)S(1)}, bf16[2,224,256]{2,1,0:T(8,128)(2,1)S(1)}, u32[]{:S(2)}, u32[]{:S(2)}) collective-permute-start(bf16[2,224,256]{2,1,0:T(8,128)(2,1)S(1)} %bitcast.102), channel_id=1, source_target_pairs={{0,2},{1,3},{2,0},{3,1},{4,6},{5,7},{6,4},{7,5},{8,10},{9,11},{10,... | collective-permute-start | bytes 688136 | tf_op jit(solution)/shard_map/ppermute | solution.py:255
  19.0 9.5 %collective-permute-start.5 = (bf16[2,224,256]{2,1,0:T(8,128)(2,1)S(1)}, bf16[2,224,256]{2,1,0:T(8,128)(2,1)S(1)}, u32[]{:S(2)}, u32[]{:S(2)}) collective-permute-start(bf16[2,224,256]{2,1,0:T(8,128)(2,1)S(1)} %bitcast.103), channel_id=1, source_target_pairs={{0,3},{1,0},{2,1},{3,2},{4,7},{5,4},{6,5},{7,6},{8,11},{9,8},{10,9... | collective-permute-start | bytes 688136 | tf_op jit(solution)/shard_map/ppermute | solution.py:255
  20.2 7.0 %collective-permute-start.1 = (bf16[224,256]{1,0:T(8,128)(2,1)S(1)}, bf16[224,256]{1,0:T(8,128)(2,1)S(1)}, u32[]{:S(2)}, u32[]{:S(2)}) collective-permute-start(bf16[224,256]{1,0:T(8,128)(2,1)S(1)} %pad_maximum_fusion.6), channel_id=1, source_target_pairs={{0,32},{16,48},{32,0},{48,16},{1,33},{17,49},{33,1},{49,17},{2,34}... | collective-permute-start | bytes 344072 | tf_op jit(solution)/shard_map/ppermute | solution.py:249
  23.2 4.9 %collective-permute-start.2 = (bf16[224,256]{1,0:T(8,128)(2,1)S(1)}, bf16[224,256]{1,0:T(8,128)(2,1)S(1)}, u32[]{:S(2)}, u32[]{:S(2)}) collective-permute-start(bf16[224,256]{1,0:T(8,128)(2,1)S(1)} %pad_maximum_fusion.6), channel_id=1, source_target_pairs={{0,48},{16,0},{32,16},{48,32},{1,49},{17,1},{33,17},{49,33},{2,50}... | collective-permute-start | bytes 344072 | tf_op jit(solution)/shard_map/ppermute | solution.py:249
  28.6 8.6 %collective-permute-start.9 = (bf16[2,224,256]{2,1,0:T(8,128)(2,1)S(1)}, bf16[2,224,256]{2,1,0:T(8,128)(2,1)S(1)}, u32[]{:S(2)}, u32[]{:S(2)}) collective-permute-start(bf16[2,224,256]{2,1,0:T(8,128)(2,1)S(1)} %get-tuple-element.61), channel_id=1, source_target_pairs={{0,16},{16,32},{32,48},{48,0},{1,17},{17,33},{33,49},{49,1},{2,18}... | collective-permute-start | bytes 688136 | tf_op jit(solution)/shard_map/ppermute | solution.py:263
  31.6 18.1 %collective-permute-start.6 = (bf16[4,224,256]{2,1,0:T(8,128)(2,1)S(1)}, bf16[4,224,256]{2,1,0:T(8,128)(2,1)S(1)}, u32[]{:S(2)}, u32[]{:S(2)}) collective-permute-start(bf16[4,224,256]{2,1,0:T(8,128)(2,1)S(1)} %pad_maximum_fusion.3.kv0), channel_id=1, source_target_pairs={{0,4},{4,8},{8,12},{12,0},{1,5},{5,9},{9,13},{13,1},{2,6},{6,10},{... | collective-permute-start | bytes 1376264 | tf_op jit(solution)/shard_map/ppermute | solution.py:259
  32.9 21.4 %collective-permute-start.7 = (bf16[4,224,256]{2,1,0:T(8,128)(2,1)S(1)}, bf16[4,224,256]{2,1,0:T(8,128)(2,1)S(1)}, u32[]{:S(2)}, u32[]{:S(2)}) collective-permute-start(bf16[4,224,256]{2,1,0:T(8,128)(2,1)S(1)} %pad_maximum_fusion.3.kv0), channel_id=1, source_target_pairs={{0,8},{4,12},{8,0},{12,4},{1,9},{5,13},{9,1},{13,5},{2,10},{6,14},... | collective-permute-start | bytes 1376264 | tf_op jit(solution)/shard_map/ppermute | solution.py:259
  35.5 19.3 %collective-permute-start.8 = (bf16[4,224,256]{2,1,0:T(8,128)(2,1)S(1)}, bf16[4,224,256]{2,1,0:T(8,128)(2,1)S(1)}, u32[]{:S(2)}, u32[]{:S(2)}) collective-permute-start(bf16[4,224,256]{2,1,0:T(8,128)(2,1)S(1)} %pad_maximum_fusion.3.kv0), channel_id=1, source_target_pairs={{0,12},{4,0},{8,4},{12,8},{1,13},{5,1},{9,5},{13,9},{2,14},{6,2},{... | collective-permute-start | bytes 1376264 | tf_op jit(solution)/shard_map/ppermute | solution.py:259
  36.6 13.0 %collective-permute-start.10 = (bf16[2,224,256]{2,1,0:T(8,128)(2,1)S(1)}, bf16[2,224,256]{2,1,0:T(8,128)(2,1)S(1)}, u32[]{:S(2)}, u32[]{:S(2)}) collective-permute-start(bf16[2,224,256]{2,1,0:T(8,128)(2,1)S(1)} %get-tuple-element.60), channel_id=1, source_target_pairs={{0,32},{16,48},{32,0},{48,16},{1,33},{17,49},{33,1},{49,17},{2,34}... | collective-permute-start | bytes 688136 | tf_op jit(solution)/shard_map/ppermute | solution.py:263
  37.2 12.4 %collective-permute-start.11 = (bf16[2,224,256]{2,1,0:T(8,128)(2,1)S(1)}, bf16[2,224,256]{2,1,0:T(8,128)(2,1)S(1)}, u32[]{:S(2)}, u32[]{:S(2)}) collective-permute-start(bf16[2,224,256]{2,1,0:T(8,128)(2,1)S(1)} %get-tuple-element.59), channel_id=1, source_target_pairs={{0,48},{16,0},{32,16},{48,32},{1,49},{17,1},{33,17},{49,33},{2,50}... | collective-permute-start | bytes 688136 | tf_op jit(solution)/shard_map/ppermute | solution.py:263
  55.0 4.6 %copy-start.3 = (s32[16]{0:T(128)S(1)}, s32[16]{0:T(128)}, u32[]{:S(2)}) copy-start(s32[16]{0:T(128)} %param.13) | copy-start | bytes 196
  55.0 4.6 %copy-start.4 = (s32[1,6]{1,0:T(1,128)S(1)}, s32[1,6]{1,0:T(1,128)}, u32[]{:S(2)}) copy-start(s32[1,6]{1,0:T(1,128)} %param.12) | copy-start | bytes 76
  55.0 4.7 %copy-start.1 = (bf16[1,224,1024]{2,1,0:T(8,128)(2,1)S(1)}, bf16[1,224,1024]{2,1,0:T(8,128)(2,1)}, u32[]{:S(2)}) copy-start(bf16[1,224,1024]{2,1,0:T(8,128)(2,1)} %param.8) | copy-start | bytes 1376260
  55.1 4.7 %copy-start.2 = (bf16[1,224,1024]{2,1,0:T(8,128)(2,1)S(1)}, bf16[1,224,1024]{2,1,0:T(8,128)(2,1)}, u32[]{:S(2)}) copy-start(bf16[1,224,1024]{2,1,0:T(8,128)(2,1)} %param.11) | copy-start | bytes 1376260
  55.1 3.6 %collective-permute-start.18 = (bf16[4,224,256]{2,1,0:T(8,128)(2,1)S(1)}, bf16[4,224,256]{2,1,0:T(8,128)(2,1)S(1)}, u32[]{:S(2)}, u32[]{:S(2)}) collective-permute-start(bf16[4,224,256]{2,1,0:T(8,128)(2,1)S(1)} %get-tuple-element.58), channel_id=1, source_target_pairs={{0,64},{64,0},{1,65},{65,1},{2,66},{66,2},{3,67},{67,3},{4,68},{68... | collective-permute-start | bytes 1376264 | tf_op jit(solution)/shard_map/ppermute | solution.py:268
  70.3 21.2 %collective-permute-start.14 = (bf16[4,224,256]{2,1,0:T(8,128)(2,1)S(1)}, bf16[4,224,256]{2,1,0:T(8,128)(2,1)S(1)}, u32[]{:S(2)}, u32[]{:S(2)}) collective-permute-start(bf16[4,224,256]{2,1,0:T(8,128)(2,1)S(1)} %get-tuple-element.45), channel_id=1, source_target_pairs={{0,12},{4,0},{8,4},{12,8},{1,13},{5,1},{9,5},{13,9},{2,14},{6,2},{... | collective-permute-start | bytes 1376264 | tf_op jit(solution)/shard_map/ppermute | solution.py:274
  72.2 19.3 %collective-permute-start.13 = (bf16[4,224,256]{2,1,0:T(8,128)(2,1)S(1)}, bf16[4,224,256]{2,1,0:T(8,128)(2,1)S(1)}, u32[]{:S(2)}, u32[]{:S(2)}) collective-permute-start(bf16[4,224,256]{2,1,0:T(8,128)(2,1)S(1)} %get-tuple-element.44), channel_id=1, source_target_pairs={{0,8},{4,12},{8,0},{12,4},{1,9},{5,13},{9,1},{13,5},{2,10},{6,14},... | collective-permute-start | bytes 1376264 | tf_op jit(solution)/shard_map/ppermute | solution.py:274
  73.1 23.0 %collective-permute-start.12 = (bf16[4,224,256]{2,1,0:T(8,128)(2,1)S(1)}, bf16[4,224,256]{2,1,0:T(8,128)(2,1)S(1)}, u32[]{:S(2)}, u32[]{:S(2)}) collective-permute-start(bf16[4,224,256]{2,1,0:T(8,128)(2,1)S(1)} %get-tuple-element.43), channel_id=1, source_target_pairs={{0,4},{4,8},{8,12},{12,0},{1,5},{5,9},{9,13},{13,1},{2,6},{6,10},{... | collective-permute-start | bytes 1376264 | tf_op jit(solution)/shard_map/ppermute | solution.py:274
  96.3 5.7 %collective-permute-start.17 = (bf16[224,256]{1,0:T(8,128)(2,1)S(1)}, bf16[224,256]{1,0:T(8,128)(2,1)S(1)}, u32[]{:S(2)}, u32[]{:S(2)}) collective-permute-start(bf16[224,256]{1,0:T(8,128)(2,1)S(1)} %get-tuple-element.55), channel_id=1, source_target_pairs={{0,48},{16,0},{32,16},{48,32},{1,49},{17,1},{33,17},{49,33},{2,50}... | collective-permute-start | bytes 344072 | tf_op jit(solution)/shard_map/ppermute | solution.py:276
  96.4 10.3 %collective-permute-start.16 = (bf16[224,256]{1,0:T(8,128)(2,1)S(1)}, bf16[224,256]{1,0:T(8,128)(2,1)S(1)}, u32[]{:S(2)}, u32[]{:S(2)}) collective-permute-start(bf16[224,256]{1,0:T(8,128)(2,1)S(1)} %get-tuple-element.56), channel_id=1, source_target_pairs={{0,32},{16,48},{32,0},{48,16},{1,33},{17,49},{33,1},{49,17},{2,34}... | collective-permute-start | bytes 344072 | tf_op jit(solution)/shard_map/ppermute | solution.py:276
  96.5 10.2 %collective-permute-start.15 = (bf16[224,256]{1,0:T(8,128)(2,1)S(1)}, bf16[224,256]{1,0:T(8,128)(2,1)S(1)}, u32[]{:S(2)}, u32[]{:S(2)}) collective-permute-start(bf16[224,256]{1,0:T(8,128)(2,1)S(1)} %get-tuple-element.54), channel_id=1, source_target_pairs={{0,16},{16,32},{32,48},{48,0},{1,17},{17,33},{33,49},{49,1},{2,18}... | collective-permute-start | bytes 344072 | tf_op jit(solution)/shard_map/ppermute | solution.py:276
  106.8 4.6 %collective-permute-start.21 = (bf16[224,256]{1,0:T(8,128)(2,1)S(1)}, bf16[224,256]{1,0:T(8,128)(2,1)S(1)}, u32[]{:S(2)}, u32[]{:S(2)}) collective-permute-start(bf16[224,256]{1,0:T(8,128)(2,1)S(1)} %fusion.2), channel_id=1, source_target_pairs={{0,48},{16,0},{32,16},{48,32},{1,49},{17,1},{33,17},{49,33},{2,50}... | collective-permute-start | bytes 344072 | tf_op jit(solution)/shard_map/ppermute | solution.py:279
  108.5 11.9 %collective-permute-start.20 = (bf16[224,256]{1,0:T(8,128)(2,1)S(1)}, bf16[224,256]{1,0:T(8,128)(2,1)S(1)}, u32[]{:S(2)}, u32[]{:S(2)}) collective-permute-start(bf16[224,256]{1,0:T(8,128)(2,1)S(1)} %fusion.2), channel_id=1, source_target_pairs={{0,32},{16,48},{32,0},{48,16},{1,33},{17,49},{33,1},{49,17},{2,34}... | collective-permute-start | bytes 344072 | tf_op jit(solution)/shard_map/ppermute | solution.py:279
  110.0 10.4 %collective-permute-start.19 = (bf16[224,256]{1,0:T(8,128)(2,1)S(1)}, bf16[224,256]{1,0:T(8,128)(2,1)S(1)}, u32[]{:S(2)}, u32[]{:S(2)}) collective-permute-start(bf16[224,256]{1,0:T(8,128)(2,1)S(1)} %fusion.2), channel_id=1, source_target_pairs={{0,16},{16,32},{32,48},{48,0},{1,17},{17,33},{33,49},{49,1},{2,18}... | collective-permute-start | bytes 344072 | tf_op jit(solution)/shard_map/ppermute | solution.py:279
  120.5 2.5 %collective-permute-start.22 = (bf16[4,224,256]{2,1,0:T(8,128)(2,1)S(1)}, bf16[4,224,256]{2,1,0:T(8,128)(2,1)S(1)}, u32[]{:S(2)}, u32[]{:S(2)}) collective-permute-start(bf16[4,224,256]{2,1,0:T(8,128)(2,1)S(1)} %pad_maximum_fusion.4.refs_0_), channel_id=1, source_target_pairs={{0,64},{64,0},{1,65},{65,1},{2,66},{66,2},{3,67},{67,3},{4,68},{68... | collective-permute-start | bytes 1376264 | tf_op jit(solution)/shard_map/ppermute | solution.py:280
  123.0 2.0 %copy-start = (bf16[7168,256]{1,0:T(8,128)(2,1)S(1)}, bf16[7168,256]{1,0:T(8,128)(2,1)}, u32[]{:S(2)}) copy-start(bf16[7168,256]{1,0:T(8,128)(2,1)} %all-gather.3.cloned.1.call-done) | copy-start | bytes 11010052
  127.1 5.0 %collective-permute-start.25 = (bf16[4,16,1024]{2,1,0:T(8,128)(2,1)S(1)}, bf16[4,16,1024]{2,1,0:T(8,128)(2,1)S(1)}, u32[]{:S(2)}, u32[]{:S(2)}) collective-permute-start(bf16[4,16,1024]{2,1,0:T(8,128)(2,1)S(1)} %get-tuple-element.53), channel_id=1, source_target_pairs={{0,12},{4,0},{8,4},{12,8},{1,13},{5,1},{9,5},{13,9},{2,14},{6,2},{... | collective-permute-start | bytes 393224 | tf_op jit(solution)/shard_map/ppermute | solution.py:282
  127.4 5.9 %collective-permute-start.24 = (bf16[4,16,1024]{2,1,0:T(8,128)(2,1)S(1)}, bf16[4,16,1024]{2,1,0:T(8,128)(2,1)S(1)}, u32[]{:S(2)}, u32[]{:S(2)}) collective-permute-start(bf16[4,16,1024]{2,1,0:T(8,128)(2,1)S(1)} %get-tuple-element.52), channel_id=1, source_target_pairs={{0,8},{4,12},{8,0},{12,4},{1,9},{5,13},{9,1},{13,5},{2,10},{6,14},... | collective-permute-start | bytes 393224 | tf_op jit(solution)/shard_map/ppermute | solution.py:282
  128.9 8.1 %collective-permute-start.23 = (bf16[4,16,1024]{2,1,0:T(8,128)(2,1)S(1)}, bf16[4,16,1024]{2,1,0:T(8,128)(2,1)S(1)}, u32[]{:S(2)}, u32[]{:S(2)}) collective-permute-start(bf16[4,16,1024]{2,1,0:T(8,128)(2,1)S(1)} %get-tuple-element.51), channel_id=1, source_target_pairs={{0,4},{4,8},{8,12},{12,0},{1,5},{5,9},{9,13},{13,1},{2,6},{6,10},{... | collective-permute-start | bytes 393224 | tf_op jit(solution)/shard_map/ppermute | solution.py:282
  137.1 11.2 %collective-permute-start.26 = (bf16[2,16,1024]{2,1,0:T(8,128)(2,1)S(1)}, bf16[2,16,1024]{2,1,0:T(8,128)(2,1)S(1)}, u32[]{:S(2)}, u32[]{:S(2)}) collective-permute-start(bf16[2,16,1024]{2,1,0:T(8,128)(2,1)S(1)} %fusion.6), channel_id=1, source_target_pairs={{0,128},{128,0},{1,129},{129,1},{2,130},{130,2},{3,131},{131,3},{4... | collective-permute-start | bytes 196616 | tf_op jit(solution)/shard_map/ppermute | solution.py:286
  148.3 7.1 %collective-permute-start.27 = (f32[16,1024]{1,0:T(8,128)S(1)}, f32[16,1024]{1,0:T(8,128)S(1)}, u32[]{:S(2)}, u32[]{:S(2)}) collective-permute-start(f32[16,1024]{1,0:T(8,128)S(1)} %get-tuple-element.69), channel_id=1, source_target_pairs={{0,0},{1,32},{2,64},{3,96},{4,4},{5,36},{6,68},{7,100},{8,8},{9,40... | collective-permute-start | bytes 196616 | tf_op jit(solution)/shard_map/ppermute | solution.py:290
  151.5 4.7 %collective-permute-start.28 = (f32[16,1024]{1,0:T(8,128)S(1)}, f32[16,1024]{1,0:T(8,128)S(1)}, u32[]{:S(2)}, u32[]{:S(2)}) collective-permute-start(f32[16,1024]{1,0:T(8,128)S(1)} %get-tuple-element.70), channel_id=1, source_target_pairs={{0,16},{1,48},{2,80},{3,112},{4,20},{5,52},{6,84},{7,116},{8,24},{... | collective-permute-start | bytes 196616 | tf_op jit(solution)/shard_map/ppermute | solution.py:290
Sparse Core Ops, SparseCore 0:
  59.8 45.9 all-gather.2

commit v4 on v3

--- a/solution.py
+++ b/solution.py
@@ -200,22 +200,46 @@
     return functools.reduce(lambda a, b: a + b, [x.astype(F32) for x in xs])
 
 
-def owner(v):
+def owner(w, v):
     pairs = []
     for index in np.ndindex(*SIZES):
         zh, co, zl, y, x = index
-        target = (zh, x >> 1, (x & 1) * 2 + (v ^ co), y, zl)
+        target = (w ^ zh, x >> 1, (x & 1) * 2 + (v ^ co), y, zl)
         pairs.append(tuple(int(np.ravel_multi_index(i, SIZES)) for i in (index, target)))
     return pairs
 
 
-def product_kernel(facts, hidden, *refs):
+def runs_kernel(where, hidden, *runs):
+    half = hidden.shape[1] // 2
+    width = half // 4
+    for j, run in enumerate(runs):
+        q = lax.rem(where[0] + j, 4)
+        for h in range(2):
+            at = pl.ds(pl.multiple_of(h * half + q * width, width), width)
+            run[:, h * width : (h + 1) * width] = hidden[:, at]
+
+
+def hidden_runs(x, hidden):
+    vmem = pl.BlockSpec(memory_space=pltpu.VMEM)
+    return pl.pallas_call(
+        runs_kernel,
+        out_shape=(jax.ShapeDtypeStruct((ROWS, 512), BF),) * 4,
+        in_specs=[pl.BlockSpec(memory_space=pltpu.SMEM), vmem],
+        out_specs=(vmem,) * 4,
+        compiler_params=pltpu.CompilerParams(vmem_limit_bytes=8 * 2**20),
+        cost_estimate=pl.CostEstimate(flops=0, bytes_accessed=2 * 10**6, transcendentals=0),
+    )(x.reshape(1).astype(jnp.int32), hidden)
+
+
+def product_kernel(facts, hid0, hid1, hid2, hid3, *refs):
     rows, outs, acc = refs[:-5], refs[-5:-1], refs[-1]
-    my_y = facts[DOCS + RANKS + 1]
-    for run in range(4):
+    my_y, my_x = facts[DOCS + RANKS + 1], facts[DOCS + RANKS + 2]
+    for j, hidden in enumerate((hid0, hid1, hid2, hid3)):
+        run = lax.rem(my_x + 4 - j, 4)
+        columns = pl.ds(pl.multiple_of(run * 256, 256), 256)
         total = None
         for i, piece in enumerate(rows):
-            tokens = hidden[run, i * ROWS * 4 : (i + 1) * ROWS * 4, :]
+            tokens = hidden[i * ROWS * 4 : (i + 1) * ROWS * 4, :]
             part = dot(piece[...].reshape(4 * ROWS, 2 * DH), tokens, 0, 0)
             total = part if total is None else total + part
         acc[...] = total
@@ -223,7 +247,7 @@
             y = lax.rem(my_y + shift, 4)
             for block in range(4):
                 at = pl.ds(pl.multiple_of(block * 64 + y * 16, 16), 16)
-                out[block, :, run * 256 : (run + 1) * 256] = acc[at, :].astype(BF)
+                out[block, :, columns] = acc[at, :].astype(BF)
 
 
 def weight_product(facts, hidden, rows):
@@ -231,66 +255,70 @@
     return pl.pallas_call(
         product_kernel,
         out_shape=(jax.ShapeDtypeStruct((4, 16, 1024), BF),) * 4,
-        in_specs=[pl.BlockSpec(memory_space=pltpu.SMEM)] + [vmem] * (1 + len(rows)),
+        in_specs=[pl.BlockSpec(memory_space=pltpu.SMEM)] + [vmem] * (4 + len(rows)),
         out_specs=(vmem,) * 4,
         scratch_shapes=[pltpu.VMEM((2 * DH, 256), F32)],
         compiler_params=pltpu.CompilerParams(vmem_limit_bytes=24 * 2**20),
         cost_estimate=pl.CostEstimate(flops=10**9, bytes_accessed=6 * 10**6, transcendentals=0),
-    )(facts, hidden, *rows)
+    )(facts, *hidden, *rows)
+
+
+def after(value, *others):
+    return lax.optimization_barrier((value, others))[0]
 
 
 def per_device(hidden_in, queries, keys_in, values_in, out_grad, doc_lengths, pair_perm):
     zl, y, x = (lax.axis_index(a) for a in ("zl", "y", "x"))
     zh, core = lax.axis_index("zh"), lax.axis_index("co")
     swap = [(0, 1), (1, 0)]
-    facts = jnp.concatenate([doc_lengths[0], pair_perm, jnp.stack([zl, y]).astype(jnp.int32)])
+    facts = jnp.concatenate([doc_lengths[0], pair_perm, jnp.stack([zl, y, x]).astype(jnp.int32)])
+
+    def moved(value, axis, shift):
+        return lax.ppermute(value, axis, ring(shift))
 
     own = jnp.concatenate([keys_in[0], values_in[0]], axis=1)
-    column = [own] + [lax.ppermute(own, "zl", ring(a)) for a in (1, 2, 3)]
-    halves = hidden_in[0].reshape(ROWS, 2, 4, -1)
-    runs = []
-    for j in range(4):
-        run = lax.dynamic_index_in_dim(halves, lax.rem(x + j, 4), 2, False)
-        run = run.transpose(1, 0, 2)
-        runs.append(run if j == 0 else lax.ppermute(run, "x", ring(j)))
-    column, runs = lax.optimization_barrier((column, runs))
-
-    column, runs = jnp.stack(column), jnp.stack(runs)
-    kvs = [column] + [lax.ppermute(column, "y", ring(s)) for s in (1, 2, 3)]
+    column = jnp.stack([own] + [moved(own, "zl", a) for a in (1, 2, 3)])
+    runs = hidden_runs(x, hidden_in[0])
+    runs = [runs[0]] + [moved(runs[j], "x", j) for j in (1, 2, 3)]
+    kvs = [column] + [moved(column, "y", s) for s in (1, 2, 3)]
+
+    runs = jnp.stack(after(runs, kvs[1]))
     tokens = []
     for s in range(4):
         block = lax.dynamic_index_in_dim(runs, lax.rem(x - zl - s + 8, 4), 0, False)
-        tokens.append(block if s == 0 else lax.ppermute(block, "zl", ring(s)))
-    kvs, tokens = lax.optimization_barrier((kvs, tokens))
-
+        tokens.append(block if s == 0 else moved(block, "zl", s))
+
+    dq, *dkv = attention(facts, queries[0], out_grad[0], kvs)
+
+    dkv, tokens = lax.optimization_barrier((dkv, tokens))
+    got = [dkv[0]] + [moved(dkv[s], "y", s) for s in (1, 2, 3)]
     tokens = jnp.stack(tokens)
-    mine = lax.dynamic_index_in_dim(tokens, core, 1, False)
-    theirs = lax.ppermute(lax.dynamic_index_in_dim(tokens, 1 - core, 1, False), "co", swap)
+    mine = lax.dynamic_slice_in_dim(tokens, core * 256, 256, 2)
+    theirs = lax.ppermute(lax.dynamic_slice_in_dim(tokens, (1 - core) * 256, 256, 2), "co", swap)
     hidden = jnp.concatenate([mine.reshape(4 * ROWS, -1), theirs.reshape(4 * ROWS, -1)], axis=0)
-    hidden = lax.all_gather(hidden, "x", axis=0, tiled=False)
-
-    dq, *dkv = attention(facts, queries[0], out_grad[0], kvs)
-
-    got = [dkv[0]] + [lax.ppermute(dkv[s], "y", ring(s)) for s in (1, 2, 3)]
+    hidden = after(hidden, got[1])
+    hidden = [hidden] + [moved(hidden, "x", j) for j in (1, 2, 3)]
+
     parts = [add_up(*[g[a] for g in got]) for a in range(4)]
-    parts = [parts[0]] + [lax.ppermute(parts[a].astype(BF), "zl", ring(a)) for a in (1, 2, 3)]
+    parts = [parts[0]] + [moved(parts[a].astype(BF), "zl", a) for a in (1, 2, 3)]
     grads = add_up(*parts).astype(BF)
 
-    rows = jnp.stack([grads] + [lax.ppermute(grads, "zl", ring(s)) for s in (1, 2, 3)])
+    rows = jnp.stack([grads] + [moved(grads, "zl", s) for s in (1, 2, 3)])
     rows = (rows, lax.ppermute(rows, "co", swap))
     shares = weight_product(facts, hidden, rows)
-    shares = [shares[0]] + [lax.ppermute(shares[s], "y", ring(s)) for s in (1, 2, 3)]
-    share = add_up(*shares).reshape(2, 2, 16, -1)
-    kept = lax.dynamic_index_in_dim(share, zh, 0, False)
-    sent = lax.dynamic_index_in_dim(share, 1 - zh, 0, False).astype(BF)
-    share = kept + lax.ppermute(sent, "zh", swap).astype(F32)
-    blocks = []
+    shares = [shares[0]] + [moved(shares[s], "y", s) for s in (1, 2, 3)]
+    share = add_up(*shares).astype(BF).reshape(2, 2, 16, -1)
+    halves = []
     for v in range(2):
-        block = lax.dynamic_index_in_dim(share, lax.rem(core + v, 2), 0, False)
-        blocks.append(lax.ppermute(block, CARDINAL, owner(v)))
+        blocks = []
+        for w in range(2):
+            block = lax.dynamic_index_in_dim(share, lax.rem(zh + w, 2), 0, False)
+            block = lax.dynamic_index_in_dim(block, lax.rem(core + v, 2), 0, False)
+            blocks.append(lax.ppermute(block, CARDINAL, owner(w, v)))
+        halves.append(add_up(*blocks))
     even = lax.rem(zl, 2) == 0
-    left = jnp.where(even, blocks[0], blocks[1])
-    right = jnp.where(even, blocks[1], blocks[0])
+    left = jnp.where(even, halves[0], halves[1])
+    right = jnp.where(even, halves[1], halves[0])
     grad_weight = jnp.concatenate([left, right], axis=1)
     return dq[None], grads[None, :, :DH], grads[None, :, DH:], grad_weight
 

time: 166 us -> 160 us (0.964); the launches traced: 164 us -> 161 us
  waiting for transfers between devices: 77.2 us -> 96.8 us
  between operations: 14.3 us -> 0.83 us
  local copies, waits for them, and re-layouts: 7.38 us -> 0.92 us
  Pallas kernels: 12.6 us -> 10.3 us
    ppermute x28 -> x32, waiting for transfers between devices: 75.8 us -> 95.4 us  [the longest x27 87 us: moved(): return lax.ppermute(value, axis, ring(shift))]
    another operation x1 -> x0, local copies, waits for them, and re-layouts: 2.48 us -> none  [per_device(): halves = hidden_in[0].reshape(ROWS, 2, 4, -1)]
    pallas_call x1, Pallas kernels: 10.6 us -> 8.18 us  [attention(): pl.pallas_call(attention_kernel, out_shape=(jax.ShapeDtypeStruct((ROWS, H...]
    unnamed x10, local copies, waits for them, and re-layouts: 2.06 us -> 0.02 us
    dynamic_slice x6 -> x1, local copies, waits for them, and re-layouts: 2.08 us -> 0.07 us  [per_device(): mine = lax.dynamic_slice_in_dim(tokens, core * 256, 256, 2)]
    ppermute x1, starting transfers between devices: 1.08 us -> 3.01 us  [per_device(): rows = (rows, lax.ppermute(rows, 'co', swap))]
    ppermute x28 -> x32, starting transfers between devices: 47.8 us -> 46.7 us  [the longest x27 34.1 us: moved(): return lax.ppermute(value, axis, ring(shift))]
  transfers between devices with their start and end apart: 30 -> 33, of which waited for: 19 -> 20; matrix products, arithmetic and copies ran while one was open for 3% -> 1% of each run, Pallas kernels for 6% -> 5%
where the time goes in v4:
time: 160 us; the launch traced here: 161 us
  waiting for transfers between devices  96.8 us (60%)
  starting transfers between devices  49.8 us (31%)
  Pallas kernels  10.3 us (6%)
  other arithmetic  2.4 us (2%)
    ppermute x27, waiting for transfers between devices, moved(): return lax.ppermute(value, axis, ring(shift))  87 us
    ppermute x27, starting transfers between devices, moved(): return lax.ppermute(value, axis, ring(shift))  34.1 us
    ppermute x4, starting transfers between devices, per_device(): blocks.append(lax.ppermute(block, CARDINAL, owner(w, v)))  12 us
    ppermute x4, waiting for transfers between devices, per_device(): blocks.append(lax.ppermute(block, CARDINAL, owner(w, v)))  8.35 us
    pallas_call x1, Pallas kernels, attention(): pl.pallas_call(attention_kernel, out_shape=(jax.ShapeDtypeStruct((ROWS, H...  8.18 us
  transfers between devices with their start and end apart: 33, of which 20 were waited for; matrix products, arithmetic and copies ran while one was open for 1% of the time, Pallas kernels for 5%

profile of v4, /device:TPU:1, one launch (start us, length us, event | category | flops | bytes accessed | tf_op | source)
XLA Modules:
  0.0 161.0 jit_solution(1834748523721313346)
XLA Ops:
  0.6 0.9 fusion.8
  1.6 5.3 %collective-permute-start.2 = (bf16[224,256]{1,0:T(8,128)(2,1)S(1)}, bf16[224,256]{1,0:T(8,128)(2,1)S(1)}, u32[]{:S(2)}, u32[]{:S(2)}) collective-permute-start(bf16[224,256]{1,0:T(8,128)(2,1)S(1)} %get-tuple-element.74), channel_id=1, source_target_pairs={{0,48},{16,0},{32,16},{48,32},{1,49},{17,1},{33,17},{49,33},{2,50}... | collective-permute-start | bytes 344072 | tf_op jit(solution)/shard_map/ppermute | solution.py:277
  6.8 0.4 collective-permute-start
  7.2 1.4 collective-permute-done.2
  8.6 8.1 %collective-permute-done.1 = bf16[224,256]{1,0:T(8,128)(2,1)S(1)} collective-permute-done((bf16[224,256]{1,0:T(8,128)(2,1)S(1)}, bf16[224,256]{1,0:T(8,128)(2,1)S(1)}, u32[]{:S(2)}, u32[]{:S(2)}) %collective-permute-start.1) | collective-permute-done | bytes 114720 | tf_op jit(solution)/shard_map/ppermute | solution.py:277
  16.8 1.4 collective-permute-start.3
  18.2 0.1 shard_map.103
  18.3 1.3 collective-permute-start.6
  19.6 2.5 %collective-permute-start.7 = (bf16[224,512]{1,0:T(8,128)(2,1)S(1)}, bf16[224,512]{1,0:T(8,128)(2,1)S(1)}, u32[]{:S(2)}, u32[]{:S(2)}) collective-permute-start(bf16[224,512]{1,0:T(8,128)(2,1)S(1)} %get-tuple-element.37), channel_id=1, source_target_pairs={{0,2},{1,3},{2,0},{3,1},{4,6},{5,7},{6,4},{7,5},{8,10},{9,11},{10,... | collective-permute-start | bytes 688136 | tf_op jit(solution)/shard_map/ppermute | solution.py:277
  22.0 1.2 collective-permute-start.8
  23.2 2.6 %collective-permute-start.4 = (bf16[4,224,256]{2,1,0:T(8,128)(2,1)S(1)}, bf16[4,224,256]{2,1,0:T(8,128)(2,1)S(1)}, u32[]{:S(2)}, u32[]{:S(2)}) collective-permute-start(bf16[4,224,256]{2,1,0:T(8,128)(2,1)S(1)} %pad_maximum_fusion.3.kv0), channel_id=1, source_target_pairs={{0,8},{4,12},{8,0},{12,4},{1,9},{5,13},{9,1},{13,5},{2,10},{6,14},... | collective-permute-start | bytes 1376264 | tf_op jit(solution)/shard_map/ppermute | solution.py:277
  25.8 1.1 collective-permute-start.5
  26.9 0.1 concatenate.12.facts
  27.0 4.3 %collective-permute-done.7 = bf16[224,512]{1,0:T(8,128)(2,1)S(1)} collective-permute-done((bf16[224,512]{1,0:T(8,128)(2,1)S(1)}, bf16[224,512]{1,0:T(8,128)(2,1)S(1)}, u32[]{:S(2)}, u32[]{:S(2)}) %collective-permute-start.7) | collective-permute-done | bytes 229408 | tf_op jit(solution)/shard_map/ppermute | solution.py:277
  31.2 0.1 pad_maximum_fusion
  31.4 0.1 dynamic-slice_bitcast_fusion
  31.5 0.1 collective-permute-start.9
  31.5 1.7 %collective-permute-start.10 = (bf16[224,512]{1,0:T(8,128)(2,1)S(1)}, bf16[224,512]{1,0:T(8,128)(2,1)S(1)}, u32[]{:S(2)}, u32[]{:S(2)}) collective-permute-start(bf16[224,512]{1,0:T(8,128)(2,1)S(1)} %get-tuple-element.62), channel_id=1, source_target_pairs={{0,32},{16,48},{32,0},{48,16},{1,33},{17,49},{33,1},{49,17},{2,34}... | collective-permute-start | bytes 688136 | tf_op jit(solution)/shard_map/ppermute | solution.py:277
  33.2 2.3 %collective-permute-start.11 = (bf16[224,512]{1,0:T(8,128)(2,1)S(1)}, bf16[224,512]{1,0:T(8,128)(2,1)S(1)}, u32[]{:S(2)}, u32[]{:S(2)}) collective-permute-start(bf16[224,512]{1,0:T(8,128)(2,1)S(1)} %get-tuple-element.61), channel_id=1, source_target_pairs={{0,48},{16,0},{32,16},{48,32},{1,49},{17,1},{33,17},{49,33},{2,50}... | collective-permute-start | bytes 688136 | tf_op jit(solution)/shard_map/ppermute | solution.py:277
  35.5 4.6 %collective-permute-done.4.kv2 = bf16[4,224,256]{2,1,0:T(8,128)(2,1)S(1)} collective-permute-done((bf16[4,224,256]{2,1,0:T(8,128)(2,1)S(1)}, bf16[4,224,256]{2,1,0:T(8,128)(2,1)S(1)}, u32[]{:S(2)}, u32[]{:S(2)}) %collective-permute-start.4) | collective-permute-done | bytes 458784 | tf_op jit(solution)/shard_map/ppermute | solution.py:277
  40.1 4.9 %collective-permute-done.5.kv3 = bf16[4,224,256]{2,1,0:T(8,128)(2,1)S(1)} collective-permute-done((bf16[4,224,256]{2,1,0:T(8,128)(2,1)S(1)}, bf16[4,224,256]{2,1,0:T(8,128)(2,1)S(1)}, u32[]{:S(2)}, u32[]{:S(2)}) %collective-permute-start.5) | collective-permute-done | bytes 458784 | tf_op jit(solution)/shard_map/ppermute | solution.py:277
  45.0 8.2 %shard_map.102 = (bf16[224,1024]{1,0:T(8,128)(2,1)}, bf16[4,224,256]{2,1,0:T(8,128)(2,1)S(1)}, bf16[4,224,256]{2,1,0:T(8,128)(2,1)S(1)}, bf16[4,224,256]{2,1,0:T(8,128)(2,1)S(1)}, bf16[4,224,256]{2,1,0:T(8,128)(2,1)S(1)}) custom-call(s32[25]{0:T(128)S(1)} %concatenate.12.facts, bf16[224,1024]{1,0:T(8,128)(2,1)S(1)} %bitcast.66, ...), custom_call_target="tpu_custom_call" | custom-call | flops 6000000000 | bytes 6000000 | tf_op jit(solution)/shard_map/pallas_call | solution.py:169
  53.2 7.0 %collective-permute-start.14 = (bf16[4,224,256]{2,1,0:T(8,128)(2,1)S(1)}, bf16[4,224,256]{2,1,0:T(8,128)(2,1)S(1)}, u32[]{:S(2)}, u32[]{:S(2)}) collective-permute-start(bf16[4,224,256]{2,1,0:T(8,128)(2,1)S(1)} %get-tuple-element.46), channel_id=1, source_target_pairs={{0,12},{4,0},{8,4},{12,8},{1,13},{5,1},{9,5},{13,9},{2,14},{6,2},{... | collective-permute-start | bytes 1376264 | tf_op jit(solution)/shard_map/ppermute | solution.py:277
  60.3 0.9 collective-permute-start.12
  61.1 0.1 pad_maximum_fusion.1
  61.2 0.1 constant_dynamic-slice_fusion.1
  61.3 0.7 collective-permute-start.18
  62.0 17.0 %collective-permute-done.14 = bf16[4,224,256]{2,1,0:T(8,128)(2,1)S(1)} collective-permute-done((bf16[4,224,256]{2,1,0:T(8,128)(2,1)S(1)}, bf16[4,224,256]{2,1,0:T(8,128)(2,1)S(1)}, u32[]{:S(2)}, u32[]{:S(2)}) %collective-permute-start.14) | collective-permute-done | bytes 458784 | tf_op jit(solution)/shard_map/ppermute | solution.py:277
  79.0 3.9 %collective-permute-done.12 = bf16[4,224,256]{2,1,0:T(8,128)(2,1)S(1)} collective-permute-done((bf16[4,224,256]{2,1,0:T(8,128)(2,1)S(1)}, bf16[4,224,256]{2,1,0:T(8,128)(2,1)S(1)}, u32[]{:S(2)}, u32[]{:S(2)}) %collective-permute-start.12) | collective-permute-done | bytes 458784 | tf_op jit(solution)/shard_map/ppermute | solution.py:277
  82.9 0.2 fusion.3
  83.1 1.3 collective-permute-start.17
  84.4 0.4 collective-permute-start.15
  84.7 0.1 pad_maximum_fusion.2.hid0
  84.8 0.8 collective-permute-start.19
  85.6 0.4 collective-permute-start.20
  86.0 1.4 collective-permute-done.17
  87.4 0.7 collective-permute-start.21
  88.1 7.0 %collective-permute-done.16 = bf16[224,256]{1,0:T(8,128)(2,1)S(1)} collective-permute-done((bf16[224,256]{1,0:T(8,128)(2,1)S(1)}, bf16[224,256]{1,0:T(8,128)(2,1)S(1)}, u32[]{:S(2)}, u32[]{:S(2)}) %collective-permute-start.16) | collective-permute-done | bytes 114720 | tf_op jit(solution)/shard_map/ppermute | solution.py:277
  95.1 0.1 fusion.2
  95.2 0.1 collective-permute-start.24
  95.3 1.0 collective-permute-start.23
  96.3 3.4 %collective-permute-done.24 = bf16[224,256]{1,0:T(8,128)(2,1)S(1)} collective-permute-done((bf16[224,256]{1,0:T(8,128)(2,1)S(1)}, bf16[224,256]{1,0:T(8,128)(2,1)S(1)}, u32[]{:S(2)}, u32[]{:S(2)}) %collective-permute-start.24) | collective-permute-done | bytes 114720 | tf_op jit(solution)/shard_map/ppermute | solution.py:277
  99.7 4.2 %collective-permute-done.23 = bf16[224,256]{1,0:T(8,128)(2,1)S(1)} collective-permute-done((bf16[224,256]{1,0:T(8,128)(2,1)S(1)}, bf16[224,256]{1,0:T(8,128)(2,1)S(1)}, u32[]{:S(2)}, u32[]{:S(2)}) %collective-permute-start.23) | collective-permute-done | bytes 114720 | tf_op jit(solution)/shard_map/ppermute | solution.py:277
  103.9 1.4 collective-permute-done.22
  105.3 3.0 %collective-permute-start.25 = (bf16[4,224,256]{2,1,0:T(8,128)(2,1)S(1)}, bf16[4,224,256]{2,1,0:T(8,128)(2,1)S(1)}, u32[]{:S(2)}, u32[]{:S(2)}) collective-permute-start(bf16[4,224,256]{2,1,0:T(8,128)(2,1)S(1)} %pad_maximum_fusion.4.refs_0_), channel_id=1, source_target_pairs={{0,64},{64,0},{1,65},{65,1},{2,66},{66,2},{3,67},{67,3},{4,68},{68... | collective-permute-start | bytes 1376264 | tf_op jit(solution)/shard_map/ppermute | solution.py:307
  108.3 1.4 collective-permute-done.25.refs_1_
  109.8 14.9 %collective-permute-done.20.hid2 = bf16[1792,256]{1,0:T(8,128)(2,1)S(1)} collective-permute-done((bf16[1792,256]{1,0:T(8,128)(2,1)S(1)}, bf16[1792,256]{1,0:T(8,128)(2,1)S(1)}, u32[]{:S(2)}, u32[]{:S(2)}) %collective-permute-start.20) | collective-permute-done | bytes 917536 | tf_op jit(solution)/shard_map/ppermute | solution.py:277
  124.6 2.9 %collective-permute-done.21.hid3 = bf16[1792,256]{1,0:T(8,128)(2,1)S(1)} collective-permute-done((bf16[1792,256]{1,0:T(8,128)(2,1)S(1)}, bf16[1792,256]{1,0:T(8,128)(2,1)S(1)}, u32[]{:S(2)}, u32[]{:S(2)}) %collective-permute-start.21) | collective-permute-done | bytes 917536 | tf_op jit(solution)/shard_map/ppermute | solution.py:277
  127.6 2.0 %shard_map.104 = (bf16[4,16,1024]{2,1,0:T(8,128)(2,1)S(1)}, bf16[4,16,1024]{2,1,0:T(8,128)(2,1)S(1)}, bf16[4,16,1024]{2,1,0:T(8,128)(2,1)S(1)}, bf16[4,16,1024]{2,1,0:T(8,128)(2,1)S(1)}) custom-call(s32[25]{0:T(128)S(1)} %concatenate.12.facts, bf16[1792,256]{1,0:T(8,128)(2,1)S(1)} %pad_maximum_fusion.2.hid0, ...), custom_call_target="tpu_custom_call" | custom-call | flops 1000000000 | bytes 6000000 | tf_op jit(solution)/shard_map/pallas_call | solution.py:255
  129.6 0.9 collective-permute-start.28
  130.5 0.4 collective-permute-start.27
  130.8 0.8 collective-permute-start.26
  131.6 1.9 %collective-permute-done.28 = bf16[4,16,1024]{2,1,0:T(8,128)(2,1)S(1)} collective-permute-done((bf16[4,16,1024]{2,1,0:T(8,128)(2,1)S(1)}, bf16[4,16,1024]{2,1,0:T(8,128)(2,1)S(1)}, u32[]{:S(2)}, u32[]{:S(2)}) %collective-permute-start.28) | collective-permute-done | bytes 131104 | tf_op jit(solution)/shard_map/ppermute | solution.py:277
  133.5 2.4 %collective-permute-done.27 = bf16[4,16,1024]{2,1,0:T(8,128)(2,1)S(1)} collective-permute-done((bf16[4,16,1024]{2,1,0:T(8,128)(2,1)S(1)}, bf16[4,16,1024]{2,1,0:T(8,128)(2,1)S(1)}, u32[]{:S(2)}, u32[]{:S(2)}) %collective-permute-start.27) | collective-permute-done | bytes 131104 | tf_op jit(solution)/shard_map/ppermute | solution.py:277
  135.9 3.4 %collective-permute-done.26 = bf16[4,16,1024]{2,1,0:T(8,128)(2,1)S(1)} collective-permute-done((bf16[4,16,1024]{2,1,0:T(8,128)(2,1)S(1)}, bf16[4,16,1024]{2,1,0:T(8,128)(2,1)S(1)}, u32[]{:S(2)}, u32[]{:S(2)}) %collective-permute-start.26) | collective-permute-done | bytes 131104 | tf_op jit(solution)/shard_map/ppermute | solution.py:277
  139.3 0.1 add_convert_fusion
  139.4 6.7 %collective-permute-start.30 = (bf16[16,1024]{1,0:T(8,128)(2,1)S(1)}, bf16[16,1024]{1,0:T(8,128)(2,1)S(1)}, u32[]{:S(2)}, u32[]{:S(2)}) collective-permute-start(bf16[16,1024]{1,0:T(8,128)(2,1)S(1)} %get-tuple-element.69), channel_id=1, source_target_pairs={{0,128},{1,160},{2,192},{3,224},{4,132},{5,164},{6,196},{7,228},{8... | collective-permute-start | bytes 98312 | tf_op jit(solution)/shard_map/ppermute | solution.py:317
  146.1 4.7 %collective-permute-start.29 = (bf16[16,1024]{1,0:T(8,128)(2,1)S(1)}, bf16[16,1024]{1,0:T(8,128)(2,1)S(1)}, u32[]{:S(2)}, u32[]{:S(2)}) collective-permute-start(bf16[16,1024]{1,0:T(8,128)(2,1)S(1)} %get-tuple-element.70), channel_id=1, source_target_pairs={{0,0},{1,32},{2,64},{3,96},{4,4},{5,36},{6,68},{7,100},{8,8},{9,40... | collective-permute-start | bytes 98312 | tf_op jit(solution)/shard_map/ppermute | solution.py:317
  150.9 0.1 collective-permute-start.32
  151.0 0.4 collective-permute-start.31
  151.4 0.6 slice_bitcast_fusion
  152.0 0.8 collective-permute-done.29
  152.8 7.5 %collective-permute-done.32 = bf16[16,1024]{1,0:T(8,128)(2,1)S(1)} collective-permute-done((bf16[16,1024]{1,0:T(8,128)(2,1)S(1)}, bf16[16,1024]{1,0:T(8,128)(2,1)S(1)}, u32[]{:S(2)}, u32[]{:S(2)}) %collective-permute-start.32) | collective-permute-done | bytes 32800 | tf_op jit(solution)/shard_map/ppermute | solution.py:317
  160.4 0.7 pad_maximum_fusion.5
  (31 shorter events, 0.2 us)
Async XLA Ops:
  0.6 17.5 %copy-start = (bf16[1,224,2048]{2,1,0:T(8,128)(2,1)S(1)}, bf16[1,224,2048]{2,1,0:T(8,128)(2,1)}, u32[]{:S(2)}) copy-start(bf16[1,224,2048]{2,1,0:T(8,128)(2,1)} %param.7) | copy-start | bytes 2752516
  1.6 7.0 %collective-permute-start.2 = (bf16[224,256]{1,0:T(8,128)(2,1)S(1)}, bf16[224,256]{1,0:T(8,128)(2,1)S(1)}, u32[]{:S(2)}, u32[]{:S(2)}) collective-permute-start(bf16[224,256]{1,0:T(8,128)(2,1)S(1)} %get-tuple-element.74), channel_id=1, source_target_pairs={{0,48},{16,0},{32,16},{48,32},{1,49},{17,1},{33,17},{49,33},{2,50}... | collective-permute-start | bytes 344072 | tf_op jit(solution)/shard_map/ppermute | solution.py:277
  6.8 9.9 %collective-permute-start.1 = (bf16[224,256]{1,0:T(8,128)(2,1)S(1)}, bf16[224,256]{1,0:T(8,128)(2,1)S(1)}, u32[]{:S(2)}, u32[]{:S(2)}) collective-permute-start(bf16[224,256]{1,0:T(8,128)(2,1)S(1)} %get-tuple-element.74), channel_id=1, source_target_pairs={{0,32},{16,48},{32,0},{48,16},{1,33},{17,49},{33,1},{49,17},{2,34}... | collective-permute-start | bytes 344072 | tf_op jit(solution)/shard_map/ppermute | solution.py:277
  6.8 9.9 %collective-permute-start = (bf16[224,256]{1,0:T(8,128)(2,1)S(1)}, bf16[224,256]{1,0:T(8,128)(2,1)S(1)}, u32[]{:S(2)}, u32[]{:S(2)}) collective-permute-start(bf16[224,256]{1,0:T(8,128)(2,1)S(1)} %get-tuple-element.74), channel_id=1, source_target_pairs={{0,16},{16,32},{32,48},{48,0},{1,17},{17,33},{33,49},{49,1},{2,18}... | collective-permute-start | bytes 344072 | tf_op jit(solution)/shard_map/ppermute | solution.py:277
  16.7 10.2 %copy-start.3 = (s32[1,6]{1,0:T(1,128)S(1)}, s32[1,6]{1,0:T(1,128)}, u32[]{:S(2)}) copy-start(s32[1,6]{1,0:T(1,128)} %param.12) | copy-start | bytes 76
  16.7 10.2 %copy-start.4 = (s32[16]{0:T(128)S(1)}, s32[16]{0:T(128)}, u32[]{:S(2)}) copy-start(s32[16]{0:T(128)} %param.13) | copy-start | bytes 196
  16.8 14.4 %collective-permute-start.3 = (bf16[4,224,256]{2,1,0:T(8,128)(2,1)S(1)}, bf16[4,224,256]{2,1,0:T(8,128)(2,1)S(1)}, u32[]{:S(2)}, u32[]{:S(2)}) collective-permute-start(bf16[4,224,256]{2,1,0:T(8,128)(2,1)S(1)} %pad_maximum_fusion.3.kv0), channel_id=1, source_target_pairs={{0,4},{4,8},{8,12},{12,0},{1,5},{5,9},{9,13},{13,1},{2,6},{6,10},{... | collective-permute-start | bytes 1376264 | tf_op jit(solution)/shard_map/ppermute | solution.py:277
  18.3 7.5 %collective-permute-start.6 = (bf16[224,512]{1,0:T(8,128)(2,1)S(1)}, bf16[224,512]{1,0:T(8,128)(2,1)S(1)}, u32[]{:S(2)}, u32[]{:S(2)}) collective-permute-start(bf16[224,512]{1,0:T(8,128)(2,1)S(1)} %get-tuple-element.36), channel_id=1, source_target_pairs={{0,1},{1,2},{2,3},{3,0},{4,5},{5,6},{6,7},{7,4},{8,9},{9,10},{10,1... | collective-permute-start | bytes 688136 | tf_op jit(solution)/shard_map/ppermute | solution.py:277
  19.6 11.6 %collective-permute-start.7 = (bf16[224,512]{1,0:T(8,128)(2,1)S(1)}, bf16[224,512]{1,0:T(8,128)(2,1)S(1)}, u32[]{:S(2)}, u32[]{:S(2)}) collective-permute-start(bf16[224,512]{1,0:T(8,128)(2,1)S(1)} %get-tuple-element.37), channel_id=1, source_target_pairs={{0,2},{1,3},{2,0},{3,1},{4,6},{5,7},{6,4},{7,5},{8,10},{9,11},{10,... | collective-permute-start | bytes 688136 | tf_op jit(solution)/shard_map/ppermute | solution.py:277
  22.0 9.2 %collective-permute-start.8 = (bf16[224,512]{1,0:T(8,128)(2,1)S(1)}, bf16[224,512]{1,0:T(8,128)(2,1)S(1)}, u32[]{:S(2)}, u32[]{:S(2)}) collective-permute-start(bf16[224,512]{1,0:T(8,128)(2,1)S(1)} %get-tuple-element.38), channel_id=1, source_target_pairs={{0,3},{1,0},{2,1},{3,2},{4,7},{5,4},{6,5},{7,6},{8,11},{9,8},{10,9... | collective-permute-start | bytes 688136 | tf_op jit(solution)/shard_map/ppermute | solution.py:277
  23.2 16.9 %collective-permute-start.4 = (bf16[4,224,256]{2,1,0:T(8,128)(2,1)S(1)}, bf16[4,224,256]{2,1,0:T(8,128)(2,1)S(1)}, u32[]{:S(2)}, u32[]{:S(2)}) collective-permute-start(bf16[4,224,256]{2,1,0:T(8,128)(2,1)S(1)} %pad_maximum_fusion.3.kv0), channel_id=1, source_target_pairs={{0,8},{4,12},{8,0},{12,4},{1,9},{5,13},{9,1},{13,5},{2,10},{6,14},... | collective-permute-start | bytes 1376264 | tf_op jit(solution)/shard_map/ppermute | solution.py:277
  25.8 19.2 %collective-permute-start.5 = (bf16[4,224,256]{2,1,0:T(8,128)(2,1)S(1)}, bf16[4,224,256]{2,1,0:T(8,128)(2,1)S(1)}, u32[]{:S(2)}, u32[]{:S(2)}) collective-permute-start(bf16[4,224,256]{2,1,0:T(8,128)(2,1)S(1)} %pad_maximum_fusion.3.kv0), channel_id=1, source_target_pairs={{0,12},{4,0},{8,4},{12,8},{1,13},{5,1},{9,5},{13,9},{2,14},{6,2},{... | collective-permute-start | bytes 1376264 | tf_op jit(solution)/shard_map/ppermute | solution.py:277
  31.4 13.7 %copy-start.1 = (bf16[1,224,1024]{2,1,0:T(8,128)(2,1)S(1)}, bf16[1,224,1024]{2,1,0:T(8,128)(2,1)}, u32[]{:S(2)}) copy-start(bf16[1,224,1024]{2,1,0:T(8,128)(2,1)} %param.8) | copy-start | bytes 1376260
  31.4 13.7 %copy-start.2 = (bf16[1,224,1024]{2,1,0:T(8,128)(2,1)S(1)}, bf16[1,224,1024]{2,1,0:T(8,128)(2,1)}, u32[]{:S(2)}) copy-start(bf16[1,224,1024]{2,1,0:T(8,128)(2,1)} %param.11) | copy-start | bytes 1376260
  31.5 21.8 %collective-permute-start.9 = (bf16[224,512]{1,0:T(8,128)(2,1)S(1)}, bf16[224,512]{1,0:T(8,128)(2,1)S(1)}, u32[]{:S(2)}, u32[]{:S(2)}) collective-permute-start(bf16[224,512]{1,0:T(8,128)(2,1)S(1)} %get-tuple-element.63), channel_id=1, source_target_pairs={{0,16},{16,32},{32,48},{48,0},{1,17},{17,33},{33,49},{49,1},{2,18}... | collective-permute-start | bytes 688136 | tf_op jit(solution)/shard_map/ppermute | solution.py:277
  31.5 21.7 %collective-permute-start.10 = (bf16[224,512]{1,0:T(8,128)(2,1)S(1)}, bf16[224,512]{1,0:T(8,128)(2,1)S(1)}, u32[]{:S(2)}, u32[]{:S(2)}) collective-permute-start(bf16[224,512]{1,0:T(8,128)(2,1)S(1)} %get-tuple-element.62), channel_id=1, source_target_pairs={{0,32},{16,48},{32,0},{48,16},{1,33},{17,49},{33,1},{49,17},{2,34}... | collective-permute-start | bytes 688136 | tf_op jit(solution)/shard_map/ppermute | solution.py:277
  33.2 20.0 %collective-permute-start.11 = (bf16[224,512]{1,0:T(8,128)(2,1)S(1)}, bf16[224,512]{1,0:T(8,128)(2,1)S(1)}, u32[]{:S(2)}, u32[]{:S(2)}) collective-permute-start(bf16[224,512]{1,0:T(8,128)(2,1)S(1)} %get-tuple-element.61), channel_id=1, source_target_pairs={{0,48},{16,0},{32,16},{48,32},{1,49},{17,1},{33,17},{49,33},{2,50}... | collective-permute-start | bytes 688136 | tf_op jit(solution)/shard_map/ppermute | solution.py:277
  53.2 25.8 %collective-permute-start.14 = (bf16[4,224,256]{2,1,0:T(8,128)(2,1)S(1)}, bf16[4,224,256]{2,1,0:T(8,128)(2,1)S(1)}, u32[]{:S(2)}, u32[]{:S(2)}) collective-permute-start(bf16[4,224,256]{2,1,0:T(8,128)(2,1)S(1)} %get-tuple-element.46), channel_id=1, source_target_pairs={{0,12},{4,0},{8,4},{12,8},{1,13},{5,1},{9,5},{13,9},{2,14},{6,2},{... | collective-permute-start | bytes 1376264 | tf_op jit(solution)/shard_map/ppermute | solution.py:277
  60.3 18.8 %collective-permute-start.13 = (bf16[4,224,256]{2,1,0:T(8,128)(2,1)S(1)}, bf16[4,224,256]{2,1,0:T(8,128)(2,1)S(1)}, u32[]{:S(2)}, u32[]{:S(2)}) collective-permute-start(bf16[4,224,256]{2,1,0:T(8,128)(2,1)S(1)} %get-tuple-element.45), channel_id=1, source_target_pairs={{0,8},{4,12},{8,0},{12,4},{1,9},{5,13},{9,1},{13,5},{2,10},{6,14},... | collective-permute-start | bytes 1376264 | tf_op jit(solution)/shard_map/ppermute | solution.py:277
  60.3 22.7 %collective-permute-start.12 = (bf16[4,224,256]{2,1,0:T(8,128)(2,1)S(1)}, bf16[4,224,256]{2,1,0:T(8,128)(2,1)S(1)}, u32[]{:S(2)}, u32[]{:S(2)}) collective-permute-start(bf16[4,224,256]{2,1,0:T(8,128)(2,1)S(1)} %get-tuple-element.44), channel_id=1, source_target_pairs={{0,4},{4,8},{8,12},{12,0},{1,5},{5,9},{9,13},{13,1},{2,6},{6,10},{... | collective-permute-start | bytes 1376264 | tf_op jit(solution)/shard_map/ppermute | solution.py:277
  61.3 23.4 %collective-permute-start.18 = (bf16[4,224,256]{2,1,0:T(8,128)(2,1)S(1)}, bf16[4,224,256]{2,1,0:T(8,128)(2,1)S(1)}, u32[]{:S(2)}, u32[]{:S(2)}) collective-permute-start(bf16[4,224,256]{2,1,0:T(8,128)(2,1)S(1)} %get-tuple-element.60), channel_id=1, source_target_pairs={{0,64},{64,0},{1,65},{65,1},{2,66},{66,2},{3,67},{67,3},{4,68},{68... | collective-permute-start | bytes 1376264 | tf_op jit(solution)/shard_map/ppermute | solution.py:297
  83.1 4.3 %collective-permute-start.17 = (bf16[224,256]{1,0:T(8,128)(2,1)S(1)}, bf16[224,256]{1,0:T(8,128)(2,1)S(1)}, u32[]{:S(2)}, u32[]{:S(2)}) collective-permute-start(bf16[224,256]{1,0:T(8,128)(2,1)S(1)} %get-tuple-element.57), channel_id=1, source_target_pairs={{0,48},{16,0},{32,16},{48,32},{1,49},{17,1},{33,17},{49,33},{2,50}... | collective-permute-start | bytes 344072 | tf_op jit(solution)/shard_map/ppermute | solution.py:277
  84.4 10.7 %collective-permute-start.16 = (bf16[224,256]{1,0:T(8,128)(2,1)S(1)}, bf16[224,256]{1,0:T(8,128)(2,1)S(1)}, u32[]{:S(2)}, u32[]{:S(2)}) collective-permute-start(bf16[224,256]{1,0:T(8,128)(2,1)S(1)} %get-tuple-element.58), channel_id=1, source_target_pairs={{0,32},{16,48},{32,0},{48,16},{1,33},{17,49},{33,1},{49,17},{2,34}... | collective-permute-start | bytes 344072 | tf_op jit(solution)/shard_map/ppermute | solution.py:277
  84.4 10.7 %collective-permute-start.15 = (bf16[224,256]{1,0:T(8,128)(2,1)S(1)}, bf16[224,256]{1,0:T(8,128)(2,1)S(1)}, u32[]{:S(2)}, u32[]{:S(2)}) collective-permute-start(bf16[224,256]{1,0:T(8,128)(2,1)S(1)} %get-tuple-element.56), channel_id=1, source_target_pairs={{0,16},{16,32},{32,48},{48,0},{1,17},{17,33},{33,49},{49,1},{2,18}... | collective-permute-start | bytes 344072 | tf_op jit(solution)/shard_map/ppermute | solution.py:277
  84.8 25.0 %collective-permute-start.19 = (bf16[1792,256]{1,0:T(8,128)(2,1)S(1)}, bf16[1792,256]{1,0:T(8,128)(2,1)S(1)}, u32[]{:S(2)}, u32[]{:S(2)}) collective-permute-start(bf16[1792,256]{1,0:T(8,128)(2,1)S(1)} %pad_maximum_fusion.2.hid0), channel_id=1, source_target_pairs={{0,1},{1,2},{2,3},{3,0},{4,5},{5,6},{6,7},{7,4},{8,9},{9,10},{10,1... | collective-permute-start | bytes 2752520 | tf_op jit(solution)/shard_map/ppermute | solution.py:277
  85.6 39.1 %collective-permute-start.20 = (bf16[1792,256]{1,0:T(8,128)(2,1)S(1)}, bf16[1792,256]{1,0:T(8,128)(2,1)S(1)}, u32[]{:S(2)}, u32[]{:S(2)}) collective-permute-start(bf16[1792,256]{1,0:T(8,128)(2,1)S(1)} %pad_maximum_fusion.2.hid0), channel_id=1, source_target_pairs={{0,2},{1,3},{2,0},{3,1},{4,6},{5,7},{6,4},{7,5},{8,10},{9,11},{10,... | collective-permute-start | bytes 2752520 | tf_op jit(solution)/shard_map/ppermute | solution.py:277
  87.4 40.2 %collective-permute-start.21 = (bf16[1792,256]{1,0:T(8,128)(2,1)S(1)}, bf16[1792,256]{1,0:T(8,128)(2,1)S(1)}, u32[]{:S(2)}, u32[]{:S(2)}) collective-permute-start(bf16[1792,256]{1,0:T(8,128)(2,1)S(1)} %pad_maximum_fusion.2.hid0), channel_id=1, source_target_pairs={{0,3},{1,0},{2,1},{3,2},{4,7},{5,4},{6,5},{7,6},{8,11},{9,8},{10,9... | collective-permute-start | bytes 2752520 | tf_op jit(solution)/shard_map/ppermute | solution.py:277
  95.2 4.5 %collective-permute-start.24 = (bf16[224,256]{1,0:T(8,128)(2,1)S(1)}, bf16[224,256]{1,0:T(8,128)(2,1)S(1)}, u32[]{:S(2)}, u32[]{:S(2)}) collective-permute-start(bf16[224,256]{1,0:T(8,128)(2,1)S(1)} %fusion.2), channel_id=1, source_target_pairs={{0,48},{16,0},{32,16},{48,32},{1,49},{17,1},{33,17},{49,33},{2,50}... | collective-permute-start | bytes 344072 | tf_op jit(solution)/shard_map/ppermute | solution.py:277
  95.3 8.6 %collective-permute-start.23 = (bf16[224,256]{1,0:T(8,128)(2,1)S(1)}, bf16[224,256]{1,0:T(8,128)(2,1)S(1)}, u32[]{:S(2)}, u32[]{:S(2)}) collective-permute-start(bf16[224,256]{1,0:T(8,128)(2,1)S(1)} %fusion.2), channel_id=1, source_target_pairs={{0,32},{16,48},{32,0},{48,16},{1,33},{17,49},{33,1},{49,17},{2,34}... | collective-permute-start | bytes 344072 | tf_op jit(solution)/shard_map/ppermute | solution.py:277
  99.7 5.5 %collective-permute-start.22 = (bf16[224,256]{1,0:T(8,128)(2,1)S(1)}, bf16[224,256]{1,0:T(8,128)(2,1)S(1)}, u32[]{:S(2)}, u32[]{:S(2)}) collective-permute-start(bf16[224,256]{1,0:T(8,128)(2,1)S(1)} %fusion.2), channel_id=1, source_target_pairs={{0,16},{16,32},{32,48},{48,0},{1,17},{17,33},{33,49},{49,1},{2,18}... | collective-permute-start | bytes 344072 | tf_op jit(solution)/shard_map/ppermute | solution.py:277
  105.3 4.5 %collective-permute-start.25 = (bf16[4,224,256]{2,1,0:T(8,128)(2,1)S(1)}, bf16[4,224,256]{2,1,0:T(8,128)(2,1)S(1)}, u32[]{:S(2)}, u32[]{:S(2)}) collective-permute-start(bf16[4,224,256]{2,1,0:T(8,128)(2,1)S(1)} %pad_maximum_fusion.4.refs_0_), channel_id=1, source_target_pairs={{0,64},{64,0},{1,65},{65,1},{2,66},{66,2},{3,67},{67,3},{4,68},{68... | collective-permute-start | bytes 1376264 | tf_op jit(solution)/shard_map/ppermute | solution.py:307
  129.6 3.9 %collective-permute-start.28 = (bf16[4,16,1024]{2,1,0:T(8,128)(2,1)S(1)}, bf16[4,16,1024]{2,1,0:T(8,128)(2,1)S(1)}, u32[]{:S(2)}, u32[]{:S(2)}) collective-permute-start(bf16[4,16,1024]{2,1,0:T(8,128)(2,1)S(1)} %get-tuple-element.55), channel_id=1, source_target_pairs={{0,12},{4,0},{8,4},{12,8},{1,13},{5,1},{9,5},{13,9},{2,14},{6,2},{... | collective-permute-start | bytes 393224 | tf_op jit(solution)/shard_map/ppermute | solution.py:277
  130.5 5.4 %collective-permute-start.27 = (bf16[4,16,1024]{2,1,0:T(8,128)(2,1)S(1)}, bf16[4,16,1024]{2,1,0:T(8,128)(2,1)S(1)}, u32[]{:S(2)}, u32[]{:S(2)}) collective-permute-start(bf16[4,16,1024]{2,1,0:T(8,128)(2,1)S(1)} %get-tuple-element.54), channel_id=1, source_target_pairs={{0,8},{4,12},{8,0},{12,4},{1,9},{5,13},{9,1},{13,5},{2,10},{6,14},... | collective-permute-start | bytes 393224 | tf_op jit(solution)/shard_map/ppermute | solution.py:277
  130.8 8.4 %collective-permute-start.26 = (bf16[4,16,1024]{2,1,0:T(8,128)(2,1)S(1)}, bf16[4,16,1024]{2,1,0:T(8,128)(2,1)S(1)}, u32[]{:S(2)}, u32[]{:S(2)}) collective-permute-start(bf16[4,16,1024]{2,1,0:T(8,128)(2,1)S(1)} %get-tuple-element.53), channel_id=1, source_target_pairs={{0,4},{4,8},{8,12},{12,0},{1,5},{5,9},{9,13},{13,1},{2,6},{6,10},{... | collective-permute-start | bytes 393224 | tf_op jit(solution)/shard_map/ppermute | solution.py:277
  139.4 12.6 %collective-permute-start.30 = (bf16[16,1024]{1,0:T(8,128)(2,1)S(1)}, bf16[16,1024]{1,0:T(8,128)(2,1)S(1)}, u32[]{:S(2)}, u32[]{:S(2)}) collective-permute-start(bf16[16,1024]{1,0:T(8,128)(2,1)S(1)} %get-tuple-element.69), channel_id=1, source_target_pairs={{0,128},{1,160},{2,192},{3,224},{4,132},{5,164},{6,196},{7,228},{8... | collective-permute-start | bytes 98312 | tf_op jit(solution)/shard_map/ppermute | solution.py:317
  146.1 6.7 %collective-permute-start.29 = (bf16[16,1024]{1,0:T(8,128)(2,1)S(1)}, bf16[16,1024]{1,0:T(8,128)(2,1)S(1)}, u32[]{:S(2)}, u32[]{:S(2)}) collective-permute-start(bf16[16,1024]{1,0:T(8,128)(2,1)S(1)} %get-tuple-element.70), channel_id=1, source_target_pairs={{0,0},{1,32},{2,64},{3,96},{4,4},{5,36},{6,68},{7,100},{8,8},{9,40... | collective-permute-start | bytes 98312 | tf_op jit(solution)/shard_map/ppermute | solution.py:317
  150.9 9.5 %collective-permute-start.32 = (bf16[16,1024]{1,0:T(8,128)(2,1)S(1)}, bf16[16,1024]{1,0:T(8,128)(2,1)S(1)}, u32[]{:S(2)}, u32[]{:S(2)}) collective-permute-start(bf16[16,1024]{1,0:T(8,128)(2,1)S(1)} %get-tuple-element.68), channel_id=1, source_target_pairs={{0,144},{1,176},{2,208},{3,240},{4,148},{5,180},{6,212},{7,244},{8... | collective-permute-start | bytes 98312 | tf_op jit(solution)/shard_map/ppermute | solution.py:317
  151.0 9.4 %collective-permute-start.31 = (bf16[16,1024]{1,0:T(8,128)(2,1)S(1)}, bf16[16,1024]{1,0:T(8,128)(2,1)S(1)}, u32[]{:S(2)}, u32[]{:S(2)}) collective-permute-start(bf16[16,1024]{1,0:T(8,128)(2,1)S(1)} %get-tuple-element.67), channel_id=1, source_target_pairs={{0,16},{1,48},{2,80},{3,112},{4,20},{5,52},{6,84},{7,116},{8,24},{... | collective-permute-start | bytes 98312 | tf_op jit(solution)/shard_map/ppermute | solution.py:317

commit v5 on v4

--- a/solution.py
+++ b/solution.py
@@ -16,6 +16,7 @@
 RANKS = 16
 BLOCKS = 2 * RANKS
 SEQ = ROWS * RANKS
+RUN = 512
 DOCS = 6
 MAX_DOC = 1194
 SPAN = 256
@@ -209,58 +210,62 @@
     return pairs
 
 
-def runs_kernel(where, hidden, *runs):
-    half = hidden.shape[1] // 2
-    width = half // 4
+def first_kernel(where, keys, values, hidden, own, *runs):
+    own[:, 0:DH] = keys[...]
+    own[:, DH : 2 * DH] = values[...]
     for j, run in enumerate(runs):
         q = lax.rem(where[0] + j, 4)
-        for h in range(2):
-            at = pl.ds(pl.multiple_of(h * half + q * width, width), width)
-            run[:, h * width : (h + 1) * width] = hidden[:, at]
-
-
-def hidden_runs(x, hidden):
+        run[...] = hidden[:, pl.ds(pl.multiple_of(q * RUN, RUN), RUN)]
+
+
+def first_messages(x, keys, values, hidden):
     vmem = pl.BlockSpec(memory_space=pltpu.VMEM)
     return pl.pallas_call(
-        runs_kernel,
-        out_shape=(jax.ShapeDtypeStruct((ROWS, 512), BF),) * 4,
-        in_specs=[pl.BlockSpec(memory_space=pltpu.SMEM), vmem],
-        out_specs=(vmem,) * 4,
+        first_kernel,
+        out_shape=(jax.ShapeDtypeStruct((ROWS, 2 * DH), BF),)
+        + (jax.ShapeDtypeStruct((ROWS, RUN), BF),) * 4,
+        in_specs=[pl.BlockSpec(memory_space=pltpu.SMEM)] + [vmem] * 3,
+        out_specs=(vmem,) * 5,
         compiler_params=pltpu.CompilerParams(vmem_limit_bytes=8 * 2**20),
         cost_estimate=pl.CostEstimate(flops=0, bytes_accessed=2 * 10**6, transcendentals=0),
-    )(x.reshape(1).astype(jnp.int32), hidden)
-
-
-def product_kernel(facts, hid0, hid1, hid2, hid3, *refs):
-    rows, outs, acc = refs[:-5], refs[-5:-1], refs[-1]
-    my_y, my_x = facts[DOCS + RANKS + 1], facts[DOCS + RANKS + 2]
+    )(x.reshape(1).astype(jnp.int32), keys, values, hidden)
+
+
+def product_kernel(facts, hid0, hid1, hid2, hid3, rows, kept, sent, acc):
+    my_y, my_x, core = (facts[DOCS + RANKS + i] for i in (1, 2, 3))
     for j, hidden in enumerate((hid0, hid1, hid2, hid3)):
         run = lax.rem(my_x + 4 - j, 4)
-        columns = pl.ds(pl.multiple_of(run * 256, 256), 256)
-        total = None
-        for i, piece in enumerate(rows):
-            tokens = hidden[i * ROWS * 4 : (i + 1) * ROWS * 4, :]
-            part = dot(piece[...].reshape(4 * ROWS, 2 * DH), tokens, 0, 0)
-            total = part if total is None else total + part
-        acc[...] = total
-        for shift, out in enumerate(outs):
-            y = lax.rem(my_y + shift, 4)
-            for block in range(4):
-                at = pl.ds(pl.multiple_of(block * 64 + y * 16, 16), 16)
-                out[block, :, columns] = acc[at, :].astype(BF)
+        half, place = run // 2, lax.rem(run, 2)
+        columns = pl.ds(pl.multiple_of(place * RUN, RUN), RUN)
+        acc[...] = dot(rows[...].reshape(4 * ROWS, 2 * DH), hidden[...], 0, 0)
+
+        def store(out):
+            for shift in range(4):
+                y = lax.rem(my_y + shift, 4)
+                for block in range(4):
+                    at = pl.ds(pl.multiple_of(block * 64 + y * 16, 16), 16)
+                    out[shift, block, :, columns] = acc[at, :].astype(BF)
+
+        @pl.when(half == core)
+        def _():
+            store(kept)
+
+        @pl.when(half != core)
+        def _():
+            store(sent)
 
 
 def weight_product(facts, hidden, rows):
     vmem = pl.BlockSpec(memory_space=pltpu.VMEM)
     return pl.pallas_call(
         product_kernel,
-        out_shape=(jax.ShapeDtypeStruct((4, 16, 1024), BF),) * 4,
-        in_specs=[pl.BlockSpec(memory_space=pltpu.SMEM)] + [vmem] * (4 + len(rows)),
-        out_specs=(vmem,) * 4,
-        scratch_shapes=[pltpu.VMEM((2 * DH, 256), F32)],
+        out_shape=(jax.ShapeDtypeStruct((4, 4, 16, 2 * RUN), BF),) * 2,
+        in_specs=[pl.BlockSpec(memory_space=pltpu.SMEM)] + [vmem] * 5,
+        out_specs=(vmem,) * 2,
+        scratch_shapes=[pltpu.VMEM((2 * DH, RUN), F32)],
         compiler_params=pltpu.CompilerParams(vmem_limit_bytes=24 * 2**20),
         cost_estimate=pl.CostEstimate(flops=10**9, bytes_accessed=6 * 10**6, transcendentals=0),
-    )(facts, *hidden, *rows)
+    )(facts, *hidden, rows)
 
 
 def after(value, *others):
@@ -271,15 +276,15 @@
     zl, y, x = (lax.axis_index(a) for a in ("zl", "y", "x"))
     zh, core = lax.axis_index("zh"), lax.axis_index("co")
     swap = [(0, 1), (1, 0)]
-    facts = jnp.concatenate([doc_lengths[0], pair_perm, jnp.stack([zl, y, x]).astype(jnp.int32)])
+    facts = jnp.concatenate([doc_lengths[0], pair_perm, jnp.stack([zl, y, x, core]).astype(jnp.int32)])
 
     def moved(value, axis, shift):
         return lax.ppermute(value, axis, ring(shift))
 
-    own = jnp.concatenate([keys_in[0], values_in[0]], axis=1)
+    own, *runs = first_messages(x, keys_in[0], values_in[0], hidden_in[0])
     column = jnp.stack([own] + [moved(own, "zl", a) for a in (1, 2, 3)])
-    runs = hidden_runs(x, hidden_in[0])
     runs = [runs[0]] + [moved(runs[j], "x", j) for j in (1, 2, 3)]
+    column, runs = lax.optimization_barrier((column, runs))
     kvs = [column] + [moved(column, "y", s) for s in (1, 2, 3)]
 
     runs = jnp.stack(after(runs, kvs[1]))
@@ -290,13 +295,8 @@
 
     dq, *dkv = attention(facts, queries[0], out_grad[0], kvs)
 
-    dkv, tokens = lax.optimization_barrier((dkv, tokens))
     got = [dkv[0]] + [moved(dkv[s], "y", s) for s in (1, 2, 3)]
-    tokens = jnp.stack(tokens)
-    mine = lax.dynamic_slice_in_dim(tokens, core * 256, 256, 2)
-    theirs = lax.ppermute(lax.dynamic_slice_in_dim(tokens, (1 - core) * 256, 256, 2), "co", swap)
-    hidden = jnp.concatenate([mine.reshape(4 * ROWS, -1), theirs.reshape(4 * ROWS, -1)], axis=0)
-    hidden = after(hidden, got[1])
+    hidden = jnp.stack(after(tokens, dkv)).reshape(4 * ROWS, RUN)
     hidden = [hidden] + [moved(hidden, "x", j) for j in (1, 2, 3)]
 
     parts = [add_up(*[g[a] for g in got]) for a in range(4)]
@@ -304,8 +304,9 @@
     grads = add_up(*parts).astype(BF)
 
     rows = jnp.stack([grads] + [moved(grads, "zl", s) for s in (1, 2, 3)])
-    rows = (rows, lax.ppermute(rows, "co", swap))
-    shares = weight_product(facts, hidden, rows)
+    kept, sent = weight_product(facts, hidden, rows)
+    sent = lax.ppermute(sent, "co", swap)
+    shares = [add_up(kept[s], sent[s]).astype(BF) for s in range(4)]
     shares = [shares[0]] + [moved(shares[s], "y", s) for s in (1, 2, 3)]
     share = add_up(*shares).astype(BF).reshape(2, 2, 16, -1)
     halves = []

time: 160 us -> 157 us (0.981)
  waiting for transfers between devices: 96.8 us -> 78.8 us
  starting transfers between devices: 49.8 us -> 61.1 us
  local copies, waits for them, and re-layouts: 0.92 us -> 4.31 us
    ppermute x27, waiting for transfers between devices: 87 us -> 68.8 us  [moved(): return lax.ppermute(value, axis, ring(shift))]
    ppermute x27, starting transfers between devices: 34.1 us -> 48.5 us  [moved(): return lax.ppermute(value, axis, ring(shift))]
    unnamed x10 -> x14, local copies, waits for them, and re-layouts: 0.02 us -> 3.49 us
    ppermute x2 -> x1, starting transfers between devices: 3.71 us -> 1.44 us  [per_device(): sent = lax.ppermute(sent, 'co', swap)]
  transfers between devices with their start and end apart: 33 -> 32, of which waited for: 20 -> 21; matrix products, arithmetic and copies ran while one was open for 1% -> 1% of each run, Pallas kernels for 5% -> 5%
where the time goes in v5:
time: 157 us
  waiting for transfers between devices  78.8 us (50%)
  starting transfers between devices  61.1 us (39%)
  Pallas kernels  10.8 us (7%)
  local copies, waits for them, and re-layouts  4.31 us (3%)
    ppermute x27, waiting for transfers between devices, moved(): return lax.ppermute(value, axis, ring(shift))  68.8 us
    ppermute x27, starting transfers between devices, moved(): return lax.ppermute(value, axis, ring(shift))  48.5 us
    ppermute x4, starting transfers between devices, per_device(): blocks.append(lax.ppermute(block, CARDINAL, owner(w, v)))  11.2 us
    ppermute x4, waiting for transfers between devices, per_device(): blocks.append(lax.ppermute(block, CARDINAL, owner(w, v)))  8.45 us
    pallas_call x1, Pallas kernels, attention(): pl.pallas_call(attention_kernel, out_shape=(jax.ShapeDtypeStruct((ROWS, H...  8.18 us
    unnamed x14, local copies, waits for them, and re-layouts  3.49 us
  transfers between devices with their start and end apart: 32, of which 21 were waited for; matrix products, arithmetic and copies ran while one was open for 1% of the time, Pallas kernels for 5%

profile of v5, /device:TPU:1, one launch (start us, length us, event | category | flops | bytes accessed | tf_op | source)
XLA Modules:
  0.0 157.3 jit_solution(6449783873167409679)
XLA Ops:
  0.6 1.2 copy-done
  1.8 0.8 copy-done.1
  2.6 0.8 copy-done.2
  3.5 5.3 %collective-permute-start.2 = (bf16[224,256]{1,0:T(8,128)(2,1)S(1)}, bf16[224,256]{1,0:T(8,128)(2,1)S(1)}, u32[]{:S(2)}, u32[]{:S(2)}) collective-permute-start(bf16[224,256]{1,0:T(8,128)(2,1)S(1)} %get-tuple-element.29), channel_id=1, source_target_pairs={{0,48},{16,0},{32,16},{48,32},{1,49},{17,1},{33,17},{49,33},{2,50}... | collective-permute-start | bytes 344072 | tf_op jit(solution)/shard_map/ppermute | solution.py:282
  8.8 0.4 collective-permute-start
  9.2 1.2 collective-permute-start.3
  10.4 2.4 %collective-permute-start.4 = (bf16[224,512]{1,0:T(8,128)(2,1)S(1)}, bf16[224,512]{1,0:T(8,128)(2,1)S(1)}, u32[]{:S(2)}, u32[]{:S(2)}) collective-permute-start(bf16[224,512]{1,0:T(8,128)(2,1)S(1)} %get-tuple-element.32), channel_id=1, source_target_pairs={{0,2},{1,3},{2,0},{3,1},{4,6},{5,7},{6,4},{7,5},{8,10},{9,11},{10,... | collective-permute-start | bytes 688136 | tf_op jit(solution)/shard_map/ppermute | solution.py:282
  12.8 1.2 collective-permute-start.5
  14.0 4.7 %collective-permute-done.1 = bf16[224,256]{1,0:T(8,128)(2,1)S(1)} collective-permute-done((bf16[224,256]{1,0:T(8,128)(2,1)S(1)}, bf16[224,256]{1,0:T(8,128)(2,1)S(1)}, u32[]{:S(2)}, u32[]{:S(2)}) %collective-permute-start.1) | collective-permute-done | bytes 114720 | tf_op jit(solution)/shard_map/ppermute | solution.py:282
  18.7 3.4 %collective-permute-done.4 = bf16[224,512]{1,0:T(8,128)(2,1)S(1)} collective-permute-done((bf16[224,512]{1,0:T(8,128)(2,1)S(1)}, bf16[224,512]{1,0:T(8,128)(2,1)S(1)}, u32[]{:S(2)}, u32[]{:S(2)}) %collective-permute-start.4) | collective-permute-done | bytes 229408 | tf_op jit(solution)/shard_map/ppermute | solution.py:282
  22.1 1.3 collective-permute-start.6
  23.4 2.6 %collective-permute-start.7 = (bf16[4,224,256]{2,1,0:T(8,128)(2,1)S(1)}, bf16[4,224,256]{2,1,0:T(8,128)(2,1)S(1)}, u32[]{:S(2)}, u32[]{:S(2)}) collective-permute-start(bf16[4,224,256]{2,1,0:T(8,128)(2,1)S(1)} %pad_maximum_fusion.2.kv0), channel_id=1, source_target_pairs={{0,8},{4,12},{8,0},{12,4},{1,9},{5,13},{9,1},{13,5},{2,10},{6,14},... | collective-permute-start | bytes 1376264 | tf_op jit(solution)/shard_map/ppermute | solution.py:282
  26.1 1.1 collective-permute-start.8
  27.1 0.7 copy-done.5
  27.9 5.4 %collective-permute-done.6.kv1 = bf16[4,224,256]{2,1,0:T(8,128)(2,1)S(1)} collective-permute-done((bf16[4,224,256]{2,1,0:T(8,128)(2,1)S(1)}, bf16[4,224,256]{2,1,0:T(8,128)(2,1)S(1)}, u32[]{:S(2)}, u32[]{:S(2)}) %collective-permute-start.6) | collective-permute-done | bytes 458784 | tf_op jit(solution)/shard_map/ppermute | solution.py:282
  33.3 0.1 pad_maximum_fusion
  33.5 1.8 %collective-permute-start.15 = (bf16[224,512]{1,0:T(8,128)(2,1)S(1)}, bf16[224,512]{1,0:T(8,128)(2,1)S(1)}, u32[]{:S(2)}, u32[]{:S(2)}) collective-permute-start(bf16[224,512]{1,0:T(8,128)(2,1)S(1)} %get-tuple-element.62), channel_id=1, source_target_pairs={{0,16},{16,32},{32,48},{48,0},{1,17},{17,33},{33,49},{49,1},{2,18}... | collective-permute-start | bytes 688136 | tf_op jit(solution)/shard_map/ppermute | solution.py:282
  35.3 8.9 %collective-permute-done.7.kv2 = bf16[4,224,256]{2,1,0:T(8,128)(2,1)S(1)} collective-permute-done((bf16[4,224,256]{2,1,0:T(8,128)(2,1)S(1)}, bf16[4,224,256]{2,1,0:T(8,128)(2,1)S(1)}, u32[]{:S(2)}, u32[]{:S(2)}) %collective-permute-start.7) | collective-permute-done | bytes 458784 | tf_op jit(solution)/shard_map/ppermute | solution.py:282
  44.3 1.0 collective-permute-done.8.kv3
  45.3 8.2 %shard_map.103 = (bf16[224,1024]{1,0:T(8,128)(2,1)}, bf16[4,224,256]{2,1,0:T(8,128)(2,1)S(1)}, bf16[4,224,256]{2,1,0:T(8,128)(2,1)S(1)}, bf16[4,224,256]{2,1,0:T(8,128)(2,1)S(1)}, bf16[4,224,256]{2,1,0:T(8,128)(2,1)S(1)}) custom-call(s32[26]{0:T(128)S(1)} %concatenate.6.facts, bf16[224,1024]{1,0:T(8,128)(2,1)S(1)} %bitcast.83, ...), custom_call_target="tpu_custom_call" | custom-call | flops 6000000000 | bytes 6000000 | tf_op jit(solution)/shard_map/pallas_call | solution.py:170
  53.4 7.0 %collective-permute-start.11 = (bf16[4,224,256]{2,1,0:T(8,128)(2,1)S(1)}, bf16[4,224,256]{2,1,0:T(8,128)(2,1)S(1)}, u32[]{:S(2)}, u32[]{:S(2)}) collective-permute-start(bf16[4,224,256]{2,1,0:T(8,128)(2,1)S(1)} %get-tuple-element.39), channel_id=1, source_target_pairs={{0,12},{4,0},{8,4},{12,8},{1,13},{5,1},{9,5},{13,9},{2,14},{6,2},{... | collective-permute-start | bytes 1376264 | tf_op jit(solution)/shard_map/ppermute | solution.py:282
  60.4 0.7 collective-permute-start.9
  61.1 3.2 %collective-permute-start.16 = (bf16[224,512]{1,0:T(8,128)(2,1)S(1)}, bf16[224,512]{1,0:T(8,128)(2,1)S(1)}, u32[]{:S(2)}, u32[]{:S(2)}) collective-permute-start(bf16[224,512]{1,0:T(8,128)(2,1)S(1)} %get-tuple-element.61), channel_id=1, source_target_pairs={{0,32},{16,48},{32,0},{48,16},{1,33},{17,49},{33,1},{49,17},{2,34}... | collective-permute-start | bytes 688136 | tf_op jit(solution)/shard_map/ppermute | solution.py:282
  64.3 6.1 %collective-permute-done.16 = bf16[224,512]{1,0:T(8,128)(2,1)S(1)} collective-permute-done((bf16[224,512]{1,0:T(8,128)(2,1)S(1)}, bf16[224,512]{1,0:T(8,128)(2,1)S(1)}, u32[]{:S(2)}, u32[]{:S(2)}) %collective-permute-start.16) | collective-permute-done | bytes 229408 | tf_op jit(solution)/shard_map/ppermute | solution.py:282
  70.4 4.4 %collective-permute-done.17 = bf16[224,512]{1,0:T(8,128)(2,1)S(1)} collective-permute-done((bf16[224,512]{1,0:T(8,128)(2,1)S(1)}, bf16[224,512]{1,0:T(8,128)(2,1)S(1)}, u32[]{:S(2)}, u32[]{:S(2)}) %collective-permute-start.17) | collective-permute-done | bytes 229408 | tf_op jit(solution)/shard_map/ppermute | solution.py:282
  74.9 0.1 pad_maximum_fusion.1
  75.0 3.0 %collective-permute-start.18 = (bf16[896,512]{1,0:T(8,128)(2,1)S(1)}, bf16[896,512]{1,0:T(8,128)(2,1)S(1)}, u32[]{:S(2)}, u32[]{:S(2)}) collective-permute-start(bf16[896,512]{1,0:T(8,128)(2,1)S(1)} %bitcast.74), channel_id=1, source_target_pairs={{0,1},{1,2},{2,3},{3,0},{4,5},{5,6},{6,7},{7,4},{8,9},{9,10},{10,1... | collective-permute-start | bytes 2752520 | tf_op jit(solution)/shard_map/ppermute | solution.py:282
  78.0 1.4 collective-permute-start.19
  79.4 1.0 collective-permute-done.11
  80.4 3.1 %collective-permute-start.20 = (bf16[896,512]{1,0:T(8,128)(2,1)S(1)}, bf16[896,512]{1,0:T(8,128)(2,1)S(1)}, u32[]{:S(2)}, u32[]{:S(2)}) collective-permute-start(bf16[896,512]{1,0:T(8,128)(2,1)S(1)} %bitcast.76), channel_id=1, source_target_pairs={{0,3},{1,0},{2,1},{3,2},{4,7},{5,4},{6,5},{7,6},{8,11},{9,8},{10,9... | collective-permute-start | bytes 2752520 | tf_op jit(solution)/shard_map/ppermute | solution.py:282
  83.5 0.5 collective-permute-done.9
  83.9 0.2 fusion.10
  84.1 0.1 collective-permute-start.14
  84.2 1.3 collective-permute-start.13
  85.6 2.9 %collective-permute-done.14 = bf16[224,256]{1,0:T(8,128)(2,1)S(1)} collective-permute-done((bf16[224,256]{1,0:T(8,128)(2,1)S(1)}, bf16[224,256]{1,0:T(8,128)(2,1)S(1)}, u32[]{:S(2)}, u32[]{:S(2)}) %collective-permute-start.14) | collective-permute-done | bytes 114720 | tf_op jit(solution)/shard_map/ppermute | solution.py:282
  88.5 0.3 collective-permute-start.12
  88.7 2.4 %collective-permute-done.13 = bf16[224,256]{1,0:T(8,128)(2,1)S(1)} collective-permute-done((bf16[224,256]{1,0:T(8,128)(2,1)S(1)}, bf16[224,256]{1,0:T(8,128)(2,1)S(1)}, u32[]{:S(2)}, u32[]{:S(2)}) %collective-permute-start.13) | collective-permute-done | bytes 114720 | tf_op jit(solution)/shard_map/ppermute | solution.py:282
  91.1 2.8 %collective-permute-done.12 = bf16[224,256]{1,0:T(8,128)(2,1)S(1)} collective-permute-done((bf16[224,256]{1,0:T(8,128)(2,1)S(1)}, bf16[224,256]{1,0:T(8,128)(2,1)S(1)}, u32[]{:S(2)}, u32[]{:S(2)}) %collective-permute-start.12) | collective-permute-done | bytes 114720 | tf_op jit(solution)/shard_map/ppermute | solution.py:282
  93.9 0.1 fusion.5
  94.0 2.3 %collective-permute-start.23 = (bf16[224,256]{1,0:T(8,128)(2,1)S(1)}, bf16[224,256]{1,0:T(8,128)(2,1)S(1)}, u32[]{:S(2)}, u32[]{:S(2)}) collective-permute-start(bf16[224,256]{1,0:T(8,128)(2,1)S(1)} %fusion.5), channel_id=1, source_target_pairs={{0,48},{16,0},{32,16},{48,32},{1,49},{17,1},{33,17},{49,33},{2,50}... | collective-permute-start | bytes 344072 | tf_op jit(solution)/shard_map/ppermute | solution.py:282
  96.3 1.7 %collective-permute-start.22 = (bf16[224,256]{1,0:T(8,128)(2,1)S(1)}, bf16[224,256]{1,0:T(8,128)(2,1)S(1)}, u32[]{:S(2)}, u32[]{:S(2)}) collective-permute-start(bf16[224,256]{1,0:T(8,128)(2,1)S(1)} %fusion.5), channel_id=1, source_target_pairs={{0,32},{16,48},{32,0},{48,16},{1,33},{17,49},{33,1},{49,17},{2,34}... | collective-permute-start | bytes 344072 | tf_op jit(solution)/shard_map/ppermute | solution.py:282
  98.0 0.5 collective-permute-done.23
  98.4 2.8 %collective-permute-start.21 = (bf16[224,256]{1,0:T(8,128)(2,1)S(1)}, bf16[224,256]{1,0:T(8,128)(2,1)S(1)}, u32[]{:S(2)}, u32[]{:S(2)}) collective-permute-start(bf16[224,256]{1,0:T(8,128)(2,1)S(1)} %fusion.5), channel_id=1, source_target_pairs={{0,16},{16,32},{32,48},{48,0},{1,17},{17,33},{33,49},{49,1},{2,18}... | collective-permute-start | bytes 344072 | tf_op jit(solution)/shard_map/ppermute | solution.py:282
  101.2 5.5 %collective-permute-done.22 = bf16[224,256]{1,0:T(8,128)(2,1)S(1)} collective-permute-done((bf16[224,256]{1,0:T(8,128)(2,1)S(1)}, bf16[224,256]{1,0:T(8,128)(2,1)S(1)}, u32[]{:S(2)}, u32[]{:S(2)}) %collective-permute-start.22) | collective-permute-done | bytes 114720 | tf_op jit(solution)/shard_map/ppermute | solution.py:282
  106.8 12.2 %collective-permute-done.19.hid2 = bf16[896,512]{1,0:T(8,128)(2,1)S(1)} collective-permute-done((bf16[896,512]{1,0:T(8,128)(2,1)S(1)}, bf16[896,512]{1,0:T(8,128)(2,1)S(1)}, u32[]{:S(2)}, u32[]{:S(2)}) %collective-permute-start.19) | collective-permute-done | bytes 917536 | tf_op jit(solution)/shard_map/ppermute | solution.py:282
  119.0 2.5 %shard_map.104 = (bf16[4,4,16,1024]{3,2,1,0:T(8,128)(2,1)S(1)}, bf16[4,4,16,1024]{3,2,1,0:T(8,128)(2,1)S(1)}) custom-call(s32[26]{0:T(128)S(1)} %concatenate.6.facts, bf16[896,512]{1,0:T(8,128)(2,1)S(1)} %bitcast.77, bf16[896,512]{1,0:T(8,128)(2,1)S(1)} %collective-permute-done.18.hid1, bf16[896,512]{1,0:T(8,128)(2,1)S(1)} %collective-permute-done.19.hid2, ...), custom_call_target="tpu_custom_call" | custom-call | flops 1000000000 | bytes 6000000 | tf_op jit(solution)/shard_map/pallas_call | solution.py:260
  121.5 1.4 collective-permute-start.24
  123.0 1.5 collective-permute-done.24
  124.5 0.1 fusion.7
  124.6 2.3 %collective-permute-start.27 = (bf16[4,16,1024]{2,1,0:T(8,128)(2,1)S(1)}, bf16[4,16,1024]{2,1,0:T(8,128)(2,1)S(1)}, u32[]{:S(2)}, u32[]{:S(2)}) collective-permute-start(bf16[4,16,1024]{2,1,0:T(8,128)(2,1)S(1)} %get-tuple-element.58), channel_id=1, source_target_pairs={{0,12},{4,0},{8,4},{12,8},{1,13},{5,1},{9,5},{13,9},{2,14},{6,2},{... | collective-permute-start | bytes 393224 | tf_op jit(solution)/shard_map/ppermute | solution.py:282
  127.0 1.7 %collective-permute-start.26 = (bf16[4,16,1024]{2,1,0:T(8,128)(2,1)S(1)}, bf16[4,16,1024]{2,1,0:T(8,128)(2,1)S(1)}, u32[]{:S(2)}, u32[]{:S(2)}) collective-permute-start(bf16[4,16,1024]{2,1,0:T(8,128)(2,1)S(1)} %get-tuple-element.59), channel_id=1, source_target_pairs={{0,8},{4,12},{8,0},{12,4},{1,9},{5,13},{9,1},{13,5},{2,10},{6,14},... | collective-permute-start | bytes 393224 | tf_op jit(solution)/shard_map/ppermute | solution.py:282
  128.7 0.4 collective-permute-start.25
  129.0 1.4 collective-permute-done.27
  130.5 2.4 %collective-permute-done.26 = bf16[4,16,1024]{2,1,0:T(8,128)(2,1)S(1)} collective-permute-done((bf16[4,16,1024]{2,1,0:T(8,128)(2,1)S(1)}, bf16[4,16,1024]{2,1,0:T(8,128)(2,1)S(1)}, u32[]{:S(2)}, u32[]{:S(2)}) %collective-permute-start.26) | collective-permute-done | bytes 131104 | tf_op jit(solution)/shard_map/ppermute | solution.py:282
  132.9 3.3 %collective-permute-done.25 = bf16[4,16,1024]{2,1,0:T(8,128)(2,1)S(1)} collective-permute-done((bf16[4,16,1024]{2,1,0:T(8,128)(2,1)S(1)}, bf16[4,16,1024]{2,1,0:T(8,128)(2,1)S(1)}, u32[]{:S(2)}, u32[]{:S(2)}) %collective-permute-start.25) | collective-permute-done | bytes 131104 | tf_op jit(solution)/shard_map/ppermute | solution.py:282
  136.2 0.1 fusion.2
  136.3 8.8 %collective-permute-start.29 = (bf16[16,1024]{1,0:T(8,128)(2,1)S(1)}, bf16[16,1024]{1,0:T(8,128)(2,1)S(1)}, u32[]{:S(2)}, u32[]{:S(2)}) collective-permute-start(bf16[16,1024]{1,0:T(8,128)(2,1)S(1)} %get-tuple-element.68), channel_id=1, source_target_pairs={{0,128},{1,160},{2,192},{3,224},{4,132},{5,164},{6,196},{7,228},{8... | collective-permute-start | bytes 98312 | tf_op jit(solution)/shard_map/ppermute | solution.py:318
  145.1 1.9 %collective-permute-start.28 = (bf16[16,1024]{1,0:T(8,128)(2,1)S(1)}, bf16[16,1024]{1,0:T(8,128)(2,1)S(1)}, u32[]{:S(2)}, u32[]{:S(2)}) collective-permute-start(bf16[16,1024]{1,0:T(8,128)(2,1)S(1)} %get-tuple-element.69), channel_id=1, source_target_pairs={{0,0},{1,32},{2,64},{3,96},{4,4},{5,36},{6,68},{7,100},{8,8},{9,40... | collective-permute-start | bytes 98312 | tf_op jit(solution)/shard_map/ppermute | solution.py:318
  147.1 0.1 collective-permute-start.31
  147.2 0.4 collective-permute-start.30
  147.6 0.6 slice_bitcast_fusion
  148.2 3.7 %collective-permute-done.28 = bf16[16,1024]{1,0:T(8,128)(2,1)S(1)} collective-permute-done((bf16[16,1024]{1,0:T(8,128)(2,1)S(1)}, bf16[16,1024]{1,0:T(8,128)(2,1)S(1)}, u32[]{:S(2)}, u32[]{:S(2)}) %collective-permute-start.28) | collective-permute-done | bytes 32800 | tf_op jit(solution)/shard_map/ppermute | solution.py:318
  151.9 4.8 %collective-permute-done.31 = bf16[16,1024]{1,0:T(8,128)(2,1)S(1)} collective-permute-done((bf16[16,1024]{1,0:T(8,128)(2,1)S(1)}, bf16[16,1024]{1,0:T(8,128)(2,1)S(1)}, u32[]{:S(2)}, u32[]{:S(2)}) %collective-permute-start.31) | collective-permute-done | bytes 32800 | tf_op jit(solution)/shard_map/ppermute | solution.py:318
  156.7 0.7 pad_maximum_fusion.4
  (31 shorter events, 0.5 us)
Async XLA Ops:
  0.6 1.2 copy-start
  1.8 0.8 copy-start.1
  2.6 0.8 copy-start.2
  3.5 9.3 %collective-permute-start.2 = (bf16[224,256]{1,0:T(8,128)(2,1)S(1)}, bf16[224,256]{1,0:T(8,128)(2,1)S(1)}, u32[]{:S(2)}, u32[]{:S(2)}) collective-permute-start(bf16[224,256]{1,0:T(8,128)(2,1)S(1)} %get-tuple-element.29), channel_id=1, source_target_pairs={{0,48},{16,0},{32,16},{48,32},{1,49},{17,1},{33,17},{49,33},{2,50}... | collective-permute-start | bytes 344072 | tf_op jit(solution)/shard_map/ppermute | solution.py:282
  8.8 9.9 %collective-permute-start.1 = (bf16[224,256]{1,0:T(8,128)(2,1)S(1)}, bf16[224,256]{1,0:T(8,128)(2,1)S(1)}, u32[]{:S(2)}, u32[]{:S(2)}) collective-permute-start(bf16[224,256]{1,0:T(8,128)(2,1)S(1)} %get-tuple-element.29), channel_id=1, source_target_pairs={{0,32},{16,48},{32,0},{48,16},{1,33},{17,49},{33,1},{49,17},{2,34}... | collective-permute-start | bytes 344072 | tf_op jit(solution)/shard_map/ppermute | solution.py:282
  8.8 9.9 %collective-permute-start = (bf16[224,256]{1,0:T(8,128)(2,1)S(1)}, bf16[224,256]{1,0:T(8,128)(2,1)S(1)}, u32[]{:S(2)}, u32[]{:S(2)}) collective-permute-start(bf16[224,256]{1,0:T(8,128)(2,1)S(1)} %get-tuple-element.29), channel_id=1, source_target_pairs={{0,16},{16,32},{32,48},{48,0},{1,17},{17,33},{33,49},{49,1},{2,18}... | collective-permute-start | bytes 344072 | tf_op jit(solution)/shard_map/ppermute | solution.py:282
  9.2 9.6 %collective-permute-start.3 = (bf16[224,512]{1,0:T(8,128)(2,1)S(1)}, bf16[224,512]{1,0:T(8,128)(2,1)S(1)}, u32[]{:S(2)}, u32[]{:S(2)}) collective-permute-start(bf16[224,512]{1,0:T(8,128)(2,1)S(1)} %get-tuple-element.31), channel_id=1, source_target_pairs={{0,1},{1,2},{2,3},{3,0},{4,5},{5,6},{6,7},{7,4},{8,9},{9,10},{10,1... | collective-permute-start | bytes 688136 | tf_op jit(solution)/shard_map/ppermute | solution.py:282
  10.4 11.8 %collective-permute-start.4 = (bf16[224,512]{1,0:T(8,128)(2,1)S(1)}, bf16[224,512]{1,0:T(8,128)(2,1)S(1)}, u32[]{:S(2)}, u32[]{:S(2)}) collective-permute-start(bf16[224,512]{1,0:T(8,128)(2,1)S(1)} %get-tuple-element.32), channel_id=1, source_target_pairs={{0,2},{1,3},{2,0},{3,1},{4,6},{5,7},{6,4},{7,5},{8,10},{9,11},{10,... | collective-permute-start | bytes 688136 | tf_op jit(solution)/shard_map/ppermute | solution.py:282
  12.8 9.3 %collective-permute-start.5 = (bf16[224,512]{1,0:T(8,128)(2,1)S(1)}, bf16[224,512]{1,0:T(8,128)(2,1)S(1)}, u32[]{:S(2)}, u32[]{:S(2)}) collective-permute-start(bf16[224,512]{1,0:T(8,128)(2,1)S(1)} %get-tuple-element.33), channel_id=1, source_target_pairs={{0,3},{1,0},{2,1},{3,2},{4,7},{5,4},{6,5},{7,6},{8,11},{9,8},{10,9... | collective-permute-start | bytes 688136 | tf_op jit(solution)/shard_map/ppermute | solution.py:282
  22.1 11.2 %collective-permute-start.6 = (bf16[4,224,256]{2,1,0:T(8,128)(2,1)S(1)}, bf16[4,224,256]{2,1,0:T(8,128)(2,1)S(1)}, u32[]{:S(2)}, u32[]{:S(2)}) collective-permute-start(bf16[4,224,256]{2,1,0:T(8,128)(2,1)S(1)} %pad_maximum_fusion.2.kv0), channel_id=1, source_target_pairs={{0,4},{4,8},{8,12},{12,0},{1,5},{5,9},{9,13},{13,1},{2,6},{6,10},{... | collective-permute-start | bytes 1376264 | tf_op jit(solution)/shard_map/ppermute | solution.py:282
  23.4 20.8 %collective-permute-start.7 = (bf16[4,224,256]{2,1,0:T(8,128)(2,1)S(1)}, bf16[4,224,256]{2,1,0:T(8,128)(2,1)S(1)}, u32[]{:S(2)}, u32[]{:S(2)}) collective-permute-start(bf16[4,224,256]{2,1,0:T(8,128)(2,1)S(1)} %pad_maximum_fusion.2.kv0), channel_id=1, source_target_pairs={{0,8},{4,12},{8,0},{12,4},{1,9},{5,13},{9,1},{13,5},{2,10},{6,14},... | collective-permute-start | bytes 1376264 | tf_op jit(solution)/shard_map/ppermute | solution.py:282
  26.1 19.2 %collective-permute-start.8 = (bf16[4,224,256]{2,1,0:T(8,128)(2,1)S(1)}, bf16[4,224,256]{2,1,0:T(8,128)(2,1)S(1)}, u32[]{:S(2)}, u32[]{:S(2)}) collective-permute-start(bf16[4,224,256]{2,1,0:T(8,128)(2,1)S(1)} %pad_maximum_fusion.2.kv0), channel_id=1, source_target_pairs={{0,12},{4,0},{8,4},{12,8},{1,13},{5,1},{9,5},{13,9},{2,14},{6,2},{... | collective-permute-start | bytes 1376264 | tf_op jit(solution)/shard_map/ppermute | solution.py:282
  27.1 0.7 copy-start.5
  27.1 0.7 copy-start.6
  33.4 11.8 %copy-start.3 = (bf16[1,224,1024]{2,1,0:T(8,128)(2,1)S(1)}, bf16[1,224,1024]{2,1,0:T(8,128)(2,1)}, u32[]{:S(2)}) copy-start(bf16[1,224,1024]{2,1,0:T(8,128)(2,1)} %param.8) | copy-start | bytes 1376260
  33.5 11.8 %copy-start.4 = (bf16[1,224,1024]{2,1,0:T(8,128)(2,1)S(1)}, bf16[1,224,1024]{2,1,0:T(8,128)(2,1)}, u32[]{:S(2)}) copy-start(bf16[1,224,1024]{2,1,0:T(8,128)(2,1)} %param.11) | copy-start | bytes 1376260
  33.5 30.8 %collective-permute-start.15 = (bf16[224,512]{1,0:T(8,128)(2,1)S(1)}, bf16[224,512]{1,0:T(8,128)(2,1)S(1)}, u32[]{:S(2)}, u32[]{:S(2)}) collective-permute-start(bf16[224,512]{1,0:T(8,128)(2,1)S(1)} %get-tuple-element.62), channel_id=1, source_target_pairs={{0,16},{16,32},{32,48},{48,0},{1,17},{17,33},{33,49},{49,1},{2,18}... | collective-permute-start | bytes 688136 | tf_op jit(solution)/shard_map/ppermute | solution.py:282
  53.4 27.0 %collective-permute-start.11 = (bf16[4,224,256]{2,1,0:T(8,128)(2,1)S(1)}, bf16[4,224,256]{2,1,0:T(8,128)(2,1)S(1)}, u32[]{:S(2)}, u32[]{:S(2)}) collective-permute-start(bf16[4,224,256]{2,1,0:T(8,128)(2,1)S(1)} %get-tuple-element.39), channel_id=1, source_target_pairs={{0,12},{4,0},{8,4},{12,8},{1,13},{5,1},{9,5},{13,9},{2,14},{6,2},{... | collective-permute-start | bytes 1376264 | tf_op jit(solution)/shard_map/ppermute | solution.py:282
  60.4 23.0 %collective-permute-start.10 = (bf16[4,224,256]{2,1,0:T(8,128)(2,1)S(1)}, bf16[4,224,256]{2,1,0:T(8,128)(2,1)S(1)}, u32[]{:S(2)}, u32[]{:S(2)}) collective-permute-start(bf16[4,224,256]{2,1,0:T(8,128)(2,1)S(1)} %get-tuple-element.38), channel_id=1, source_target_pairs={{0,8},{4,12},{8,0},{12,4},{1,9},{5,13},{9,1},{13,5},{2,10},{6,14},... | collective-permute-start | bytes 1376264 | tf_op jit(solution)/shard_map/ppermute | solution.py:282
  60.4 23.5 %collective-permute-start.9 = (bf16[4,224,256]{2,1,0:T(8,128)(2,1)S(1)}, bf16[4,224,256]{2,1,0:T(8,128)(2,1)S(1)}, u32[]{:S(2)}, u32[]{:S(2)}) collective-permute-start(bf16[4,224,256]{2,1,0:T(8,128)(2,1)S(1)} %get-tuple-element.37), channel_id=1, source_target_pairs={{0,4},{4,8},{8,12},{12,0},{1,5},{5,9},{9,13},{13,1},{2,6},{6,10},{... | collective-permute-start | bytes 1376264 | tf_op jit(solution)/shard_map/ppermute | solution.py:282
  61.1 9.3 %collective-permute-start.16 = (bf16[224,512]{1,0:T(8,128)(2,1)S(1)}, bf16[224,512]{1,0:T(8,128)(2,1)S(1)}, u32[]{:S(2)}, u32[]{:S(2)}) collective-permute-start(bf16[224,512]{1,0:T(8,128)(2,1)S(1)} %get-tuple-element.61), channel_id=1, source_target_pairs={{0,32},{16,48},{32,0},{48,16},{1,33},{17,49},{33,1},{49,17},{2,34}... | collective-permute-start | bytes 688136 | tf_op jit(solution)/shard_map/ppermute | solution.py:282
  64.3 10.5 %collective-permute-start.17 = (bf16[224,512]{1,0:T(8,128)(2,1)S(1)}, bf16[224,512]{1,0:T(8,128)(2,1)S(1)}, u32[]{:S(2)}, u32[]{:S(2)}) collective-permute-start(bf16[224,512]{1,0:T(8,128)(2,1)S(1)} %get-tuple-element.60), channel_id=1, source_target_pairs={{0,48},{16,0},{32,16},{48,32},{1,49},{17,1},{33,17},{49,33},{2,50}... | collective-permute-start | bytes 688136 | tf_op jit(solution)/shard_map/ppermute | solution.py:282
  75.0 31.8 %collective-permute-start.18 = (bf16[896,512]{1,0:T(8,128)(2,1)S(1)}, bf16[896,512]{1,0:T(8,128)(2,1)S(1)}, u32[]{:S(2)}, u32[]{:S(2)}) collective-permute-start(bf16[896,512]{1,0:T(8,128)(2,1)S(1)} %bitcast.74), channel_id=1, source_target_pairs={{0,1},{1,2},{2,3},{3,0},{4,5},{5,6},{6,7},{7,4},{8,9},{9,10},{10,1... | collective-permute-start | bytes 2752520 | tf_op jit(solution)/shard_map/ppermute | solution.py:282
  78.0 41.1 %collective-permute-start.19 = (bf16[896,512]{1,0:T(8,128)(2,1)S(1)}, bf16[896,512]{1,0:T(8,128)(2,1)S(1)}, u32[]{:S(2)}, u32[]{:S(2)}) collective-permute-start(bf16[896,512]{1,0:T(8,128)(2,1)S(1)} %bitcast.75), channel_id=1, source_target_pairs={{0,2},{1,3},{2,0},{3,1},{4,6},{5,7},{6,4},{7,5},{8,10},{9,11},{10,... | collective-permute-start | bytes 2752520 | tf_op jit(solution)/shard_map/ppermute | solution.py:282
  80.4 38.6 %collective-permute-start.20 = (bf16[896,512]{1,0:T(8,128)(2,1)S(1)}, bf16[896,512]{1,0:T(8,128)(2,1)S(1)}, u32[]{:S(2)}, u32[]{:S(2)}) collective-permute-start(bf16[896,512]{1,0:T(8,128)(2,1)S(1)} %bitcast.76), channel_id=1, source_target_pairs={{0,3},{1,0},{2,1},{3,2},{4,7},{5,4},{6,5},{7,6},{8,11},{9,8},{10,9... | collective-permute-start | bytes 2752520 | tf_op jit(solution)/shard_map/ppermute | solution.py:282
  84.1 4.3 %collective-permute-start.14 = (bf16[224,256]{1,0:T(8,128)(2,1)S(1)}, bf16[224,256]{1,0:T(8,128)(2,1)S(1)}, u32[]{:S(2)}, u32[]{:S(2)}) collective-permute-start(bf16[224,256]{1,0:T(8,128)(2,1)S(1)} %get-tuple-element.55), channel_id=1, source_target_pairs={{0,48},{16,0},{32,16},{48,32},{1,49},{17,1},{33,17},{49,33},{2,50}... | collective-permute-start | bytes 344072 | tf_op jit(solution)/shard_map/ppermute | solution.py:282
  84.2 6.9 %collective-permute-start.13 = (bf16[224,256]{1,0:T(8,128)(2,1)S(1)}, bf16[224,256]{1,0:T(8,128)(2,1)S(1)}, u32[]{:S(2)}, u32[]{:S(2)}) collective-permute-start(bf16[224,256]{1,0:T(8,128)(2,1)S(1)} %get-tuple-element.56), channel_id=1, source_target_pairs={{0,32},{16,48},{32,0},{48,16},{1,33},{17,49},{33,1},{49,17},{2,34}... | collective-permute-start | bytes 344072 | tf_op jit(solution)/shard_map/ppermute | solution.py:282
  88.5 5.4 %collective-permute-start.12 = (bf16[224,256]{1,0:T(8,128)(2,1)S(1)}, bf16[224,256]{1,0:T(8,128)(2,1)S(1)}, u32[]{:S(2)}, u32[]{:S(2)}) collective-permute-start(bf16[224,256]{1,0:T(8,128)(2,1)S(1)} %get-tuple-element.54), channel_id=1, source_target_pairs={{0,16},{16,32},{32,48},{48,0},{1,17},{17,33},{33,49},{49,1},{2,18}... | collective-permute-start | bytes 344072 | tf_op jit(solution)/shard_map/ppermute | solution.py:282
  94.0 4.4 %collective-permute-start.23 = (bf16[224,256]{1,0:T(8,128)(2,1)S(1)}, bf16[224,256]{1,0:T(8,128)(2,1)S(1)}, u32[]{:S(2)}, u32[]{:S(2)}) collective-permute-start(bf16[224,256]{1,0:T(8,128)(2,1)S(1)} %fusion.5), channel_id=1, source_target_pairs={{0,48},{16,0},{32,16},{48,32},{1,49},{17,1},{33,17},{49,33},{2,50}... | collective-permute-start | bytes 344072 | tf_op jit(solution)/shard_map/ppermute | solution.py:282
  96.3 10.4 %collective-permute-start.22 = (bf16[224,256]{1,0:T(8,128)(2,1)S(1)}, bf16[224,256]{1,0:T(8,128)(2,1)S(1)}, u32[]{:S(2)}, u32[]{:S(2)}) collective-permute-start(bf16[224,256]{1,0:T(8,128)(2,1)S(1)} %fusion.5), channel_id=1, source_target_pairs={{0,32},{16,48},{32,0},{48,16},{1,33},{17,49},{33,1},{49,17},{2,34}... | collective-permute-start | bytes 344072 | tf_op jit(solution)/shard_map/ppermute | solution.py:282
  98.4 8.3 %collective-permute-start.21 = (bf16[224,256]{1,0:T(8,128)(2,1)S(1)}, bf16[224,256]{1,0:T(8,128)(2,1)S(1)}, u32[]{:S(2)}, u32[]{:S(2)}) collective-permute-start(bf16[224,256]{1,0:T(8,128)(2,1)S(1)} %fusion.5), channel_id=1, source_target_pairs={{0,16},{16,32},{32,48},{48,0},{1,17},{17,33},{33,49},{49,1},{2,18}... | collective-permute-start | bytes 344072 | tf_op jit(solution)/shard_map/ppermute | solution.py:282
  121.5 3.0 %collective-permute-start.24 = (bf16[4,4,16,1024]{3,2,1,0:T(8,128)(2,1)S(1)}, bf16[4,4,16,1024]{3,2,1,0:T(8,128)(2,1)S(1)}, u32[]{:S(2)}, u32[]{:S(2)}) collective-permute-start(bf16[4,4,16,1024]{3,2,1,0:T(8,128)(2,1)S(1)} %get-tuple-element.53), channel_id=1, source_target_pairs={{0,64},{64,0},{1,65},{65,1},{2,66},{66,2},{3,67},{67,3},{4,68},{68... | collective-permute-start | bytes 1572872 | tf_op jit(solution)/shard_map/ppermute | solution.py:308
  124.6 5.8 %collective-permute-start.27 = (bf16[4,16,1024]{2,1,0:T(8,128)(2,1)S(1)}, bf16[4,16,1024]{2,1,0:T(8,128)(2,1)S(1)}, u32[]{:S(2)}, u32[]{:S(2)}) collective-permute-start(bf16[4,16,1024]{2,1,0:T(8,128)(2,1)S(1)} %get-tuple-element.58), channel_id=1, source_target_pairs={{0,12},{4,0},{8,4},{12,8},{1,13},{5,1},{9,5},{13,9},{2,14},{6,2},{... | collective-permute-start | bytes 393224 | tf_op jit(solution)/shard_map/ppermute | solution.py:282
  127.0 5.9 %collective-permute-start.26 = (bf16[4,16,1024]{2,1,0:T(8,128)(2,1)S(1)}, bf16[4,16,1024]{2,1,0:T(8,128)(2,1)S(1)}, u32[]{:S(2)}, u32[]{:S(2)}) collective-permute-start(bf16[4,16,1024]{2,1,0:T(8,128)(2,1)S(1)} %get-tuple-element.59), channel_id=1, source_target_pairs={{0,8},{4,12},{8,0},{12,4},{1,9},{5,13},{9,1},{13,5},{2,10},{6,14},... | collective-permute-start | bytes 393224 | tf_op jit(solution)/shard_map/ppermute | solution.py:282
  128.7 7.5 %collective-permute-start.25 = (bf16[4,16,1024]{2,1,0:T(8,128)(2,1)S(1)}, bf16[4,16,1024]{2,1,0:T(8,128)(2,1)S(1)}, u32[]{:S(2)}, u32[]{:S(2)}) collective-permute-start(bf16[4,16,1024]{2,1,0:T(8,128)(2,1)S(1)} %get-tuple-element.57), channel_id=1, source_target_pairs={{0,4},{4,8},{8,12},{12,0},{1,5},{5,9},{9,13},{13,1},{2,6},{6,10},{... | collective-permute-start | bytes 393224 | tf_op jit(solution)/shard_map/ppermute | solution.py:282
  136.3 11.9 %collective-permute-start.29 = (bf16[16,1024]{1,0:T(8,128)(2,1)S(1)}, bf16[16,1024]{1,0:T(8,128)(2,1)S(1)}, u32[]{:S(2)}, u32[]{:S(2)}) collective-permute-start(bf16[16,1024]{1,0:T(8,128)(2,1)S(1)} %get-tuple-element.68), channel_id=1, source_target_pairs={{0,128},{1,160},{2,192},{3,224},{4,132},{5,164},{6,196},{7,228},{8... | collective-permute-start | bytes 98312 | tf_op jit(solution)/shard_map/ppermute | solution.py:318
  145.1 6.7 %collective-permute-start.28 = (bf16[16,1024]{1,0:T(8,128)(2,1)S(1)}, bf16[16,1024]{1,0:T(8,128)(2,1)S(1)}, u32[]{:S(2)}, u32[]{:S(2)}) collective-permute-start(bf16[16,1024]{1,0:T(8,128)(2,1)S(1)} %get-tuple-element.69), channel_id=1, source_target_pairs={{0,0},{1,32},{2,64},{3,96},{4,4},{5,36},{6,68},{7,100},{8,8},{9,40... | collective-permute-start | bytes 98312 | tf_op jit(solution)/shard_map/ppermute | solution.py:318
  147.1 9.6 %collective-permute-start.31 = (bf16[16,1024]{1,0:T(8,128)(2,1)S(1)}, bf16[16,1024]{1,0:T(8,128)(2,1)S(1)}, u32[]{:S(2)}, u32[]{:S(2)}) collective-permute-start(bf16[16,1024]{1,0:T(8,128)(2,1)S(1)} %get-tuple-element.67), channel_id=1, source_target_pairs={{0,144},{1,176},{2,208},{3,240},{4,148},{5,180},{6,212},{7,244},{8... | collective-permute-start | bytes 98312 | tf_op jit(solution)/shard_map/ppermute | solution.py:318
  147.2 9.5 %collective-permute-start.30 = (bf16[16,1024]{1,0:T(8,128)(2,1)S(1)}, bf16[16,1024]{1,0:T(8,128)(2,1)S(1)}, u32[]{:S(2)}, u32[]{:S(2)}) collective-permute-start(bf16[16,1024]{1,0:T(8,128)(2,1)S(1)} %get-tuple-element.66), channel_id=1, source_target_pairs={{0,16},{1,48},{2,80},{3,112},{4,20},{5,52},{6,84},{7,116},{8,24},{... | collective-permute-start | bytes 98312 | tf_op jit(solution)/shard_map/ppermute | solution.py:318

commit v6 on v1

v6 whole, which is shorter than its diff:
```python
import functools

import jax
import jax.numpy as jnp
import numpy as np
from jax import lax
from jax.experimental import pallas as pl
from jax.experimental.pallas import tpu as pltpu
from jax.sharding import Mesh, PartitionSpec as P

DH = 128
HEADS = 8
HALF = 112
ROWS = 2 * HALF
LANES = HEADS * HALF
RANKS = 16
BLOCKS = 2 * RANKS
SEQ = ROWS * RANKS
DOCS = 6
MAX_DOC = 1194
SPAN = 256
STEPS = -(-(MAX_DOC - 1 + HALF) // SPAN)
PAD = SPAN
SCALE = DH**-0.5
LOG2E = 1.4426950408889634
MASKED = -1e30
CARDINAL = ("zh", "co", "zl", "y", "x")
SIZES = (2, 2, 4, 4, 4)
BF = jnp.bfloat16
F32 = jnp.float32


def dot(a, b, ca, cb):
    return lax.dot_general(a, b, (((ca,), (cb,)), ((), ())), preferred_element_type=F32)


def fold(x, op):
    return op(x.reshape(x.shape[0] // 8, 8, x.shape[1]), axis=0)


class Place:
    def __init__(self, facts):
        self.facts = facts
        self.zl, self.y = facts[DOCS + RANKS], facts[DOCS + RANKS + 1]

    def pair(self, rank):
        return self.facts[DOCS + rank]

    def rows(self, zl, y, half):
        pair = self.pair(zl * 4 + y)
        block = pair if half == 0 else BLOCKS - 1 - pair
        return pl.ds(pl.multiple_of(PAD + block * HALF, 16), HALF)

    def gather(self, refs, buf):
        buf[0:PAD, :] = jnp.zeros((PAD, DH), BF)
        for s, ref in enumerate(refs):
            for a in range(4):
                zl, y = lax.rem(self.zl + 4 - a, 4), lax.rem(self.y + 4 - s, 4)
                for half in range(2):
                    rows = slice(half * HALF, (half + 1) * HALF)
                    buf[self.rows(zl, y, half), :] = ref[a, rows, :]

    def scatter(self, acc, refs, scale):
        for s, ref in enumerate(refs):
            for a in range(4):
                zl, y = lax.rem(self.zl + a, 4), lax.rem(self.y + s, 4)
                for half in range(2):
                    rows = slice(half * HALF, (half + 1) * HALF)
                    ref[a, rows, :] = (acc[self.rows(zl, y, half), :] * scale).astype(BF)


class Window:
    def __init__(self, place, half):
        pair = place.pair(place.zl * 4 + place.y)
        block = jnp.where(half == 0, pair, BLOCKS - 1 - pair)
        lane = lax.broadcasted_iota(jnp.int32, (1, LANES), 1)
        within = lane
        for h in range(1, HEADS):
            within = jnp.where(lane >= h * HALF, lane - h * HALF, within)
        first = block * HALF
        self.pos = within + first
        self.low = jnp.zeros_like(self.pos)
        low0 = jnp.int32(0)
        end = jnp.int32(0)
        for d in range(DOCS - 1):
            end = end + place.facts[d]
            self.low = jnp.where(self.pos >= end, end, self.low)
            low0 = jnp.where(first >= end, end, low0)
        stop = first + HALF
        self.count = lax.div(stop - low0 + (SPAN - 1), SPAN)
        self.start = stop - self.count * SPAN

    def keys(self, t):
        return pl.ds(pl.multiple_of(PAD + self.start + t * SPAN, 16), SPAN)

    def kept(self, t):
        return pl.ds(pl.multiple_of(t * SPAN, SPAN), SPAN)

    def scores(self, t, kbuf, qs):
        s = dot(kbuf[self.keys(t), :], qs[...], 1, 1) * (SCALE * LOG2E)
        key = lax.broadcasted_iota(jnp.int32, (SPAN, LANES), 0) + (self.start + t * SPAN)
        return jnp.where((key >= self.low) & (key <= self.pos), s, MASKED)


def heads_apart(ref, half, stack):
    row0 = pl.multiple_of(half * HALF, 16)
    for h in range(HEADS):
        stack[h * HALF : (h + 1) * HALF, :] = ref[pl.ds(row0, HALF), h * DH : (h + 1) * DH]


def forward_kernel(
    facts, q_ref, do_ref, k0, k1, k2, k3, stats, out0, out1, out2, out3,
    kbuf, dvacc, s_scr, qs, dos,
):
    place = Place(facts)
    place.gather((k0, k1, k2, k3), kbuf)
    dvacc[...] = jnp.zeros_like(dvacc)

    def one_block(half, carry):
        heads_apart(q_ref, half, qs)
        heads_apart(do_ref, half, dos)
        window = Window(place, half)

        def score(t, top):
            s = window.scores(t, kbuf, qs)
            s_scr[window.kept(t), :] = s
            return jnp.maximum(top, fold(s, jnp.max))

        top = lax.fori_loop(0, window.count, score, jnp.full((8, LANES), MASKED, F32))
        top = jnp.max(top, axis=0, keepdims=True)

        def weigh(t, mass):
            e = jnp.exp2(s_scr[window.kept(t), :] - top)
            s_scr[window.kept(t), :] = e
            return mass + fold(e, jnp.sum)

        mass = lax.fori_loop(0, window.count, weigh, jnp.zeros((8, LANES), F32))
        inverse = 1.0 / jnp.sum(mass, axis=0, keepdims=True)

        def spread(t, carry):
            p = (s_scr[window.kept(t), :] * inverse).astype(BF)
            dvacc[window.keys(t), :] += dot(p, dos[...], 1, 0)
            return carry

        lax.fori_loop(0, window.count, spread, 0)
        stats[2 * half] = top
        stats[2 * half + 1] = inverse
        return carry

    lax.fori_loop(0, 2, one_block, 0)
    place.scatter(dvacc, (out0, out1, out2, out3), 1.0)


def backward_kernel(
    facts, q_ref, do_ref, k0, k1, k2, k3, v0, v1, v2, v3, stats,
    dq_ref, out0, out1, out2, out3,
    kbuf, vbuf, dkacc, p_scr, dp_scr, qs, dos,
):
    place = Place(facts)
    place.gather((k0, k1, k2, k3), kbuf)
    place.gather((v0, v1, v2, v3), vbuf)
    dkacc[...] = jnp.zeros_like(dkacc)

    def one_block(half, carry):
        heads_apart(q_ref, half, qs)
        heads_apart(do_ref, half, dos)
        window = Window(place, half)
        top, inverse = stats[2 * half], stats[2 * half + 1]

        def weigh(t, moment):
            p = jnp.exp2(window.scores(t, kbuf, qs) - top) * inverse
            dp = dot(vbuf[window.keys(t), :], dos[...], 1, 1)
            p_scr[window.kept(t), :] = p
            dp_scr[window.kept(t), :] = dp
            return moment + fold(p * dp, jnp.sum)

        moment = lax.fori_loop(0, window.count, weigh, jnp.zeros((8, LANES), F32))
        delta = jnp.sum(moment, axis=0, keepdims=True)

        def spread(t, dqt):
            g = (p_scr[window.kept(t), :] * (dp_scr[window.kept(t), :] - delta)).astype(BF)
            at = window.keys(t)
            dkacc[at, :] += dot(g, qs[...], 1, 0)
            return dqt + dot(kbuf[at, :], g, 0, 0)

        dqt = lax.fori_loop(0, window.count, spread, jnp.zeros((DH, LANES), F32))
        dq = (dqt * SCALE).T.astype(BF)
        row0 = pl.multiple_of(half * HALF, 16)
        for h in range(HEADS):
            dq_ref[pl.ds(row0, HALF), h * DH : (h + 1) * DH] = dq[h * HALF : (h + 1) * HALF, :]
        return carry

    lax.fori_loop(0, 2, one_block, 0)
    place.scatter(dkacc, (out0, out1, out2, out3), SCALE)


SHARES = (jax.ShapeDtypeStruct((4, ROWS, DH), BF),) * 4


def forward(facts, q, do, ks):
    vmem = pl.BlockSpec(memory_space=pltpu.VMEM)
    return pl.pallas_call(
        forward_kernel,
        out_shape=(jax.ShapeDtypeStruct((4, 1, LANES), F32),) + SHARES,
        in_specs=[pl.BlockSpec(memory_space=pltpu.SMEM)] + [vmem] * 6,
        out_specs=(vmem,) * 5,
        scratch_shapes=[
            pltpu.VMEM((PAD + SEQ, DH), BF),
            pltpu.VMEM((PAD + SEQ, DH), F32),
            pltpu.VMEM((STEPS * SPAN, LANES), F32),
            pltpu.VMEM((LANES, DH), BF),
            pltpu.VMEM((LANES, DH), BF),
        ],
        compiler_params=pltpu.CompilerParams(vmem_limit_bytes=32 * 2**20),
        cost_estimate=pl.CostEstimate(
            flops=3 * 10**9, bytes_accessed=4 * 10**6, transcendentals=2 * 10**6
        ),
    )(facts, q, do, *ks)


def backward(facts, q, do, ks, vs, stats):
    vmem = pl.BlockSpec(memory_space=pltpu.VMEM)
    return pl.pallas_call(
        backward_kernel,
        out_shape=(jax.ShapeDtypeStruct((ROWS, HEADS * DH), BF),) + SHARES,
        in_specs=[pl.BlockSpec(memory_space=pltpu.SMEM)] + [vmem] * 11,
        out_specs=(vmem,) * 5,
        scratch_shapes=[
            pltpu.VMEM((PAD + SEQ, DH), BF),
            pltpu.VMEM((PAD + SEQ, DH), BF),
            pltpu.VMEM((PAD + SEQ, DH), F32),
            pltpu.VMEM((STEPS * SPAN, LANES), F32),
            pltpu.VMEM((STEPS * SPAN, LANES), F32),
            pltpu.VMEM((LANES, DH), BF),
            pltpu.VMEM((LANES, DH), BF),
        ],
        compiler_params=pltpu.CompilerParams(vmem_limit_bytes=32 * 2**20),
        cost_estimate=pl.CostEstimate(
            flops=5 * 10**9, bytes_accessed=5 * 10**6, transcendentals=2 * 10**6
        ),
    )(facts, q, do, *ks, *vs, stats)


def ring(shift):
    return [(i, (i + shift) % 4) for i in range(4)]


def add_up(*xs):
    return functools.reduce(lambda a, b: a + b, [x.astype(F32) for x in xs])


def copy_kernel(*refs):
    for source, target in zip(refs[: len(refs) // 2], refs[len(refs) // 2 :]):
        target[...] = source[...]


def near(*arrays):
    vmem = pl.BlockSpec(memory_space=pltpu.VMEM)
    return pl.pallas_call(
        copy_kernel,
        out_shape=tuple(jax.ShapeDtypeStruct(a.shape, a.dtype) for a in arrays),
        in_specs=[vmem] * len(arrays),
        out_specs=(vmem,) * len(arrays),
        compiler_params=pltpu.CompilerParams(vmem_limit_bytes=16 * 2**20),
    )(*arrays)


def columns_kernel(c0, c1, c2, c3, keys, values):
    for a, ref in enumerate((c0, c1, c2, c3)):
        keys[a] = ref[:, 0:DH]
        values[a] = ref[:, DH : 2 * DH]


def columns_of(pieces):
    vmem = pl.BlockSpec(memory_space=pltpu.VMEM)
    return pl.pallas_call(
        columns_kernel,
        out_shape=SHARES[:2],
        in_specs=[vmem] * 4,
        out_specs=(vmem,) * 2,
        compiler_params=pltpu.CompilerParams(vmem_limit_bytes=16 * 2**20),
    )(*pieces)


def product_kernel(facts, mine, theirs, own, other, row1, row2, row3, out0, out1, out2, out3, acc):
    my_zl, my_y, my_x, core = (facts[DOCS + RANKS + i] for i in range(4))
    for j, row in enumerate(((own, other), row1, row2, row3)):
        group = lax.rem(my_x + 4 - j, 4)

        @pl.when(group // 2 == core)
        def _():
            if j == 0:
                first, second = own[...], other[...]
            else:
                first, second = row[0:ROWS, :], row[ROWS : 2 * ROWS, :]
            for c in range(4):
                columns = slice(c * 512, (c + 1) * 512)
                acc[...] = dot(first, mine[:, columns], 0, 0) + dot(second, theirs[:, columns], 0, 0)
                for s, out in enumerate((out0, out1, out2, out3)):
                    y = lax.rem(my_y + s, 4)
                    for low in range(2):
                        at = pl.ds(pl.multiple_of(low * 64 + y * 16, 16), 16)
                        a = lax.rem(lax.rem(group, 2) * 2 + low + 4 - my_zl, 4)
                        out[a, :, columns] = acc[at, :].astype(BF)


def weight_product(facts, *operands):
    vmem = pl.BlockSpec(memory_space=pltpu.VMEM)
    return pl.pallas_call(
        product_kernel,
        out_shape=(jax.ShapeDtypeStruct((4, 16, 2048), BF),) * 4,
        in_specs=[pl.BlockSpec(memory_space=pltpu.SMEM)] + [vmem] * 7,
        out_specs=(vmem,) * 4,
        scratch_shapes=[pltpu.VMEM((DH, 512), F32)],
        compiler_params=pltpu.CompilerParams(vmem_limit_bytes=24 * 2**20),
        cost_estimate=pl.CostEstimate(flops=10**9, bytes_accessed=4 * 10**6, transcendentals=0),
    )(facts, *operands)


def after(value, *others):
    return lax.optimization_barrier((value, others))[0]


def per_device(hidden_in, queries, keys_in, values_in, out_grad, doc_lengths, pair_perm):
    zl, y, x = (lax.axis_index(a) for a in ("zl", "y", "x"))
    zh, core = lax.axis_index("zh"), lax.axis_index("co")
    swap = [(0, 1), (1, 0)]
    facts = jnp.concatenate([doc_lengths[0], pair_perm, jnp.stack([zl, y, x, core]).astype(jnp.int32)])

    def moved(value, axis, shift):
        return lax.ppermute(value, axis, ring(shift))

    own = jnp.concatenate([keys_in[0], values_in[0]], axis=1)
    pieces = [own] + [moved(own, "zl", a) for a in (1, 2, 3)]
    rows_in = near(queries[0], out_grad[0])
    hidden = hidden_in[0]
    hidden = (hidden, lax.ppermute(hidden, "co", swap))
    pieces, rows_in, hidden = lax.optimization_barrier((pieces, rows_in, hidden))
    ks, vs = columns_of(pieces)
    ks = [ks] + [moved(ks, "y", s) for s in (1, 2, 3)]
    vs = after(vs, ks[1])
    vs = [vs] + [moved(vs, "y", s) for s in (1, 2, 3)]

    def received(shares):
        return [shares[0]] + [moved(shares[s], "y", s) for s in (1, 2, 3)]

    def summed(got):
        parts = [add_up(*[g[a] for g in got]) for a in range(4)]
        return add_up(parts[0], *[moved(parts[a].astype(BF), "zl", a) for a in (1, 2, 3)])

    cross = [
        (x0 + 4 * c, x0 + 4 * (1 - c)) for c in range(2) for x0 in range(4) if x0 // 2 == 1 - c
    ]

    def along(j):
        return [
            (x0 + 4 * c, (x0 + j) % 4 + 4 * c) for c in range(2) for x0 in range(4) if x0 // 2 == c
        ]

    def product(grads):
        other = lax.ppermute(grads, ("co", "x"), cross)
        both = jnp.concatenate([grads, other], axis=0)
        rows = [lax.ppermute(both, ("co", "x"), along(j)) for j in (1, 2, 3)]
        return weight_product(facts, *hidden, grads, other, *rows)

    stats, *dvs = forward(facts, *rows_in, ks)
    dvs = received(dvs)
    dq, *dks = backward(facts, *rows_in, ks, vs, stats)
    dks = received(after(dks, dvs))
    value_grads = summed(dvs).astype(BF)
    key_grads = summed(dks).astype(BF)
    value_weight = summed(received(product(value_grads)))
    key_weight = summed(received(product(key_grads)))
    kept = jnp.where(zh == 0, key_weight, value_weight)
    sent = jnp.where(zh == 0, value_weight, key_weight).astype(BF)
    grad_weight = kept + lax.ppermute(sent, "zh", swap).astype(F32)
    return dq[None], key_grads[None], value_grads[None], grad_weight


def solution(mesh):
    fine = Mesh(mesh.devices.reshape(SIZES), CARDINAL)
    dp, ctx, tp = ("zh", "co"), ("zl", "y"), "x"
    tokens = P(dp, ctx, tp)
    return jax.shard_map(
        per_device,
        mesh=fine,
        in_specs=(tokens,) * 5 + (P(dp, None), P()),
        out_specs=(tokens,) * 3 + (P(dp + ctx, tp),),
        check_vma=False,
    )
```

time: 182 us -> 142 us (0.78)
  blocking collectives: 111 us -> 0 us
  starting transfers between devices: 17.8 us -> 75.6 us
  waiting for transfers between devices: 32.6 us -> 49.4 us
  Pallas kernels: 6.43 us -> 11.9 us
  local copies, waits for them, and re-layouts: 8.01 us -> 2.8 us
  matrix products: 2.31 us -> 0 us
    all_to_all x4 -> x0, blocking collectives: 85.3 us -> none  [the longest x1 28.6 us: per_device(): w = total(lax.all_to_all(w, 'y', 0, 0)).astype(BF)]
    ppermute x6 -> x43, starting transfers between devices: 11.8 us -> 75.6 us  [the longest x33 49 us: moved(): return lax.ppermute(value, axis, ring(shift))]
    all_gather x2 -> x0, blocking collectives: 26.2 us -> none  [the longest x1 15.4 us: per_device(): column = lax.all_gather(own, 'zl', axis=0, tiled=False)]
    ppermute x6 -> x43, waiting for transfers between devices: 24.2 us -> 49.4 us  [the longest x33 31.8 us: moved(): return lax.ppermute(value, axis, ring(shift))]
    all_to_all x1 -> x0, waiting for transfers between devices: 8.4 us -> none  [per_device(): grads = total(lax.all_to_all(part, 'zl', 0, 0)).astype(BF)]
    all_to_all x1 -> x0, starting transfers between devices: 5.93 us -> none  [per_device(): grads = total(lax.all_to_all(part, 'zl', 0, 0)).astype(BF)]
    pallas_call x1 -> x6, Pallas kernels: 6.43 us -> 11.9 us  [the longest x1 5.07 us: backward(): pl.pallas_call(backward_kernel, out_shape=(jax.ShapeDtypeStruct((ROWS, HE...]
    dot_general x1 -> x0, matrix products: 2.31 us -> none  [dot(): lax.dot_general(a, b, (((ca,), (cb,)), ((), ())), preferred_element_type=...]
  transfers between devices with their start and end apart: 7 -> 43, of which waited for: 6 -> 16; matrix products, arithmetic and copies ran while one was open for 2% -> 1% of each run, Pallas kernels for 0% -> 8%
where the time goes in v6:
time: 142 us; the launch traced here: 143 us
  starting transfers between devices  75.6 us (53%)
  waiting for transfers between devices  49.4 us (35%)
  Pallas kernels  11.9 us (8%)
  local copies, waits for them, and re-layouts  2.8 us (2%)
  other arithmetic  2.2 us (2%)
    ppermute x33, starting transfers between devices, moved(): return lax.ppermute(value, axis, ring(shift))  49 us
    ppermute x33, waiting for transfers between devices, moved(): return lax.ppermute(value, axis, ring(shift))  31.8 us
    ppermute x2, starting transfers between devices, product(): other = lax.ppermute(grads, ('co', 'x'), cross)  14.4 us
    ppermute x6, waiting for transfers between devices, product(): rows = [lax.ppermute(both, ('co', 'x'), along(j)) for j in (1, 2, 3)]  12.9 us
    ppermute x6, starting transfers between devices, product(): rows = [lax.ppermute(both, ('co', 'x'), along(j)) for j in (1, 2, 3)]  6.49 us
    pallas_call x1, Pallas kernels, backward(): pl.pallas_call(backward_kernel, out_shape=(jax.ShapeDtypeStruct((ROWS, HE...  5.07 us
    ppermute x1, waiting for transfers between devices, per_device(): grad_weight = kept + lax.ppermute(sent, 'zh', swap).astype(F32)  4.71 us
    pallas_call x1, Pallas kernels, forward(): pl.pallas_call(forward_kernel, out_shape=(jax.ShapeDtypeStruct((4, 1, LAN...  3.37 us
  transfers between devices with their start and end apart: 43, of which 16 were waited for; matrix products, arithmetic and copies ran while one was open for 1% of the time, Pallas kernels for 8%

profile of v6, /device:TPU:1, one launch (start us, length us, event | category | flops | bytes accessed | tf_op | source)
XLA Modules:
  0.0 142.9 jit_solution(15059332486605121667)
XLA Ops:
  0.6 3.3 %collective-permute-start.3 = (bf16[224,2048]{1,0:T(8,128)(2,1)}, bf16[224,2048]{1,0:T(8,128)(2,1)S(1)}, u32[]{:S(2)}, u32[]{:S(2)}) collective-permute-start(bf16[224,2048]{1,0:T(8,128)(2,1)} %bitcast.71), channel_id=1, source_target_pairs={{0,64},{64,0},{1,65},{65,1},{2,66},{66,2},{3,67},{67,3},{4,68},{68... | collective-permute-start | bytes 2752520 | tf_op jit(solution)/shard_map/ppermute | solution.py:337
  4.0 0.9 pad_maximum_fusion.c0
  4.8 2.7 %collective-permute-start.2 = (bf16[224,256]{1,0:T(8,128)(2,1)S(1)}, bf16[224,256]{1,0:T(8,128)(2,1)S(1)}, u32[]{:S(2)}, u32[]{:S(2)}) collective-permute-start(bf16[224,256]{1,0:T(8,128)(2,1)S(1)} %pad_maximum_fusion.c0), channel_id=1, source_target_pairs={{0,48},{16,0},{32,16},{48,32},{1,49},{17,1},{33,17},{49,33},{2,50}... | collective-permute-start | bytes 344072 | tf_op jit(solution)/shard_map/ppermute | solution.py:331
  7.5 0.4 collective-permute-start
  7.9 1.0 copy-done
  8.9 1.0 copy-done.1
  10.0 0.1 collective-permute-done.2.c3
  10.1 8.0 %collective-permute-done.1.c2 = bf16[224,256]{1,0:T(8,128)(2,1)S(1)} collective-permute-done((bf16[224,256]{1,0:T(8,128)(2,1)S(1)}, bf16[224,256]{1,0:T(8,128)(2,1)S(1)}, u32[]{:S(2)}, u32[]{:S(2)}) %collective-permute-start.1) | collective-permute-done | bytes 114720 | tf_op jit(solution)/shard_map/ppermute | solution.py:331
  18.2 1.4 collective-permute-start.4
  19.6 1.5 %collective-permute-start.6 = (bf16[4,224,128]{2,1,0:T(8,128)(2,1)S(1)}, bf16[4,224,128]{2,1,0:T(8,128)(2,1)S(1)}, u32[]{:S(2)}, u32[]{:S(2)}) collective-permute-start(bf16[4,224,128]{2,1,0:T(8,128)(2,1)S(1)} %get-tuple-element.47.k0), channel_id=1, source_target_pairs={{0,12},{4,0},{8,4},{12,8},{1,13},{5,1},{9,5},{13,9},{2,14},{6,2},{... | collective-permute-start | bytes 688136 | tf_op jit(solution)/shard_map/ppermute | solution.py:331
  21.1 1.6 %collective-permute-start.5 = (bf16[4,224,128]{2,1,0:T(8,128)(2,1)S(1)}, bf16[4,224,128]{2,1,0:T(8,128)(2,1)S(1)}, u32[]{:S(2)}, u32[]{:S(2)}) collective-permute-start(bf16[4,224,128]{2,1,0:T(8,128)(2,1)S(1)} %get-tuple-element.47.k0), channel_id=1, source_target_pairs={{0,8},{4,12},{8,0},{12,4},{1,9},{5,13},{9,1},{13,5},{2,10},{6,14},... | collective-permute-start | bytes 688136 | tf_op jit(solution)/shard_map/ppermute | solution.py:331
  22.6 0.7 copy-done.5
  23.4 2.7 %collective-permute-done.4.k1 = bf16[4,224,128]{2,1,0:T(8,128)(2,1)S(1)} collective-permute-done((bf16[4,224,128]{2,1,0:T(8,128)(2,1)S(1)}, bf16[4,224,128]{2,1,0:T(8,128)(2,1)S(1)}, u32[]{:S(2)}, u32[]{:S(2)}) %collective-permute-start.4) | collective-permute-done | bytes 229408 | tf_op jit(solution)/shard_map/ppermute | solution.py:331
  26.1 1.4 collective-permute-start.9
  27.5 0.3 collective-permute-start.8
  27.8 0.8 collective-permute-start.7
  28.6 3.5 %collective-permute-done.5.k2 = bf16[4,224,128]{2,1,0:T(8,128)(2,1)S(1)} collective-permute-done((bf16[4,224,128]{2,1,0:T(8,128)(2,1)S(1)}, bf16[4,224,128]{2,1,0:T(8,128)(2,1)S(1)}, u32[]{:S(2)}, u32[]{:S(2)}) %collective-permute-start.5) | collective-permute-done | bytes 229408 | tf_op jit(solution)/shard_map/ppermute | solution.py:331
  32.1 3.4 %shard_map.104 = (f32[4,1,896]{2,1,0:T(1,128)S(1)}, bf16[4,224,128]{2,1,0:T(8,128)(2,1)S(1)}, bf16[4,224,128]{2,1,0:T(8,128)(2,1)S(1)}, bf16[4,224,128]{2,1,0:T(8,128)(2,1)S(1)}, bf16[4,224,128]{2,1,0:T(8,128)(2,1)S(1)}) custom-call(s32[26]{0:T(128)S(1)} %concatenate.12.facts, bf16[224,1024]{1,0:T(8,128)(2,1)S(1)} %get-tuple-element.41.q_ref, ...), custom_call_target="tpu_custom_call" | custom-call | flops 3000000000 | bytes 4000000 | tf_op jit(solution)/shard_map/pallas_call | solution.py:202
  35.5 5.2 %collective-permute-start.10 = (bf16[4,224,128]{2,1,0:T(8,128)(2,1)S(1)}, bf16[4,224,128]{2,1,0:T(8,128)(2,1)S(1)}, u32[]{:S(2)}, u32[]{:S(2)}) collective-permute-start(bf16[4,224,128]{2,1,0:T(8,128)(2,1)S(1)} %get-tuple-element.57), channel_id=1, source_target_pairs={{0,4},{4,8},{8,12},{12,0},{1,5},{5,9},{9,13},{13,1},{2,6},{6,10},{... | collective-permute-start | bytes 688136 | tf_op jit(solution)/shard_map/ppermute | solution.py:331
  40.7 0.8 collective-permute-start.11
  41.5 1.7 %collective-permute-start.12 = (bf16[4,224,128]{2,1,0:T(8,128)(2,1)S(1)}, bf16[4,224,128]{2,1,0:T(8,128)(2,1)S(1)}, u32[]{:S(2)}, u32[]{:S(2)}) collective-permute-start(bf16[4,224,128]{2,1,0:T(8,128)(2,1)S(1)} %get-tuple-element.59), channel_id=1, source_target_pairs={{0,12},{4,0},{8,4},{12,8},{1,13},{5,1},{9,5},{13,9},{2,14},{6,2},{... | collective-permute-start | bytes 688136 | tf_op jit(solution)/shard_map/ppermute | solution.py:331
  43.2 5.1 %shard_map.105 = (bf16[224,1024]{1,0:T(8,128)(2,1)}, bf16[4,224,128]{2,1,0:T(8,128)(2,1)S(1)}, bf16[4,224,128]{2,1,0:T(8,128)(2,1)S(1)}, bf16[4,224,128]{2,1,0:T(8,128)(2,1)S(1)}, bf16[4,224,128]{2,1,0:T(8,128)(2,1)S(1)}) custom-call(s32[26]{0:T(128)S(1)} %concatenate.12.facts, bf16[224,1024]{1,0:T(8,128)(2,1)S(1)} %get-tuple-element.41.q_ref, ...), custom_call_target="tpu_custom_call" | custom-call | flops 5000000000 | bytes 5000000 | tf_op jit(solution)/shard_map/pallas_call | solution.py:223
  48.3 0.7 collective-permute-done.10
  48.9 1.1 collective-permute-done.11
  50.1 3.6 %collective-permute-start.13 = (bf16[4,224,128]{2,1,0:T(8,128)(2,1)S(1)}, bf16[4,224,128]{2,1,0:T(8,128)(2,1)S(1)}, u32[]{:S(2)}, u32[]{:S(2)}) collective-permute-start(bf16[4,224,128]{2,1,0:T(8,128)(2,1)S(1)} %get-tuple-element.61), channel_id=1, source_target_pairs={{0,4},{4,8},{8,12},{12,0},{1,5},{5,9},{9,13},{13,1},{2,6},{6,10},{... | collective-permute-start | bytes 688136 | tf_op jit(solution)/shard_map/ppermute | solution.py:331
  53.7 1.2 collective-permute-start.14
  54.9 1.3 collective-permute-start.15
  56.3 3.3 %collective-permute-start.21 = (bf16[224,128]{1,0:T(8,128)(2,1)S(1)}, bf16[224,128]{1,0:T(8,128)(2,1)S(1)}, u32[]{:S(2)}, u32[]{:S(2)}) collective-permute-start(bf16[224,128]{1,0:T(8,128)(2,1)S(1)} %get-tuple-element.84), channel_id=1, source_target_pairs={{0,48},{16,0},{32,16},{48,32},{1,49},{17,1},{33,17},{49,33},{2,50}... | collective-permute-start | bytes 172040 | tf_op jit(solution)/shard_map/ppermute | solution.py:331
  59.6 3.0 %collective-permute-start.20 = (bf16[224,128]{1,0:T(8,128)(2,1)S(1)}, bf16[224,128]{1,0:T(8,128)(2,1)S(1)}, u32[]{:S(2)}, u32[]{:S(2)}) collective-permute-start(bf16[224,128]{1,0:T(8,128)(2,1)S(1)} %get-tuple-element.85), channel_id=1, source_target_pairs={{0,32},{16,48},{32,0},{48,16},{1,33},{17,49},{33,1},{49,17},{2,34}... | collective-permute-start | bytes 172040 | tf_op jit(solution)/shard_map/ppermute | solution.py:331
  62.6 1.5 %collective-permute-done.14 = bf16[4,224,128]{2,1,0:T(8,128)(2,1)S(1)} collective-permute-done((bf16[4,224,128]{2,1,0:T(8,128)(2,1)S(1)}, bf16[4,224,128]{2,1,0:T(8,128)(2,1)S(1)}, u32[]{:S(2)}, u32[]{:S(2)}) %collective-permute-start.14) | collective-permute-done | bytes 229408 | tf_op jit(solution)/shard_map/ppermute | solution.py:331
  64.4 3.3 %collective-permute-start.18 = (bf16[224,128]{1,0:T(8,128)(2,1)S(1)}, bf16[224,128]{1,0:T(8,128)(2,1)S(1)}, u32[]{:S(2)}, u32[]{:S(2)}) collective-permute-start(bf16[224,128]{1,0:T(8,128)(2,1)S(1)} %get-tuple-element.87), channel_id=1, source_target_pairs={{0,48},{16,0},{32,16},{48,32},{1,49},{17,1},{33,17},{49,33},{2,50}... | collective-permute-start | bytes 172040 | tf_op jit(solution)/shard_map/ppermute | solution.py:331
  67.7 10.9 %collective-permute-start.32 = (bf16[224,128]{1,0:T(8,128)(2,1)S(1)}, bf16[224,128]{1,0:T(8,128)(2,1)S(1)}, u32[]{:S(2)}, u32[]{:S(2)}) collective-permute-start(bf16[224,128]{1,0:T(8,128)(2,1)S(1)} %fusion.6.own), channel_id=1, source_target_pairs={{2,66},{3,67},{64,0},{65,1},{6,70},{7,71},{68,4},{69,5},{10,74},{1... | collective-permute-start | bytes 172040 | tf_op jit(solution)/shard_map/ppermute | solution.py:361
  78.7 3.5 %collective-permute-start.22 = (bf16[224,128]{1,0:T(8,128)(2,1)S(1)}, bf16[224,128]{1,0:T(8,128)(2,1)S(1)}, u32[]{:S(2)}, u32[]{:S(2)}) collective-permute-start(bf16[224,128]{1,0:T(8,128)(2,1)S(1)} %fusion.9.own), channel_id=1, source_target_pairs={{2,66},{3,67},{64,0},{65,1},{6,70},{7,71},{68,4},{69,5},{10,74},{1... | collective-permute-start | bytes 172040 | tf_op jit(solution)/shard_map/ppermute | solution.py:361
  82.3 0.7 collective-permute-start.35
  83.0 1.3 collective-permute-start.34
  84.3 1.3 collective-permute-start.33
  85.6 0.7 collective-permute-start.25
  86.3 4.4 %collective-permute-done.34.row2 = bf16[448,128]{1,0:T(8,128)(2,1)S(1)} collective-permute-done((bf16[448,128]{1,0:T(8,128)(2,1)S(1)}, bf16[448,128]{1,0:T(8,128)(2,1)S(1)}, u32[]{:S(2)}, u32[]{:S(2)}) %collective-permute-start.34) | collective-permute-done | bytes 114720 | tf_op jit(solution)/shard_map/ppermute | solution.py:363
  90.7 2.5 %collective-permute-done.33.row1 = bf16[448,128]{1,0:T(8,128)(2,1)S(1)} collective-permute-done((bf16[448,128]{1,0:T(8,128)(2,1)S(1)}, bf16[448,128]{1,0:T(8,128)(2,1)S(1)}, u32[]{:S(2)}, u32[]{:S(2)}) %collective-permute-start.33) | collective-permute-done | bytes 114720 | tf_op jit(solution)/shard_map/ppermute | solution.py:363
  93.2 1.7 %shard_map.107 = (bf16[4,16,2048]{2,1,0:T(8,128)(2,1)S(1)}, bf16[4,16,2048]{2,1,0:T(8,128)(2,1)S(1)}, bf16[4,16,2048]{2,1,0:T(8,128)(2,1)S(1)}, bf16[4,16,2048]{2,1,0:T(8,128)(2,1)S(1)}) custom-call(s32[26]{0:T(128)S(1)} %concatenate.12.facts, bf16[224,2048]{1,0:T(8,128)(2,1)S(1)} %bitcast.72, bf16[224,2048]{1,0:T(8,128)(2,1)S(1)} %collective-permute-done.3.theirs, ...), custom_call_target="tpu_custom_call" | custom-call | flops 1000000000 | bytes 4000000 | tf_op jit(solution)/shard_map/pallas_call | solution.py:309
  94.9 0.4 collective-permute-start.36
  95.2 3.0 %collective-permute-start.37 = (bf16[4,16,2048]{2,1,0:T(8,128)(2,1)S(1)}, bf16[4,16,2048]{2,1,0:T(8,128)(2,1)S(1)}, u32[]{:S(2)}, u32[]{:S(2)}) collective-permute-start(bf16[4,16,2048]{2,1,0:T(8,128)(2,1)S(1)} %get-tuple-element.72), channel_id=1, source_target_pairs={{0,8},{4,12},{8,0},{12,4},{1,9},{5,13},{9,1},{13,5},{2,10},{6,14},... | collective-permute-start | bytes 786440 | tf_op jit(solution)/shard_map/ppermute | solution.py:331
  98.2 1.3 collective-permute-start.24
  99.5 1.3 collective-permute-start.23
  100.8 4.7 %collective-permute-done.24.row2 = bf16[448,128]{1,0:T(8,128)(2,1)S(1)} collective-permute-done((bf16[448,128]{1,0:T(8,128)(2,1)S(1)}, bf16[448,128]{1,0:T(8,128)(2,1)S(1)}, u32[]{:S(2)}, u32[]{:S(2)}) %collective-permute-start.24) | collective-permute-done | bytes 114720 | tf_op jit(solution)/shard_map/ppermute | solution.py:363
  105.5 1.2 collective-permute-done.23.row1
  106.8 1.7 %shard_map.106 = (bf16[4,16,2048]{2,1,0:T(8,128)(2,1)S(1)}, bf16[4,16,2048]{2,1,0:T(8,128)(2,1)S(1)}, bf16[4,16,2048]{2,1,0:T(8,128)(2,1)S(1)}, bf16[4,16,2048]{2,1,0:T(8,128)(2,1)S(1)}) custom-call(s32[26]{0:T(128)S(1)} %concatenate.12.facts, bf16[224,2048]{1,0:T(8,128)(2,1)S(1)} %bitcast.73, bf16[224,2048]{1,0:T(8,128)(2,1)S(1)} %collective-permute-done.3.theirs, ...), custom_call_target="tpu_custom_call" | custom-call | flops 1000000000 | bytes 4000000 | tf_op jit(solution)/shard_map/pallas_call | solution.py:309
  108.4 1.5 %collective-permute-start.26 = (bf16[4,16,2048]{2,1,0:T(8,128)(2,1)S(1)}, bf16[4,16,2048]{2,1,0:T(8,128)(2,1)S(1)}, u32[]{:S(2)}, u32[]{:S(2)}) collective-permute-start(bf16[4,16,2048]{2,1,0:T(8,128)(2,1)S(1)} %get-tuple-element.67), channel_id=1, source_target_pairs={{0,4},{4,8},{8,12},{12,0},{1,5},{5,9},{9,13},{13,1},{2,6},{6,10},{... | collective-permute-start | bytes 786440 | tf_op jit(solution)/shard_map/ppermute | solution.py:331
  109.9 0.6 collective-permute-start.27
  110.5 2.0 %collective-permute-start.28 = (bf16[4,16,2048]{2,1,0:T(8,128)(2,1)S(1)}, bf16[4,16,2048]{2,1,0:T(8,128)(2,1)S(1)}, u32[]{:S(2)}, u32[]{:S(2)}) collective-permute-start(bf16[4,16,2048]{2,1,0:T(8,128)(2,1)S(1)} %get-tuple-element.69), channel_id=1, source_target_pairs={{0,12},{4,0},{8,4},{12,8},{1,13},{5,1},{9,5},{13,9},{2,14},{6,2},{... | collective-permute-start | bytes 786440 | tf_op jit(solution)/shard_map/ppermute | solution.py:331
  112.4 0.1 fusion.13
  112.6 0.1 collective-permute-start.39
  112.7 3.2 %collective-permute-start.41 = (bf16[16,2048]{1,0:T(8,128)(2,1)S(1)}, bf16[16,2048]{1,0:T(8,128)(2,1)S(1)}, u32[]{:S(2)}, u32[]{:S(2)}) collective-permute-start(bf16[16,2048]{1,0:T(8,128)(2,1)S(1)} %get-tuple-element.78), channel_id=1, source_target_pairs={{0,48},{16,0},{32,16},{48,32},{1,49},{17,1},{33,17},{49,33},{2,50}... | collective-permute-start | bytes 196616 | tf_op jit(solution)/shard_map/ppermute | solution.py:331
  115.9 7.7 %collective-permute-done.26 = bf16[4,16,2048]{2,1,0:T(8,128)(2,1)S(1)} collective-permute-done((bf16[4,16,2048]{2,1,0:T(8,128)(2,1)S(1)}, bf16[4,16,2048]{2,1,0:T(8,128)(2,1)S(1)}, u32[]{:S(2)}, u32[]{:S(2)}) %collective-permute-start.26) | collective-permute-done | bytes 262176 | tf_op jit(solution)/shard_map/ppermute | solution.py:331
  123.6 1.4 %collective-permute-start.40 = (bf16[16,2048]{1,0:T(8,128)(2,1)S(1)}, bf16[16,2048]{1,0:T(8,128)(2,1)S(1)}, u32[]{:S(2)}, u32[]{:S(2)}) collective-permute-start(bf16[16,2048]{1,0:T(8,128)(2,1)S(1)} %get-tuple-element.79), channel_id=1, source_target_pairs={{0,32},{16,48},{32,0},{48,16},{1,33},{17,49},{33,1},{49,17},{2,34}... | collective-permute-start | bytes 196616 | tf_op jit(solution)/shard_map/ppermute | solution.py:331
  125.0 0.1 fusion.10
  125.2 3.3 %collective-permute-start.31 = (bf16[16,2048]{1,0:T(8,128)(2,1)S(1)}, bf16[16,2048]{1,0:T(8,128)(2,1)S(1)}, u32[]{:S(2)}, u32[]{:S(2)}) collective-permute-start(bf16[16,2048]{1,0:T(8,128)(2,1)S(1)} %get-tuple-element.81), channel_id=1, source_target_pairs={{0,48},{16,0},{32,16},{48,32},{1,49},{17,1},{33,17},{49,33},{2,50}... | collective-permute-start | bytes 196616 | tf_op jit(solution)/shard_map/ppermute | solution.py:331
  128.5 0.8 collective-permute-done.40
  129.3 1.0 collective-permute-done.29
  130.3 4.6 %collective-permute-done.30 = bf16[16,2048]{1,0:T(8,128)(2,1)S(1)} collective-permute-done((bf16[16,2048]{1,0:T(8,128)(2,1)S(1)}, bf16[16,2048]{1,0:T(8,128)(2,1)S(1)}, u32[]{:S(2)}, u32[]{:S(2)}) %collective-permute-start.30) | collective-permute-done | bytes 65568 | tf_op jit(solution)/shard_map/ppermute | solution.py:331
  134.9 0.1 select_convert_fusion
  135.1 2.4 %collective-permute-start.42 = (bf16[16,2048]{1,0:T(8,128)(2,1)S(1)}, bf16[16,2048]{1,0:T(8,128)(2,1)S(1)}, u32[]{:S(2)}, u32[]{:S(2)}) collective-permute-start(bf16[16,2048]{1,0:T(8,128)(2,1)S(1)} %get-tuple-element.74), channel_id=1, source_target_pairs={{0,128},{128,0},{1,129},{129,1},{2,130},{130,2},{3,131},{131,3},{4... | collective-permute-start | bytes 196616 | tf_op jit(solution)/shard_map/ppermute | solution.py:376
  137.5 4.7 %collective-permute-done.42 = bf16[16,2048]{1,0:T(8,128)(2,1)S(1)} collective-permute-done((bf16[16,2048]{1,0:T(8,128)(2,1)S(1)}, bf16[16,2048]{1,0:T(8,128)(2,1)S(1)}, u32[]{:S(2)}, u32[]{:S(2)}) %collective-permute-start.42) | collective-permute-done | bytes 65568 | tf_op jit(solution)/shard_map/ppermute | solution.py:376
  142.2 0.7 convert_add_fusion
  (54 shorter events, 0.9 us)
Async XLA Ops:
  0.6 17.5 %collective-permute-start.3 = (bf16[224,2048]{1,0:T(8,128)(2,1)}, bf16[224,2048]{1,0:T(8,128)(2,1)S(1)}, u32[]{:S(2)}, u32[]{:S(2)}) collective-permute-start(bf16[224,2048]{1,0:T(8,128)(2,1)} %bitcast.71), channel_id=1, source_target_pairs={{0,64},{64,0},{1,65},{65,1},{2,66},{66,2},{3,67},{67,3},{4,68},{68... | collective-permute-start | bytes 2752520 | tf_op jit(solution)/shard_map/ppermute | solution.py:337
  4.8 5.3 %collective-permute-start.2 = (bf16[224,256]{1,0:T(8,128)(2,1)S(1)}, bf16[224,256]{1,0:T(8,128)(2,1)S(1)}, u32[]{:S(2)}, u32[]{:S(2)}) collective-permute-start(bf16[224,256]{1,0:T(8,128)(2,1)S(1)} %pad_maximum_fusion.c0), channel_id=1, source_target_pairs={{0,48},{16,0},{32,16},{48,32},{1,49},{17,1},{33,17},{49,33},{2,50}... | collective-permute-start | bytes 344072 | tf_op jit(solution)/shard_map/ppermute | solution.py:331
  7.5 10.6 %collective-permute-start.1 = (bf16[224,256]{1,0:T(8,128)(2,1)S(1)}, bf16[224,256]{1,0:T(8,128)(2,1)S(1)}, u32[]{:S(2)}, u32[]{:S(2)}) collective-permute-start(bf16[224,256]{1,0:T(8,128)(2,1)S(1)} %pad_maximum_fusion.c0), channel_id=1, source_target_pairs={{0,32},{16,48},{32,0},{48,16},{1,33},{17,49},{33,1},{49,17},{2,34}... | collective-permute-start | bytes 344072 | tf_op jit(solution)/shard_map/ppermute | solution.py:331
  7.5 10.6 %collective-permute-start = (bf16[224,256]{1,0:T(8,128)(2,1)S(1)}, bf16[224,256]{1,0:T(8,128)(2,1)S(1)}, u32[]{:S(2)}, u32[]{:S(2)}) collective-permute-start(bf16[224,256]{1,0:T(8,128)(2,1)S(1)} %pad_maximum_fusion.c0), channel_id=1, source_target_pairs={{0,16},{16,32},{32,48},{48,0},{1,17},{17,33},{33,49},{49,1},{2,18}... | collective-permute-start | bytes 344072 | tf_op jit(solution)/shard_map/ppermute | solution.py:331
  7.9 1.0 copy-start
  8.9 1.0 copy-start.1
  18.2 7.9 %collective-permute-start.4 = (bf16[4,224,128]{2,1,0:T(8,128)(2,1)S(1)}, bf16[4,224,128]{2,1,0:T(8,128)(2,1)S(1)}, u32[]{:S(2)}, u32[]{:S(2)}) collective-permute-start(bf16[4,224,128]{2,1,0:T(8,128)(2,1)S(1)} %get-tuple-element.47.k0), channel_id=1, source_target_pairs={{0,4},{4,8},{8,12},{12,0},{1,5},{5,9},{9,13},{13,1},{2,6},{6,10},{... | collective-permute-start | bytes 688136 | tf_op jit(solution)/shard_map/ppermute | solution.py:331
  19.6 9.0 %collective-permute-start.6 = (bf16[4,224,128]{2,1,0:T(8,128)(2,1)S(1)}, bf16[4,224,128]{2,1,0:T(8,128)(2,1)S(1)}, u32[]{:S(2)}, u32[]{:S(2)}) collective-permute-start(bf16[4,224,128]{2,1,0:T(8,128)(2,1)S(1)} %get-tuple-element.47.k0), channel_id=1, source_target_pairs={{0,12},{4,0},{8,4},{12,8},{1,13},{5,1},{9,5},{13,9},{2,14},{6,2},{... | collective-permute-start | bytes 688136 | tf_op jit(solution)/shard_map/ppermute | solution.py:331
  21.1 11.0 %collective-permute-start.5 = (bf16[4,224,128]{2,1,0:T(8,128)(2,1)S(1)}, bf16[4,224,128]{2,1,0:T(8,128)(2,1)S(1)}, u32[]{:S(2)}, u32[]{:S(2)}) collective-permute-start(bf16[4,224,128]{2,1,0:T(8,128)(2,1)S(1)} %get-tuple-element.47.k0), channel_id=1, source_target_pairs={{0,8},{4,12},{8,0},{12,4},{1,9},{5,13},{9,1},{13,5},{2,10},{6,14},... | collective-permute-start | bytes 688136 | tf_op jit(solution)/shard_map/ppermute | solution.py:331
  22.6 0.7 copy-start.5
  22.6 0.7 copy-start.6
  26.1 15.4 %collective-permute-start.9 = (bf16[4,224,128]{2,1,0:T(8,128)(2,1)S(1)}, bf16[4,224,128]{2,1,0:T(8,128)(2,1)S(1)}, u32[]{:S(2)}, u32[]{:S(2)}) collective-permute-start(bf16[4,224,128]{2,1,0:T(8,128)(2,1)S(1)} %get-tuple-element.49.v0), channel_id=1, source_target_pairs={{0,12},{4,0},{8,4},{12,8},{1,13},{5,1},{9,5},{13,9},{2,14},{6,2},{... | collective-permute-start | bytes 688136 | tf_op jit(solution)/shard_map/ppermute | solution.py:331
  27.5 15.7 %collective-permute-start.8 = (bf16[4,224,128]{2,1,0:T(8,128)(2,1)S(1)}, bf16[4,224,128]{2,1,0:T(8,128)(2,1)S(1)}, u32[]{:S(2)}, u32[]{:S(2)}) collective-permute-start(bf16[4,224,128]{2,1,0:T(8,128)(2,1)S(1)} %get-tuple-element.49.v0), channel_id=1, source_target_pairs={{0,8},{4,12},{8,0},{12,4},{1,9},{5,13},{9,1},{13,5},{2,10},{6,14},... | collective-permute-start | bytes 688136 | tf_op jit(solution)/shard_map/ppermute | solution.py:331
  27.8 15.4 %collective-permute-start.7 = (bf16[4,224,128]{2,1,0:T(8,128)(2,1)S(1)}, bf16[4,224,128]{2,1,0:T(8,128)(2,1)S(1)}, u32[]{:S(2)}, u32[]{:S(2)}) collective-permute-start(bf16[4,224,128]{2,1,0:T(8,128)(2,1)S(1)} %get-tuple-element.49.v0), channel_id=1, source_target_pairs={{0,4},{4,8},{8,12},{12,0},{1,5},{5,9},{9,13},{13,1},{2,6},{6,10},{... | collective-permute-start | bytes 688136 | tf_op jit(solution)/shard_map/ppermute | solution.py:331
  35.5 13.5 %collective-permute-start.10 = (bf16[4,224,128]{2,1,0:T(8,128)(2,1)S(1)}, bf16[4,224,128]{2,1,0:T(8,128)(2,1)S(1)}, u32[]{:S(2)}, u32[]{:S(2)}) collective-permute-start(bf16[4,224,128]{2,1,0:T(8,128)(2,1)S(1)} %get-tuple-element.57), channel_id=1, source_target_pairs={{0,4},{4,8},{8,12},{12,0},{1,5},{5,9},{9,13},{13,1},{2,6},{6,10},{... | collective-permute-start | bytes 688136 | tf_op jit(solution)/shard_map/ppermute | solution.py:331
  40.7 9.4 %collective-permute-start.11 = (bf16[4,224,128]{2,1,0:T(8,128)(2,1)S(1)}, bf16[4,224,128]{2,1,0:T(8,128)(2,1)S(1)}, u32[]{:S(2)}, u32[]{:S(2)}) collective-permute-start(bf16[4,224,128]{2,1,0:T(8,128)(2,1)S(1)} %get-tuple-element.58), channel_id=1, source_target_pairs={{0,8},{4,12},{8,0},{12,4},{1,9},{5,13},{9,1},{13,5},{2,10},{6,14},... | collective-permute-start | bytes 688136 | tf_op jit(solution)/shard_map/ppermute | solution.py:331
  41.5 8.6 %collective-permute-start.12 = (bf16[4,224,128]{2,1,0:T(8,128)(2,1)S(1)}, bf16[4,224,128]{2,1,0:T(8,128)(2,1)S(1)}, u32[]{:S(2)}, u32[]{:S(2)}) collective-permute-start(bf16[4,224,128]{2,1,0:T(8,128)(2,1)S(1)} %get-tuple-element.59), channel_id=1, source_target_pairs={{0,12},{4,0},{8,4},{12,8},{1,13},{5,1},{9,5},{13,9},{2,14},{6,2},{... | collective-permute-start | bytes 688136 | tf_op jit(solution)/shard_map/ppermute | solution.py:331
  50.1 9.5 %collective-permute-start.13 = (bf16[4,224,128]{2,1,0:T(8,128)(2,1)S(1)}, bf16[4,224,128]{2,1,0:T(8,128)(2,1)S(1)}, u32[]{:S(2)}, u32[]{:S(2)}) collective-permute-start(bf16[4,224,128]{2,1,0:T(8,128)(2,1)S(1)} %get-tuple-element.61), channel_id=1, source_target_pairs={{0,4},{4,8},{8,12},{12,0},{1,5},{5,9},{9,13},{13,1},{2,6},{6,10},{... | collective-permute-start | bytes 688136 | tf_op jit(solution)/shard_map/ppermute | solution.py:331
  53.7 10.5 %collective-permute-start.14 = (bf16[4,224,128]{2,1,0:T(8,128)(2,1)S(1)}, bf16[4,224,128]{2,1,0:T(8,128)(2,1)S(1)}, u32[]{:S(2)}, u32[]{:S(2)}) collective-permute-start(bf16[4,224,128]{2,1,0:T(8,128)(2,1)S(1)} %get-tuple-element.62), channel_id=1, source_target_pairs={{0,8},{4,12},{8,0},{12,4},{1,9},{5,13},{9,1},{13,5},{2,10},{6,14},... | collective-permute-start | bytes 688136 | tf_op jit(solution)/shard_map/ppermute | solution.py:331
  54.9 9.3 %collective-permute-start.15 = (bf16[4,224,128]{2,1,0:T(8,128)(2,1)S(1)}, bf16[4,224,128]{2,1,0:T(8,128)(2,1)S(1)}, u32[]{:S(2)}, u32[]{:S(2)}) collective-permute-start(bf16[4,224,128]{2,1,0:T(8,128)(2,1)S(1)} %get-tuple-element.63), channel_id=1, source_target_pairs={{0,12},{4,0},{8,4},{12,8},{1,13},{5,1},{9,5},{13,9},{2,14},{6,2},{... | collective-permute-start | bytes 688136 | tf_op jit(solution)/shard_map/ppermute | solution.py:331
  56.2 11.4 %collective-permute-start.19 = (bf16[224,128]{1,0:T(8,128)(2,1)S(1)}, bf16[224,128]{1,0:T(8,128)(2,1)S(1)}, u32[]{:S(2)}, u32[]{:S(2)}) collective-permute-start(bf16[224,128]{1,0:T(8,128)(2,1)S(1)} %get-tuple-element.83), channel_id=1, source_target_pairs={{0,16},{16,32},{32,48},{48,0},{1,17},{17,33},{33,49},{49,1},{2,18}... | collective-permute-start | bytes 172040 | tf_op jit(solution)/shard_map/ppermute | solution.py:331
  56.3 11.3 %collective-permute-start.21 = (bf16[224,128]{1,0:T(8,128)(2,1)S(1)}, bf16[224,128]{1,0:T(8,128)(2,1)S(1)}, u32[]{:S(2)}, u32[]{:S(2)}) collective-permute-start(bf16[224,128]{1,0:T(8,128)(2,1)S(1)} %get-tuple-element.84), channel_id=1, source_target_pairs={{0,48},{16,0},{32,16},{48,32},{1,49},{17,1},{33,17},{49,33},{2,50}... | collective-permute-start | bytes 172040 | tf_op jit(solution)/shard_map/ppermute | solution.py:331
  59.6 33.6 %copy-start.4 = (bf16[1,224,2048]{2,1,0:T(8,128)(2,1)S(1)}, bf16[1,224,2048]{2,1,0:T(8,128)(2,1)}, u32[]{:S(2)}) copy-start(bf16[1,224,2048]{2,1,0:T(8,128)(2,1)} %param.7) | copy-start | bytes 2752516
  59.6 8.0 %collective-permute-start.20 = (bf16[224,128]{1,0:T(8,128)(2,1)S(1)}, bf16[224,128]{1,0:T(8,128)(2,1)S(1)}, u32[]{:S(2)}, u32[]{:S(2)}) collective-permute-start(bf16[224,128]{1,0:T(8,128)(2,1)S(1)} %get-tuple-element.85), channel_id=1, source_target_pairs={{0,32},{16,48},{32,0},{48,16},{1,33},{17,49},{33,1},{49,17},{2,34}... | collective-permute-start | bytes 172040 | tf_op jit(solution)/shard_map/ppermute | solution.py:331
  64.3 14.3 %collective-permute-start.16 = (bf16[224,128]{1,0:T(8,128)(2,1)S(1)}, bf16[224,128]{1,0:T(8,128)(2,1)S(1)}, u32[]{:S(2)}, u32[]{:S(2)}) collective-permute-start(bf16[224,128]{1,0:T(8,128)(2,1)S(1)} %get-tuple-element.86), channel_id=1, source_target_pairs={{0,16},{16,32},{32,48},{48,0},{1,17},{17,33},{33,49},{49,1},{2,18}... | collective-permute-start | bytes 172040 | tf_op jit(solution)/shard_map/ppermute | solution.py:331
  64.4 14.2 %collective-permute-start.18 = (bf16[224,128]{1,0:T(8,128)(2,1)S(1)}, bf16[224,128]{1,0:T(8,128)(2,1)S(1)}, u32[]{:S(2)}, u32[]{:S(2)}) collective-permute-start(bf16[224,128]{1,0:T(8,128)(2,1)S(1)} %get-tuple-element.87), channel_id=1, source_target_pairs={{0,48},{16,0},{32,16},{48,32},{1,49},{17,1},{33,17},{49,33},{2,50}... | collective-permute-start | bytes 172040 | tf_op jit(solution)/shard_map/ppermute | solution.py:331
  67.6 11.0 %collective-permute-start.17 = (bf16[224,128]{1,0:T(8,128)(2,1)S(1)}, bf16[224,128]{1,0:T(8,128)(2,1)S(1)}, u32[]{:S(2)}, u32[]{:S(2)}) collective-permute-start(bf16[224,128]{1,0:T(8,128)(2,1)S(1)} %get-tuple-element.88), channel_id=1, source_target_pairs={{0,32},{16,48},{32,0},{48,16},{1,33},{17,49},{33,1},{49,17},{2,34}... | collective-permute-start | bytes 172040 | tf_op jit(solution)/shard_map/ppermute | solution.py:331
  67.7 25.5 %copy-start.2 = (bf16[224,128]{1,0:T(8,128)(2,1)}, bf16[224,128]{1,0:T(8,128)(2,1)S(1)}, u32[]{:S(2)}) copy-start(bf16[224,128]{1,0:T(8,128)(2,1)S(1)} %fusion.6.own) | copy-start | bytes 172036
  67.7 14.5 %collective-permute-start.32 = (bf16[224,128]{1,0:T(8,128)(2,1)S(1)}, bf16[224,128]{1,0:T(8,128)(2,1)S(1)}, u32[]{:S(2)}, u32[]{:S(2)}) collective-permute-start(bf16[224,128]{1,0:T(8,128)(2,1)S(1)} %fusion.6.own), channel_id=1, source_target_pairs={{2,66},{3,67},{64,0},{65,1},{6,70},{7,71},{68,4},{69,5},{10,74},{1... | collective-permute-start | bytes 172040 | tf_op jit(solution)/shard_map/ppermute | solution.py:361
  78.7 28.1 %copy-start.3 = (bf16[224,128]{1,0:T(8,128)(2,1)}, bf16[224,128]{1,0:T(8,128)(2,1)S(1)}, u32[]{:S(2)}) copy-start(bf16[224,128]{1,0:T(8,128)(2,1)S(1)} %fusion.9.own) | copy-start | bytes 172036
  78.7 6.9 %collective-permute-start.22 = (bf16[224,128]{1,0:T(8,128)(2,1)S(1)}, bf16[224,128]{1,0:T(8,128)(2,1)S(1)}, u32[]{:S(2)}, u32[]{:S(2)}) collective-permute-start(bf16[224,128]{1,0:T(8,128)(2,1)S(1)} %fusion.9.own), channel_id=1, source_target_pairs={{2,66},{3,67},{64,0},{65,1},{6,70},{7,71},{68,4},{69,5},{10,74},{1... | collective-permute-start | bytes 172040 | tf_op jit(solution)/shard_map/ppermute | solution.py:361
  82.3 4.0 %collective-permute-start.35 = (bf16[448,128]{1,0:T(8,128)(2,1)S(1)}, bf16[448,128]{1,0:T(8,128)(2,1)S(1)}, u32[]{:S(2)}, u32[]{:S(2)}) collective-permute-start(bf16[448,128]{1,0:T(8,128)(2,1)S(1)} %pad_maximum_fusion.2), channel_id=1, source_target_pairs={{0,3},{1,0},{66,65},{67,66},{4,7},{5,4},{70,69},{71,70},{8,11},{9,... | collective-permute-start | bytes 344072 | tf_op jit(solution)/shard_map/ppermute | solution.py:363
  83.0 7.7 %collective-permute-start.34 = (bf16[448,128]{1,0:T(8,128)(2,1)S(1)}, bf16[448,128]{1,0:T(8,128)(2,1)S(1)}, u32[]{:S(2)}, u32[]{:S(2)}) collective-permute-start(bf16[448,128]{1,0:T(8,128)(2,1)S(1)} %pad_maximum_fusion.2), channel_id=1, source_target_pairs={{0,2},{1,3},{66,64},{67,65},{4,6},{5,7},{70,68},{71,69},{8,10},{9,... | collective-permute-start | bytes 344072 | tf_op jit(solution)/shard_map/ppermute | solution.py:363
  84.3 8.9 %collective-permute-start.33 = (bf16[448,128]{1,0:T(8,128)(2,1)S(1)}, bf16[448,128]{1,0:T(8,128)(2,1)S(1)}, u32[]{:S(2)}, u32[]{:S(2)}) collective-permute-start(bf16[448,128]{1,0:T(8,128)(2,1)S(1)} %pad_maximum_fusion.2), channel_id=1, source_target_pairs={{0,1},{1,2},{66,67},{67,64},{4,5},{5,6},{70,71},{71,68},{8,9},{9,1... | collective-permute-start | bytes 344072 | tf_op jit(solution)/shard_map/ppermute | solution.py:363
  85.6 13.9 %collective-permute-start.25 = (bf16[448,128]{1,0:T(8,128)(2,1)S(1)}, bf16[448,128]{1,0:T(8,128)(2,1)S(1)}, u32[]{:S(2)}, u32[]{:S(2)}) collective-permute-start(bf16[448,128]{1,0:T(8,128)(2,1)S(1)} %pad_maximum_fusion.1), channel_id=1, source_target_pairs={{0,3},{1,0},{66,65},{67,66},{4,7},{5,4},{70,69},{71,70},{8,11},{9,... | collective-permute-start | bytes 344072 | tf_op jit(solution)/shard_map/ppermute | solution.py:363
  94.9 15.6 %collective-permute-start.36 = (bf16[4,16,2048]{2,1,0:T(8,128)(2,1)S(1)}, bf16[4,16,2048]{2,1,0:T(8,128)(2,1)S(1)}, u32[]{:S(2)}, u32[]{:S(2)}) collective-permute-start(bf16[4,16,2048]{2,1,0:T(8,128)(2,1)S(1)} %get-tuple-element.71), channel_id=1, source_target_pairs={{0,4},{4,8},{8,12},{12,0},{1,5},{5,9},{9,13},{13,1},{2,6},{6,10},{... | collective-permute-start | bytes 786440 | tf_op jit(solution)/shard_map/ppermute | solution.py:331
  95.2 17.2 %collective-permute-start.37 = (bf16[4,16,2048]{2,1,0:T(8,128)(2,1)S(1)}, bf16[4,16,2048]{2,1,0:T(8,128)(2,1)S(1)}, u32[]{:S(2)}, u32[]{:S(2)}) collective-permute-start(bf16[4,16,2048]{2,1,0:T(8,128)(2,1)S(1)} %get-tuple-element.72), channel_id=1, source_target_pairs={{0,8},{4,12},{8,0},{12,4},{1,9},{5,13},{9,1},{13,5},{2,10},{6,14},... | collective-permute-start | bytes 786440 | tf_op jit(solution)/shard_map/ppermute | solution.py:331
  98.2 14.3 %collective-permute-start.38 = (bf16[4,16,2048]{2,1,0:T(8,128)(2,1)S(1)}, bf16[4,16,2048]{2,1,0:T(8,128)(2,1)S(1)}, u32[]{:S(2)}, u32[]{:S(2)}) collective-permute-start(bf16[4,16,2048]{2,1,0:T(8,128)(2,1)S(1)} %get-tuple-element.73), channel_id=1, source_target_pairs={{0,12},{4,0},{8,4},{12,8},{1,13},{5,1},{9,5},{13,9},{2,14},{6,2},{... | collective-permute-start | bytes 786440 | tf_op jit(solution)/shard_map/ppermute | solution.py:331
  98.2 7.3 %collective-permute-start.24 = (bf16[448,128]{1,0:T(8,128)(2,1)S(1)}, bf16[448,128]{1,0:T(8,128)(2,1)S(1)}, u32[]{:S(2)}, u32[]{:S(2)}) collective-permute-start(bf16[448,128]{1,0:T(8,128)(2,1)S(1)} %pad_maximum_fusion.1), channel_id=1, source_target_pairs={{0,2},{1,3},{66,64},{67,65},{4,6},{5,7},{70,68},{71,69},{8,10},{9,... | collective-permute-start | bytes 344072 | tf_op jit(solution)/shard_map/ppermute | solution.py:363
  99.5 7.3 %collective-permute-start.23 = (bf16[448,128]{1,0:T(8,128)(2,1)S(1)}, bf16[448,128]{1,0:T(8,128)(2,1)S(1)}, u32[]{:S(2)}, u32[]{:S(2)}) collective-permute-start(bf16[448,128]{1,0:T(8,128)(2,1)S(1)} %pad_maximum_fusion.1), channel_id=1, source_target_pairs={{0,1},{1,2},{66,67},{67,64},{4,5},{5,6},{70,71},{71,68},{8,9},{9,1... | collective-permute-start | bytes 344072 | tf_op jit(solution)/shard_map/ppermute | solution.py:363
  108.4 15.2 %collective-permute-start.26 = (bf16[4,16,2048]{2,1,0:T(8,128)(2,1)S(1)}, bf16[4,16,2048]{2,1,0:T(8,128)(2,1)S(1)}, u32[]{:S(2)}, u32[]{:S(2)}) collective-permute-start(bf16[4,16,2048]{2,1,0:T(8,128)(2,1)S(1)} %get-tuple-element.67), channel_id=1, source_target_pairs={{0,4},{4,8},{8,12},{12,0},{1,5},{5,9},{9,13},{13,1},{2,6},{6,10},{... | collective-permute-start | bytes 786440 | tf_op jit(solution)/shard_map/ppermute | solution.py:331
  109.9 15.1 %collective-permute-start.27 = (bf16[4,16,2048]{2,1,0:T(8,128)(2,1)S(1)}, bf16[4,16,2048]{2,1,0:T(8,128)(2,1)S(1)}, u32[]{:S(2)}, u32[]{:S(2)}) collective-permute-start(bf16[4,16,2048]{2,1,0:T(8,128)(2,1)S(1)} %get-tuple-element.68), channel_id=1, source_target_pairs={{0,8},{4,12},{8,0},{12,4},{1,9},{5,13},{9,1},{13,5},{2,10},{6,14},... | collective-permute-start | bytes 786440 | tf_op jit(solution)/shard_map/ppermute | solution.py:331
  110.5 14.6 %collective-permute-start.28 = (bf16[4,16,2048]{2,1,0:T(8,128)(2,1)S(1)}, bf16[4,16,2048]{2,1,0:T(8,128)(2,1)S(1)}, u32[]{:S(2)}, u32[]{:S(2)}) collective-permute-start(bf16[4,16,2048]{2,1,0:T(8,128)(2,1)S(1)} %get-tuple-element.69), channel_id=1, source_target_pairs={{0,12},{4,0},{8,4},{12,8},{1,13},{5,1},{9,5},{13,9},{2,14},{6,2},{... | collective-permute-start | bytes 786440 | tf_op jit(solution)/shard_map/ppermute | solution.py:331
  112.6 15.9 %collective-permute-start.39 = (bf16[16,2048]{1,0:T(8,128)(2,1)S(1)}, bf16[16,2048]{1,0:T(8,128)(2,1)S(1)}, u32[]{:S(2)}, u32[]{:S(2)}) collective-permute-start(bf16[16,2048]{1,0:T(8,128)(2,1)S(1)} %get-tuple-element.77), channel_id=1, source_target_pairs={{0,16},{16,32},{32,48},{48,0},{1,17},{17,33},{33,49},{49,1},{2,18}... | collective-permute-start | bytes 196616 | tf_op jit(solution)/shard_map/ppermute | solution.py:331
  112.7 15.9 %collective-permute-start.41 = (bf16[16,2048]{1,0:T(8,128)(2,1)S(1)}, bf16[16,2048]{1,0:T(8,128)(2,1)S(1)}, u32[]{:S(2)}, u32[]{:S(2)}) collective-permute-start(bf16[16,2048]{1,0:T(8,128)(2,1)S(1)} %get-tuple-element.78), channel_id=1, source_target_pairs={{0,48},{16,0},{32,16},{48,32},{1,49},{17,1},{33,17},{49,33},{2,50}... | collective-permute-start | bytes 196616 | tf_op jit(solution)/shard_map/ppermute | solution.py:331
  123.6 5.7 %collective-permute-start.40 = (bf16[16,2048]{1,0:T(8,128)(2,1)S(1)}, bf16[16,2048]{1,0:T(8,128)(2,1)S(1)}, u32[]{:S(2)}, u32[]{:S(2)}) collective-permute-start(bf16[16,2048]{1,0:T(8,128)(2,1)S(1)} %get-tuple-element.79), channel_id=1, source_target_pairs={{0,32},{16,48},{32,0},{48,16},{1,33},{17,49},{33,1},{49,17},{2,34}... | collective-permute-start | bytes 196616 | tf_op jit(solution)/shard_map/ppermute | solution.py:331
  125.2 5.2 %collective-permute-start.29 = (bf16[16,2048]{1,0:T(8,128)(2,1)S(1)}, bf16[16,2048]{1,0:T(8,128)(2,1)S(1)}, u32[]{:S(2)}, u32[]{:S(2)}) collective-permute-start(bf16[16,2048]{1,0:T(8,128)(2,1)S(1)} %get-tuple-element.80), channel_id=1, source_target_pairs={{0,16},{16,32},{32,48},{48,0},{1,17},{17,33},{33,49},{49,1},{2,18}... | collective-permute-start | bytes 196616 | tf_op jit(solution)/shard_map/ppermute | solution.py:331
  125.2 5.1 %collective-permute-start.31 = (bf16[16,2048]{1,0:T(8,128)(2,1)S(1)}, bf16[16,2048]{1,0:T(8,128)(2,1)S(1)}, u32[]{:S(2)}, u32[]{:S(2)}) collective-permute-start(bf16[16,2048]{1,0:T(8,128)(2,1)S(1)} %get-tuple-element.81), channel_id=1, source_target_pairs={{0,48},{16,0},{32,16},{48,32},{1,49},{17,1},{33,17},{49,33},{2,50}... | collective-permute-start | bytes 196616 | tf_op jit(solution)/shard_map/ppermute | solution.py:331
  128.5 6.4 %collective-permute-start.30 = (bf16[16,2048]{1,0:T(8,128)(2,1)S(1)}, bf16[16,2048]{1,0:T(8,128)(2,1)S(1)}, u32[]{:S(2)}, u32[]{:S(2)}) collective-permute-start(bf16[16,2048]{1,0:T(8,128)(2,1)S(1)} %get-tuple-element.82), channel_id=1, source_target_pairs={{0,32},{16,48},{32,0},{48,16},{1,33},{17,49},{33,1},{49,17},{2,34}... | collective-permute-start | bytes 196616 | tf_op jit(solution)/shard_map/ppermute | solution.py:331
  135.1 7.1 %collective-permute-start.42 = (bf16[16,2048]{1,0:T(8,128)(2,1)S(1)}, bf16[16,2048]{1,0:T(8,128)(2,1)S(1)}, u32[]{:S(2)}, u32[]{:S(2)}) collective-permute-start(bf16[16,2048]{1,0:T(8,128)(2,1)S(1)} %get-tuple-element.74), channel_id=1, source_target_pairs={{0,128},{128,0},{1,129},{129,1},{2,130},{130,2},{3,131},{131,3},{4... | collective-permute-start | bytes 196616 | tf_op jit(solution)/shard_map/ppermute | solution.py:376

commit v7 on v6

--- a/solution.py
+++ b/solution.py
@@ -282,34 +282,73 @@
     )(*pieces)
 
 
-def product_kernel(facts, mine, theirs, own, other, row1, row2, row3, out0, out1, out2, out3, acc):
-    my_zl, my_y, my_x, core = (facts[DOCS + RANKS + i] for i in range(4))
-    for j, row in enumerate(((own, other), row1, row2, row3)):
+def finish_kernel(facts, *refs):
+    key_parts, value_parts, (key_out, value_out, mine, sent) = refs[:4], refs[4:8], refs[8:]
+
+    def rounded(parts):
+        return functools.reduce(lambda a, b: a + b, [p[...].astype(F32) for p in parts]).astype(BF)
+
+    key, value = rounded(key_parts), rounded(value_parts)
+    key_out[...] = key
+    value_out[...] = value
+    key, value = key.astype(F32), value.astype(F32)
+    left = lax.broadcasted_iota(jnp.int32, key.shape, 1) < DH // 2
+    low = jnp.where(left, key, pltpu.roll(value, DH // 2, 1)).astype(BF)
+    high = jnp.where(left, pltpu.roll(key, DH // 2, 1), value).astype(BF)
+    even = lax.rem(facts[DOCS + RANKS], 2) == 0
+
+    @pl.when(even)
+    def _():
+        mine[...] = low
+        sent[...] = high
+
+    @pl.when(jnp.logical_not(even))
+    def _():
+        mine[...] = high
+        sent[...] = low
+
+
+def finish(facts, key_parts, value_parts):
+    vmem = pl.BlockSpec(memory_space=pltpu.VMEM)
+    return pl.pallas_call(
+        finish_kernel,
+        out_shape=(jax.ShapeDtypeStruct((ROWS, DH), BF),) * 4,
+        in_specs=[pl.BlockSpec(memory_space=pltpu.SMEM)] + [vmem] * 8,
+        out_specs=(vmem,) * 4,
+        compiler_params=pltpu.CompilerParams(vmem_limit_bytes=8 * 2**20),
+    )(facts, *key_parts, *value_parts)
+
+
+def product_kernel(
+    facts, hid0, hid1, hid2, hid3, row0, row1, row2, row3, out0, out1, out2, out3, acc
+):
+    my_zl, my_y, my_x, core, zh = (facts[DOCS + RANKS + i] for i in range(5))
+    for j, row in enumerate((row0, row1, row2, row3)):
         group = lax.rem(my_x + 4 - j, 4)
 
         @pl.when(group // 2 == core)
         def _():
-            if j == 0:
-                first, second = own[...], other[...]
-            else:
-                first, second = row[0:ROWS, :], row[ROWS : 2 * ROWS, :]
             for c in range(4):
                 columns = slice(c * 512, (c + 1) * 512)
-                acc[...] = dot(first, mine[:, columns], 0, 0) + dot(second, theirs[:, columns], 0, 0)
+                total = None
+                for i, hidden in enumerate((hid0, hid1, hid2, hid3)):
+                    part = dot(row[i * ROWS : (i + 1) * ROWS, :], hidden[:, columns], 0, 0)
+                    total = part if total is None else total + part
+                acc[...] = total
+                side = lax.rem(lax.rem(group, 2) + my_zl // 2, 2)
                 for s, out in enumerate((out0, out1, out2, out3)):
                     y = lax.rem(my_y + s, 4)
-                    for low in range(2):
-                        at = pl.ds(pl.multiple_of(low * 64 + y * 16, 16), 16)
-                        a = lax.rem(lax.rem(group, 2) * 2 + low + 4 - my_zl, 4)
-                        out[a, :, columns] = acc[at, :].astype(BF)
+                    for kind in range(2):
+                        at = pl.ds(pl.multiple_of(kind * 64 + y * 16, 16), 16)
+                        out[lax.rem(kind + zh, 2), side, :, columns] = acc[at, :].astype(BF)
 
 
 def weight_product(facts, *operands):
     vmem = pl.BlockSpec(memory_space=pltpu.VMEM)
     return pl.pallas_call(
         product_kernel,
-        out_shape=(jax.ShapeDtypeStruct((4, 16, 2048), BF),) * 4,
-        in_specs=[pl.BlockSpec(memory_space=pltpu.SMEM)] + [vmem] * 7,
+        out_shape=(jax.ShapeDtypeStruct((2, 2, 16, 2048), BF),) * 4,
+        in_specs=[pl.BlockSpec(memory_space=pltpu.SMEM)] + [vmem] * 8,
         out_specs=(vmem,) * 4,
         scratch_shapes=[pltpu.VMEM((DH, 512), F32)],
         compiler_params=pltpu.CompilerParams(vmem_limit_bytes=24 * 2**20),
@@ -325,7 +364,7 @@
     zl, y, x = (lax.axis_index(a) for a in ("zl", "y", "x"))
     zh, core = lax.axis_index("zh"), lax.axis_index("co")
     swap = [(0, 1), (1, 0)]
-    facts = jnp.concatenate([doc_lengths[0], pair_perm, jnp.stack([zl, y, x, core]).astype(jnp.int32)])
+    facts = jnp.concatenate([doc_lengths[0], pair_perm, jnp.stack([zl, y, x, core, zh]).astype(jnp.int32)])
 
     def moved(value, axis, shift):
         return lax.ppermute(value, axis, ring(shift))
@@ -344,36 +383,42 @@
     def received(shares):
         return [shares[0]] + [moved(shares[s], "y", s) for s in (1, 2, 3)]
 
-    def summed(got):
+    def over_zl(got):
         parts = [add_up(*[g[a] for g in got]) for a in range(4)]
-        return add_up(parts[0], *[moved(parts[a].astype(BF), "zl", a) for a in (1, 2, 3)])
-
+        return [parts[0]] + [moved(parts[a].astype(BF), "zl", a) for a in (1, 2, 3)]
+
+    stats, *dvs = forward(facts, *rows_in, ks)
+    dvs = received(dvs)
+    neighbour = [(0, 1), (1, 0), (2, 3), (3, 2)]
+    beside = lax.ppermute(after(hidden[0], stats), "zl", neighbour)
+    dq, *dks = backward(facts, *rows_in, ks, vs, stats)
+    dks = received(after(dks, dvs))
+    key_grads, value_grads, mine, sent = finish(facts, over_zl(dks), over_zl(dvs))
+
+    beside = after(beside, *dks)
+    hidden = (hidden[0], beside, hidden[1], lax.ppermute(beside, "co", swap))
+    rows = jnp.stack([mine, lax.ppermute(sent, "zl", neighbour)])
     cross = [
         (x0 + 4 * c, x0 + 4 * (1 - c)) for c in range(2) for x0 in range(4) if x0 // 2 == 1 - c
     ]
+    rows = jnp.stack([rows, lax.ppermute(rows, ("co", "x"), cross)]).reshape(4 * ROWS, DH)
 
     def along(j):
         return [
             (x0 + 4 * c, (x0 + j) % 4 + 4 * c) for c in range(2) for x0 in range(4) if x0 // 2 == c
         ]
 
-    def product(grads):
-        other = lax.ppermute(grads, ("co", "x"), cross)
-        both = jnp.concatenate([grads, other], axis=0)
-        rows = [lax.ppermute(both, ("co", "x"), along(j)) for j in (1, 2, 3)]
-        return weight_product(facts, *hidden, grads, other, *rows)
-
-    stats, *dvs = forward(facts, *rows_in, ks)
-    dvs = received(dvs)
-    dq, *dks = backward(facts, *rows_in, ks, vs, stats)
-    dks = received(after(dks, dvs))
-    value_grads = summed(dvs).astype(BF)
-    key_grads = summed(dks).astype(BF)
-    value_weight = summed(received(product(value_grads)))
-    key_weight = summed(received(product(key_grads)))
-    kept = jnp.where(zh == 0, key_weight, value_weight)
-    sent = jnp.where(zh == 0, value_weight, key_weight).astype(BF)
-    grad_weight = kept + lax.ppermute(sent, "zh", swap).astype(F32)
+    rows = [rows] + [lax.ppermute(rows, ("co", "x"), along(j)) for j in (1, 2, 3)]
+    shares = received(weight_product(facts, *hidden, *rows))
+    total = add_up(*shares)
+    other_zl = [(0, 2), (2, 0), (1, 3), (3, 1)]
+    both = [(a + 4 * c, b + 4 * (1 - c)) for a, b in other_zl for c in range(2)]
+    grad_weight = add_up(
+        total[0, 0],
+        lax.ppermute(total[0, 1].astype(BF), "zl", other_zl),
+        lax.ppermute(total[1, 0].astype(BF), "zh", swap),
+        lax.ppermute(total[1, 1].astype(BF), ("zh", "zl"), both),
+    )
     return dq[None], key_grads[None], value_grads[None], grad_weight
 
 

time: 142 us -> 133 us (0.937)
  starting transfers between devices: 75.6 us -> 54.9 us
  waiting for transfers between devices: 49.4 us -> 60.1 us
    ppermute x33 -> x24, starting transfers between devices: 49 us -> 32.6 us  [moved(): return lax.ppermute(value, axis, ring(shift))]
    ppermute x33 -> x24, waiting for transfers between devices: 31.8 us -> 40.7 us  [moved(): return lax.ppermute(value, axis, ring(shift))]
    ppermute x9 -> x10, starting transfers between devices: 23.3 us -> 19 us  [the longest x1 4.27 us: per_device(): beside = lax.ppermute(after(hidden[0], stats), 'zl', neighbour)]
    ppermute x9 -> x10, waiting for transfers between devices: 17.6 us -> 19.4 us  [the longest x3 8.85 us: per_device(): lax.ppermute(rows, ('co', 'x'), along(j))]
  transfers between devices with their start and end apart: 43 -> 35, of which waited for: 16 -> 17; matrix products, arithmetic and copies ran while one was open for 1% -> 1% of each run, Pallas kernels for 8% -> 7%
where the time goes in v7:
time: 133 us
  waiting for transfers between devices  60.1 us (45%)
  starting transfers between devices  54.9 us (41%)
  Pallas kernels  12.4 us (9%)
  local copies, waits for them, and re-layouts  2.81 us (2%)
  other arithmetic  1.96 us (1%)
    ppermute x24, waiting for transfers between devices, moved(): return lax.ppermute(value, axis, ring(shift))  40.7 us
    ppermute x24, starting transfers between devices, moved(): return lax.ppermute(value, axis, ring(shift))  32.6 us
    ppermute x3, waiting for transfers between devices, per_device(): lax.ppermute(rows, ('co', 'x'), along(j))  8.85 us
    pallas_call x1, Pallas kernels, backward(): pl.pallas_call(backward_kernel, out_shape=(jax.ShapeDtypeStruct((ROWS, HE...  5.06 us
    ppermute x1, waiting for transfers between devices, per_device(): lax.ppermute(total[1, 1].astype(BF), ('zh', 'zl'), both)  4.55 us
    ppermute x1, starting transfers between devices, per_device(): beside = lax.ppermute(after(hidden[0], stats), 'zl', neighbour)  4.27 us
    ppermute x1, starting transfers between devices, per_device(): lax.ppermute(rows, ('co', 'x'), cross)  3.86 us
    pallas_call x1, Pallas kernels, forward(): pl.pallas_call(forward_kernel, out_shape=(jax.ShapeDtypeStruct((4, 1, LAN...  3.37 us
  transfers between devices with their start and end apart: 35, of which 17 were waited for; matrix products, arithmetic and copies ran while one was open for 1% of the time, Pallas kernels for 7%

profile of v7, /device:TPU:1, one launch (start us, length us, event | category | flops | bytes accessed | tf_op | source)
XLA Modules:
  0.0 133.0 jit_solution(1672160753892863172)
XLA Ops:
  0.6 3.3 %collective-permute-start.3 = (bf16[224,2048]{1,0:T(8,128)(2,1)}, bf16[224,2048]{1,0:T(8,128)(2,1)S(1)}, u32[]{:S(2)}, u32[]{:S(2)}) collective-permute-start(bf16[224,2048]{1,0:T(8,128)(2,1)} %bitcast.50), channel_id=1, source_target_pairs={{0,64},{64,0},{1,65},{65,1},{2,66},{66,2},{3,67},{67,3},{4,68},{68... | collective-permute-start | bytes 2752520 | tf_op jit(solution)/shard_map/ppermute | solution.py:376
  4.0 0.9 pad_maximum_fusion.1.c0
  4.8 2.7 %collective-permute-start.2 = (bf16[224,256]{1,0:T(8,128)(2,1)S(1)}, bf16[224,256]{1,0:T(8,128)(2,1)S(1)}, u32[]{:S(2)}, u32[]{:S(2)}) collective-permute-start(bf16[224,256]{1,0:T(8,128)(2,1)S(1)} %pad_maximum_fusion.1.c0), channel_id=1, source_target_pairs={{0,48},{16,0},{32,16},{48,32},{1,49},{17,1},{33,17},{49,33},{2,50}... | collective-permute-start | bytes 344072 | tf_op jit(solution)/shard_map/ppermute | solution.py:370
  7.5 0.4 collective-permute-start
  7.9 1.0 copy-done.1
  8.9 1.0 copy-done.2
  9.9 0.1 shard_map.102
  10.0 0.1 collective-permute-done.2.c3
  10.1 8.0 %collective-permute-done.1.c2 = bf16[224,256]{1,0:T(8,128)(2,1)S(1)} collective-permute-done((bf16[224,256]{1,0:T(8,128)(2,1)S(1)}, bf16[224,256]{1,0:T(8,128)(2,1)S(1)}, u32[]{:S(2)}, u32[]{:S(2)}) %collective-permute-start.1) | collective-permute-done | bytes 114720 | tf_op jit(solution)/shard_map/ppermute | solution.py:370
  18.1 0.1 shard_map.103
  18.2 1.4 %collective-permute-start.4 = (bf16[4,224,128]{2,1,0:T(8,128)(2,1)S(1)}, bf16[4,224,128]{2,1,0:T(8,128)(2,1)S(1)}, u32[]{:S(2)}, u32[]{:S(2)}) collective-permute-start(bf16[4,224,128]{2,1,0:T(8,128)(2,1)S(1)} %get-tuple-element.49.k0), channel_id=1, source_target_pairs={{0,4},{4,8},{8,12},{12,0},{1,5},{5,9},{9,13},{13,1},{2,6},{6,10},{... | collective-permute-start | bytes 688136 | tf_op jit(solution)/shard_map/ppermute | solution.py:370
  19.6 1.5 %collective-permute-start.6 = (bf16[4,224,128]{2,1,0:T(8,128)(2,1)S(1)}, bf16[4,224,128]{2,1,0:T(8,128)(2,1)S(1)}, u32[]{:S(2)}, u32[]{:S(2)}) collective-permute-start(bf16[4,224,128]{2,1,0:T(8,128)(2,1)S(1)} %get-tuple-element.49.k0), channel_id=1, source_target_pairs={{0,12},{4,0},{8,4},{12,8},{1,13},{5,1},{9,5},{13,9},{2,14},{6,2},{... | collective-permute-start | bytes 688136 | tf_op jit(solution)/shard_map/ppermute | solution.py:370
  21.1 1.6 %collective-permute-start.5 = (bf16[4,224,128]{2,1,0:T(8,128)(2,1)S(1)}, bf16[4,224,128]{2,1,0:T(8,128)(2,1)S(1)}, u32[]{:S(2)}, u32[]{:S(2)}) collective-permute-start(bf16[4,224,128]{2,1,0:T(8,128)(2,1)S(1)} %get-tuple-element.49.k0), channel_id=1, source_target_pairs={{0,8},{4,12},{8,0},{12,4},{1,9},{5,13},{9,1},{13,5},{2,10},{6,14},... | collective-permute-start | bytes 688136 | tf_op jit(solution)/shard_map/ppermute | solution.py:370
  22.6 0.7 copy-done.3
  23.3 0.0 copy-done.4
  23.3 0.1 concatenate.6.facts
  23.4 2.7 %collective-permute-done.4.k1 = bf16[4,224,128]{2,1,0:T(8,128)(2,1)S(1)} collective-permute-done((bf16[4,224,128]{2,1,0:T(8,128)(2,1)S(1)}, bf16[4,224,128]{2,1,0:T(8,128)(2,1)S(1)}, u32[]{:S(2)}, u32[]{:S(2)}) %collective-permute-start.4) | collective-permute-done | bytes 229408 | tf_op jit(solution)/shard_map/ppermute | solution.py:370
  26.1 1.4 %collective-permute-start.9 = (bf16[4,224,128]{2,1,0:T(8,128)(2,1)S(1)}, bf16[4,224,128]{2,1,0:T(8,128)(2,1)S(1)}, u32[]{:S(2)}, u32[]{:S(2)}) collective-permute-start(bf16[4,224,128]{2,1,0:T(8,128)(2,1)S(1)} %get-tuple-element.51.v0), channel_id=1, source_target_pairs={{0,12},{4,0},{8,4},{12,8},{1,13},{5,1},{9,5},{13,9},{2,14},{6,2},{... | collective-permute-start | bytes 688136 | tf_op jit(solution)/shard_map/ppermute | solution.py:370
  27.5 0.3 collective-permute-start.8
  27.8 0.8 collective-permute-start.7
  28.6 3.5 %collective-permute-done.5.k2 = bf16[4,224,128]{2,1,0:T(8,128)(2,1)S(1)} collective-permute-done((bf16[4,224,128]{2,1,0:T(8,128)(2,1)S(1)}, bf16[4,224,128]{2,1,0:T(8,128)(2,1)S(1)}, u32[]{:S(2)}, u32[]{:S(2)}) %collective-permute-start.5) | collective-permute-done | bytes 229408 | tf_op jit(solution)/shard_map/ppermute | solution.py:370
  32.1 3.4 %shard_map.104 = (f32[4,1,896]{2,1,0:T(1,128)S(1)}, bf16[4,224,128]{2,1,0:T(8,128)(2,1)S(1)}, bf16[4,224,128]{2,1,0:T(8,128)(2,1)S(1)}, bf16[4,224,128]{2,1,0:T(8,128)(2,1)S(1)}, bf16[4,224,128]{2,1,0:T(8,128)(2,1)S(1)}) custom-call(s32[27]{0:T(128)S(1)} %concatenate.6.facts, bf16[224,1024]{1,0:T(8,128)(2,1)S(1)} %get-tuple-element.43.q_ref, ...), custom_call_target="tpu_custom_call" | custom-call | flops 3000000000 | bytes 4000000 | tf_op jit(solution)/shard_map/pallas_call | solution.py:202
  35.5 4.3 %collective-permute-start.22 = (bf16[224,2048]{1,0:T(8,128)(2,1)S(1)}, bf16[224,2048]{1,0:T(8,128)(2,1)S(1)}, u32[]{:S(2)}, u32[]{:S(2)}) collective-permute-start(bf16[224,2048]{1,0:T(8,128)(2,1)S(1)} %bitcast.51), channel_id=1, source_target_pairs={{0,16},{16,0},{32,48},{48,32},{1,17},{17,1},{33,49},{49,33},{2,18}... | collective-permute-start | bytes 2752520 | tf_op jit(solution)/shard_map/ppermute | solution.py:393
  39.8 3.4 %collective-permute-start.11 = (bf16[4,224,128]{2,1,0:T(8,128)(2,1)S(1)}, bf16[4,224,128]{2,1,0:T(8,128)(2,1)S(1)}, u32[]{:S(2)}, u32[]{:S(2)}) collective-permute-start(bf16[4,224,128]{2,1,0:T(8,128)(2,1)S(1)} %get-tuple-element.60), channel_id=1, source_target_pairs={{0,8},{4,12},{8,0},{12,4},{1,9},{5,13},{9,1},{13,5},{2,10},{6,14},... | collective-permute-start | bytes 688136 | tf_op jit(solution)/shard_map/ppermute | solution.py:370
  43.1 0.0 collective-permute-start.12
  43.1 5.1 %shard_map.105 = (bf16[224,1024]{1,0:T(8,128)(2,1)}, bf16[4,224,128]{2,1,0:T(8,128)(2,1)S(1)}, bf16[4,224,128]{2,1,0:T(8,128)(2,1)S(1)}, bf16[4,224,128]{2,1,0:T(8,128)(2,1)S(1)}, bf16[4,224,128]{2,1,0:T(8,128)(2,1)S(1)}) custom-call(s32[27]{0:T(128)S(1)} %concatenate.6.facts, bf16[224,1024]{1,0:T(8,128)(2,1)S(1)} %get-tuple-element.43.q_ref, ...), custom_call_target="tpu_custom_call" | custom-call | flops 5000000000 | bytes 5000000 | tf_op jit(solution)/shard_map/pallas_call | solution.py:223
  48.2 1.4 %collective-permute-done.11 = bf16[4,224,128]{2,1,0:T(8,128)(2,1)S(1)} collective-permute-done((bf16[4,224,128]{2,1,0:T(8,128)(2,1)S(1)}, bf16[4,224,128]{2,1,0:T(8,128)(2,1)S(1)}, u32[]{:S(2)}, u32[]{:S(2)}) %collective-permute-start.11) | collective-permute-done | bytes 229408 | tf_op jit(solution)/shard_map/ppermute | solution.py:370
  49.6 0.7 collective-permute-done.12
  50.3 1.2 collective-permute-start.13
  51.5 4.7 %collective-permute-start.14 = (bf16[4,224,128]{2,1,0:T(8,128)(2,1)S(1)}, bf16[4,224,128]{2,1,0:T(8,128)(2,1)S(1)}, u32[]{:S(2)}, u32[]{:S(2)}) collective-permute-start(bf16[4,224,128]{2,1,0:T(8,128)(2,1)S(1)} %get-tuple-element.64), channel_id=1, source_target_pairs={{0,8},{4,12},{8,0},{12,4},{1,9},{5,13},{9,1},{13,5},{2,10},{6,14},... | collective-permute-start | bytes 688136 | tf_op jit(solution)/shard_map/ppermute | solution.py:370
  56.2 0.1 fusion.8
  56.3 0.1 collective-permute-start.21
  56.4 2.0 %collective-permute-done.13 = bf16[4,224,128]{2,1,0:T(8,128)(2,1)S(1)} collective-permute-done((bf16[4,224,128]{2,1,0:T(8,128)(2,1)S(1)}, bf16[4,224,128]{2,1,0:T(8,128)(2,1)S(1)}, u32[]{:S(2)}, u32[]{:S(2)}) %collective-permute-start.13) | collective-permute-done | bytes 229408 | tf_op jit(solution)/shard_map/ppermute | solution.py:370
  58.4 1.7 %collective-permute-start.20 = (bf16[224,128]{1,0:T(8,128)(2,1)S(1)}, bf16[224,128]{1,0:T(8,128)(2,1)S(1)}, u32[]{:S(2)}, u32[]{:S(2)}) collective-permute-start(bf16[224,128]{1,0:T(8,128)(2,1)S(1)} %get-tuple-element.81), channel_id=1, source_target_pairs={{0,32},{16,48},{32,0},{48,16},{1,33},{17,49},{33,1},{49,17},{2,34}... | collective-permute-start | bytes 172040 | tf_op jit(solution)/shard_map/ppermute | solution.py:370
  60.2 4.7 %collective-permute-done.14 = bf16[4,224,128]{2,1,0:T(8,128)(2,1)S(1)} collective-permute-done((bf16[4,224,128]{2,1,0:T(8,128)(2,1)S(1)}, bf16[4,224,128]{2,1,0:T(8,128)(2,1)S(1)}, u32[]{:S(2)}, u32[]{:S(2)}) %collective-permute-start.14) | collective-permute-done | bytes 229408 | tf_op jit(solution)/shard_map/ppermute | solution.py:370
  64.9 3.3 %collective-permute-start.19 = (bf16[224,128]{1,0:T(8,128)(2,1)S(1)}, bf16[224,128]{1,0:T(8,128)(2,1)S(1)}, u32[]{:S(2)}, u32[]{:S(2)}) collective-permute-start(bf16[224,128]{1,0:T(8,128)(2,1)S(1)} %get-tuple-element.82), channel_id=1, source_target_pairs={{0,16},{16,32},{32,48},{48,0},{1,17},{17,33},{33,49},{49,1},{2,18}... | collective-permute-start | bytes 172040 | tf_op jit(solution)/shard_map/ppermute | solution.py:370
  68.2 1.8 %collective-permute-start.23 = (bf16[224,2048]{1,0:T(8,128)(2,1)S(1)}, bf16[224,2048]{1,0:T(8,128)(2,1)S(1)}, u32[]{:S(2)}, u32[]{:S(2)}) collective-permute-start(bf16[224,2048]{1,0:T(8,128)(2,1)S(1)} %collective-permute-done.22.hid1), channel_id=1, source_target_pairs={{0,64},{64,0},{1,65},{65,1},{2,66},{66,2},{3,67},{67,3},{4,68},{68... | collective-permute-start | bytes 2752520 | tf_op jit(solution)/shard_map/ppermute | solution.py:399
  70.1 0.1 fusion.5
  70.2 3.2 %collective-permute-start.18 = (bf16[224,128]{1,0:T(8,128)(2,1)S(1)}, bf16[224,128]{1,0:T(8,128)(2,1)S(1)}, u32[]{:S(2)}, u32[]{:S(2)}) collective-permute-start(bf16[224,128]{1,0:T(8,128)(2,1)S(1)} %get-tuple-element.84), channel_id=1, source_target_pairs={{0,48},{16,0},{32,16},{48,32},{1,49},{17,1},{33,17},{49,33},{2,50}... | collective-permute-start | bytes 172040 | tf_op jit(solution)/shard_map/ppermute | solution.py:370
  73.4 0.6 collective-permute-start.17
  74.0 1.4 %collective-permute-start.16 = (bf16[224,128]{1,0:T(8,128)(2,1)S(1)}, bf16[224,128]{1,0:T(8,128)(2,1)S(1)}, u32[]{:S(2)}, u32[]{:S(2)}) collective-permute-start(bf16[224,128]{1,0:T(8,128)(2,1)S(1)} %get-tuple-element.86), channel_id=1, source_target_pairs={{0,16},{16,32},{32,48},{48,0},{1,17},{17,33},{33,49},{49,1},{2,18}... | collective-permute-start | bytes 172040 | tf_op jit(solution)/shard_map/ppermute | solution.py:370
  75.4 4.9 %collective-permute-done.17.refs_2_ = bf16[224,128]{1,0:T(8,128)(2,1)S(1)} collective-permute-done((bf16[224,128]{1,0:T(8,128)(2,1)S(1)}, bf16[224,128]{1,0:T(8,128)(2,1)S(1)}, u32[]{:S(2)}, u32[]{:S(2)}) %collective-permute-start.17) | collective-permute-done | bytes 57376 | tf_op jit(solution)/shard_map/ppermute | solution.py:370
  80.3 1.3 shard_map.106
  81.7 3.0 %collective-permute-done.24 = bf16[224,128]{1,0:T(8,128)(2,1)S(1)} collective-permute-done((bf16[224,128]{1,0:T(8,128)(2,1)S(1)}, bf16[224,128]{1,0:T(8,128)(2,1)S(1)}, u32[]{:S(2)}, u32[]{:S(2)}) %collective-permute-start.24) | collective-permute-done | bytes 57376 | tf_op jit(solution)/shard_map/ppermute | solution.py:400
  84.7 3.9 %collective-permute-start.25 = (bf16[2,224,128]{2,1,0:T(8,128)(2,1)S(1)}, bf16[2,224,128]{2,1,0:T(8,128)(2,1)S(1)}, u32[]{:S(2)}, u32[]{:S(2)}) collective-permute-start(bf16[2,224,128]{2,1,0:T(8,128)(2,1)S(1)} %get-tuple-element.92), channel_id=1, source_target_pairs={{2,66},{3,67},{64,0},{65,1},{6,70},{7,71},{68,4},{69,5},{10,74},{1... | collective-permute-start | bytes 344072 | tf_op jit(solution)/shard_map/ppermute | solution.py:404
  88.6 0.9 collective-permute-done.25
  89.5 0.7 collective-permute-start.28
  90.2 1.3 collective-permute-start.27
  91.5 1.3 collective-permute-start.26
  92.8 6.3 %collective-permute-done.27.row2 = bf16[896,128]{1,0:T(8,128)(2,1)S(1)} collective-permute-done((bf16[896,128]{1,0:T(8,128)(2,1)S(1)}, bf16[896,128]{1,0:T(8,128)(2,1)S(1)}, u32[]{:S(2)}, u32[]{:S(2)}) %collective-permute-start.27) | collective-permute-done | bytes 229408 | tf_op jit(solution)/shard_map/ppermute | solution.py:411
  99.1 2.5 %collective-permute-done.26.row1 = bf16[896,128]{1,0:T(8,128)(2,1)S(1)} collective-permute-done((bf16[896,128]{1,0:T(8,128)(2,1)S(1)}, bf16[896,128]{1,0:T(8,128)(2,1)S(1)}, u32[]{:S(2)}, u32[]{:S(2)}) %collective-permute-start.26) | collective-permute-done | bytes 229408 | tf_op jit(solution)/shard_map/ppermute | solution.py:411
  101.7 2.5 %shard_map.107 = (bf16[2,2,16,2048]{3,2,1,0:T(8,128)(2,1)S(1)}, bf16[2,2,16,2048]{3,2,1,0:T(8,128)(2,1)S(1)}, bf16[2,2,16,2048]{3,2,1,0:T(8,128)(2,1)S(1)}, bf16[2,2,16,2048]{3,2,1,0:T(8,128)(2,1)S(1)}) custom-call(s32[27]{0:T(128)S(1)} %concatenate.6.facts, bf16[224,2048]{1,0:T(8,128)(2,1)S(1)} %bitcast.52, ...), custom_call_target="tpu_custom_call" | custom-call | flops 1000000000 | bytes 4000000 | tf_op jit(solution)/shard_map/pallas_call | solution.py:348
  104.2 0.1 collective-permute-start.29
  104.3 1.8 %collective-permute-start.30 = (bf16[2,2,16,2048]{3,2,1,0:T(8,128)(2,1)S(1)}, bf16[2,2,16,2048]{3,2,1,0:T(8,128)(2,1)S(1)}, u32[]{:S(2)}, u32[]{:S(2)}) collective-permute-start(bf16[2,2,16,2048]{3,2,1,0:T(8,128)(2,1)S(1)} %get-tuple-element.76), channel_id=1, source_target_pairs={{0,8},{4,12},{8,0},{12,4},{1,9},{5,13},{9,1},{13,5},{2,10},{6,14},... | collective-permute-start | bytes 786440 | tf_op jit(solution)/shard_map/ppermute | solution.py:370
  106.1 1.1 collective-permute-start.31
  107.1 12.2 %collective-permute-done.29 = bf16[2,2,16,2048]{3,2,1,0:T(8,128)(2,1)S(1)} collective-permute-done((bf16[2,2,16,2048]{3,2,1,0:T(8,128)(2,1)S(1)}, bf16[2,2,16,2048]{3,2,1,0:T(8,128)(2,1)S(1)}, u32[]{:S(2)}, u32[]{:S(2)}) %collective-permute-start.29) | collective-permute-done | bytes 262176 | tf_op jit(solution)/shard_map/ppermute | solution.py:370
  119.4 0.4 collective-permute-done.31
  119.8 0.1 fusion.10
  120.0 1.3 collective-permute-start.32
  121.3 3.2 %collective-permute-start.34 = (bf16[16,2048]{1,0:T(8,128)(2,1)S(1)}, bf16[16,2048]{1,0:T(8,128)(2,1)S(1)}, u32[]{:S(2)}, u32[]{:S(2)}) collective-permute-start(bf16[16,2048]{1,0:T(8,128)(2,1)S(1)} %get-tuple-element.89), channel_id=1, source_target_pairs={{0,160},{128,32},{32,128},{160,0},{16,176},{144,48},{48,144},{176,... | collective-permute-start | bytes 196616 | tf_op jit(solution)/shard_map/ppermute | solution.py:420
  124.5 1.3 collective-permute-start.33
  125.7 4.6 %collective-permute-done.34 = bf16[16,2048]{1,0:T(8,128)(2,1)S(1)} collective-permute-done((bf16[16,2048]{1,0:T(8,128)(2,1)S(1)}, bf16[16,2048]{1,0:T(8,128)(2,1)S(1)}, u32[]{:S(2)}, u32[]{:S(2)}) %collective-permute-start.34) | collective-permute-done | bytes 65568 | tf_op jit(solution)/shard_map/ppermute | solution.py:420
  130.3 2.0 %collective-permute-done.33 = bf16[16,2048]{1,0:T(8,128)(2,1)S(1)} collective-permute-done((bf16[16,2048]{1,0:T(8,128)(2,1)S(1)}, bf16[16,2048]{1,0:T(8,128)(2,1)S(1)}, u32[]{:S(2)}, u32[]{:S(2)}) %collective-permute-start.33) | collective-permute-done | bytes 65568 | tf_op jit(solution)/shard_map/ppermute | solution.py:419
  132.3 0.7 fusion.2
  (31 shorter events, 0.1 us)
Async XLA Ops:
  0.6 17.5 %collective-permute-start.3 = (bf16[224,2048]{1,0:T(8,128)(2,1)}, bf16[224,2048]{1,0:T(8,128)(2,1)S(1)}, u32[]{:S(2)}, u32[]{:S(2)}) collective-permute-start(bf16[224,2048]{1,0:T(8,128)(2,1)} %bitcast.50), channel_id=1, source_target_pairs={{0,64},{64,0},{1,65},{65,1},{2,66},{66,2},{3,67},{67,3},{4,68},{68... | collective-permute-start | bytes 2752520 | tf_op jit(solution)/shard_map/ppermute | solution.py:376
  4.8 5.3 %collective-permute-start.2 = (bf16[224,256]{1,0:T(8,128)(2,1)S(1)}, bf16[224,256]{1,0:T(8,128)(2,1)S(1)}, u32[]{:S(2)}, u32[]{:S(2)}) collective-permute-start(bf16[224,256]{1,0:T(8,128)(2,1)S(1)} %pad_maximum_fusion.1.c0), channel_id=1, source_target_pairs={{0,48},{16,0},{32,16},{48,32},{1,49},{17,1},{33,17},{49,33},{2,50}... | collective-permute-start | bytes 344072 | tf_op jit(solution)/shard_map/ppermute | solution.py:370
  7.5 10.6 %collective-permute-start.1 = (bf16[224,256]{1,0:T(8,128)(2,1)S(1)}, bf16[224,256]{1,0:T(8,128)(2,1)S(1)}, u32[]{:S(2)}, u32[]{:S(2)}) collective-permute-start(bf16[224,256]{1,0:T(8,128)(2,1)S(1)} %pad_maximum_fusion.1.c0), channel_id=1, source_target_pairs={{0,32},{16,48},{32,0},{48,16},{1,33},{17,49},{33,1},{49,17},{2,34}... | collective-permute-start | bytes 344072 | tf_op jit(solution)/shard_map/ppermute | solution.py:370
  7.5 10.6 %collective-permute-start = (bf16[224,256]{1,0:T(8,128)(2,1)S(1)}, bf16[224,256]{1,0:T(8,128)(2,1)S(1)}, u32[]{:S(2)}, u32[]{:S(2)}) collective-permute-start(bf16[224,256]{1,0:T(8,128)(2,1)S(1)} %pad_maximum_fusion.1.c0), channel_id=1, source_target_pairs={{0,16},{16,32},{32,48},{48,0},{1,17},{17,33},{33,49},{49,1},{2,18}... | collective-permute-start | bytes 344072 | tf_op jit(solution)/shard_map/ppermute | solution.py:370
  7.9 1.0 copy-start.1
  8.9 1.0 copy-start.2
  18.2 7.9 %collective-permute-start.4 = (bf16[4,224,128]{2,1,0:T(8,128)(2,1)S(1)}, bf16[4,224,128]{2,1,0:T(8,128)(2,1)S(1)}, u32[]{:S(2)}, u32[]{:S(2)}) collective-permute-start(bf16[4,224,128]{2,1,0:T(8,128)(2,1)S(1)} %get-tuple-element.49.k0), channel_id=1, source_target_pairs={{0,4},{4,8},{8,12},{12,0},{1,5},{5,9},{9,13},{13,1},{2,6},{6,10},{... | collective-permute-start | bytes 688136 | tf_op jit(solution)/shard_map/ppermute | solution.py:370
  19.6 9.0 %collective-permute-start.6 = (bf16[4,224,128]{2,1,0:T(8,128)(2,1)S(1)}, bf16[4,224,128]{2,1,0:T(8,128)(2,1)S(1)}, u32[]{:S(2)}, u32[]{:S(2)}) collective-permute-start(bf16[4,224,128]{2,1,0:T(8,128)(2,1)S(1)} %get-tuple-element.49.k0), channel_id=1, source_target_pairs={{0,12},{4,0},{8,4},{12,8},{1,13},{5,1},{9,5},{13,9},{2,14},{6,2},{... | collective-permute-start | bytes 688136 | tf_op jit(solution)/shard_map/ppermute | solution.py:370
  21.1 11.0 %collective-permute-start.5 = (bf16[4,224,128]{2,1,0:T(8,128)(2,1)S(1)}, bf16[4,224,128]{2,1,0:T(8,128)(2,1)S(1)}, u32[]{:S(2)}, u32[]{:S(2)}) collective-permute-start(bf16[4,224,128]{2,1,0:T(8,128)(2,1)S(1)} %get-tuple-element.49.k0), channel_id=1, source_target_pairs={{0,8},{4,12},{8,0},{12,4},{1,9},{5,13},{9,1},{13,5},{2,10},{6,14},... | collective-permute-start | bytes 688136 | tf_op jit(solution)/shard_map/ppermute | solution.py:370
  22.6 0.7 copy-start.3
  22.6 0.7 copy-start.4
  26.1 9.4 %copy-start = (bf16[1,224,2048]{2,1,0:T(8,128)(2,1)S(1)}, bf16[1,224,2048]{2,1,0:T(8,128)(2,1)}, u32[]{:S(2)}) copy-start(bf16[1,224,2048]{2,1,0:T(8,128)(2,1)} %param.7) | copy-start | bytes 2752516
  26.1 13.7 %collective-permute-start.9 = (bf16[4,224,128]{2,1,0:T(8,128)(2,1)S(1)}, bf16[4,224,128]{2,1,0:T(8,128)(2,1)S(1)}, u32[]{:S(2)}, u32[]{:S(2)}) collective-permute-start(bf16[4,224,128]{2,1,0:T(8,128)(2,1)S(1)} %get-tuple-element.51.v0), channel_id=1, source_target_pairs={{0,12},{4,0},{8,4},{12,8},{1,13},{5,1},{9,5},{13,9},{2,14},{6,2},{... | collective-permute-start | bytes 688136 | tf_op jit(solution)/shard_map/ppermute | solution.py:370
  27.5 15.7 %collective-permute-start.8 = (bf16[4,224,128]{2,1,0:T(8,128)(2,1)S(1)}, bf16[4,224,128]{2,1,0:T(8,128)(2,1)S(1)}, u32[]{:S(2)}, u32[]{:S(2)}) collective-permute-start(bf16[4,224,128]{2,1,0:T(8,128)(2,1)S(1)} %get-tuple-element.51.v0), channel_id=1, source_target_pairs={{0,8},{4,12},{8,0},{12,4},{1,9},{5,13},{9,1},{13,5},{2,10},{6,14},... | collective-permute-start | bytes 688136 | tf_op jit(solution)/shard_map/ppermute | solution.py:370
  27.8 15.3 %collective-permute-start.7 = (bf16[4,224,128]{2,1,0:T(8,128)(2,1)S(1)}, bf16[4,224,128]{2,1,0:T(8,128)(2,1)S(1)}, u32[]{:S(2)}, u32[]{:S(2)}) collective-permute-start(bf16[4,224,128]{2,1,0:T(8,128)(2,1)S(1)} %get-tuple-element.51.v0), channel_id=1, source_target_pairs={{0,4},{4,8},{8,12},{12,0},{1,5},{5,9},{9,13},{13,1},{2,6},{6,10},{... | collective-permute-start | bytes 688136 | tf_op jit(solution)/shard_map/ppermute | solution.py:370
  35.5 32.8 %collective-permute-start.22 = (bf16[224,2048]{1,0:T(8,128)(2,1)S(1)}, bf16[224,2048]{1,0:T(8,128)(2,1)S(1)}, u32[]{:S(2)}, u32[]{:S(2)}) collective-permute-start(bf16[224,2048]{1,0:T(8,128)(2,1)S(1)} %bitcast.51), channel_id=1, source_target_pairs={{0,16},{16,0},{32,48},{48,32},{1,17},{17,1},{33,49},{49,33},{2,18}... | collective-permute-start | bytes 2752520 | tf_op jit(solution)/shard_map/ppermute | solution.py:393
  39.7 8.4 %collective-permute-start.10 = (bf16[4,224,128]{2,1,0:T(8,128)(2,1)S(1)}, bf16[4,224,128]{2,1,0:T(8,128)(2,1)S(1)}, u32[]{:S(2)}, u32[]{:S(2)}) collective-permute-start(bf16[4,224,128]{2,1,0:T(8,128)(2,1)S(1)} %get-tuple-element.59), channel_id=1, source_target_pairs={{0,4},{4,8},{8,12},{12,0},{1,5},{5,9},{9,13},{13,1},{2,6},{6,10},{... | collective-permute-start | bytes 688136 | tf_op jit(solution)/shard_map/ppermute | solution.py:370
  39.8 9.8 %collective-permute-start.11 = (bf16[4,224,128]{2,1,0:T(8,128)(2,1)S(1)}, bf16[4,224,128]{2,1,0:T(8,128)(2,1)S(1)}, u32[]{:S(2)}, u32[]{:S(2)}) collective-permute-start(bf16[4,224,128]{2,1,0:T(8,128)(2,1)S(1)} %get-tuple-element.60), channel_id=1, source_target_pairs={{0,8},{4,12},{8,0},{12,4},{1,9},{5,13},{9,1},{13,5},{2,10},{6,14},... | collective-permute-start | bytes 688136 | tf_op jit(solution)/shard_map/ppermute | solution.py:370
  43.1 7.2 %collective-permute-start.12 = (bf16[4,224,128]{2,1,0:T(8,128)(2,1)S(1)}, bf16[4,224,128]{2,1,0:T(8,128)(2,1)S(1)}, u32[]{:S(2)}, u32[]{:S(2)}) collective-permute-start(bf16[4,224,128]{2,1,0:T(8,128)(2,1)S(1)} %get-tuple-element.61), channel_id=1, source_target_pairs={{0,12},{4,0},{8,4},{12,8},{1,13},{5,1},{9,5},{13,9},{2,14},{6,2},{... | collective-permute-start | bytes 688136 | tf_op jit(solution)/shard_map/ppermute | solution.py:370
  50.3 8.2 %collective-permute-start.13 = (bf16[4,224,128]{2,1,0:T(8,128)(2,1)S(1)}, bf16[4,224,128]{2,1,0:T(8,128)(2,1)S(1)}, u32[]{:S(2)}, u32[]{:S(2)}) collective-permute-start(bf16[4,224,128]{2,1,0:T(8,128)(2,1)S(1)} %get-tuple-element.63), channel_id=1, source_target_pairs={{0,4},{4,8},{8,12},{12,0},{1,5},{5,9},{9,13},{13,1},{2,6},{6,10},{... | collective-permute-start | bytes 688136 | tf_op jit(solution)/shard_map/ppermute | solution.py:370
  51.5 13.4 %collective-permute-start.14 = (bf16[4,224,128]{2,1,0:T(8,128)(2,1)S(1)}, bf16[4,224,128]{2,1,0:T(8,128)(2,1)S(1)}, u32[]{:S(2)}, u32[]{:S(2)}) collective-permute-start(bf16[4,224,128]{2,1,0:T(8,128)(2,1)S(1)} %get-tuple-element.64), channel_id=1, source_target_pairs={{0,8},{4,12},{8,0},{12,4},{1,9},{5,13},{9,1},{13,5},{2,10},{6,14},... | collective-permute-start | bytes 688136 | tf_op jit(solution)/shard_map/ppermute | solution.py:370
  56.2 12.0 %collective-permute-start.15 = (bf16[4,224,128]{2,1,0:T(8,128)(2,1)S(1)}, bf16[4,224,128]{2,1,0:T(8,128)(2,1)S(1)}, u32[]{:S(2)}, u32[]{:S(2)}) collective-permute-start(bf16[4,224,128]{2,1,0:T(8,128)(2,1)S(1)} %get-tuple-element.65), channel_id=1, source_target_pairs={{0,12},{4,0},{8,4},{12,8},{1,13},{5,1},{9,5},{13,9},{2,14},{6,2},{... | collective-permute-start | bytes 688136 | tf_op jit(solution)/shard_map/ppermute | solution.py:370
  56.3 17.1 %collective-permute-start.21 = (bf16[224,128]{1,0:T(8,128)(2,1)S(1)}, bf16[224,128]{1,0:T(8,128)(2,1)S(1)}, u32[]{:S(2)}, u32[]{:S(2)}) collective-permute-start(bf16[224,128]{1,0:T(8,128)(2,1)S(1)} %get-tuple-element.80), channel_id=1, source_target_pairs={{0,48},{16,0},{32,16},{48,32},{1,49},{17,1},{33,17},{49,33},{2,50}... | collective-permute-start | bytes 172040 | tf_op jit(solution)/shard_map/ppermute | solution.py:370
  58.4 15.6 %collective-permute-start.20 = (bf16[224,128]{1,0:T(8,128)(2,1)S(1)}, bf16[224,128]{1,0:T(8,128)(2,1)S(1)}, u32[]{:S(2)}, u32[]{:S(2)}) collective-permute-start(bf16[224,128]{1,0:T(8,128)(2,1)S(1)} %get-tuple-element.81), channel_id=1, source_target_pairs={{0,32},{16,48},{32,0},{48,16},{1,33},{17,49},{33,1},{49,17},{2,34}... | collective-permute-start | bytes 172040 | tf_op jit(solution)/shard_map/ppermute | solution.py:370
  64.9 10.5 %collective-permute-start.19 = (bf16[224,128]{1,0:T(8,128)(2,1)S(1)}, bf16[224,128]{1,0:T(8,128)(2,1)S(1)}, u32[]{:S(2)}, u32[]{:S(2)}) collective-permute-start(bf16[224,128]{1,0:T(8,128)(2,1)S(1)} %get-tuple-element.82), channel_id=1, source_target_pairs={{0,16},{16,32},{32,48},{48,0},{1,17},{17,33},{33,49},{49,1},{2,18}... | collective-permute-start | bytes 172040 | tf_op jit(solution)/shard_map/ppermute | solution.py:370
  68.2 33.5 %collective-permute-start.23 = (bf16[224,2048]{1,0:T(8,128)(2,1)S(1)}, bf16[224,2048]{1,0:T(8,128)(2,1)S(1)}, u32[]{:S(2)}, u32[]{:S(2)}) collective-permute-start(bf16[224,2048]{1,0:T(8,128)(2,1)S(1)} %collective-permute-done.22.hid1), channel_id=1, source_target_pairs={{0,64},{64,0},{1,65},{65,1},{2,66},{66,2},{3,67},{67,3},{4,68},{68... | collective-permute-start | bytes 2752520 | tf_op jit(solution)/shard_map/ppermute | solution.py:399
  70.2 5.2 %collective-permute-start.18 = (bf16[224,128]{1,0:T(8,128)(2,1)S(1)}, bf16[224,128]{1,0:T(8,128)(2,1)S(1)}, u32[]{:S(2)}, u32[]{:S(2)}) collective-permute-start(bf16[224,128]{1,0:T(8,128)(2,1)S(1)} %get-tuple-element.84), channel_id=1, source_target_pairs={{0,48},{16,0},{32,16},{48,32},{1,49},{17,1},{33,17},{49,33},{2,50}... | collective-permute-start | bytes 172040 | tf_op jit(solution)/shard_map/ppermute | solution.py:370
  73.4 6.9 %collective-permute-start.17 = (bf16[224,128]{1,0:T(8,128)(2,1)S(1)}, bf16[224,128]{1,0:T(8,128)(2,1)S(1)}, u32[]{:S(2)}, u32[]{:S(2)}) collective-permute-start(bf16[224,128]{1,0:T(8,128)(2,1)S(1)} %get-tuple-element.85), channel_id=1, source_target_pairs={{0,32},{16,48},{32,0},{48,16},{1,33},{17,49},{33,1},{49,17},{2,34}... | collective-permute-start | bytes 172040 | tf_op jit(solution)/shard_map/ppermute | solution.py:370
  74.0 6.3 %collective-permute-start.16 = (bf16[224,128]{1,0:T(8,128)(2,1)S(1)}, bf16[224,128]{1,0:T(8,128)(2,1)S(1)}, u32[]{:S(2)}, u32[]{:S(2)}) collective-permute-start(bf16[224,128]{1,0:T(8,128)(2,1)S(1)} %get-tuple-element.86), channel_id=1, source_target_pairs={{0,16},{16,32},{32,48},{48,0},{1,17},{17,33},{33,49},{49,1},{2,18}... | collective-permute-start | bytes 172040 | tf_op jit(solution)/shard_map/ppermute | solution.py:370
  81.7 3.0 %collective-permute-start.24 = (bf16[224,128]{1,0:T(8,128)(2,1)S(1)}, bf16[224,128]{1,0:T(8,128)(2,1)S(1)}, u32[]{:S(2)}, u32[]{:S(2)}) collective-permute-start(bf16[224,128]{1,0:T(8,128)(2,1)S(1)} %get-tuple-element.73), channel_id=1, source_target_pairs={{0,16},{16,0},{32,48},{48,32},{1,17},{17,1},{33,49},{49,33},{2,18}... | collective-permute-start | bytes 172040 | tf_op jit(solution)/shard_map/ppermute | solution.py:400
  84.7 4.8 %collective-permute-start.25 = (bf16[2,224,128]{2,1,0:T(8,128)(2,1)S(1)}, bf16[2,224,128]{2,1,0:T(8,128)(2,1)S(1)}, u32[]{:S(2)}, u32[]{:S(2)}) collective-permute-start(bf16[2,224,128]{2,1,0:T(8,128)(2,1)S(1)} %get-tuple-element.92), channel_id=1, source_target_pairs={{2,66},{3,67},{64,0},{65,1},{6,70},{7,71},{68,4},{69,5},{10,74},{1... | collective-permute-start | bytes 344072 | tf_op jit(solution)/shard_map/ppermute | solution.py:404
  89.5 3.3 %collective-permute-start.28 = (bf16[896,128]{1,0:T(8,128)(2,1)S(1)}, bf16[896,128]{1,0:T(8,128)(2,1)S(1)}, u32[]{:S(2)}, u32[]{:S(2)}) collective-permute-start(bf16[896,128]{1,0:T(8,128)(2,1)S(1)} %bitcast.53), channel_id=1, source_target_pairs={{0,3},{1,0},{66,65},{67,66},{4,7},{5,4},{70,69},{71,70},{8,11},{9,... | collective-permute-start | bytes 688136 | tf_op jit(solution)/shard_map/ppermute | solution.py:411
  90.2 8.9 %collective-permute-start.27 = (bf16[896,128]{1,0:T(8,128)(2,1)S(1)}, bf16[896,128]{1,0:T(8,128)(2,1)S(1)}, u32[]{:S(2)}, u32[]{:S(2)}) collective-permute-start(bf16[896,128]{1,0:T(8,128)(2,1)S(1)} %bitcast.54), channel_id=1, source_target_pairs={{0,2},{1,3},{66,64},{67,65},{4,6},{5,7},{70,68},{71,69},{8,10},{9,... | collective-permute-start | bytes 688136 | tf_op jit(solution)/shard_map/ppermute | solution.py:411
  91.5 10.2 %collective-permute-start.26 = (bf16[896,128]{1,0:T(8,128)(2,1)S(1)}, bf16[896,128]{1,0:T(8,128)(2,1)S(1)}, u32[]{:S(2)}, u32[]{:S(2)}) collective-permute-start(bf16[896,128]{1,0:T(8,128)(2,1)S(1)} %bitcast.55), channel_id=1, source_target_pairs={{0,1},{1,2},{66,67},{67,64},{4,5},{5,6},{70,71},{71,68},{8,9},{9,1... | collective-permute-start | bytes 688136 | tf_op jit(solution)/shard_map/ppermute | solution.py:411
  104.2 15.2 %collective-permute-start.29 = (bf16[2,2,16,2048]{3,2,1,0:T(8,128)(2,1)S(1)}, bf16[2,2,16,2048]{3,2,1,0:T(8,128)(2,1)S(1)}, u32[]{:S(2)}, u32[]{:S(2)}) collective-permute-start(bf16[2,2,16,2048]{3,2,1,0:T(8,128)(2,1)S(1)} %get-tuple-element.75), channel_id=1, source_target_pairs={{0,4},{4,8},{8,12},{12,0},{1,5},{5,9},{9,13},{13,1},{2,6},{6,10},{... | collective-permute-start | bytes 786440 | tf_op jit(solution)/shard_map/ppermute | solution.py:370
  104.3 15.1 %collective-permute-start.30 = (bf16[2,2,16,2048]{3,2,1,0:T(8,128)(2,1)S(1)}, bf16[2,2,16,2048]{3,2,1,0:T(8,128)(2,1)S(1)}, u32[]{:S(2)}, u32[]{:S(2)}) collective-permute-start(bf16[2,2,16,2048]{3,2,1,0:T(8,128)(2,1)S(1)} %get-tuple-element.76), channel_id=1, source_target_pairs={{0,8},{4,12},{8,0},{12,4},{1,9},{5,13},{9,1},{13,5},{2,10},{6,14},... | collective-permute-start | bytes 786440 | tf_op jit(solution)/shard_map/ppermute | solution.py:370
  106.1 13.7 %collective-permute-start.31 = (bf16[2,2,16,2048]{3,2,1,0:T(8,128)(2,1)S(1)}, bf16[2,2,16,2048]{3,2,1,0:T(8,128)(2,1)S(1)}, u32[]{:S(2)}, u32[]{:S(2)}) collective-permute-start(bf16[2,2,16,2048]{3,2,1,0:T(8,128)(2,1)S(1)} %get-tuple-element.77), channel_id=1, source_target_pairs={{0,12},{4,0},{8,4},{12,8},{1,13},{5,1},{9,5},{13,9},{2,14},{6,2},{... | collective-permute-start | bytes 786440 | tf_op jit(solution)/shard_map/ppermute | solution.py:370
  120.0 5.7 %collective-permute-start.32 = (bf16[16,2048]{1,0:T(8,128)(2,1)S(1)}, bf16[16,2048]{1,0:T(8,128)(2,1)S(1)}, u32[]{:S(2)}, u32[]{:S(2)}) collective-permute-start(bf16[16,2048]{1,0:T(8,128)(2,1)S(1)} %get-tuple-element.88), channel_id=1, source_target_pairs={{0,32},{32,0},{16,48},{48,16},{1,33},{33,1},{17,49},{49,17},{2,34}... | collective-permute-start | bytes 196616 | tf_op jit(solution)/shard_map/ppermute | solution.py:418
  121.3 9.0 %collective-permute-start.34 = (bf16[16,2048]{1,0:T(8,128)(2,1)S(1)}, bf16[16,2048]{1,0:T(8,128)(2,1)S(1)}, u32[]{:S(2)}, u32[]{:S(2)}) collective-permute-start(bf16[16,2048]{1,0:T(8,128)(2,1)S(1)} %get-tuple-element.89), channel_id=1, source_target_pairs={{0,160},{128,32},{32,128},{160,0},{16,176},{144,48},{48,144},{176,... | collective-permute-start | bytes 196616 | tf_op jit(solution)/shard_map/ppermute | solution.py:420
  124.5 7.9 %collective-permute-start.33 = (bf16[16,2048]{1,0:T(8,128)(2,1)S(1)}, bf16[16,2048]{1,0:T(8,128)(2,1)S(1)}, u32[]{:S(2)}, u32[]{:S(2)}) collective-permute-start(bf16[16,2048]{1,0:T(8,128)(2,1)S(1)} %get-tuple-element.90), channel_id=1, source_target_pairs={{0,128},{128,0},{1,129},{129,1},{2,130},{130,2},{3,131},{131,3},{4... | collective-permute-start | bytes 196616 | tf_op jit(solution)/shard_map/ppermute | solution.py:419

commit v8 on v7

--- a/solution.py
+++ b/solution.py
@@ -51,14 +51,15 @@
         block = pair if half == 0 else BLOCKS - 1 - pair
         return pl.ds(pl.multiple_of(PAD + block * HALF, 16), HALF)
 
-    def gather(self, refs, buf):
+    def gather(self, refs, buf, by_zl=False):
         buf[0:PAD, :] = jnp.zeros((PAD, DH), BF)
-        for s, ref in enumerate(refs):
-            for a in range(4):
+        for i, ref in enumerate(refs):
+            for j in range(4):
+                a, s = (i, j) if by_zl else (j, i)
                 zl, y = lax.rem(self.zl + 4 - a, 4), lax.rem(self.y + 4 - s, 4)
                 for half in range(2):
                     rows = slice(half * HALF, (half + 1) * HALF)
-                    buf[self.rows(zl, y, half), :] = ref[a, rows, :]
+                    buf[self.rows(zl, y, half), :] = ref[j, rows, :]
 
     def scatter(self, acc, refs, scale):
         for s, ref in enumerate(refs):
@@ -113,7 +114,7 @@
     kbuf, dvacc, s_scr, qs, dos,
 ):
     place = Place(facts)
-    place.gather((k0, k1, k2, k3), kbuf)
+    place.gather((k0, k1, k2, k3), kbuf, by_zl=True)
     dvacc[...] = jnp.zeros_like(dvacc)
 
     def one_block(half, carry):
@@ -121,30 +122,21 @@
         heads_apart(do_ref, half, dos)
         window = Window(place, half)
 
-        def score(t, top):
+        def score(t, mass):
             s = window.scores(t, kbuf, qs)
             s_scr[window.kept(t), :] = s
-            return jnp.maximum(top, fold(s, jnp.max))
-
-        top = lax.fori_loop(0, window.count, score, jnp.full((8, LANES), MASKED, F32))
-        top = jnp.max(top, axis=0, keepdims=True)
-
-        def weigh(t, mass):
-            e = jnp.exp2(s_scr[window.kept(t), :] - top)
-            s_scr[window.kept(t), :] = e
-            return mass + fold(e, jnp.sum)
-
-        mass = lax.fori_loop(0, window.count, weigh, jnp.zeros((8, LANES), F32))
-        inverse = 1.0 / jnp.sum(mass, axis=0, keepdims=True)
+            return mass + fold(jnp.exp2(s), jnp.sum)
+
+        mass = lax.fori_loop(0, window.count, score, jnp.zeros((8, LANES), F32))
+        log_sum = jnp.log2(jnp.sum(mass, axis=0, keepdims=True))
 
         def spread(t, carry):
-            p = (s_scr[window.kept(t), :] * inverse).astype(BF)
+            p = jnp.exp2(s_scr[window.kept(t), :] - log_sum).astype(BF)
             dvacc[window.keys(t), :] += dot(p, dos[...], 1, 0)
             return carry
 
         lax.fori_loop(0, window.count, spread, 0)
-        stats[2 * half] = top
-        stats[2 * half + 1] = inverse
+        stats[half] = log_sum
         return carry
 
     lax.fori_loop(0, 2, one_block, 0)
@@ -157,7 +149,7 @@
     kbuf, vbuf, dkacc, p_scr, dp_scr, qs, dos,
 ):
     place = Place(facts)
-    place.gather((k0, k1, k2, k3), kbuf)
+    place.gather((k0, k1, k2, k3), kbuf, by_zl=True)
     place.gather((v0, v1, v2, v3), vbuf)
     dkacc[...] = jnp.zeros_like(dkacc)
 
@@ -165,10 +157,10 @@
         heads_apart(q_ref, half, qs)
         heads_apart(do_ref, half, dos)
         window = Window(place, half)
-        top, inverse = stats[2 * half], stats[2 * half + 1]
+        log_sum = stats[half]
 
         def weigh(t, moment):
-            p = jnp.exp2(window.scores(t, kbuf, qs) - top) * inverse
+            p = jnp.exp2(window.scores(t, kbuf, qs) - log_sum)
             dp = dot(vbuf[window.keys(t), :], dos[...], 1, 1)
             p_scr[window.kept(t), :] = p
             dp_scr[window.kept(t), :] = dp
@@ -201,7 +193,7 @@
     vmem = pl.BlockSpec(memory_space=pltpu.VMEM)
     return pl.pallas_call(
         forward_kernel,
-        out_shape=(jax.ShapeDtypeStruct((4, 1, LANES), F32),) + SHARES,
+        out_shape=(jax.ShapeDtypeStruct((2, 1, LANES), F32),) + SHARES,
         in_specs=[pl.BlockSpec(memory_space=pltpu.SMEM)] + [vmem] * 6,
         out_specs=(vmem,) * 5,
         scratch_shapes=[
@@ -212,9 +204,7 @@
             pltpu.VMEM((LANES, DH), BF),
         ],
         compiler_params=pltpu.CompilerParams(vmem_limit_bytes=32 * 2**20),
-        cost_estimate=pl.CostEstimate(
-            flops=3 * 10**9, bytes_accessed=4 * 10**6, transcendentals=2 * 10**6
-        ),
+        cost_estimate=pl.CostEstimate(flops=3 * 10**9, bytes_accessed=4 * 10**6, transcendentals=2 * 10**6),
     )(facts, q, do, *ks)
 
 
@@ -265,21 +255,20 @@
     )(*arrays)
 
 
-def columns_kernel(c0, c1, c2, c3, keys, values):
-    for a, ref in enumerate((c0, c1, c2, c3)):
-        keys[a] = ref[:, 0:DH]
-        values[a] = ref[:, DH : 2 * DH]
-
-
-def columns_of(pieces):
-    vmem = pl.BlockSpec(memory_space=pltpu.VMEM)
-    return pl.pallas_call(
-        columns_kernel,
+def stack_kernel(*refs):
+    for i, ref in enumerate(refs[:-2]):
+        refs[-2 + i // 4][i % 4] = ref[...]
+
+
+def stacked(ks, vs):
+    vmem = pl.BlockSpec(memory_space=pltpu.VMEM)
+    return pl.pallas_call(
+        stack_kernel,
         out_shape=SHARES[:2],
-        in_specs=[vmem] * 4,
+        in_specs=[vmem] * 8,
         out_specs=(vmem,) * 2,
         compiler_params=pltpu.CompilerParams(vmem_limit_bytes=16 * 2**20),
-    )(*pieces)
+    )(*ks, *vs)
 
 
 def finish_kernel(facts, *refs):
@@ -369,16 +358,15 @@
     def moved(value, axis, shift):
         return lax.ppermute(value, axis, ring(shift))
 
-    own = jnp.concatenate([keys_in[0], values_in[0]], axis=1)
-    pieces = [own] + [moved(own, "zl", a) for a in (1, 2, 3)]
+    key, value = keys_in[0], values_in[0]
+    ks = [key] + [moved(key, "y", s) for s in (1, 2, 3)]
+    vs = [value] + [moved(value, "zl", a) for a in (1, 2, 3)]
     rows_in = near(queries[0], out_grad[0])
-    hidden = hidden_in[0]
-    hidden = (hidden, lax.ppermute(hidden, "co", swap))
-    pieces, rows_in, hidden = lax.optimization_barrier((pieces, rows_in, hidden))
-    ks, vs = columns_of(pieces)
-    ks = [ks] + [moved(ks, "y", s) for s in (1, 2, 3)]
-    vs = after(vs, ks[1])
+    ks, vs, rows_in = lax.optimization_barrier((ks, vs, rows_in))
+    ks, vs = stacked(ks, vs)
+    ks = [ks] + [moved(ks, "zl", a) for a in (1, 2, 3)]
     vs = [vs] + [moved(vs, "y", s) for s in (1, 2, 3)]
+    ks, vs = lax.optimization_barrier((ks, vs))
 
     def received(shares):
         return [shares[0]] + [moved(shares[s], "y", s) for s in (1, 2, 3)]
@@ -390,18 +378,26 @@
     stats, *dvs = forward(facts, *rows_in, ks)
     dvs = received(dvs)
     neighbour = [(0, 1), (1, 0), (2, 3), (3, 2)]
-    beside = lax.ppermute(after(hidden[0], stats), "zl", neighbour)
+    hidden = hidden_in[0]
+    beside = lax.ppermute(after(hidden, stats), "zl", neighbour)
     dq, *dks = backward(facts, *rows_in, ks, vs, stats)
-    dks = received(after(dks, dvs))
-    key_grads, value_grads, mine, sent = finish(facts, over_zl(dks), over_zl(dvs))
-
-    beside = after(beside, *dks)
-    hidden = (hidden[0], beside, hidden[1], lax.ppermute(beside, "co", swap))
-    rows = jnp.stack([mine, lax.ppermute(sent, "zl", neighbour)])
-    cross = [
-        (x0 + 4 * c, x0 + 4 * (1 - c)) for c in range(2) for x0 in range(4) if x0 // 2 == 1 - c
-    ]
-    rows = jnp.stack([rows, lax.ppermute(rows, ("co", "x"), cross)]).reshape(4 * ROWS, DH)
+    dks = received(after(dks, *dvs, beside))
+    value_parts = over_zl(dvs)
+    dks, hidden, beside = after((dks, hidden, beside), *value_parts)
+    key_grads, value_grads, mine, sent = finish(facts, over_zl(dks), value_parts)
+
+    hidden = (hidden, beside) + tuple(lax.ppermute(h, "co", swap) for h in (hidden, beside))
+    def to_worker(other_core, other_zl):
+        index = [(c, z, x0) for c in range(2) for z in range(4) for x0 in range(4)]
+        pairs = [
+            (i, ((c ^ other_core) * 4 + (z ^ other_zl)) * 4 + x0)
+            for i, (c, z, x0) in enumerate(index)
+            if x0 // 2 == c ^ other_core
+        ]
+        return lax.ppermute(sent if other_zl else mine, ("co", "zl", "x"), pairs)
+
+    rows = jnp.stack([mine, to_worker(0, 1), to_worker(1, 0), to_worker(1, 1)])
+    rows = rows.reshape(4 * ROWS, DH)
 
     def along(j):
         return [

time: 133 us -> 141 us (1.060)
  starting transfers between devices: 54.9 us -> 65.8 us
  waiting for transfers between devices: 60.1 us -> 56.4 us
    ppermute x24 -> x27, starting transfers between devices: 32.6 us -> 46.3 us  [moved(): return lax.ppermute(value, axis, ring(shift))]
    ppermute x24 -> x27, waiting for transfers between devices: 40.7 us -> 36.6 us  [moved(): return lax.ppermute(value, axis, ring(shift))]
    ppermute x1, waiting for transfers between devices: 2.04 us -> 5.81 us  [per_device(): lax.ppermute(total[1, 0].astype(BF), 'zh', swap)]
    ppermute x5 -> x6, starting transfers between devices: 13.3 us -> 9.65 us  [the longest x3 5.75 us: to_worker(): return lax.ppermute(sent if other_zl else mine, ('co', 'zl', 'x'), pairs)]
    ppermute x1, waiting for transfers between devices: 4.55 us -> 1.23 us  [per_device(): lax.ppermute(total[1, 1].astype(BF), ('zh', 'zl'), both)]
    ppermute x5 -> x6, waiting for transfers between devices: 3.97 us -> 3.07 us  [the longest x1 2.5 us: per_device(): beside = lax.ppermute(after(hidden, stats), 'zl', neighbour)]
  transfers between devices with their start and end apart: 35 -> 39, of which waited for: 17 -> 16; matrix products, arithmetic and copies ran while one was open for 1% -> 0% of each run, Pallas kernels for 7% -> 5%
where the time goes in v8:
time: 141 us; the launch traced here: 140 us
  starting transfers between devices  65.8 us (47%)
  waiting for transfers between devices  56.4 us (40%)
  Pallas kernels  13.6 us (10%)
  local copies, waits for them, and re-layouts  2.81 us (2%)
    ppermute x27, starting transfers between devices, moved(): return lax.ppermute(value, axis, ring(shift))  46.3 us
    ppermute x27, waiting for transfers between devices, moved(): return lax.ppermute(value, axis, ring(shift))  36.6 us
    ppermute x3, waiting for transfers between devices, per_device(): lax.ppermute(rows, ('co', 'x'), along(j))  9.69 us
    ppermute x1, waiting for transfers between devices, per_device(): lax.ppermute(total[1, 0].astype(BF), 'zh', swap)  5.81 us
    pallas_call x1, Pallas kernels, backward(): pl.pallas_call(backward_kernel, out_shape=(jax.ShapeDtypeStruct((ROWS, HE...  5.8 us
    ppermute x3, starting transfers between devices, to_worker(): return lax.ppermute(sent if other_zl else mine, ('co', 'zl', 'x'), pairs)  5.75 us
    pallas_call x1, Pallas kernels, forward(): pl.pallas_call(forward_kernel, out_shape=(jax.ShapeDtypeStruct((2, 1, LAN...  3.77 us
    ppermute x1, starting transfers between devices, per_device(): lax.ppermute(total[1, 1].astype(BF), ('zh', 'zl'), both)  3.49 us
  transfers between devices with their start and end apart: 39, of which 16 were waited for; matrix products, arithmetic and copies ran while one was open for 0% of the time, Pallas kernels for 5%

profile of v8, /device:TPU:1, one launch (start us, length us, event | category | flops | bytes accessed | tf_op | source)
XLA Modules:
  0.0 140.5 jit_solution(18285863763108676598)
XLA Ops:
  0.6 3.6 %collective-permute-start.2 = (bf16[224,128]{1,0:T(8,128)(2,1)}, bf16[224,128]{1,0:T(8,128)(2,1)S(1)}, u32[]{:S(2)}, u32[]{:S(2)}) collective-permute-start(bf16[224,128]{1,0:T(8,128)(2,1)} %bitcast.58), channel_id=1, source_target_pairs={{0,12},{4,0},{8,4},{12,8},{1,13},{5,1},{9,5},{13,9},{2,14},{6,2},{... | collective-permute-start | bytes 172040 | tf_op jit(solution)/shard_map/ppermute | solution.py:359
  4.3 0.3 collective-permute-start.1
  4.6 0.7 collective-permute-start
  5.3 4.3 %collective-permute-start.5 = (bf16[224,128]{1,0:T(8,128)(2,1)}, bf16[224,128]{1,0:T(8,128)(2,1)S(1)}, u32[]{:S(2)}, u32[]{:S(2)}) collective-permute-start(bf16[224,128]{1,0:T(8,128)(2,1)} %bitcast.62), channel_id=1, source_target_pairs={{0,48},{16,0},{32,16},{48,32},{1,49},{17,1},{33,17},{49,33},{2,50}... | collective-permute-start | bytes 172040 | tf_op jit(solution)/shard_map/ppermute | solution.py:359
  9.7 0.3 collective-permute-start.3
  10.0 1.0 copy-done.1
  11.0 1.0 copy-done.2
  12.0 0.1 shard_map.102
  12.1 2.9 %collective-permute-done.4.refs_6_ = bf16[224,128]{1,0:T(8,128)(2,1)S(1)} collective-permute-done((bf16[224,128]{1,0:T(8,128)(2,1)}, bf16[224,128]{1,0:T(8,128)(2,1)S(1)}, u32[]{:S(2)}, u32[]{:S(2)}) %collective-permute-start.4) | collective-permute-done | bytes 57376 | tf_op jit(solution)/shard_map/ppermute | solution.py:359
  15.1 0.8 collective-permute-start.8
  15.9 1.2 collective-permute-start.7
  17.1 1.4 collective-permute-start.6
  18.5 2.0 %collective-permute-start.11 = (bf16[4,224,128]{2,1,0:T(8,128)(2,1)S(1)}, bf16[4,224,128]{2,1,0:T(8,128)(2,1)S(1)}, u32[]{:S(2)}, u32[]{:S(2)}) collective-permute-start(bf16[4,224,128]{2,1,0:T(8,128)(2,1)S(1)} %get-tuple-element.73.v0), channel_id=1, source_target_pairs={{0,12},{4,0},{8,4},{12,8},{1,13},{5,1},{9,5},{13,9},{2,14},{6,2},{... | collective-permute-start | bytes 688136 | tf_op jit(solution)/shard_map/ppermute | solution.py:359
  20.4 1.4 %collective-permute-start.10 = (bf16[4,224,128]{2,1,0:T(8,128)(2,1)S(1)}, bf16[4,224,128]{2,1,0:T(8,128)(2,1)S(1)}, u32[]{:S(2)}, u32[]{:S(2)}) collective-permute-start(bf16[4,224,128]{2,1,0:T(8,128)(2,1)S(1)} %get-tuple-element.73.v0), channel_id=1, source_target_pairs={{0,8},{4,12},{8,0},{12,4},{1,9},{5,13},{9,1},{13,5},{2,10},{6,14},... | collective-permute-start | bytes 688136 | tf_op jit(solution)/shard_map/ppermute | solution.py:359
  21.9 0.6 copy-done.5
  22.5 0.0 copy-done.6
  22.5 0.1 concatenate.3.facts
  22.6 12.9 %collective-permute-done.7.k2 = bf16[4,224,128]{2,1,0:T(8,128)(2,1)S(1)} collective-permute-done((bf16[4,224,128]{2,1,0:T(8,128)(2,1)S(1)}, bf16[4,224,128]{2,1,0:T(8,128)(2,1)S(1)}, u32[]{:S(2)}, u32[]{:S(2)}) %collective-permute-start.7) | collective-permute-done | bytes 229408 | tf_op jit(solution)/shard_map/ppermute | solution.py:359
  35.5 3.8 %shard_map.104 = (f32[2,1,896]{2,1,0:T(1,128)S(1)}, bf16[4,224,128]{2,1,0:T(8,128)(2,1)S(1)}, bf16[4,224,128]{2,1,0:T(8,128)(2,1)S(1)}, bf16[4,224,128]{2,1,0:T(8,128)(2,1)S(1)}, bf16[4,224,128]{2,1,0:T(8,128)(2,1)S(1)}) custom-call(s32[27]{0:T(128)S(1)} %concatenate.3.facts, bf16[224,1024]{1,0:T(8,128)(2,1)S(1)} %get-tuple-element.57.q_ref, ...), custom_call_target="tpu_custom_call" | custom-call | flops 3000000000 | bytes 4000000 | tf_op jit(solution)/shard_map/pallas_call | solution.py:194
  39.3 1.1 collective-permute-start.15
  40.4 3.4 %collective-permute-start.12 = (bf16[4,224,128]{2,1,0:T(8,128)(2,1)S(1)}, bf16[4,224,128]{2,1,0:T(8,128)(2,1)S(1)}, u32[]{:S(2)}, u32[]{:S(2)}) collective-permute-start(bf16[4,224,128]{2,1,0:T(8,128)(2,1)S(1)} %get-tuple-element.84), channel_id=1, source_target_pairs={{0,4},{4,8},{8,12},{12,0},{1,5},{5,9},{9,13},{13,1},{2,6},{6,10},{... | collective-permute-start | bytes 688136 | tf_op jit(solution)/shard_map/ppermute | solution.py:359
  43.8 1.1 collective-permute-start.13
  44.9 1.4 collective-permute-start.14
  46.3 5.8 %shard_map.105 = (bf16[224,1024]{1,0:T(8,128)(2,1)}, bf16[4,224,128]{2,1,0:T(8,128)(2,1)S(1)}, bf16[4,224,128]{2,1,0:T(8,128)(2,1)S(1)}, bf16[4,224,128]{2,1,0:T(8,128)(2,1)S(1)}, bf16[4,224,128]{2,1,0:T(8,128)(2,1)S(1)}) custom-call(s32[27]{0:T(128)S(1)} %concatenate.3.facts, bf16[224,1024]{1,0:T(8,128)(2,1)S(1)} %get-tuple-element.57.q_ref, ...), custom_call_target="tpu_custom_call" | custom-call | flops 5000000000 | bytes 5000000 | tf_op jit(solution)/shard_map/pallas_call | solution.py:213
  52.1 2.5 %collective-permute-done.15.hid1 = bf16[224,2048]{1,0:T(8,128)(2,1)S(1)} collective-permute-done((bf16[224,2048]{1,0:T(8,128)(2,1)S(1)}, bf16[224,2048]{1,0:T(8,128)(2,1)S(1)}, u32[]{:S(2)}, u32[]{:S(2)}) %collective-permute-start.15) | collective-permute-done | bytes 917536 | tf_op jit(solution)/shard_map/ppermute | solution.py:382
  54.6 7.5 %collective-permute-start.16 = (bf16[4,224,128]{2,1,0:T(8,128)(2,1)S(1)}, bf16[4,224,128]{2,1,0:T(8,128)(2,1)S(1)}, u32[]{:S(2)}, u32[]{:S(2)}) collective-permute-start(bf16[4,224,128]{2,1,0:T(8,128)(2,1)S(1)} %get-tuple-element.89), channel_id=1, source_target_pairs={{0,4},{4,8},{8,12},{12,0},{1,5},{5,9},{9,13},{13,1},{2,6},{6,10},{... | collective-permute-start | bytes 688136 | tf_op jit(solution)/shard_map/ppermute | solution.py:359
  62.1 2.4 %collective-permute-start.18 = (bf16[4,224,128]{2,1,0:T(8,128)(2,1)S(1)}, bf16[4,224,128]{2,1,0:T(8,128)(2,1)S(1)}, u32[]{:S(2)}, u32[]{:S(2)}) collective-permute-start(bf16[4,224,128]{2,1,0:T(8,128)(2,1)S(1)} %get-tuple-element.91), channel_id=1, source_target_pairs={{0,12},{4,0},{8,4},{12,8},{1,13},{5,1},{9,5},{13,9},{2,14},{6,2},{... | collective-permute-start | bytes 688136 | tf_op jit(solution)/shard_map/ppermute | solution.py:359
  64.5 0.1 fusion.5
  64.7 6.1 %collective-permute-start.21 = (bf16[224,128]{1,0:T(8,128)(2,1)S(1)}, bf16[224,128]{1,0:T(8,128)(2,1)S(1)}, u32[]{:S(2)}, u32[]{:S(2)}) collective-permute-start(bf16[224,128]{1,0:T(8,128)(2,1)S(1)} %get-tuple-element.112), channel_id=1, source_target_pairs={{0,48},{16,0},{32,16},{48,32},{1,49},{17,1},{33,17},{49,33},{2,50}... | collective-permute-start | bytes 172040 | tf_op jit(solution)/shard_map/ppermute | solution.py:359
  70.8 0.7 collective-permute-start.20
  71.5 0.6 collective-permute-done.21.refs_7_
  72.1 1.4 %collective-permute-start.19 = (bf16[224,128]{1,0:T(8,128)(2,1)S(1)}, bf16[224,128]{1,0:T(8,128)(2,1)S(1)}, u32[]{:S(2)}, u32[]{:S(2)}) collective-permute-start(bf16[224,128]{1,0:T(8,128)(2,1)S(1)} %get-tuple-element.114), channel_id=1, source_target_pairs={{0,16},{16,32},{32,48},{48,0},{1,17},{17,33},{33,49},{49,1},{2,18}... | collective-permute-start | bytes 172040 | tf_op jit(solution)/shard_map/ppermute | solution.py:359
  73.5 1.8 %collective-permute-done.20.refs_6_ = bf16[224,128]{1,0:T(8,128)(2,1)S(1)} collective-permute-done((bf16[224,128]{1,0:T(8,128)(2,1)S(1)}, bf16[224,128]{1,0:T(8,128)(2,1)S(1)}, u32[]{:S(2)}, u32[]{:S(2)}) %collective-permute-start.20) | collective-permute-done | bytes 57376 | tf_op jit(solution)/shard_map/ppermute | solution.py:359
  75.4 2.1 %collective-permute-done.19.refs_5_ = bf16[224,128]{1,0:T(8,128)(2,1)S(1)} collective-permute-done((bf16[224,128]{1,0:T(8,128)(2,1)S(1)}, bf16[224,128]{1,0:T(8,128)(2,1)S(1)}, u32[]{:S(2)}, u32[]{:S(2)}) %collective-permute-start.19) | collective-permute-done | bytes 57376 | tf_op jit(solution)/shard_map/ppermute | solution.py:359
  77.5 2.7 %collective-permute-start.25 = (bf16[224,2048]{1,0:T(8,128)(2,1)S(1)}, bf16[224,2048]{1,0:T(8,128)(2,1)S(1)}, u32[]{:S(2)}, u32[]{:S(2)}) collective-permute-start(bf16[224,2048]{1,0:T(8,128)(2,1)S(1)} %bitcast.50), channel_id=1, source_target_pairs={{0,64},{64,0},{1,65},{65,1},{2,66},{66,2},{3,67},{67,3},{4,68},{68... | collective-permute-start | bytes 2752520 | tf_op jit(solution)/shard_map/ppermute | solution.py:389
  80.2 0.1 collective-permute-start.26
  80.3 0.1 fusion.8
  80.5 1.8 %collective-permute-start.24 = (bf16[224,128]{1,0:T(8,128)(2,1)S(1)}, bf16[224,128]{1,0:T(8,128)(2,1)S(1)}, u32[]{:S(2)}, u32[]{:S(2)}) collective-permute-start(bf16[224,128]{1,0:T(8,128)(2,1)S(1)} %get-tuple-element.108), channel_id=1, source_target_pairs={{0,48},{16,0},{32,16},{48,32},{1,49},{17,1},{33,17},{49,33},{2,50}... | collective-permute-start | bytes 172040 | tf_op jit(solution)/shard_map/ppermute | solution.py:359
  82.3 0.4 collective-permute-start.22
  82.7 0.9 collective-permute-done.24.refs_3_
  83.6 2.7 %collective-permute-done.23.refs_2_ = bf16[224,128]{1,0:T(8,128)(2,1)S(1)} collective-permute-done((bf16[224,128]{1,0:T(8,128)(2,1)S(1)}, bf16[224,128]{1,0:T(8,128)(2,1)S(1)}, u32[]{:S(2)}, u32[]{:S(2)}) %collective-permute-start.23) | collective-permute-done | bytes 57376 | tf_op jit(solution)/shard_map/ppermute | solution.py:359
  86.3 1.2 collective-permute-done.22.refs_1_
  87.5 1.3 shard_map.106
  88.8 3.8 %collective-permute-start.28 = (bf16[224,128]{1,0:T(8,128)(2,1)S(1)}, bf16[224,128]{1,0:T(8,128)(2,1)S(1)}, u32[]{:S(2)}, u32[]{:S(2)}) collective-permute-start(bf16[224,128]{1,0:T(8,128)(2,1)S(1)} %get-tuple-element.100), channel_id=1, source_target_pairs={{2,66},{3,67},{18,82},{19,83},{34,98},{35,99},{50,114},{51,115},{6... | collective-permute-start | bytes 172040 | tf_op jit(solution)/shard_map/ppermute | solution.py:397
  92.6 1.3 collective-permute-start.29
  93.9 0.7 collective-permute-start.27
  94.6 0.6 collective-permute-done.29
  95.2 0.7 collective-permute-start.32
  95.9 1.3 collective-permute-start.31
  97.2 1.3 collective-permute-start.30
  98.5 7.2 %collective-permute-done.31.row2 = bf16[896,128]{1,0:T(8,128)(2,1)S(1)} collective-permute-done((bf16[896,128]{1,0:T(8,128)(2,1)S(1)}, bf16[896,128]{1,0:T(8,128)(2,1)S(1)}, u32[]{:S(2)}, u32[]{:S(2)}) %collective-permute-start.31) | collective-permute-done | bytes 229408 | tf_op jit(solution)/shard_map/ppermute | solution.py:407
  105.8 2.4 %collective-permute-done.30.row1 = bf16[896,128]{1,0:T(8,128)(2,1)S(1)} collective-permute-done((bf16[896,128]{1,0:T(8,128)(2,1)S(1)}, bf16[896,128]{1,0:T(8,128)(2,1)S(1)}, u32[]{:S(2)}, u32[]{:S(2)}) %collective-permute-start.30) | collective-permute-done | bytes 229408 | tf_op jit(solution)/shard_map/ppermute | solution.py:407
  108.2 2.6 %shard_map.107 = (bf16[2,2,16,2048]{3,2,1,0:T(8,128)(2,1)S(1)}, bf16[2,2,16,2048]{3,2,1,0:T(8,128)(2,1)S(1)}, bf16[2,2,16,2048]{3,2,1,0:T(8,128)(2,1)S(1)}, bf16[2,2,16,2048]{3,2,1,0:T(8,128)(2,1)S(1)}) custom-call(s32[27]{0:T(128)S(1)} %concatenate.3.facts, bf16[224,2048]{1,0:T(8,128)(2,1)S(1)} %bitcast.51, ...), custom_call_target="tpu_custom_call" | custom-call | flops 1000000000 | bytes 4000000 | tf_op jit(solution)/shard_map/pallas_call | solution.py:337
  110.8 0.1 collective-permute-start.33
  110.9 3.9 %collective-permute-start.34 = (bf16[2,2,16,2048]{3,2,1,0:T(8,128)(2,1)S(1)}, bf16[2,2,16,2048]{3,2,1,0:T(8,128)(2,1)S(1)}, u32[]{:S(2)}, u32[]{:S(2)}) collective-permute-start(bf16[2,2,16,2048]{3,2,1,0:T(8,128)(2,1)S(1)} %get-tuple-element.104), channel_id=1, source_target_pairs={{0,8},{4,12},{8,0},{12,4},{1,9},{5,13},{9,1},{13,5},{2,10},{6,14},... | collective-permute-start | bytes 786440 | tf_op jit(solution)/shard_map/ppermute | solution.py:359
  114.8 3.2 %collective-permute-done.33 = bf16[2,2,16,2048]{3,2,1,0:T(8,128)(2,1)S(1)} collective-permute-done((bf16[2,2,16,2048]{3,2,1,0:T(8,128)(2,1)S(1)}, bf16[2,2,16,2048]{3,2,1,0:T(8,128)(2,1)S(1)}, u32[]{:S(2)}, u32[]{:S(2)}) %collective-permute-start.33) | collective-permute-done | bytes 262176 | tf_op jit(solution)/shard_map/ppermute | solution.py:359
  118.0 8.0 %collective-permute-done.34 = bf16[2,2,16,2048]{3,2,1,0:T(8,128)(2,1)S(1)} collective-permute-done((bf16[2,2,16,2048]{3,2,1,0:T(8,128)(2,1)S(1)}, bf16[2,2,16,2048]{3,2,1,0:T(8,128)(2,1)S(1)}, u32[]{:S(2)}, u32[]{:S(2)}) %collective-permute-start.34) | collective-permute-done | bytes 262176 | tf_op jit(solution)/shard_map/ppermute | solution.py:359
  126.0 0.1 fusion.9
  126.2 1.7 %collective-permute-start.36 = (bf16[16,2048]{1,0:T(8,128)(2,1)S(1)}, bf16[16,2048]{1,0:T(8,128)(2,1)S(1)}, u32[]{:S(2)}, u32[]{:S(2)}) collective-permute-start(bf16[16,2048]{1,0:T(8,128)(2,1)S(1)} %get-tuple-element.116), channel_id=1, source_target_pairs={{0,32},{32,0},{16,48},{48,16},{1,33},{33,1},{17,49},{49,17},{2,34}... | collective-permute-start | bytes 196616 | tf_op jit(solution)/shard_map/ppermute | solution.py:414
  127.9 3.5 %collective-permute-start.38 = (bf16[16,2048]{1,0:T(8,128)(2,1)S(1)}, bf16[16,2048]{1,0:T(8,128)(2,1)S(1)}, u32[]{:S(2)}, u32[]{:S(2)}) collective-permute-start(bf16[16,2048]{1,0:T(8,128)(2,1)S(1)} %get-tuple-element.117), channel_id=1, source_target_pairs={{0,160},{128,32},{32,128},{160,0},{16,176},{144,48},{48,144},{176,... | collective-permute-start | bytes 196616 | tf_op jit(solution)/shard_map/ppermute | solution.py:416
  131.4 1.4 collective-permute-start.37
  132.8 1.2 collective-permute-done.38
  134.0 5.8 %collective-permute-done.37 = bf16[16,2048]{1,0:T(8,128)(2,1)S(1)} collective-permute-done((bf16[16,2048]{1,0:T(8,128)(2,1)S(1)}, bf16[16,2048]{1,0:T(8,128)(2,1)S(1)}, u32[]{:S(2)}, u32[]{:S(2)}) %collective-permute-start.37) | collective-permute-done | bytes 65568 | tf_op jit(solution)/shard_map/ppermute | solution.py:415
  139.8 0.7 fusion.2
  (41 shorter events, 0.2 us)
Async XLA Ops:
  0.6 9.0 %collective-permute-start.2 = (bf16[224,128]{1,0:T(8,128)(2,1)}, bf16[224,128]{1,0:T(8,128)(2,1)S(1)}, u32[]{:S(2)}, u32[]{:S(2)}) collective-permute-start(bf16[224,128]{1,0:T(8,128)(2,1)} %bitcast.58), channel_id=1, source_target_pairs={{0,12},{4,0},{8,4},{12,8},{1,13},{5,1},{9,5},{13,9},{2,14},{6,2},{... | collective-permute-start | bytes 172040 | tf_op jit(solution)/shard_map/ppermute | solution.py:359
  4.3 7.8 %collective-permute-start.1 = (bf16[224,128]{1,0:T(8,128)(2,1)}, bf16[224,128]{1,0:T(8,128)(2,1)S(1)}, u32[]{:S(2)}, u32[]{:S(2)}) collective-permute-start(bf16[224,128]{1,0:T(8,128)(2,1)} %bitcast.59), channel_id=1, source_target_pairs={{0,8},{4,12},{8,0},{12,4},{1,9},{5,13},{9,1},{13,5},{2,10},{6,14},... | collective-permute-start | bytes 172040 | tf_op jit(solution)/shard_map/ppermute | solution.py:359
  4.6 7.4 %collective-permute-start = (bf16[224,128]{1,0:T(8,128)(2,1)}, bf16[224,128]{1,0:T(8,128)(2,1)S(1)}, u32[]{:S(2)}, u32[]{:S(2)}) collective-permute-start(bf16[224,128]{1,0:T(8,128)(2,1)} %bitcast.60), channel_id=1, source_target_pairs={{0,4},{4,8},{8,12},{12,0},{1,5},{5,9},{9,13},{13,1},{2,6},{6,10},{... | collective-permute-start | bytes 172040 | tf_op jit(solution)/shard_map/ppermute | solution.py:359
  5.3 6.8 %collective-permute-start.5 = (bf16[224,128]{1,0:T(8,128)(2,1)}, bf16[224,128]{1,0:T(8,128)(2,1)S(1)}, u32[]{:S(2)}, u32[]{:S(2)}) collective-permute-start(bf16[224,128]{1,0:T(8,128)(2,1)} %bitcast.62), channel_id=1, source_target_pairs={{0,48},{16,0},{32,16},{48,32},{1,49},{17,1},{33,17},{49,33},{2,50}... | collective-permute-start | bytes 172040 | tf_op jit(solution)/shard_map/ppermute | solution.py:359
  9.7 5.4 %collective-permute-start.4 = (bf16[224,128]{1,0:T(8,128)(2,1)}, bf16[224,128]{1,0:T(8,128)(2,1)S(1)}, u32[]{:S(2)}, u32[]{:S(2)}) collective-permute-start(bf16[224,128]{1,0:T(8,128)(2,1)} %bitcast.63), channel_id=1, source_target_pairs={{0,32},{16,48},{32,0},{48,16},{1,33},{17,49},{33,1},{49,17},{2,34}... | collective-permute-start | bytes 172040 | tf_op jit(solution)/shard_map/ppermute | solution.py:359
  9.7 5.4 %collective-permute-start.3 = (bf16[224,128]{1,0:T(8,128)(2,1)}, bf16[224,128]{1,0:T(8,128)(2,1)S(1)}, u32[]{:S(2)}, u32[]{:S(2)}) collective-permute-start(bf16[224,128]{1,0:T(8,128)(2,1)} %bitcast.64), channel_id=1, source_target_pairs={{0,16},{16,32},{32,48},{48,0},{1,17},{17,33},{33,49},{49,1},{2,18}... | collective-permute-start | bytes 172040 | tf_op jit(solution)/shard_map/ppermute | solution.py:359
  10.0 1.0 copy-start.1
  11.0 1.0 copy-start.2
  12.0 3.0 %copy-start.3 = (bf16[1,224,128]{2,1,0:T(8,128)(2,1)S(1)}, bf16[1,224,128]{2,1,0:T(8,128)(2,1)}, u32[]{:S(2)}) copy-start(bf16[1,224,128]{2,1,0:T(8,128)(2,1)} %param.9) | copy-start | bytes 172036
  12.0 3.0 %copy-start.4 = (bf16[1,224,128]{2,1,0:T(8,128)(2,1)S(1)}, bf16[1,224,128]{2,1,0:T(8,128)(2,1)}, u32[]{:S(2)}) copy-start(bf16[1,224,128]{2,1,0:T(8,128)(2,1)} %param.10) | copy-start | bytes 172036
  15.1 6.8 %collective-permute-start.8 = (bf16[4,224,128]{2,1,0:T(8,128)(2,1)S(1)}, bf16[4,224,128]{2,1,0:T(8,128)(2,1)S(1)}, u32[]{:S(2)}, u32[]{:S(2)}) collective-permute-start(bf16[4,224,128]{2,1,0:T(8,128)(2,1)S(1)} %get-tuple-element.69.k0), channel_id=1, source_target_pairs={{0,48},{16,0},{32,16},{48,32},{1,49},{17,1},{33,17},{49,33},{2,50}... | collective-permute-start | bytes 688136 | tf_op jit(solution)/shard_map/ppermute | solution.py:359
  15.9 19.6 %collective-permute-start.7 = (bf16[4,224,128]{2,1,0:T(8,128)(2,1)S(1)}, bf16[4,224,128]{2,1,0:T(8,128)(2,1)S(1)}, u32[]{:S(2)}, u32[]{:S(2)}) collective-permute-start(bf16[4,224,128]{2,1,0:T(8,128)(2,1)S(1)} %get-tuple-element.69.k0), channel_id=1, source_target_pairs={{0,32},{16,48},{32,0},{48,16},{1,33},{17,49},{33,1},{49,17},{2,34}... | collective-permute-start | bytes 688136 | tf_op jit(solution)/shard_map/ppermute | solution.py:359
  17.1 18.4 %collective-permute-start.6 = (bf16[4,224,128]{2,1,0:T(8,128)(2,1)S(1)}, bf16[4,224,128]{2,1,0:T(8,128)(2,1)S(1)}, u32[]{:S(2)}, u32[]{:S(2)}) collective-permute-start(bf16[4,224,128]{2,1,0:T(8,128)(2,1)S(1)} %get-tuple-element.69.k0), channel_id=1, source_target_pairs={{0,16},{16,32},{32,48},{48,0},{1,17},{17,33},{33,49},{49,1},{2,18}... | collective-permute-start | bytes 688136 | tf_op jit(solution)/shard_map/ppermute | solution.py:359
  18.5 17.1 %collective-permute-start.11 = (bf16[4,224,128]{2,1,0:T(8,128)(2,1)S(1)}, bf16[4,224,128]{2,1,0:T(8,128)(2,1)S(1)}, u32[]{:S(2)}, u32[]{:S(2)}) collective-permute-start(bf16[4,224,128]{2,1,0:T(8,128)(2,1)S(1)} %get-tuple-element.73.v0), channel_id=1, source_target_pairs={{0,12},{4,0},{8,4},{12,8},{1,13},{5,1},{9,5},{13,9},{2,14},{6,2},{... | collective-permute-start | bytes 688136 | tf_op jit(solution)/shard_map/ppermute | solution.py:359
  20.4 15.1 %collective-permute-start.10 = (bf16[4,224,128]{2,1,0:T(8,128)(2,1)S(1)}, bf16[4,224,128]{2,1,0:T(8,128)(2,1)S(1)}, u32[]{:S(2)}, u32[]{:S(2)}) collective-permute-start(bf16[4,224,128]{2,1,0:T(8,128)(2,1)S(1)} %get-tuple-element.73.v0), channel_id=1, source_target_pairs={{0,8},{4,12},{8,0},{12,4},{1,9},{5,13},{9,1},{13,5},{2,10},{6,14},... | collective-permute-start | bytes 688136 | tf_op jit(solution)/shard_map/ppermute | solution.py:359
  21.9 13.7 %collective-permute-start.9 = (bf16[4,224,128]{2,1,0:T(8,128)(2,1)S(1)}, bf16[4,224,128]{2,1,0:T(8,128)(2,1)S(1)}, u32[]{:S(2)}, u32[]{:S(2)}) collective-permute-start(bf16[4,224,128]{2,1,0:T(8,128)(2,1)S(1)} %get-tuple-element.73.v0), channel_id=1, source_target_pairs={{0,4},{4,8},{8,12},{12,0},{1,5},{5,9},{9,13},{13,1},{2,6},{6,10},{... | collective-permute-start | bytes 688136 | tf_op jit(solution)/shard_map/ppermute | solution.py:359
  21.9 0.7 copy-start.5
  21.9 0.7 copy-start.6
  22.6 16.7 %copy-start = (bf16[1,224,2048]{2,1,0:T(8,128)(2,1)S(1)}, bf16[1,224,2048]{2,1,0:T(8,128)(2,1)}, u32[]{:S(2)}) copy-start(bf16[1,224,2048]{2,1,0:T(8,128)(2,1)} %param.7) | copy-start | bytes 2752516
  39.3 15.3 %collective-permute-start.15 = (bf16[224,2048]{1,0:T(8,128)(2,1)S(1)}, bf16[224,2048]{1,0:T(8,128)(2,1)S(1)}, u32[]{:S(2)}, u32[]{:S(2)}) collective-permute-start(bf16[224,2048]{1,0:T(8,128)(2,1)S(1)} %bitcast.49), channel_id=1, source_target_pairs={{0,16},{16,0},{32,48},{48,32},{1,17},{17,1},{33,49},{49,33},{2,18}... | collective-permute-start | bytes 2752520 | tf_op jit(solution)/shard_map/ppermute | solution.py:382
  40.4 11.7 %collective-permute-start.12 = (bf16[4,224,128]{2,1,0:T(8,128)(2,1)S(1)}, bf16[4,224,128]{2,1,0:T(8,128)(2,1)S(1)}, u32[]{:S(2)}, u32[]{:S(2)}) collective-permute-start(bf16[4,224,128]{2,1,0:T(8,128)(2,1)S(1)} %get-tuple-element.84), channel_id=1, source_target_pairs={{0,4},{4,8},{8,12},{12,0},{1,5},{5,9},{9,13},{13,1},{2,6},{6,10},{... | collective-permute-start | bytes 688136 | tf_op jit(solution)/shard_map/ppermute | solution.py:359
  43.8 8.3 %collective-permute-start.13 = (bf16[4,224,128]{2,1,0:T(8,128)(2,1)S(1)}, bf16[4,224,128]{2,1,0:T(8,128)(2,1)S(1)}, u32[]{:S(2)}, u32[]{:S(2)}) collective-permute-start(bf16[4,224,128]{2,1,0:T(8,128)(2,1)S(1)} %get-tuple-element.85), channel_id=1, source_target_pairs={{0,8},{4,12},{8,0},{12,4},{1,9},{5,13},{9,1},{13,5},{2,10},{6,14},... | collective-permute-start | bytes 688136 | tf_op jit(solution)/shard_map/ppermute | solution.py:359
  44.9 7.2 %collective-permute-start.14 = (bf16[4,224,128]{2,1,0:T(8,128)(2,1)S(1)}, bf16[4,224,128]{2,1,0:T(8,128)(2,1)S(1)}, u32[]{:S(2)}, u32[]{:S(2)}) collective-permute-start(bf16[4,224,128]{2,1,0:T(8,128)(2,1)S(1)} %get-tuple-element.86), channel_id=1, source_target_pairs={{0,12},{4,0},{8,4},{12,8},{1,13},{5,1},{9,5},{13,9},{2,14},{6,2},{... | collective-permute-start | bytes 688136 | tf_op jit(solution)/shard_map/ppermute | solution.py:359
  54.6 22.9 %collective-permute-start.16 = (bf16[4,224,128]{2,1,0:T(8,128)(2,1)S(1)}, bf16[4,224,128]{2,1,0:T(8,128)(2,1)S(1)}, u32[]{:S(2)}, u32[]{:S(2)}) collective-permute-start(bf16[4,224,128]{2,1,0:T(8,128)(2,1)S(1)} %get-tuple-element.89), channel_id=1, source_target_pairs={{0,4},{4,8},{8,12},{12,0},{1,5},{5,9},{9,13},{13,1},{2,6},{6,10},{... | collective-permute-start | bytes 688136 | tf_op jit(solution)/shard_map/ppermute | solution.py:359
  62.1 15.4 %collective-permute-start.17 = (bf16[4,224,128]{2,1,0:T(8,128)(2,1)S(1)}, bf16[4,224,128]{2,1,0:T(8,128)(2,1)S(1)}, u32[]{:S(2)}, u32[]{:S(2)}) collective-permute-start(bf16[4,224,128]{2,1,0:T(8,128)(2,1)S(1)} %get-tuple-element.90), channel_id=1, source_target_pairs={{0,8},{4,12},{8,0},{12,4},{1,9},{5,13},{9,1},{13,5},{2,10},{6,14},... | collective-permute-start | bytes 688136 | tf_op jit(solution)/shard_map/ppermute | solution.py:359
  62.1 15.4 %collective-permute-start.18 = (bf16[4,224,128]{2,1,0:T(8,128)(2,1)S(1)}, bf16[4,224,128]{2,1,0:T(8,128)(2,1)S(1)}, u32[]{:S(2)}, u32[]{:S(2)}) collective-permute-start(bf16[4,224,128]{2,1,0:T(8,128)(2,1)S(1)} %get-tuple-element.91), channel_id=1, source_target_pairs={{0,12},{4,0},{8,4},{12,8},{1,13},{5,1},{9,5},{13,9},{2,14},{6,2},{... | collective-permute-start | bytes 688136 | tf_op jit(solution)/shard_map/ppermute | solution.py:359
  64.7 7.4 %collective-permute-start.21 = (bf16[224,128]{1,0:T(8,128)(2,1)S(1)}, bf16[224,128]{1,0:T(8,128)(2,1)S(1)}, u32[]{:S(2)}, u32[]{:S(2)}) collective-permute-start(bf16[224,128]{1,0:T(8,128)(2,1)S(1)} %get-tuple-element.112), channel_id=1, source_target_pairs={{0,48},{16,0},{32,16},{48,32},{1,49},{17,1},{33,17},{49,33},{2,50}... | collective-permute-start | bytes 172040 | tf_op jit(solution)/shard_map/ppermute | solution.py:359
  70.8 4.5 %collective-permute-start.20 = (bf16[224,128]{1,0:T(8,128)(2,1)S(1)}, bf16[224,128]{1,0:T(8,128)(2,1)S(1)}, u32[]{:S(2)}, u32[]{:S(2)}) collective-permute-start(bf16[224,128]{1,0:T(8,128)(2,1)S(1)} %get-tuple-element.113), channel_id=1, source_target_pairs={{0,32},{16,48},{32,0},{48,16},{1,33},{17,49},{33,1},{49,17},{2,34}... | collective-permute-start | bytes 172040 | tf_op jit(solution)/shard_map/ppermute | solution.py:359
  72.1 5.4 %collective-permute-start.19 = (bf16[224,128]{1,0:T(8,128)(2,1)S(1)}, bf16[224,128]{1,0:T(8,128)(2,1)S(1)}, u32[]{:S(2)}, u32[]{:S(2)}) collective-permute-start(bf16[224,128]{1,0:T(8,128)(2,1)S(1)} %get-tuple-element.114), channel_id=1, source_target_pairs={{0,16},{16,32},{32,48},{48,0},{1,17},{17,33},{33,49},{49,1},{2,18}... | collective-permute-start | bytes 172040 | tf_op jit(solution)/shard_map/ppermute | solution.py:359
  77.5 30.7 %collective-permute-start.25 = (bf16[224,2048]{1,0:T(8,128)(2,1)S(1)}, bf16[224,2048]{1,0:T(8,128)(2,1)S(1)}, u32[]{:S(2)}, u32[]{:S(2)}) collective-permute-start(bf16[224,2048]{1,0:T(8,128)(2,1)S(1)} %bitcast.50), channel_id=1, source_target_pairs={{0,64},{64,0},{1,65},{65,1},{2,66},{66,2},{3,67},{67,3},{4,68},{68... | collective-permute-start | bytes 2752520 | tf_op jit(solution)/shard_map/ppermute | solution.py:389
  80.2 28.0 %collective-permute-start.26 = (bf16[224,2048]{1,0:T(8,128)(2,1)S(1)}, bf16[224,2048]{1,0:T(8,128)(2,1)S(1)}, u32[]{:S(2)}, u32[]{:S(2)}) collective-permute-start(bf16[224,2048]{1,0:T(8,128)(2,1)S(1)} %collective-permute-done.15.hid1), channel_id=1, source_target_pairs={{0,64},{64,0},{1,65},{65,1},{2,66},{66,2},{3,67},{67,3},{4,68},{68... | collective-permute-start | bytes 2752520 | tf_op jit(solution)/shard_map/ppermute | solution.py:389
  80.5 3.1 %collective-permute-start.24 = (bf16[224,128]{1,0:T(8,128)(2,1)S(1)}, bf16[224,128]{1,0:T(8,128)(2,1)S(1)}, u32[]{:S(2)}, u32[]{:S(2)}) collective-permute-start(bf16[224,128]{1,0:T(8,128)(2,1)S(1)} %get-tuple-element.108), channel_id=1, source_target_pairs={{0,48},{16,0},{32,16},{48,32},{1,49},{17,1},{33,17},{49,33},{2,50}... | collective-permute-start | bytes 172040 | tf_op jit(solution)/shard_map/ppermute | solution.py:359
  82.3 4.0 %collective-permute-start.23 = (bf16[224,128]{1,0:T(8,128)(2,1)S(1)}, bf16[224,128]{1,0:T(8,128)(2,1)S(1)}, u32[]{:S(2)}, u32[]{:S(2)}) collective-permute-start(bf16[224,128]{1,0:T(8,128)(2,1)S(1)} %get-tuple-element.109), channel_id=1, source_target_pairs={{0,32},{16,48},{32,0},{48,16},{1,33},{17,49},{33,1},{49,17},{2,34}... | collective-permute-start | bytes 172040 | tf_op jit(solution)/shard_map/ppermute | solution.py:359
  82.3 5.2 %collective-permute-start.22 = (bf16[224,128]{1,0:T(8,128)(2,1)S(1)}, bf16[224,128]{1,0:T(8,128)(2,1)S(1)}, u32[]{:S(2)}, u32[]{:S(2)}) collective-permute-start(bf16[224,128]{1,0:T(8,128)(2,1)S(1)} %get-tuple-element.110), channel_id=1, source_target_pairs={{0,16},{16,32},{32,48},{48,0},{1,17},{17,33},{33,49},{49,1},{2,18}... | collective-permute-start | bytes 172040 | tf_op jit(solution)/shard_map/ppermute | solution.py:359
  88.8 5.8 %collective-permute-start.28 = (bf16[224,128]{1,0:T(8,128)(2,1)S(1)}, bf16[224,128]{1,0:T(8,128)(2,1)S(1)}, u32[]{:S(2)}, u32[]{:S(2)}) collective-permute-start(bf16[224,128]{1,0:T(8,128)(2,1)S(1)} %get-tuple-element.100), channel_id=1, source_target_pairs={{2,66},{3,67},{18,82},{19,83},{34,98},{35,99},{50,114},{51,115},{6... | collective-permute-start | bytes 172040 | tf_op jit(solution)/shard_map/ppermute | solution.py:397
  92.6 2.5 %collective-permute-start.29 = (bf16[224,128]{1,0:T(8,128)(2,1)S(1)}, bf16[224,128]{1,0:T(8,128)(2,1)S(1)}, u32[]{:S(2)}, u32[]{:S(2)}) collective-permute-start(bf16[224,128]{1,0:T(8,128)(2,1)S(1)} %get-tuple-element.101), channel_id=1, source_target_pairs={{2,82},{3,83},{18,66},{19,67},{34,114},{35,115},{50,98},{51,99},{6... | collective-permute-start | bytes 172040 | tf_op jit(solution)/shard_map/ppermute | solution.py:397
  93.9 1.2 collective-permute-start.27
  95.2 3.3 %collective-permute-start.32 = (bf16[896,128]{1,0:T(8,128)(2,1)S(1)}, bf16[896,128]{1,0:T(8,128)(2,1)S(1)}, u32[]{:S(2)}, u32[]{:S(2)}) collective-permute-start(bf16[896,128]{1,0:T(8,128)(2,1)S(1)} %bitcast.52), channel_id=1, source_target_pairs={{0,3},{1,0},{66,65},{67,66},{4,7},{5,4},{70,69},{71,70},{8,11},{9,... | collective-permute-start | bytes 688136 | tf_op jit(solution)/shard_map/ppermute | solution.py:407
  95.9 9.9 %collective-permute-start.31 = (bf16[896,128]{1,0:T(8,128)(2,1)S(1)}, bf16[896,128]{1,0:T(8,128)(2,1)S(1)}, u32[]{:S(2)}, u32[]{:S(2)}) collective-permute-start(bf16[896,128]{1,0:T(8,128)(2,1)S(1)} %bitcast.53), channel_id=1, source_target_pairs={{0,2},{1,3},{66,64},{67,65},{4,6},{5,7},{70,68},{71,69},{8,10},{9,... | collective-permute-start | bytes 688136 | tf_op jit(solution)/shard_map/ppermute | solution.py:407
  97.2 11.0 %collective-permute-start.30 = (bf16[896,128]{1,0:T(8,128)(2,1)S(1)}, bf16[896,128]{1,0:T(8,128)(2,1)S(1)}, u32[]{:S(2)}, u32[]{:S(2)}) collective-permute-start(bf16[896,128]{1,0:T(8,128)(2,1)S(1)} %bitcast.54), channel_id=1, source_target_pairs={{0,1},{1,2},{66,67},{67,64},{4,5},{5,6},{70,71},{71,68},{8,9},{9,1... | collective-permute-start | bytes 688136 | tf_op jit(solution)/shard_map/ppermute | solution.py:407
  110.8 7.2 %collective-permute-start.33 = (bf16[2,2,16,2048]{3,2,1,0:T(8,128)(2,1)S(1)}, bf16[2,2,16,2048]{3,2,1,0:T(8,128)(2,1)S(1)}, u32[]{:S(2)}, u32[]{:S(2)}) collective-permute-start(bf16[2,2,16,2048]{3,2,1,0:T(8,128)(2,1)S(1)} %get-tuple-element.103), channel_id=1, source_target_pairs={{0,4},{4,8},{8,12},{12,0},{1,5},{5,9},{9,13},{13,1},{2,6},{6,10},{... | collective-permute-start | bytes 786440 | tf_op jit(solution)/shard_map/ppermute | solution.py:359
  110.9 15.1 %collective-permute-start.34 = (bf16[2,2,16,2048]{3,2,1,0:T(8,128)(2,1)S(1)}, bf16[2,2,16,2048]{3,2,1,0:T(8,128)(2,1)S(1)}, u32[]{:S(2)}, u32[]{:S(2)}) collective-permute-start(bf16[2,2,16,2048]{3,2,1,0:T(8,128)(2,1)S(1)} %get-tuple-element.104), channel_id=1, source_target_pairs={{0,8},{4,12},{8,0},{12,4},{1,9},{5,13},{9,1},{13,5},{2,10},{6,14},... | collective-permute-start | bytes 786440 | tf_op jit(solution)/shard_map/ppermute | solution.py:359
  114.8 11.3 %collective-permute-start.35 = (bf16[2,2,16,2048]{3,2,1,0:T(8,128)(2,1)S(1)}, bf16[2,2,16,2048]{3,2,1,0:T(8,128)(2,1)S(1)}, u32[]{:S(2)}, u32[]{:S(2)}) collective-permute-start(bf16[2,2,16,2048]{3,2,1,0:T(8,128)(2,1)S(1)} %get-tuple-element.105), channel_id=1, source_target_pairs={{0,12},{4,0},{8,4},{12,8},{1,13},{5,1},{9,5},{13,9},{2,14},{6,2},{... | collective-permute-start | bytes 786440 | tf_op jit(solution)/shard_map/ppermute | solution.py:359
  126.2 6.6 %collective-permute-start.36 = (bf16[16,2048]{1,0:T(8,128)(2,1)S(1)}, bf16[16,2048]{1,0:T(8,128)(2,1)S(1)}, u32[]{:S(2)}, u32[]{:S(2)}) collective-permute-start(bf16[16,2048]{1,0:T(8,128)(2,1)S(1)} %get-tuple-element.116), channel_id=1, source_target_pairs={{0,32},{32,0},{16,48},{48,16},{1,33},{33,1},{17,49},{49,17},{2,34}... | collective-permute-start | bytes 196616 | tf_op jit(solution)/shard_map/ppermute | solution.py:414
  127.9 6.1 %collective-permute-start.38 = (bf16[16,2048]{1,0:T(8,128)(2,1)S(1)}, bf16[16,2048]{1,0:T(8,128)(2,1)S(1)}, u32[]{:S(2)}, u32[]{:S(2)}) collective-permute-start(bf16[16,2048]{1,0:T(8,128)(2,1)S(1)} %get-tuple-element.117), channel_id=1, source_target_pairs={{0,160},{128,32},{32,128},{160,0},{16,176},{144,48},{48,144},{176,... | collective-permute-start | bytes 196616 | tf_op jit(solution)/shard_map/ppermute | solution.py:416
  131.4 8.4 %collective-permute-start.37 = (bf16[16,2048]{1,0:T(8,128)(2,1)S(1)}, bf16[16,2048]{1,0:T(8,128)(2,1)S(1)}, u32[]{:S(2)}, u32[]{:S(2)}) collective-permute-start(bf16[16,2048]{1,0:T(8,128)(2,1)S(1)} %get-tuple-element.118), channel_id=1, source_target_pairs={{0,128},{128,0},{1,129},{129,1},{2,130},{130,2},{3,131},{131,3},{4... | collective-permute-start | bytes 196616 | tf_op jit(solution)/shard_map/ppermute | solution.py:415

commit v9 on v7

--- a/solution.py
+++ b/solution.py
@@ -18,7 +18,7 @@
 SEQ = ROWS * RANKS
 DOCS = 6
 MAX_DOC = 1194
-SPAN = 256
+SPAN = 2 * HALF
 STEPS = -(-(MAX_DOC - 1 + HALF) // SPAN)
 PAD = SPAN
 SCALE = DH**-0.5
@@ -78,14 +78,17 @@
         for h in range(1, HEADS):
             within = jnp.where(lane >= h * HALF, lane - h * HALF, within)
         first = block * HALF
+        self.first = first
         self.pos = within + first
         self.low = jnp.zeros_like(self.pos)
         low0 = jnp.int32(0)
+        self.last_low = jnp.int32(0)
         end = jnp.int32(0)
         for d in range(DOCS - 1):
             end = end + place.facts[d]
             self.low = jnp.where(self.pos >= end, end, self.low)
             low0 = jnp.where(first >= end, end, low0)
+            self.last_low = jnp.where(first + HALF - 1 >= end, end, self.last_low)
         stop = first + HALF
         self.count = lax.div(stop - low0 + (SPAN - 1), SPAN)
         self.start = stop - self.count * SPAN
@@ -97,9 +100,15 @@
         return pl.ds(pl.multiple_of(t * SPAN, SPAN), SPAN)
 
     def scores(self, t, kbuf, qs):
-        s = dot(kbuf[self.keys(t), :], qs[...], 1, 1) * (SCALE * LOG2E)
+        return dot(kbuf[self.keys(t), :], qs[...], 1, 1) * (SCALE * LOG2E)
+
+    def masked(self, t, s):
         key = lax.broadcasted_iota(jnp.int32, (SPAN, LANES), 0) + (self.start + t * SPAN)
         return jnp.where((key >= self.low) & (key <= self.pos), s, MASKED)
+
+    def all_allowed(self, t):
+        first_key = self.start + t * SPAN
+        return (first_key >= self.last_low) & (first_key + SPAN <= self.first + 1)
 
 
 def heads_apart(ref, half, stack):
@@ -121,30 +130,25 @@
         heads_apart(do_ref, half, dos)
         window = Window(place, half)
 
-        def score(t, top):
-            s = window.scores(t, kbuf, qs)
-            s_scr[window.kept(t), :] = s
-            return jnp.maximum(top, fold(s, jnp.max))
-
-        top = lax.fori_loop(0, window.count, score, jnp.full((8, LANES), MASKED, F32))
-        top = jnp.max(top, axis=0, keepdims=True)
-
-        def weigh(t, mass):
-            e = jnp.exp2(s_scr[window.kept(t), :] - top)
-            s_scr[window.kept(t), :] = e
-            return mass + fold(e, jnp.sum)
-
-        mass = lax.fori_loop(0, window.count, weigh, jnp.zeros((8, LANES), F32))
-        inverse = 1.0 / jnp.sum(mass, axis=0, keepdims=True)
+        def score(t, mass):
+            def some(masked):
+                s = window.scores(t, kbuf, qs)
+                s = window.masked(t, s) if masked else s
+                s_scr[window.kept(t), :] = s
+                return mass + fold(jnp.exp2(s), jnp.sum)
+
+            return lax.cond(window.all_allowed(t), lambda: some(False), lambda: some(True))
+
+        mass = lax.fori_loop(0, window.count, score, jnp.zeros((8, LANES), F32))
+        log_sum = jnp.log2(jnp.sum(mass, axis=0, keepdims=True))
 
         def spread(t, carry):
-            p = (s_scr[window.kept(t), :] * inverse).astype(BF)
+            p = jnp.exp2(s_scr[window.kept(t), :] - log_sum).astype(BF)
             dvacc[window.keys(t), :] += dot(p, dos[...], 1, 0)
             return carry
 
         lax.fori_loop(0, window.count, spread, 0)
-        stats[2 * half] = top
-        stats[2 * half + 1] = inverse
+        stats[half] = log_sum
         return carry
 
     lax.fori_loop(0, 2, one_block, 0)
@@ -165,14 +169,19 @@
         heads_apart(q_ref, half, qs)
         heads_apart(do_ref, half, dos)
         window = Window(place, half)
-        top, inverse = stats[2 * half], stats[2 * half + 1]
+        log_sum = stats[half]
 
         def weigh(t, moment):
-            p = jnp.exp2(window.scores(t, kbuf, qs) - top) * inverse
-            dp = dot(vbuf[window.keys(t), :], dos[...], 1, 1)
-            p_scr[window.kept(t), :] = p
-            dp_scr[window.kept(t), :] = dp
-            return moment + fold(p * dp, jnp.sum)
+            def some(masked):
+                s = window.scores(t, kbuf, qs)
+                s = window.masked(t, s) if masked else s
+                p = jnp.exp2(s - log_sum)
+                dp = dot(vbuf[window.keys(t), :], dos[...], 1, 1)
+                p_scr[window.kept(t), :] = p
+                dp_scr[window.kept(t), :] = dp
+                return moment + fold(p * dp, jnp.sum)
+
+            return lax.cond(window.all_allowed(t), lambda: some(False), lambda: some(True))
 
         moment = lax.fori_loop(0, window.count, weigh, jnp.zeros((8, LANES), F32))
         delta = jnp.sum(moment, axis=0, keepdims=True)
@@ -201,7 +210,7 @@
     vmem = pl.BlockSpec(memory_space=pltpu.VMEM)
     return pl.pallas_call(
         forward_kernel,
-        out_shape=(jax.ShapeDtypeStruct((4, 1, LANES), F32),) + SHARES,
+        out_shape=(jax.ShapeDtypeStruct((2, 1, LANES), F32),) + SHARES,
         in_specs=[pl.BlockSpec(memory_space=pltpu.SMEM)] + [vmem] * 6,
         out_specs=(vmem,) * 5,
         scratch_shapes=[
@@ -212,9 +221,7 @@
             pltpu.VMEM((LANES, DH), BF),
         ],
         compiler_params=pltpu.CompilerParams(vmem_limit_bytes=32 * 2**20),
-        cost_estimate=pl.CostEstimate(
-            flops=3 * 10**9, bytes_accessed=4 * 10**6, transcendentals=2 * 10**6
-        ),
+        cost_estimate=pl.CostEstimate(flops=3 * 10**9, bytes_accessed=4 * 10**6, transcendentals=2 * 10**6),
     )(facts, q, do, *ks)
 
 
@@ -364,6 +371,7 @@
     zl, y, x = (lax.axis_index(a) for a in ("zl", "y", "x"))
     zh, core = lax.axis_index("zh"), lax.axis_index("co")
     swap = [(0, 1), (1, 0)]
+    neighbour = [(0, 1), (1, 0), (2, 3), (3, 2)]
     facts = jnp.concatenate([doc_lengths[0], pair_perm, jnp.stack([zl, y, x, core, zh]).astype(jnp.int32)])
 
     def moved(value, axis, shift):
@@ -378,7 +386,8 @@
     ks, vs = columns_of(pieces)
     ks = [ks] + [moved(ks, "y", s) for s in (1, 2, 3)]
     vs = after(vs, ks[1])
-    vs = [vs] + [moved(vs, "y", s) for s in (1, 2, 3)]
+    beside = lax.ppermute(after(hidden[0], ks[1]), "zl", neighbour)
+    vs = [vs] + [moved(vs, "y", s) if s != 2 else vs for s in (1, 2, 3)]
 
     def received(shares):
         return [shares[0]] + [moved(shares[s], "y", s) for s in (1, 2, 3)]
@@ -389,8 +398,7 @@
 
     stats, *dvs = forward(facts, *rows_in, ks)
     dvs = received(dvs)
-    neighbour = [(0, 1), (1, 0), (2, 3), (3, 2)]
-    beside = lax.ppermute(after(hidden[0], stats), "zl", neighbour)
+    vs[2] = moved(after(vs[0], stats), "y", 2)
     dq, *dks = backward(facts, *rows_in, ks, vs, stats)
     dks = received(after(dks, dvs))
     key_grads, value_grads, mine, sent = finish(facts, over_zl(dks), over_zl(dvs))

time: 133 us -> 134 us (level); the launches traced: 133 us -> 132 us
  waiting for transfers between devices: 60.1 us -> 55.6 us
  Pallas kernels: 12.4 us -> 15.9 us
    ppermute x1, starting transfers between devices: 1.85 us -> 6.85 us  [per_device(): hidden = (hidden[0], beside, hidden[1], lax.ppermute(beside, 'co', swap))]
    ppermute x1, starting transfers between devices: 4.27 us -> 0.01 us  [per_device(): beside = lax.ppermute(after(hidden[0], ks[1]), 'zl', neighbour)]
    ppermute x1, waiting for transfers between devices: 4.55 us -> 0.86 us  [per_device(): lax.ppermute(total[1, 1].astype(BF), ('zh', 'zl'), both)]
    pallas_call x1, Pallas kernels: 5.06 us -> 7.09 us  [backward(): pl.pallas_call(backward_kernel, out_shape=(jax.ShapeDtypeStruct((ROWS, HE...]
    ppermute x1, starting transfers between devices: 1.26 us -> 3.28 us  [per_device(): lax.ppermute(total[1, 0].astype(BF), 'zh', swap)]
    ppermute x1, starting transfers between devices: 3.17 us -> 1.39 us  [per_device(): lax.ppermute(total[1, 1].astype(BF), ('zh', 'zl'), both)]
    ppermute x24, waiting for transfers between devices: 40.7 us -> 39 us  [moved(): return lax.ppermute(value, axis, ring(shift))]
    pallas_call x1, Pallas kernels: 3.37 us -> 4.8 us  [forward(): pl.pallas_call(forward_kernel, out_shape=(jax.ShapeDtypeStruct((2, 1, LAN...]
  transfers between devices with their start and end apart: 35 -> 35, of which waited for: 17 -> 18; matrix products, arithmetic and copies ran while one was open for 1% -> 1% of each run, Pallas kernels for 7% -> 10%
where the time goes in v9:
time: 134 us; the launch traced here: 132 us
  waiting for transfers between devices  55.6 us (41%)
  starting transfers between devices  55.3 us (41%)
  Pallas kernels  15.9 us (12%)
  local copies, waits for them, and re-layouts  2.81 us (2%)
  other arithmetic  1.96 us (1%)
    ppermute x24, waiting for transfers between devices, moved(): return lax.ppermute(value, axis, ring(shift))  39 us
    ppermute x24, starting transfers between devices, moved(): return lax.ppermute(value, axis, ring(shift))  31.9 us
    ppermute x3, waiting for transfers between devices, per_device(): lax.ppermute(rows, ('co', 'x'), along(j))  8.85 us
    pallas_call x1, Pallas kernels, backward(): pl.pallas_call(backward_kernel, out_shape=(jax.ShapeDtypeStruct((ROWS, HE...  7.09 us
    ppermute x1, starting transfers between devices, per_device(): hidden = (hidden[0], beside, hidden[1], lax.ppermute(beside, 'co', swap))  6.85 us
    pallas_call x1, Pallas kernels, forward(): pl.pallas_call(forward_kernel, out_shape=(jax.ShapeDtypeStruct((2, 1, LAN...  4.8 us
    ppermute x1, starting transfers between devices, per_device(): lax.ppermute(rows, ('co', 'x'), cross)  4.2 us
    ppermute x1, starting transfers between devices, per_device(): hidden = (hidden, lax.ppermute(hidden, 'co', swap))  3.33 us
  transfers between devices with their start and end apart: 35, of which 18 were waited for; matrix products, arithmetic and copies ran while one was open for 1% of the time, Pallas kernels for 10%

profile of v9, /device:TPU:1, one launch (start us, length us, event | category | flops | bytes accessed | tf_op | source)
XLA Modules:
  0.0 132.3 jit_solution(6770896084674687794)
XLA Ops:
  0.6 3.3 %collective-permute-start.3 = (bf16[224,2048]{1,0:T(8,128)(2,1)}, bf16[224,2048]{1,0:T(8,128)(2,1)S(1)}, u32[]{:S(2)}, u32[]{:S(2)}) collective-permute-start(bf16[224,2048]{1,0:T(8,128)(2,1)} %bitcast.50), channel_id=1, source_target_pairs={{0,64},{64,0},{1,65},{65,1},{2,66},{66,2},{3,67},{67,3},{4,68},{68... | collective-permute-start | bytes 2752520 | tf_op jit(solution)/shard_map/ppermute | solution.py:384
  4.0 0.9 pad_maximum_fusion.1.c0
  4.8 2.7 %collective-permute-start.2 = (bf16[224,256]{1,0:T(8,128)(2,1)S(1)}, bf16[224,256]{1,0:T(8,128)(2,1)S(1)}, u32[]{:S(2)}, u32[]{:S(2)}) collective-permute-start(bf16[224,256]{1,0:T(8,128)(2,1)S(1)} %pad_maximum_fusion.1.c0), channel_id=1, source_target_pairs={{0,48},{16,0},{32,16},{48,32},{1,49},{17,1},{33,17},{49,33},{2,50}... | collective-permute-start | bytes 344072 | tf_op jit(solution)/shard_map/ppermute | solution.py:378
  7.5 0.4 collective-permute-start
  7.9 1.0 copy-done.1
  8.9 1.0 copy-done.2
  9.9 0.1 shard_map.102
  10.0 0.1 collective-permute-done.2.c3
  10.1 8.0 %collective-permute-done.1.c2 = bf16[224,256]{1,0:T(8,128)(2,1)S(1)} collective-permute-done((bf16[224,256]{1,0:T(8,128)(2,1)S(1)}, bf16[224,256]{1,0:T(8,128)(2,1)S(1)}, u32[]{:S(2)}, u32[]{:S(2)}) %collective-permute-start.1) | collective-permute-done | bytes 114720 | tf_op jit(solution)/shard_map/ppermute | solution.py:378
  18.1 0.0 collective-permute-done.c1
  18.1 0.1 shard_map.103
  18.2 1.4 %collective-permute-start.4 = (bf16[4,224,128]{2,1,0:T(8,128)(2,1)S(1)}, bf16[4,224,128]{2,1,0:T(8,128)(2,1)S(1)}, u32[]{:S(2)}, u32[]{:S(2)}) collective-permute-start(bf16[4,224,128]{2,1,0:T(8,128)(2,1)S(1)} %get-tuple-element.50.k0), channel_id=1, source_target_pairs={{0,4},{4,8},{8,12},{12,0},{1,5},{5,9},{9,13},{13,1},{2,6},{6,10},{... | collective-permute-start | bytes 688136 | tf_op jit(solution)/shard_map/ppermute | solution.py:378
  19.6 1.5 %collective-permute-start.6 = (bf16[4,224,128]{2,1,0:T(8,128)(2,1)S(1)}, bf16[4,224,128]{2,1,0:T(8,128)(2,1)S(1)}, u32[]{:S(2)}, u32[]{:S(2)}) collective-permute-start(bf16[4,224,128]{2,1,0:T(8,128)(2,1)S(1)} %get-tuple-element.50.k0), channel_id=1, source_target_pairs={{0,12},{4,0},{8,4},{12,8},{1,13},{5,1},{9,5},{13,9},{2,14},{6,2},{... | collective-permute-start | bytes 688136 | tf_op jit(solution)/shard_map/ppermute | solution.py:378
  21.1 1.6 %collective-permute-start.5 = (bf16[4,224,128]{2,1,0:T(8,128)(2,1)S(1)}, bf16[4,224,128]{2,1,0:T(8,128)(2,1)S(1)}, u32[]{:S(2)}, u32[]{:S(2)}) collective-permute-start(bf16[4,224,128]{2,1,0:T(8,128)(2,1)S(1)} %get-tuple-element.50.k0), channel_id=1, source_target_pairs={{0,8},{4,12},{8,0},{12,4},{1,9},{5,13},{9,1},{13,5},{2,10},{6,14},... | collective-permute-start | bytes 688136 | tf_op jit(solution)/shard_map/ppermute | solution.py:378
  22.6 0.7 copy-done.3
  23.3 0.0 copy-done.4
  23.3 0.1 concatenate.6.facts
  23.4 2.7 %collective-permute-done.4.k1 = bf16[4,224,128]{2,1,0:T(8,128)(2,1)S(1)} collective-permute-done((bf16[4,224,128]{2,1,0:T(8,128)(2,1)S(1)}, bf16[4,224,128]{2,1,0:T(8,128)(2,1)S(1)}, u32[]{:S(2)}, u32[]{:S(2)}) %collective-permute-start.4) | collective-permute-done | bytes 229408 | tf_op jit(solution)/shard_map/ppermute | solution.py:378
  26.1 1.4 %collective-permute-start.9 = (bf16[4,224,128]{2,1,0:T(8,128)(2,1)S(1)}, bf16[4,224,128]{2,1,0:T(8,128)(2,1)S(1)}, u32[]{:S(2)}, u32[]{:S(2)}) collective-permute-start(bf16[4,224,128]{2,1,0:T(8,128)(2,1)S(1)} %get-tuple-element.54.v0), channel_id=1, source_target_pairs={{0,12},{4,0},{8,4},{12,8},{1,13},{5,1},{9,5},{13,9},{2,14},{6,2},{... | collective-permute-start | bytes 688136 | tf_op jit(solution)/shard_map/ppermute | solution.py:378
  27.5 0.1 collective-permute-start.7
  27.5 4.6 %collective-permute-done.5.k2 = bf16[4,224,128]{2,1,0:T(8,128)(2,1)S(1)} collective-permute-done((bf16[4,224,128]{2,1,0:T(8,128)(2,1)S(1)}, bf16[4,224,128]{2,1,0:T(8,128)(2,1)S(1)}, u32[]{:S(2)}, u32[]{:S(2)}) %collective-permute-start.5) | collective-permute-done | bytes 229408 | tf_op jit(solution)/shard_map/ppermute | solution.py:378
  32.1 4.8 %shard_map.104 = (f32[2,1,896]{2,1,0:T(1,128)S(1)}, bf16[4,224,128]{2,1,0:T(8,128)(2,1)S(1)}, bf16[4,224,128]{2,1,0:T(8,128)(2,1)S(1)}, bf16[4,224,128]{2,1,0:T(8,128)(2,1)S(1)}, bf16[4,224,128]{2,1,0:T(8,128)(2,1)S(1)}) custom-call(s32[27]{0:T(128)S(1)} %concatenate.6.facts, bf16[224,1024]{1,0:T(8,128)(2,1)S(1)} %get-tuple-element.44.q_ref, ...), custom_call_target="tpu_custom_call" | custom-call | flops 3000000000 | bytes 4000000 | tf_op jit(solution)/shard_map/pallas_call | solution.py:211
  36.9 2.4 %collective-permute-start.8 = (bf16[4,224,128]{2,1,0:T(8,128)(2,1)S(1)}, bf16[4,224,128]{2,1,0:T(8,128)(2,1)S(1)}, u32[]{:S(2)}, u32[]{:S(2)}) collective-permute-start(bf16[4,224,128]{2,1,0:T(8,128)(2,1)S(1)} %get-tuple-element.54.v0), channel_id=1, source_target_pairs={{0,8},{4,12},{8,0},{12,4},{1,9},{5,13},{9,1},{13,5},{2,10},{6,14},... | collective-permute-start | bytes 688136 | tf_op jit(solution)/shard_map/ppermute | solution.py:378
  39.3 0.2 collective-permute-start.10
  39.5 3.4 %collective-permute-start.11 = (bf16[4,224,128]{2,1,0:T(8,128)(2,1)S(1)}, bf16[4,224,128]{2,1,0:T(8,128)(2,1)S(1)}, u32[]{:S(2)}, u32[]{:S(2)}) collective-permute-start(bf16[4,224,128]{2,1,0:T(8,128)(2,1)S(1)} %get-tuple-element.62), channel_id=1, source_target_pairs={{0,8},{4,12},{8,0},{12,4},{1,9},{5,13},{9,1},{13,5},{2,10},{6,14},... | collective-permute-start | bytes 688136 | tf_op jit(solution)/shard_map/ppermute | solution.py:378
  42.9 0.0 collective-permute-start.12
  42.9 0.5 collective-permute-done.8.v2
  43.4 7.1 %shard_map.105 = (bf16[224,1024]{1,0:T(8,128)(2,1)}, bf16[4,224,128]{2,1,0:T(8,128)(2,1)S(1)}, bf16[4,224,128]{2,1,0:T(8,128)(2,1)S(1)}, bf16[4,224,128]{2,1,0:T(8,128)(2,1)S(1)}, bf16[4,224,128]{2,1,0:T(8,128)(2,1)S(1)}) custom-call(s32[27]{0:T(128)S(1)} %concatenate.6.facts, bf16[224,1024]{1,0:T(8,128)(2,1)S(1)} %get-tuple-element.44.q_ref, ...), custom_call_target="tpu_custom_call" | custom-call | flops 5000000000 | bytes 5000000 | tf_op jit(solution)/shard_map/pallas_call | solution.py:230
  50.5 1.0 collective-permute-done.11
  51.5 1.7 %collective-permute-done.12 = bf16[4,224,128]{2,1,0:T(8,128)(2,1)S(1)} collective-permute-done((bf16[4,224,128]{2,1,0:T(8,128)(2,1)S(1)}, bf16[4,224,128]{2,1,0:T(8,128)(2,1)S(1)}, u32[]{:S(2)}, u32[]{:S(2)}) %collective-permute-start.12) | collective-permute-done | bytes 229408 | tf_op jit(solution)/shard_map/ppermute | solution.py:378
  53.2 5.0 %collective-permute-start.13 = (bf16[4,224,128]{2,1,0:T(8,128)(2,1)S(1)}, bf16[4,224,128]{2,1,0:T(8,128)(2,1)S(1)}, u32[]{:S(2)}, u32[]{:S(2)}) collective-permute-start(bf16[4,224,128]{2,1,0:T(8,128)(2,1)S(1)} %get-tuple-element.65), channel_id=1, source_target_pairs={{0,4},{4,8},{8,12},{12,0},{1,5},{5,9},{9,13},{13,1},{2,6},{6,10},{... | collective-permute-start | bytes 688136 | tf_op jit(solution)/shard_map/ppermute | solution.py:378
  58.2 2.4 %collective-permute-start.15 = (bf16[4,224,128]{2,1,0:T(8,128)(2,1)S(1)}, bf16[4,224,128]{2,1,0:T(8,128)(2,1)S(1)}, u32[]{:S(2)}, u32[]{:S(2)}) collective-permute-start(bf16[4,224,128]{2,1,0:T(8,128)(2,1)S(1)} %get-tuple-element.67), channel_id=1, source_target_pairs={{0,12},{4,0},{8,4},{12,8},{1,13},{5,1},{9,5},{13,9},{2,14},{6,2},{... | collective-permute-start | bytes 688136 | tf_op jit(solution)/shard_map/ppermute | solution.py:378
  60.6 0.1 fusion.8
  60.7 0.7 collective-permute-start.21
  61.4 2.2 %collective-permute-start.20 = (bf16[224,128]{1,0:T(8,128)(2,1)S(1)}, bf16[224,128]{1,0:T(8,128)(2,1)S(1)}, u32[]{:S(2)}, u32[]{:S(2)}) collective-permute-start(bf16[224,128]{1,0:T(8,128)(2,1)S(1)} %get-tuple-element.83), channel_id=1, source_target_pairs={{0,32},{16,48},{32,0},{48,16},{1,33},{17,49},{33,1},{49,17},{2,34}... | collective-permute-start | bytes 172040 | tf_op jit(solution)/shard_map/ppermute | solution.py:378
  63.6 2.5 %collective-permute-done.14 = bf16[4,224,128]{2,1,0:T(8,128)(2,1)S(1)} collective-permute-done((bf16[4,224,128]{2,1,0:T(8,128)(2,1)S(1)}, bf16[4,224,128]{2,1,0:T(8,128)(2,1)S(1)}, u32[]{:S(2)}, u32[]{:S(2)}) %collective-permute-start.14) | collective-permute-done | bytes 229408 | tf_op jit(solution)/shard_map/ppermute | solution.py:378
  66.1 6.8 %collective-permute-start.23 = (bf16[224,2048]{1,0:T(8,128)(2,1)S(1)}, bf16[224,2048]{1,0:T(8,128)(2,1)S(1)}, u32[]{:S(2)}, u32[]{:S(2)}) collective-permute-start(bf16[224,2048]{1,0:T(8,128)(2,1)S(1)} %collective-permute-done.22.hid1), channel_id=1, source_target_pairs={{0,64},{64,0},{1,65},{65,1},{2,66},{66,2},{3,67},{67,3},{4,68},{68... | collective-permute-start | bytes 2752520 | tf_op jit(solution)/shard_map/ppermute | solution.py:407
  73.0 0.1 fusion.5
  73.1 2.7 %collective-permute-start.18 = (bf16[224,128]{1,0:T(8,128)(2,1)S(1)}, bf16[224,128]{1,0:T(8,128)(2,1)S(1)}, u32[]{:S(2)}, u32[]{:S(2)}) collective-permute-start(bf16[224,128]{1,0:T(8,128)(2,1)S(1)} %get-tuple-element.86), channel_id=1, source_target_pairs={{0,48},{16,0},{32,16},{48,32},{1,49},{17,1},{33,17},{49,33},{2,50}... | collective-permute-start | bytes 172040 | tf_op jit(solution)/shard_map/ppermute | solution.py:378
  75.8 0.8 collective-permute-start.17
  76.7 1.7 %collective-permute-done.18.refs_3_ = bf16[224,128]{1,0:T(8,128)(2,1)S(1)} collective-permute-done((bf16[224,128]{1,0:T(8,128)(2,1)S(1)}, bf16[224,128]{1,0:T(8,128)(2,1)S(1)}, u32[]{:S(2)}, u32[]{:S(2)}) %collective-permute-start.18) | collective-permute-done | bytes 57376 | tf_op jit(solution)/shard_map/ppermute | solution.py:378
  78.4 3.7 %collective-permute-done.17.refs_2_ = bf16[224,128]{1,0:T(8,128)(2,1)S(1)} collective-permute-done((bf16[224,128]{1,0:T(8,128)(2,1)S(1)}, bf16[224,128]{1,0:T(8,128)(2,1)S(1)}, u32[]{:S(2)}, u32[]{:S(2)}) %collective-permute-start.17) | collective-permute-done | bytes 57376 | tf_op jit(solution)/shard_map/ppermute | solution.py:378
  82.1 1.3 shard_map.106
  83.4 3.0 %collective-permute-done.24 = bf16[224,128]{1,0:T(8,128)(2,1)S(1)} collective-permute-done((bf16[224,128]{1,0:T(8,128)(2,1)S(1)}, bf16[224,128]{1,0:T(8,128)(2,1)S(1)}, u32[]{:S(2)}, u32[]{:S(2)}) %collective-permute-start.24) | collective-permute-done | bytes 57376 | tf_op jit(solution)/shard_map/ppermute | solution.py:408
  86.5 4.2 %collective-permute-start.25 = (bf16[2,224,128]{2,1,0:T(8,128)(2,1)S(1)}, bf16[2,224,128]{2,1,0:T(8,128)(2,1)S(1)}, u32[]{:S(2)}, u32[]{:S(2)}) collective-permute-start(bf16[2,224,128]{2,1,0:T(8,128)(2,1)S(1)} %get-tuple-element.94), channel_id=1, source_target_pairs={{2,66},{3,67},{64,0},{65,1},{6,70},{7,71},{68,4},{69,5},{10,74},{1... | collective-permute-start | bytes 344072 | tf_op jit(solution)/shard_map/ppermute | solution.py:412
  90.7 0.9 collective-permute-done.25
  91.6 0.7 collective-permute-start.28
  92.3 1.3 collective-permute-start.27
  93.6 1.3 collective-permute-start.26
  94.9 6.3 %collective-permute-done.27.row2 = bf16[896,128]{1,0:T(8,128)(2,1)S(1)} collective-permute-done((bf16[896,128]{1,0:T(8,128)(2,1)S(1)}, bf16[896,128]{1,0:T(8,128)(2,1)S(1)}, u32[]{:S(2)}, u32[]{:S(2)}) %collective-permute-start.27) | collective-permute-done | bytes 229408 | tf_op jit(solution)/shard_map/ppermute | solution.py:419
  101.2 2.5 %collective-permute-done.26.row1 = bf16[896,128]{1,0:T(8,128)(2,1)S(1)} collective-permute-done((bf16[896,128]{1,0:T(8,128)(2,1)S(1)}, bf16[896,128]{1,0:T(8,128)(2,1)S(1)}, u32[]{:S(2)}, u32[]{:S(2)}) %collective-permute-start.26) | collective-permute-done | bytes 229408 | tf_op jit(solution)/shard_map/ppermute | solution.py:419
  103.8 2.6 %shard_map.107 = (bf16[2,2,16,2048]{3,2,1,0:T(8,128)(2,1)S(1)}, bf16[2,2,16,2048]{3,2,1,0:T(8,128)(2,1)S(1)}, bf16[2,2,16,2048]{3,2,1,0:T(8,128)(2,1)S(1)}, bf16[2,2,16,2048]{3,2,1,0:T(8,128)(2,1)S(1)}) custom-call(s32[27]{0:T(128)S(1)} %concatenate.6.facts, bf16[224,2048]{1,0:T(8,128)(2,1)S(1)} %bitcast.52, ...), custom_call_target="tpu_custom_call" | custom-call | flops 1000000000 | bytes 4000000 | tf_op jit(solution)/shard_map/pallas_call | solution.py:355
  106.3 0.1 collective-permute-start.29
  106.4 2.0 %collective-permute-start.30 = (bf16[2,2,16,2048]{3,2,1,0:T(8,128)(2,1)S(1)}, bf16[2,2,16,2048]{3,2,1,0:T(8,128)(2,1)S(1)}, u32[]{:S(2)}, u32[]{:S(2)}) collective-permute-start(bf16[2,2,16,2048]{3,2,1,0:T(8,128)(2,1)S(1)} %get-tuple-element.78), channel_id=1, source_target_pairs={{0,8},{4,12},{8,0},{12,4},{1,9},{5,13},{9,1},{13,5},{2,10},{6,14},... | collective-permute-start | bytes 786440 | tf_op jit(solution)/shard_map/ppermute | solution.py:378
  108.5 0.9 collective-permute-start.31
  109.4 12.2 %collective-permute-done.29 = bf16[2,2,16,2048]{3,2,1,0:T(8,128)(2,1)S(1)} collective-permute-done((bf16[2,2,16,2048]{3,2,1,0:T(8,128)(2,1)S(1)}, bf16[2,2,16,2048]{3,2,1,0:T(8,128)(2,1)S(1)}, u32[]{:S(2)}, u32[]{:S(2)}) %collective-permute-start.29) | collective-permute-done | bytes 262176 | tf_op jit(solution)/shard_map/ppermute | solution.py:378
  121.5 0.4 collective-permute-done.31
  121.9 0.1 fusion.10
  122.1 1.1 collective-permute-start.32
  123.2 1.4 %collective-permute-start.34 = (bf16[16,2048]{1,0:T(8,128)(2,1)S(1)}, bf16[16,2048]{1,0:T(8,128)(2,1)S(1)}, u32[]{:S(2)}, u32[]{:S(2)}) collective-permute-start(bf16[16,2048]{1,0:T(8,128)(2,1)S(1)} %get-tuple-element.91), channel_id=1, source_target_pairs={{0,160},{128,32},{32,128},{160,0},{16,176},{144,48},{48,144},{176,... | collective-permute-start | bytes 196616 | tf_op jit(solution)/shard_map/ppermute | solution.py:428
  124.6 3.3 %collective-permute-start.33 = (bf16[16,2048]{1,0:T(8,128)(2,1)S(1)}, bf16[16,2048]{1,0:T(8,128)(2,1)S(1)}, u32[]{:S(2)}, u32[]{:S(2)}) collective-permute-start(bf16[16,2048]{1,0:T(8,128)(2,1)S(1)} %get-tuple-element.92), channel_id=1, source_target_pairs={{0,128},{128,0},{1,129},{129,1},{2,130},{130,2},{3,131},{131,3},{4... | collective-permute-start | bytes 196616 | tf_op jit(solution)/shard_map/ppermute | solution.py:427
  127.9 0.9 collective-permute-done.34
  128.7 2.9 %collective-permute-done.33 = bf16[16,2048]{1,0:T(8,128)(2,1)S(1)} collective-permute-done((bf16[16,2048]{1,0:T(8,128)(2,1)S(1)}, bf16[16,2048]{1,0:T(8,128)(2,1)S(1)}, u32[]{:S(2)}, u32[]{:S(2)}) %collective-permute-start.33) | collective-permute-done | bytes 65568 | tf_op jit(solution)/shard_map/ppermute | solution.py:427
  131.6 0.7 fusion.2
  (31 shorter events, 0.1 us)
Async XLA Ops:
  0.6 17.5 %collective-permute-start.3 = (bf16[224,2048]{1,0:T(8,128)(2,1)}, bf16[224,2048]{1,0:T(8,128)(2,1)S(1)}, u32[]{:S(2)}, u32[]{:S(2)}) collective-permute-start(bf16[224,2048]{1,0:T(8,128)(2,1)} %bitcast.50), channel_id=1, source_target_pairs={{0,64},{64,0},{1,65},{65,1},{2,66},{66,2},{3,67},{67,3},{4,68},{68... | collective-permute-start | bytes 2752520 | tf_op jit(solution)/shard_map/ppermute | solution.py:384
  4.8 5.3 %collective-permute-start.2 = (bf16[224,256]{1,0:T(8,128)(2,1)S(1)}, bf16[224,256]{1,0:T(8,128)(2,1)S(1)}, u32[]{:S(2)}, u32[]{:S(2)}) collective-permute-start(bf16[224,256]{1,0:T(8,128)(2,1)S(1)} %pad_maximum_fusion.1.c0), channel_id=1, source_target_pairs={{0,48},{16,0},{32,16},{48,32},{1,49},{17,1},{33,17},{49,33},{2,50}... | collective-permute-start | bytes 344072 | tf_op jit(solution)/shard_map/ppermute | solution.py:378
  7.5 10.6 %collective-permute-start.1 = (bf16[224,256]{1,0:T(8,128)(2,1)S(1)}, bf16[224,256]{1,0:T(8,128)(2,1)S(1)}, u32[]{:S(2)}, u32[]{:S(2)}) collective-permute-start(bf16[224,256]{1,0:T(8,128)(2,1)S(1)} %pad_maximum_fusion.1.c0), channel_id=1, source_target_pairs={{0,32},{16,48},{32,0},{48,16},{1,33},{17,49},{33,1},{49,17},{2,34}... | collective-permute-start | bytes 344072 | tf_op jit(solution)/shard_map/ppermute | solution.py:378
  7.5 10.6 %collective-permute-start = (bf16[224,256]{1,0:T(8,128)(2,1)S(1)}, bf16[224,256]{1,0:T(8,128)(2,1)S(1)}, u32[]{:S(2)}, u32[]{:S(2)}) collective-permute-start(bf16[224,256]{1,0:T(8,128)(2,1)S(1)} %pad_maximum_fusion.1.c0), channel_id=1, source_target_pairs={{0,16},{16,32},{32,48},{48,0},{1,17},{17,33},{33,49},{49,1},{2,18}... | collective-permute-start | bytes 344072 | tf_op jit(solution)/shard_map/ppermute | solution.py:378
  7.9 1.0 copy-start.1
  8.9 1.0 copy-start.2
  18.2 7.9 %collective-permute-start.4 = (bf16[4,224,128]{2,1,0:T(8,128)(2,1)S(1)}, bf16[4,224,128]{2,1,0:T(8,128)(2,1)S(1)}, u32[]{:S(2)}, u32[]{:S(2)}) collective-permute-start(bf16[4,224,128]{2,1,0:T(8,128)(2,1)S(1)} %get-tuple-element.50.k0), channel_id=1, source_target_pairs={{0,4},{4,8},{8,12},{12,0},{1,5},{5,9},{9,13},{13,1},{2,6},{6,10},{... | collective-permute-start | bytes 688136 | tf_op jit(solution)/shard_map/ppermute | solution.py:378
  19.6 8.0 %collective-permute-start.6 = (bf16[4,224,128]{2,1,0:T(8,128)(2,1)S(1)}, bf16[4,224,128]{2,1,0:T(8,128)(2,1)S(1)}, u32[]{:S(2)}, u32[]{:S(2)}) collective-permute-start(bf16[4,224,128]{2,1,0:T(8,128)(2,1)S(1)} %get-tuple-element.50.k0), channel_id=1, source_target_pairs={{0,12},{4,0},{8,4},{12,8},{1,13},{5,1},{9,5},{13,9},{2,14},{6,2},{... | collective-permute-start | bytes 688136 | tf_op jit(solution)/shard_map/ppermute | solution.py:378
  21.1 11.0 %collective-permute-start.5 = (bf16[4,224,128]{2,1,0:T(8,128)(2,1)S(1)}, bf16[4,224,128]{2,1,0:T(8,128)(2,1)S(1)}, u32[]{:S(2)}, u32[]{:S(2)}) collective-permute-start(bf16[4,224,128]{2,1,0:T(8,128)(2,1)S(1)} %get-tuple-element.50.k0), channel_id=1, source_target_pairs={{0,8},{4,12},{8,0},{12,4},{1,9},{5,13},{9,1},{13,5},{2,10},{6,14},... | collective-permute-start | bytes 688136 | tf_op jit(solution)/shard_map/ppermute | solution.py:378
  22.6 0.7 copy-start.3
  22.6 0.7 copy-start.4
  26.1 13.3 %copy-start = (bf16[1,224,2048]{2,1,0:T(8,128)(2,1)S(1)}, bf16[1,224,2048]{2,1,0:T(8,128)(2,1)}, u32[]{:S(2)}) copy-start(bf16[1,224,2048]{2,1,0:T(8,128)(2,1)} %param.7) | copy-start | bytes 2752516
  26.1 13.4 %collective-permute-start.9 = (bf16[4,224,128]{2,1,0:T(8,128)(2,1)S(1)}, bf16[4,224,128]{2,1,0:T(8,128)(2,1)S(1)}, u32[]{:S(2)}, u32[]{:S(2)}) collective-permute-start(bf16[4,224,128]{2,1,0:T(8,128)(2,1)S(1)} %get-tuple-element.54.v0), channel_id=1, source_target_pairs={{0,12},{4,0},{8,4},{12,8},{1,13},{5,1},{9,5},{13,9},{2,14},{6,2},{... | collective-permute-start | bytes 688136 | tf_op jit(solution)/shard_map/ppermute | solution.py:378
  27.5 15.4 %collective-permute-start.7 = (bf16[4,224,128]{2,1,0:T(8,128)(2,1)S(1)}, bf16[4,224,128]{2,1,0:T(8,128)(2,1)S(1)}, u32[]{:S(2)}, u32[]{:S(2)}) collective-permute-start(bf16[4,224,128]{2,1,0:T(8,128)(2,1)S(1)} %get-tuple-element.54.v0), channel_id=1, source_target_pairs={{0,4},{4,8},{8,12},{12,0},{1,5},{5,9},{9,13},{13,1},{2,6},{6,10},{... | collective-permute-start | bytes 688136 | tf_op jit(solution)/shard_map/ppermute | solution.py:378
  36.9 6.5 %collective-permute-start.8 = (bf16[4,224,128]{2,1,0:T(8,128)(2,1)S(1)}, bf16[4,224,128]{2,1,0:T(8,128)(2,1)S(1)}, u32[]{:S(2)}, u32[]{:S(2)}) collective-permute-start(bf16[4,224,128]{2,1,0:T(8,128)(2,1)S(1)} %get-tuple-element.54.v0), channel_id=1, source_target_pairs={{0,8},{4,12},{8,0},{12,4},{1,9},{5,13},{9,1},{13,5},{2,10},{6,14},... | collective-permute-start | bytes 688136 | tf_op jit(solution)/shard_map/ppermute | solution.py:378
  39.3 26.8 %collective-permute-start.22 = (bf16[224,2048]{1,0:T(8,128)(2,1)S(1)}, bf16[224,2048]{1,0:T(8,128)(2,1)S(1)}, u32[]{:S(2)}, u32[]{:S(2)}) collective-permute-start(bf16[224,2048]{1,0:T(8,128)(2,1)S(1)} %bitcast.51), channel_id=1, source_target_pairs={{0,16},{16,0},{32,48},{48,32},{1,17},{17,1},{33,49},{49,33},{2,18}... | collective-permute-start | bytes 2752520 | tf_op jit(solution)/shard_map/ppermute | solution.py:389
  39.3 11.2 %collective-permute-start.10 = (bf16[4,224,128]{2,1,0:T(8,128)(2,1)S(1)}, bf16[4,224,128]{2,1,0:T(8,128)(2,1)S(1)}, u32[]{:S(2)}, u32[]{:S(2)}) collective-permute-start(bf16[4,224,128]{2,1,0:T(8,128)(2,1)S(1)} %get-tuple-element.61), channel_id=1, source_target_pairs={{0,4},{4,8},{8,12},{12,0},{1,5},{5,9},{9,13},{13,1},{2,6},{6,10},{... | collective-permute-start | bytes 688136 | tf_op jit(solution)/shard_map/ppermute | solution.py:378
  39.5 12.0 %collective-permute-start.11 = (bf16[4,224,128]{2,1,0:T(8,128)(2,1)S(1)}, bf16[4,224,128]{2,1,0:T(8,128)(2,1)S(1)}, u32[]{:S(2)}, u32[]{:S(2)}) collective-permute-start(bf16[4,224,128]{2,1,0:T(8,128)(2,1)S(1)} %get-tuple-element.62), channel_id=1, source_target_pairs={{0,8},{4,12},{8,0},{12,4},{1,9},{5,13},{9,1},{13,5},{2,10},{6,14},... | collective-permute-start | bytes 688136 | tf_op jit(solution)/shard_map/ppermute | solution.py:378
  42.9 10.3 %collective-permute-start.12 = (bf16[4,224,128]{2,1,0:T(8,128)(2,1)S(1)}, bf16[4,224,128]{2,1,0:T(8,128)(2,1)S(1)}, u32[]{:S(2)}, u32[]{:S(2)}) collective-permute-start(bf16[4,224,128]{2,1,0:T(8,128)(2,1)S(1)} %get-tuple-element.63), channel_id=1, source_target_pairs={{0,12},{4,0},{8,4},{12,8},{1,13},{5,1},{9,5},{13,9},{2,14},{6,2},{... | collective-permute-start | bytes 688136 | tf_op jit(solution)/shard_map/ppermute | solution.py:378
  53.2 8.2 %collective-permute-start.13 = (bf16[4,224,128]{2,1,0:T(8,128)(2,1)S(1)}, bf16[4,224,128]{2,1,0:T(8,128)(2,1)S(1)}, u32[]{:S(2)}, u32[]{:S(2)}) collective-permute-start(bf16[4,224,128]{2,1,0:T(8,128)(2,1)S(1)} %get-tuple-element.65), channel_id=1, source_target_pairs={{0,4},{4,8},{8,12},{12,0},{1,5},{5,9},{9,13},{13,1},{2,6},{6,10},{... | collective-permute-start | bytes 688136 | tf_op jit(solution)/shard_map/ppermute | solution.py:378
  58.2 7.9 %collective-permute-start.14 = (bf16[4,224,128]{2,1,0:T(8,128)(2,1)S(1)}, bf16[4,224,128]{2,1,0:T(8,128)(2,1)S(1)}, u32[]{:S(2)}, u32[]{:S(2)}) collective-permute-start(bf16[4,224,128]{2,1,0:T(8,128)(2,1)S(1)} %get-tuple-element.66), channel_id=1, source_target_pairs={{0,8},{4,12},{8,0},{12,4},{1,9},{5,13},{9,1},{13,5},{2,10},{6,14},... | collective-permute-start | bytes 688136 | tf_op jit(solution)/shard_map/ppermute | solution.py:378
  58.2 7.9 %collective-permute-start.15 = (bf16[4,224,128]{2,1,0:T(8,128)(2,1)S(1)}, bf16[4,224,128]{2,1,0:T(8,128)(2,1)S(1)}, u32[]{:S(2)}, u32[]{:S(2)}) collective-permute-start(bf16[4,224,128]{2,1,0:T(8,128)(2,1)S(1)} %get-tuple-element.67), channel_id=1, source_target_pairs={{0,12},{4,0},{8,4},{12,8},{1,13},{5,1},{9,5},{13,9},{2,14},{6,2},{... | collective-permute-start | bytes 688136 | tf_op jit(solution)/shard_map/ppermute | solution.py:378
  60.7 15.1 %collective-permute-start.21 = (bf16[224,128]{1,0:T(8,128)(2,1)S(1)}, bf16[224,128]{1,0:T(8,128)(2,1)S(1)}, u32[]{:S(2)}, u32[]{:S(2)}) collective-permute-start(bf16[224,128]{1,0:T(8,128)(2,1)S(1)} %get-tuple-element.82), channel_id=1, source_target_pairs={{0,48},{16,0},{32,16},{48,32},{1,49},{17,1},{33,17},{49,33},{2,50}... | collective-permute-start | bytes 172040 | tf_op jit(solution)/shard_map/ppermute | solution.py:378
  61.4 15.2 %collective-permute-start.20 = (bf16[224,128]{1,0:T(8,128)(2,1)S(1)}, bf16[224,128]{1,0:T(8,128)(2,1)S(1)}, u32[]{:S(2)}, u32[]{:S(2)}) collective-permute-start(bf16[224,128]{1,0:T(8,128)(2,1)S(1)} %get-tuple-element.83), channel_id=1, source_target_pairs={{0,32},{16,48},{32,0},{48,16},{1,33},{17,49},{33,1},{49,17},{2,34}... | collective-permute-start | bytes 172040 | tf_op jit(solution)/shard_map/ppermute | solution.py:378
  66.1 10.6 %collective-permute-start.19 = (bf16[224,128]{1,0:T(8,128)(2,1)S(1)}, bf16[224,128]{1,0:T(8,128)(2,1)S(1)}, u32[]{:S(2)}, u32[]{:S(2)}) collective-permute-start(bf16[224,128]{1,0:T(8,128)(2,1)S(1)} %get-tuple-element.84), channel_id=1, source_target_pairs={{0,16},{16,32},{32,48},{48,0},{1,17},{17,33},{33,49},{49,1},{2,18}... | collective-permute-start | bytes 172040 | tf_op jit(solution)/shard_map/ppermute | solution.py:378
  66.1 37.7 %collective-permute-start.23 = (bf16[224,2048]{1,0:T(8,128)(2,1)S(1)}, bf16[224,2048]{1,0:T(8,128)(2,1)S(1)}, u32[]{:S(2)}, u32[]{:S(2)}) collective-permute-start(bf16[224,2048]{1,0:T(8,128)(2,1)S(1)} %collective-permute-done.22.hid1), channel_id=1, source_target_pairs={{0,64},{64,0},{1,65},{65,1},{2,66},{66,2},{3,67},{67,3},{4,68},{68... | collective-permute-start | bytes 2752520 | tf_op jit(solution)/shard_map/ppermute | solution.py:407
  73.1 5.3 %collective-permute-start.18 = (bf16[224,128]{1,0:T(8,128)(2,1)S(1)}, bf16[224,128]{1,0:T(8,128)(2,1)S(1)}, u32[]{:S(2)}, u32[]{:S(2)}) collective-permute-start(bf16[224,128]{1,0:T(8,128)(2,1)S(1)} %get-tuple-element.86), channel_id=1, source_target_pairs={{0,48},{16,0},{32,16},{48,32},{1,49},{17,1},{33,17},{49,33},{2,50}... | collective-permute-start | bytes 172040 | tf_op jit(solution)/shard_map/ppermute | solution.py:378
  75.8 6.3 %collective-permute-start.17 = (bf16[224,128]{1,0:T(8,128)(2,1)S(1)}, bf16[224,128]{1,0:T(8,128)(2,1)S(1)}, u32[]{:S(2)}, u32[]{:S(2)}) collective-permute-start(bf16[224,128]{1,0:T(8,128)(2,1)S(1)} %get-tuple-element.87), channel_id=1, source_target_pairs={{0,32},{16,48},{32,0},{48,16},{1,33},{17,49},{33,1},{49,17},{2,34}... | collective-permute-start | bytes 172040 | tf_op jit(solution)/shard_map/ppermute | solution.py:378
  76.7 5.4 %collective-permute-start.16 = (bf16[224,128]{1,0:T(8,128)(2,1)S(1)}, bf16[224,128]{1,0:T(8,128)(2,1)S(1)}, u32[]{:S(2)}, u32[]{:S(2)}) collective-permute-start(bf16[224,128]{1,0:T(8,128)(2,1)S(1)} %get-tuple-element.88), channel_id=1, source_target_pairs={{0,16},{16,32},{32,48},{48,0},{1,17},{17,33},{33,49},{49,1},{2,18}... | collective-permute-start | bytes 172040 | tf_op jit(solution)/shard_map/ppermute | solution.py:378
  83.4 3.0 %collective-permute-start.24 = (bf16[224,128]{1,0:T(8,128)(2,1)S(1)}, bf16[224,128]{1,0:T(8,128)(2,1)S(1)}, u32[]{:S(2)}, u32[]{:S(2)}) collective-permute-start(bf16[224,128]{1,0:T(8,128)(2,1)S(1)} %get-tuple-element.75), channel_id=1, source_target_pairs={{0,16},{16,0},{32,48},{48,32},{1,17},{17,1},{33,49},{49,33},{2,18}... | collective-permute-start | bytes 172040 | tf_op jit(solution)/shard_map/ppermute | solution.py:408
  86.5 5.2 %collective-permute-start.25 = (bf16[2,224,128]{2,1,0:T(8,128)(2,1)S(1)}, bf16[2,224,128]{2,1,0:T(8,128)(2,1)S(1)}, u32[]{:S(2)}, u32[]{:S(2)}) collective-permute-start(bf16[2,224,128]{2,1,0:T(8,128)(2,1)S(1)} %get-tuple-element.94), channel_id=1, source_target_pairs={{2,66},{3,67},{64,0},{65,1},{6,70},{7,71},{68,4},{69,5},{10,74},{1... | collective-permute-start | bytes 344072 | tf_op jit(solution)/shard_map/ppermute | solution.py:412
  91.6 3.3 %collective-permute-start.28 = (bf16[896,128]{1,0:T(8,128)(2,1)S(1)}, bf16[896,128]{1,0:T(8,128)(2,1)S(1)}, u32[]{:S(2)}, u32[]{:S(2)}) collective-permute-start(bf16[896,128]{1,0:T(8,128)(2,1)S(1)} %bitcast.53), channel_id=1, source_target_pairs={{0,3},{1,0},{66,65},{67,66},{4,7},{5,4},{70,69},{71,70},{8,11},{9,... | collective-permute-start | bytes 688136 | tf_op jit(solution)/shard_map/ppermute | solution.py:419
  92.3 8.9 %collective-permute-start.27 = (bf16[896,128]{1,0:T(8,128)(2,1)S(1)}, bf16[896,128]{1,0:T(8,128)(2,1)S(1)}, u32[]{:S(2)}, u32[]{:S(2)}) collective-permute-start(bf16[896,128]{1,0:T(8,128)(2,1)S(1)} %bitcast.54), channel_id=1, source_target_pairs={{0,2},{1,3},{66,64},{67,65},{4,6},{5,7},{70,68},{71,69},{8,10},{9,... | collective-permute-start | bytes 688136 | tf_op jit(solution)/shard_map/ppermute | solution.py:419
  93.6 10.2 %collective-permute-start.26 = (bf16[896,128]{1,0:T(8,128)(2,1)S(1)}, bf16[896,128]{1,0:T(8,128)(2,1)S(1)}, u32[]{:S(2)}, u32[]{:S(2)}) collective-permute-start(bf16[896,128]{1,0:T(8,128)(2,1)S(1)} %bitcast.55), channel_id=1, source_target_pairs={{0,1},{1,2},{66,67},{67,64},{4,5},{5,6},{70,71},{71,68},{8,9},{9,1... | collective-permute-start | bytes 688136 | tf_op jit(solution)/shard_map/ppermute | solution.py:419
  106.3 15.2 %collective-permute-start.29 = (bf16[2,2,16,2048]{3,2,1,0:T(8,128)(2,1)S(1)}, bf16[2,2,16,2048]{3,2,1,0:T(8,128)(2,1)S(1)}, u32[]{:S(2)}, u32[]{:S(2)}) collective-permute-start(bf16[2,2,16,2048]{3,2,1,0:T(8,128)(2,1)S(1)} %get-tuple-element.77), channel_id=1, source_target_pairs={{0,4},{4,8},{8,12},{12,0},{1,5},{5,9},{9,13},{13,1},{2,6},{6,10},{... | collective-permute-start | bytes 786440 | tf_op jit(solution)/shard_map/ppermute | solution.py:378
  106.4 15.1 %collective-permute-start.30 = (bf16[2,2,16,2048]{3,2,1,0:T(8,128)(2,1)S(1)}, bf16[2,2,16,2048]{3,2,1,0:T(8,128)(2,1)S(1)}, u32[]{:S(2)}, u32[]{:S(2)}) collective-permute-start(bf16[2,2,16,2048]{3,2,1,0:T(8,128)(2,1)S(1)} %get-tuple-element.78), channel_id=1, source_target_pairs={{0,8},{4,12},{8,0},{12,4},{1,9},{5,13},{9,1},{13,5},{2,10},{6,14},... | collective-permute-start | bytes 786440 | tf_op jit(solution)/shard_map/ppermute | solution.py:378
  108.5 13.5 %collective-permute-start.31 = (bf16[2,2,16,2048]{3,2,1,0:T(8,128)(2,1)S(1)}, bf16[2,2,16,2048]{3,2,1,0:T(8,128)(2,1)S(1)}, u32[]{:S(2)}, u32[]{:S(2)}) collective-permute-start(bf16[2,2,16,2048]{3,2,1,0:T(8,128)(2,1)S(1)} %get-tuple-element.79), channel_id=1, source_target_pairs={{0,12},{4,0},{8,4},{12,8},{1,13},{5,1},{9,5},{13,9},{2,14},{6,2},{... | collective-permute-start | bytes 786440 | tf_op jit(solution)/shard_map/ppermute | solution.py:378
  122.1 5.7 %collective-permute-start.32 = (bf16[16,2048]{1,0:T(8,128)(2,1)S(1)}, bf16[16,2048]{1,0:T(8,128)(2,1)S(1)}, u32[]{:S(2)}, u32[]{:S(2)}) collective-permute-start(bf16[16,2048]{1,0:T(8,128)(2,1)S(1)} %get-tuple-element.90), channel_id=1, source_target_pairs={{0,32},{32,0},{16,48},{48,16},{1,33},{33,1},{17,49},{49,17},{2,34}... | collective-permute-start | bytes 196616 | tf_op jit(solution)/shard_map/ppermute | solution.py:426
  123.2 5.5 %collective-permute-start.34 = (bf16[16,2048]{1,0:T(8,128)(2,1)S(1)}, bf16[16,2048]{1,0:T(8,128)(2,1)S(1)}, u32[]{:S(2)}, u32[]{:S(2)}) collective-permute-start(bf16[16,2048]{1,0:T(8,128)(2,1)S(1)} %get-tuple-element.91), channel_id=1, source_target_pairs={{0,160},{128,32},{32,128},{160,0},{16,176},{144,48},{48,144},{176,... | collective-permute-start | bytes 196616 | tf_op jit(solution)/shard_map/ppermute | solution.py:428
  124.6 7.1 %collective-permute-start.33 = (bf16[16,2048]{1,0:T(8,128)(2,1)S(1)}, bf16[16,2048]{1,0:T(8,128)(2,1)S(1)}, u32[]{:S(2)}, u32[]{:S(2)}) collective-permute-start(bf16[16,2048]{1,0:T(8,128)(2,1)S(1)} %get-tuple-element.92), channel_id=1, source_target_pairs={{0,128},{128,0},{1,129},{129,1},{2,130},{130,2},{3,131},{131,3},{4... | collective-permute-start | bytes 196616 | tf_op jit(solution)/shard_map/ppermute | solution.py:427

commit v10 on v9

--- a/solution.py
+++ b/solution.py
@@ -386,8 +386,7 @@
     ks, vs = columns_of(pieces)
     ks = [ks] + [moved(ks, "y", s) for s in (1, 2, 3)]
     vs = after(vs, ks[1])
-    beside = lax.ppermute(after(hidden[0], ks[1]), "zl", neighbour)
-    vs = [vs] + [moved(vs, "y", s) if s != 2 else vs for s in (1, 2, 3)]
+    vs = [vs] + [moved(vs if s != 2 else after(vs, *ks[2:]), "y", s) for s in (1, 2, 3)]
 
     def received(shares):
         return [shares[0]] + [moved(shares[s], "y", s) for s in (1, 2, 3)]
@@ -398,7 +397,7 @@
 
     stats, *dvs = forward(facts, *rows_in, ks)
     dvs = received(dvs)
-    vs[2] = moved(after(vs[0], stats), "y", 2)
+    beside = lax.ppermute(after(hidden[0], stats), "zl", neighbour)
     dq, *dks = backward(facts, *rows_in, ks, vs, stats)
     dks = received(after(dks, dvs))
     key_grads, value_grads, mine, sent = finish(facts, over_zl(dks), over_zl(dvs))

time: 134 us -> 132 us (0.985)
  Pallas kernels: 15.9 us -> 13 us
  waiting for transfers between devices: 55.6 us -> 57.9 us
    ppermute x1, starting transfers between devices: 6.85 us -> 4.52 us  [per_device(): hidden = (hidden[0], beside, hidden[1], lax.ppermute(beside, 'co', swap))]
    pallas_call x1, Pallas kernels: 7.09 us -> 5.49 us  [backward(): pl.pallas_call(backward_kernel, out_shape=(jax.ShapeDtypeStruct((ROWS, HE...]
    ppermute x24, starting transfers between devices: 31.9 us -> 33.4 us  [moved(): return lax.ppermute(value, axis, ring(shift))]
    ppermute x1, waiting for transfers between devices: 2.93 us -> 4.36 us  [per_device(): lax.ppermute(total[1, 0].astype(BF), 'zh', swap)]
  transfers between devices with their start and end apart: 35 -> 35, of which waited for: 18 -> 17; matrix products, arithmetic and copies ran while one was open for 1% -> 1% of each run, Pallas kernels for 10% -> 8%
where the time goes in v10:
time: 132 us; the launch traced here: 131 us
  waiting for transfers between devices  57.9 us (44%)
  starting transfers between devices  54.8 us (42%)
  Pallas kernels  13 us (10%)
  local copies, waits for them, and re-layouts  2.81 us (2%)
  other arithmetic  1.96 us (1%)
    ppermute x24, waiting for transfers between devices, moved(): return lax.ppermute(value, axis, ring(shift))  40 us
    ppermute x24, starting transfers between devices, moved(): return lax.ppermute(value, axis, ring(shift))  33.4 us
    ppermute x3, waiting for transfers between devices, per_device(): lax.ppermute(rows, ('co', 'x'), along(j))  8.85 us
    pallas_call x1, Pallas kernels, backward(): pl.pallas_call(backward_kernel, out_shape=(jax.ShapeDtypeStruct((ROWS, HE...  5.49 us
    ppermute x1, starting transfers between devices, per_device(): hidden = (hidden[0], beside, hidden[1], lax.ppermute(beside, 'co', swap))  4.52 us
    ppermute x1, waiting for transfers between devices, per_device(): lax.ppermute(total[1, 0].astype(BF), 'zh', swap)  4.36 us
    ppermute x1, starting transfers between devices, per_device(): lax.ppermute(rows, ('co', 'x'), cross)  3.57 us
    pallas_call x1, Pallas kernels, forward(): pl.pallas_call(forward_kernel, out_shape=(jax.ShapeDtypeStruct((2, 1, LAN...  3.52 us
  transfers between devices with their start and end apart: 35, of which 17 were waited for; matrix products, arithmetic and copies ran while one was open for 1% of the time, Pallas kernels for 8%

profile of v10, /device:TPU:1, one launch (start us, length us, event | category | flops | bytes accessed | tf_op | source)
XLA Modules:
  0.0 131.3 jit_solution(8802656954837904019)
XLA Ops:
  0.6 3.3 %collective-permute-start.3 = (bf16[224,2048]{1,0:T(8,128)(2,1)}, bf16[224,2048]{1,0:T(8,128)(2,1)S(1)}, u32[]{:S(2)}, u32[]{:S(2)}) collective-permute-start(bf16[224,2048]{1,0:T(8,128)(2,1)} %bitcast.50), channel_id=1, source_target_pairs={{0,64},{64,0},{1,65},{65,1},{2,66},{66,2},{3,67},{67,3},{4,68},{68... | collective-permute-start | bytes 2752520 | tf_op jit(solution)/shard_map/ppermute | solution.py:384
  4.0 0.9 pad_maximum_fusion.1.c0
  4.8 2.7 %collective-permute-start.2 = (bf16[224,256]{1,0:T(8,128)(2,1)S(1)}, bf16[224,256]{1,0:T(8,128)(2,1)S(1)}, u32[]{:S(2)}, u32[]{:S(2)}) collective-permute-start(bf16[224,256]{1,0:T(8,128)(2,1)S(1)} %pad_maximum_fusion.1.c0), channel_id=1, source_target_pairs={{0,48},{16,0},{32,16},{48,32},{1,49},{17,1},{33,17},{49,33},{2,50}... | collective-permute-start | bytes 344072 | tf_op jit(solution)/shard_map/ppermute | solution.py:378
  7.5 0.4 collective-permute-start
  7.9 1.0 copy-done.1
  8.9 1.0 copy-done.2
  9.9 0.1 shard_map.102
  10.0 0.1 collective-permute-done.2.c3
  10.1 8.0 %collective-permute-done.1.c2 = bf16[224,256]{1,0:T(8,128)(2,1)S(1)} collective-permute-done((bf16[224,256]{1,0:T(8,128)(2,1)S(1)}, bf16[224,256]{1,0:T(8,128)(2,1)S(1)}, u32[]{:S(2)}, u32[]{:S(2)}) %collective-permute-start.1) | collective-permute-done | bytes 114720 | tf_op jit(solution)/shard_map/ppermute | solution.py:378
  18.1 0.1 shard_map.103
  18.2 1.4 %collective-permute-start.4 = (bf16[4,224,128]{2,1,0:T(8,128)(2,1)S(1)}, bf16[4,224,128]{2,1,0:T(8,128)(2,1)S(1)}, u32[]{:S(2)}, u32[]{:S(2)}) collective-permute-start(bf16[4,224,128]{2,1,0:T(8,128)(2,1)S(1)} %get-tuple-element.50.k0), channel_id=1, source_target_pairs={{0,4},{4,8},{8,12},{12,0},{1,5},{5,9},{9,13},{13,1},{2,6},{6,10},{... | collective-permute-start | bytes 688136 | tf_op jit(solution)/shard_map/ppermute | solution.py:378
  19.6 1.5 %collective-permute-start.6 = (bf16[4,224,128]{2,1,0:T(8,128)(2,1)S(1)}, bf16[4,224,128]{2,1,0:T(8,128)(2,1)S(1)}, u32[]{:S(2)}, u32[]{:S(2)}) collective-permute-start(bf16[4,224,128]{2,1,0:T(8,128)(2,1)S(1)} %get-tuple-element.50.k0), channel_id=1, source_target_pairs={{0,12},{4,0},{8,4},{12,8},{1,13},{5,1},{9,5},{13,9},{2,14},{6,2},{... | collective-permute-start | bytes 688136 | tf_op jit(solution)/shard_map/ppermute | solution.py:378
  21.1 1.6 %collective-permute-start.5 = (bf16[4,224,128]{2,1,0:T(8,128)(2,1)S(1)}, bf16[4,224,128]{2,1,0:T(8,128)(2,1)S(1)}, u32[]{:S(2)}, u32[]{:S(2)}) collective-permute-start(bf16[4,224,128]{2,1,0:T(8,128)(2,1)S(1)} %get-tuple-element.50.k0), channel_id=1, source_target_pairs={{0,8},{4,12},{8,0},{12,4},{1,9},{5,13},{9,1},{13,5},{2,10},{6,14},... | collective-permute-start | bytes 688136 | tf_op jit(solution)/shard_map/ppermute | solution.py:378
  22.6 0.7 copy-done.3
  23.3 0.0 copy-done.4
  23.3 0.1 concatenate.6.facts
  23.4 2.7 %collective-permute-done.4.k1 = bf16[4,224,128]{2,1,0:T(8,128)(2,1)S(1)} collective-permute-done((bf16[4,224,128]{2,1,0:T(8,128)(2,1)S(1)}, bf16[4,224,128]{2,1,0:T(8,128)(2,1)S(1)}, u32[]{:S(2)}, u32[]{:S(2)}) %collective-permute-start.4) | collective-permute-done | bytes 229408 | tf_op jit(solution)/shard_map/ppermute | solution.py:378
  26.1 1.4 %collective-permute-start.9 = (bf16[4,224,128]{2,1,0:T(8,128)(2,1)S(1)}, bf16[4,224,128]{2,1,0:T(8,128)(2,1)S(1)}, u32[]{:S(2)}, u32[]{:S(2)}) collective-permute-start(bf16[4,224,128]{2,1,0:T(8,128)(2,1)S(1)} %get-tuple-element.53.v0), channel_id=1, source_target_pairs={{0,12},{4,0},{8,4},{12,8},{1,13},{5,1},{9,5},{13,9},{2,14},{6,2},{... | collective-permute-start | bytes 688136 | tf_op jit(solution)/shard_map/ppermute | solution.py:378
  27.5 0.1 collective-permute-start.7
  27.5 4.6 %collective-permute-done.5.k2 = bf16[4,224,128]{2,1,0:T(8,128)(2,1)S(1)} collective-permute-done((bf16[4,224,128]{2,1,0:T(8,128)(2,1)S(1)}, bf16[4,224,128]{2,1,0:T(8,128)(2,1)S(1)}, u32[]{:S(2)}, u32[]{:S(2)}) %collective-permute-start.5) | collective-permute-done | bytes 229408 | tf_op jit(solution)/shard_map/ppermute | solution.py:378
  32.1 0.4 collective-permute-start.8
  32.5 3.5 %shard_map.104 = (f32[2,1,896]{2,1,0:T(1,128)S(1)}, bf16[4,224,128]{2,1,0:T(8,128)(2,1)S(1)}, bf16[4,224,128]{2,1,0:T(8,128)(2,1)S(1)}, bf16[4,224,128]{2,1,0:T(8,128)(2,1)S(1)}, bf16[4,224,128]{2,1,0:T(8,128)(2,1)S(1)}) custom-call(s32[27]{0:T(128)S(1)} %concatenate.6.facts, bf16[224,1024]{1,0:T(8,128)(2,1)S(1)} %get-tuple-element.44.q_ref, ...), custom_call_target="tpu_custom_call" | custom-call | flops 3000000000 | bytes 4000000 | tf_op jit(solution)/shard_map/pallas_call | solution.py:211
  36.0 1.0 collective-permute-start.22
  37.0 1.0 collective-permute-start.10
  38.0 2.8 %collective-permute-done.8.v2 = bf16[4,224,128]{2,1,0:T(8,128)(2,1)S(1)} collective-permute-done((bf16[4,224,128]{2,1,0:T(8,128)(2,1)S(1)}, bf16[4,224,128]{2,1,0:T(8,128)(2,1)S(1)}, u32[]{:S(2)}, u32[]{:S(2)}) %collective-permute-start.8) | collective-permute-done | bytes 229408 | tf_op jit(solution)/shard_map/ppermute | solution.py:378
  40.8 1.3 %collective-permute-start.11 = (bf16[4,224,128]{2,1,0:T(8,128)(2,1)S(1)}, bf16[4,224,128]{2,1,0:T(8,128)(2,1)S(1)}, u32[]{:S(2)}, u32[]{:S(2)}) collective-permute-start(bf16[4,224,128]{2,1,0:T(8,128)(2,1)S(1)} %get-tuple-element.62), channel_id=1, source_target_pairs={{0,8},{4,12},{8,0},{12,4},{1,9},{5,13},{9,1},{13,5},{2,10},{6,14},... | collective-permute-start | bytes 688136 | tf_op jit(solution)/shard_map/ppermute | solution.py:378
  42.1 2.6 %collective-permute-start.12 = (bf16[4,224,128]{2,1,0:T(8,128)(2,1)S(1)}, bf16[4,224,128]{2,1,0:T(8,128)(2,1)S(1)}, u32[]{:S(2)}, u32[]{:S(2)}) collective-permute-start(bf16[4,224,128]{2,1,0:T(8,128)(2,1)S(1)} %get-tuple-element.63), channel_id=1, source_target_pairs={{0,12},{4,0},{8,4},{12,8},{1,13},{5,1},{9,5},{13,9},{2,14},{6,2},{... | collective-permute-start | bytes 688136 | tf_op jit(solution)/shard_map/ppermute | solution.py:378
  44.7 5.5 %shard_map.105 = (bf16[224,1024]{1,0:T(8,128)(2,1)}, bf16[4,224,128]{2,1,0:T(8,128)(2,1)S(1)}, bf16[4,224,128]{2,1,0:T(8,128)(2,1)S(1)}, bf16[4,224,128]{2,1,0:T(8,128)(2,1)S(1)}, bf16[4,224,128]{2,1,0:T(8,128)(2,1)S(1)}) custom-call(s32[27]{0:T(128)S(1)} %concatenate.6.facts, bf16[224,1024]{1,0:T(8,128)(2,1)S(1)} %get-tuple-element.44.q_ref, ...), custom_call_target="tpu_custom_call" | custom-call | flops 5000000000 | bytes 5000000 | tf_op jit(solution)/shard_map/pallas_call | solution.py:230
  50.2 0.0 collective-permute-done.11
  50.2 1.8 %collective-permute-done.12 = bf16[4,224,128]{2,1,0:T(8,128)(2,1)S(1)} collective-permute-done((bf16[4,224,128]{2,1,0:T(8,128)(2,1)S(1)}, bf16[4,224,128]{2,1,0:T(8,128)(2,1)S(1)}, u32[]{:S(2)}, u32[]{:S(2)}) %collective-permute-start.12) | collective-permute-done | bytes 229408 | tf_op jit(solution)/shard_map/ppermute | solution.py:378
  52.0 2.3 %collective-permute-start.13 = (bf16[4,224,128]{2,1,0:T(8,128)(2,1)S(1)}, bf16[4,224,128]{2,1,0:T(8,128)(2,1)S(1)}, u32[]{:S(2)}, u32[]{:S(2)}) collective-permute-start(bf16[4,224,128]{2,1,0:T(8,128)(2,1)S(1)} %get-tuple-element.65), channel_id=1, source_target_pairs={{0,4},{4,8},{8,12},{12,0},{1,5},{5,9},{9,13},{13,1},{2,6},{6,10},{... | collective-permute-start | bytes 688136 | tf_op jit(solution)/shard_map/ppermute | solution.py:378
  54.3 2.4 %collective-permute-start.14 = (bf16[4,224,128]{2,1,0:T(8,128)(2,1)S(1)}, bf16[4,224,128]{2,1,0:T(8,128)(2,1)S(1)}, u32[]{:S(2)}, u32[]{:S(2)}) collective-permute-start(bf16[4,224,128]{2,1,0:T(8,128)(2,1)S(1)} %get-tuple-element.66), channel_id=1, source_target_pairs={{0,8},{4,12},{8,0},{12,4},{1,9},{5,13},{9,1},{13,5},{2,10},{6,14},... | collective-permute-start | bytes 688136 | tf_op jit(solution)/shard_map/ppermute | solution.py:378
  56.7 0.1 fusion.8
  56.8 2.7 %collective-permute-start.21 = (bf16[224,128]{1,0:T(8,128)(2,1)S(1)}, bf16[224,128]{1,0:T(8,128)(2,1)S(1)}, u32[]{:S(2)}, u32[]{:S(2)}) collective-permute-start(bf16[224,128]{1,0:T(8,128)(2,1)S(1)} %get-tuple-element.82), channel_id=1, source_target_pairs={{0,48},{16,0},{32,16},{48,32},{1,49},{17,1},{33,17},{49,33},{2,50}... | collective-permute-start | bytes 172040 | tf_op jit(solution)/shard_map/ppermute | solution.py:378
  59.6 5.0 %collective-permute-start.20 = (bf16[224,128]{1,0:T(8,128)(2,1)S(1)}, bf16[224,128]{1,0:T(8,128)(2,1)S(1)}, u32[]{:S(2)}, u32[]{:S(2)}) collective-permute-start(bf16[224,128]{1,0:T(8,128)(2,1)S(1)} %get-tuple-element.83), channel_id=1, source_target_pairs={{0,32},{16,48},{32,0},{48,16},{1,33},{17,49},{33,1},{49,17},{2,34}... | collective-permute-start | bytes 172040 | tf_op jit(solution)/shard_map/ppermute | solution.py:378
  64.6 1.1 collective-permute-done.14
  65.7 4.5 %collective-permute-start.23 = (bf16[224,2048]{1,0:T(8,128)(2,1)S(1)}, bf16[224,2048]{1,0:T(8,128)(2,1)S(1)}, u32[]{:S(2)}, u32[]{:S(2)}) collective-permute-start(bf16[224,2048]{1,0:T(8,128)(2,1)S(1)} %collective-permute-done.22.hid1), channel_id=1, source_target_pairs={{0,64},{64,0},{1,65},{65,1},{2,66},{66,2},{3,67},{67,3},{4,68},{68... | collective-permute-start | bytes 2752520 | tf_op jit(solution)/shard_map/ppermute | solution.py:406
  70.2 0.1 fusion.5
  70.3 3.5 %collective-permute-start.18 = (bf16[224,128]{1,0:T(8,128)(2,1)S(1)}, bf16[224,128]{1,0:T(8,128)(2,1)S(1)}, u32[]{:S(2)}, u32[]{:S(2)}) collective-permute-start(bf16[224,128]{1,0:T(8,128)(2,1)S(1)} %get-tuple-element.86), channel_id=1, source_target_pairs={{0,48},{16,0},{32,16},{48,32},{1,49},{17,1},{33,17},{49,33},{2,50}... | collective-permute-start | bytes 172040 | tf_op jit(solution)/shard_map/ppermute | solution.py:378
  73.8 0.4 collective-permute-start.16
  74.2 0.9 collective-permute-done.18.refs_3_
  75.1 5.4 %collective-permute-done.17.refs_2_ = bf16[224,128]{1,0:T(8,128)(2,1)S(1)} collective-permute-done((bf16[224,128]{1,0:T(8,128)(2,1)S(1)}, bf16[224,128]{1,0:T(8,128)(2,1)S(1)}, u32[]{:S(2)}, u32[]{:S(2)}) %collective-permute-start.17) | collective-permute-done | bytes 57376 | tf_op jit(solution)/shard_map/ppermute | solution.py:378
  80.4 1.3 %shard_map.106 = (bf16[224,128]{1,0:T(8,128)(2,1)}, bf16[224,128]{1,0:T(8,128)(2,1)}, bf16[224,128]{1,0:T(8,128)(2,1)S(1)}, bf16[224,128]{1,0:T(8,128)(2,1)S(1)}) custom-call(s32[27]{0:T(128)S(1)} %concatenate.6.facts, f32[224,128]{1,0:T(8,128)S(1)} %get-tuple-element.89.refs_0_, bf16[224,128]{1,0:T(8,128)(2,1)S(1)} %collective-permute-done.16.refs_1_, ...), custom_call_target="tpu_custom_call" | custom-call | tf_op jit(solution)/shard_map/pallas_call | solution.py:320
  81.8 3.0 %collective-permute-done.24 = bf16[224,128]{1,0:T(8,128)(2,1)S(1)} collective-permute-done((bf16[224,128]{1,0:T(8,128)(2,1)S(1)}, bf16[224,128]{1,0:T(8,128)(2,1)S(1)}, u32[]{:S(2)}, u32[]{:S(2)}) %collective-permute-start.24) | collective-permute-done | bytes 57376 | tf_op jit(solution)/shard_map/ppermute | solution.py:407
  84.8 3.6 %collective-permute-start.25 = (bf16[2,224,128]{2,1,0:T(8,128)(2,1)S(1)}, bf16[2,224,128]{2,1,0:T(8,128)(2,1)S(1)}, u32[]{:S(2)}, u32[]{:S(2)}) collective-permute-start(bf16[2,224,128]{2,1,0:T(8,128)(2,1)S(1)} %get-tuple-element.94), channel_id=1, source_target_pairs={{2,66},{3,67},{64,0},{65,1},{6,70},{7,71},{68,4},{69,5},{10,74},{1... | collective-permute-start | bytes 344072 | tf_op jit(solution)/shard_map/ppermute | solution.py:411
  88.4 0.9 collective-permute-done.25
  89.4 0.7 collective-permute-start.28
  90.0 1.3 collective-permute-start.27
  91.3 1.3 collective-permute-start.26
  92.7 6.3 %collective-permute-done.27.row2 = bf16[896,128]{1,0:T(8,128)(2,1)S(1)} collective-permute-done((bf16[896,128]{1,0:T(8,128)(2,1)S(1)}, bf16[896,128]{1,0:T(8,128)(2,1)S(1)}, u32[]{:S(2)}, u32[]{:S(2)}) %collective-permute-start.27) | collective-permute-done | bytes 229408 | tf_op jit(solution)/shard_map/ppermute | solution.py:418
  99.0 2.5 %collective-permute-done.26.row1 = bf16[896,128]{1,0:T(8,128)(2,1)S(1)} collective-permute-done((bf16[896,128]{1,0:T(8,128)(2,1)S(1)}, bf16[896,128]{1,0:T(8,128)(2,1)S(1)}, u32[]{:S(2)}, u32[]{:S(2)}) %collective-permute-start.26) | collective-permute-done | bytes 229408 | tf_op jit(solution)/shard_map/ppermute | solution.py:418
  101.5 2.6 %shard_map.107 = (bf16[2,2,16,2048]{3,2,1,0:T(8,128)(2,1)S(1)}, bf16[2,2,16,2048]{3,2,1,0:T(8,128)(2,1)S(1)}, bf16[2,2,16,2048]{3,2,1,0:T(8,128)(2,1)S(1)}, bf16[2,2,16,2048]{3,2,1,0:T(8,128)(2,1)S(1)}) custom-call(s32[27]{0:T(128)S(1)} %concatenate.6.facts, bf16[224,2048]{1,0:T(8,128)(2,1)S(1)} %bitcast.52, ...), custom_call_target="tpu_custom_call" | custom-call | flops 1000000000 | bytes 4000000 | tf_op jit(solution)/shard_map/pallas_call | solution.py:355
  104.1 0.1 collective-permute-start.29
  104.2 0.1 collective-permute-start.30
  104.3 2.6 %collective-permute-start.31 = (bf16[2,2,16,2048]{3,2,1,0:T(8,128)(2,1)S(1)}, bf16[2,2,16,2048]{3,2,1,0:T(8,128)(2,1)S(1)}, u32[]{:S(2)}, u32[]{:S(2)}) collective-permute-start(bf16[2,2,16,2048]{3,2,1,0:T(8,128)(2,1)S(1)} %get-tuple-element.79), channel_id=1, source_target_pairs={{0,12},{4,0},{8,4},{12,8},{1,13},{5,1},{9,5},{13,9},{2,14},{6,2},{... | collective-permute-start | bytes 786440 | tf_op jit(solution)/shard_map/ppermute | solution.py:378
  106.8 12.4 %collective-permute-done.29 = bf16[2,2,16,2048]{3,2,1,0:T(8,128)(2,1)S(1)} collective-permute-done((bf16[2,2,16,2048]{3,2,1,0:T(8,128)(2,1)S(1)}, bf16[2,2,16,2048]{3,2,1,0:T(8,128)(2,1)S(1)}, u32[]{:S(2)}, u32[]{:S(2)}) %collective-permute-start.29) | collective-permute-done | bytes 262176 | tf_op jit(solution)/shard_map/ppermute | solution.py:378
  119.3 0.4 collective-permute-done.31
  119.7 0.1 fusion.10
  119.8 1.1 collective-permute-start.32
  120.9 2.3 %collective-permute-start.34 = (bf16[16,2048]{1,0:T(8,128)(2,1)S(1)}, bf16[16,2048]{1,0:T(8,128)(2,1)S(1)}, u32[]{:S(2)}, u32[]{:S(2)}) collective-permute-start(bf16[16,2048]{1,0:T(8,128)(2,1)S(1)} %get-tuple-element.91), channel_id=1, source_target_pairs={{0,160},{128,32},{32,128},{160,0},{16,176},{144,48},{48,144},{176,... | collective-permute-start | bytes 196616 | tf_op jit(solution)/shard_map/ppermute | solution.py:427
  123.2 2.4 %collective-permute-start.33 = (bf16[16,2048]{1,0:T(8,128)(2,1)S(1)}, bf16[16,2048]{1,0:T(8,128)(2,1)S(1)}, u32[]{:S(2)}, u32[]{:S(2)}) collective-permute-start(bf16[16,2048]{1,0:T(8,128)(2,1)S(1)} %get-tuple-element.92), channel_id=1, source_target_pairs={{0,128},{128,0},{1,129},{129,1},{2,130},{130,2},{3,131},{131,3},{4... | collective-permute-start | bytes 196616 | tf_op jit(solution)/shard_map/ppermute | solution.py:426
  125.6 0.7 collective-permute-done.34
  126.3 4.4 %collective-permute-done.33 = bf16[16,2048]{1,0:T(8,128)(2,1)S(1)} collective-permute-done((bf16[16,2048]{1,0:T(8,128)(2,1)S(1)}, bf16[16,2048]{1,0:T(8,128)(2,1)S(1)}, u32[]{:S(2)}, u32[]{:S(2)}) %collective-permute-start.33) | collective-permute-done | bytes 65568 | tf_op jit(solution)/shard_map/ppermute | solution.py:426
  130.7 0.7 fusion.2
  (31 shorter events, 0.1 us)
Async XLA Ops:
  0.6 17.5 %collective-permute-start.3 = (bf16[224,2048]{1,0:T(8,128)(2,1)}, bf16[224,2048]{1,0:T(8,128)(2,1)S(1)}, u32[]{:S(2)}, u32[]{:S(2)}) collective-permute-start(bf16[224,2048]{1,0:T(8,128)(2,1)} %bitcast.50), channel_id=1, source_target_pairs={{0,64},{64,0},{1,65},{65,1},{2,66},{66,2},{3,67},{67,3},{4,68},{68... | collective-permute-start | bytes 2752520 | tf_op jit(solution)/shard_map/ppermute | solution.py:384
  4.8 5.3 %collective-permute-start.2 = (bf16[224,256]{1,0:T(8,128)(2,1)S(1)}, bf16[224,256]{1,0:T(8,128)(2,1)S(1)}, u32[]{:S(2)}, u32[]{:S(2)}) collective-permute-start(bf16[224,256]{1,0:T(8,128)(2,1)S(1)} %pad_maximum_fusion.1.c0), channel_id=1, source_target_pairs={{0,48},{16,0},{32,16},{48,32},{1,49},{17,1},{33,17},{49,33},{2,50}... | collective-permute-start | bytes 344072 | tf_op jit(solution)/shard_map/ppermute | solution.py:378
  7.5 10.6 %collective-permute-start.1 = (bf16[224,256]{1,0:T(8,128)(2,1)S(1)}, bf16[224,256]{1,0:T(8,128)(2,1)S(1)}, u32[]{:S(2)}, u32[]{:S(2)}) collective-permute-start(bf16[224,256]{1,0:T(8,128)(2,1)S(1)} %pad_maximum_fusion.1.c0), channel_id=1, source_target_pairs={{0,32},{16,48},{32,0},{48,16},{1,33},{17,49},{33,1},{49,17},{2,34}... | collective-permute-start | bytes 344072 | tf_op jit(solution)/shard_map/ppermute | solution.py:378
  7.5 10.6 %collective-permute-start = (bf16[224,256]{1,0:T(8,128)(2,1)S(1)}, bf16[224,256]{1,0:T(8,128)(2,1)S(1)}, u32[]{:S(2)}, u32[]{:S(2)}) collective-permute-start(bf16[224,256]{1,0:T(8,128)(2,1)S(1)} %pad_maximum_fusion.1.c0), channel_id=1, source_target_pairs={{0,16},{16,32},{32,48},{48,0},{1,17},{17,33},{33,49},{49,1},{2,18}... | collective-permute-start | bytes 344072 | tf_op jit(solution)/shard_map/ppermute | solution.py:378
  7.9 1.0 copy-start.1
  8.9 1.0 copy-start.2
  18.2 7.9 %collective-permute-start.4 = (bf16[4,224,128]{2,1,0:T(8,128)(2,1)S(1)}, bf16[4,224,128]{2,1,0:T(8,128)(2,1)S(1)}, u32[]{:S(2)}, u32[]{:S(2)}) collective-permute-start(bf16[4,224,128]{2,1,0:T(8,128)(2,1)S(1)} %get-tuple-element.50.k0), channel_id=1, source_target_pairs={{0,4},{4,8},{8,12},{12,0},{1,5},{5,9},{9,13},{13,1},{2,6},{6,10},{... | collective-permute-start | bytes 688136 | tf_op jit(solution)/shard_map/ppermute | solution.py:378
  19.6 8.0 %collective-permute-start.6 = (bf16[4,224,128]{2,1,0:T(8,128)(2,1)S(1)}, bf16[4,224,128]{2,1,0:T(8,128)(2,1)S(1)}, u32[]{:S(2)}, u32[]{:S(2)}) collective-permute-start(bf16[4,224,128]{2,1,0:T(8,128)(2,1)S(1)} %get-tuple-element.50.k0), channel_id=1, source_target_pairs={{0,12},{4,0},{8,4},{12,8},{1,13},{5,1},{9,5},{13,9},{2,14},{6,2},{... | collective-permute-start | bytes 688136 | tf_op jit(solution)/shard_map/ppermute | solution.py:378
  21.1 11.0 %collective-permute-start.5 = (bf16[4,224,128]{2,1,0:T(8,128)(2,1)S(1)}, bf16[4,224,128]{2,1,0:T(8,128)(2,1)S(1)}, u32[]{:S(2)}, u32[]{:S(2)}) collective-permute-start(bf16[4,224,128]{2,1,0:T(8,128)(2,1)S(1)} %get-tuple-element.50.k0), channel_id=1, source_target_pairs={{0,8},{4,12},{8,0},{12,4},{1,9},{5,13},{9,1},{13,5},{2,10},{6,14},... | collective-permute-start | bytes 688136 | tf_op jit(solution)/shard_map/ppermute | solution.py:378
  22.6 0.7 copy-start.3
  22.6 0.7 copy-start.4
  26.1 9.9 %copy-start = (bf16[1,224,2048]{2,1,0:T(8,128)(2,1)S(1)}, bf16[1,224,2048]{2,1,0:T(8,128)(2,1)}, u32[]{:S(2)}) copy-start(bf16[1,224,2048]{2,1,0:T(8,128)(2,1)} %param.7) | copy-start | bytes 2752516
  26.1 16.1 %collective-permute-start.9 = (bf16[4,224,128]{2,1,0:T(8,128)(2,1)S(1)}, bf16[4,224,128]{2,1,0:T(8,128)(2,1)S(1)}, u32[]{:S(2)}, u32[]{:S(2)}) collective-permute-start(bf16[4,224,128]{2,1,0:T(8,128)(2,1)S(1)} %get-tuple-element.53.v0), channel_id=1, source_target_pairs={{0,12},{4,0},{8,4},{12,8},{1,13},{5,1},{9,5},{13,9},{2,14},{6,2},{... | collective-permute-start | bytes 688136 | tf_op jit(solution)/shard_map/ppermute | solution.py:378
  27.5 17.2 %collective-permute-start.7 = (bf16[4,224,128]{2,1,0:T(8,128)(2,1)S(1)}, bf16[4,224,128]{2,1,0:T(8,128)(2,1)S(1)}, u32[]{:S(2)}, u32[]{:S(2)}) collective-permute-start(bf16[4,224,128]{2,1,0:T(8,128)(2,1)S(1)} %get-tuple-element.53.v0), channel_id=1, source_target_pairs={{0,4},{4,8},{8,12},{12,0},{1,5},{5,9},{9,13},{13,1},{2,6},{6,10},{... | collective-permute-start | bytes 688136 | tf_op jit(solution)/shard_map/ppermute | solution.py:378
  32.1 8.7 %collective-permute-start.8 = (bf16[4,224,128]{2,1,0:T(8,128)(2,1)S(1)}, bf16[4,224,128]{2,1,0:T(8,128)(2,1)S(1)}, u32[]{:S(2)}, u32[]{:S(2)}) collective-permute-start(bf16[4,224,128]{2,1,0:T(8,128)(2,1)S(1)} %get-tuple-element.53.v0), channel_id=1, source_target_pairs={{0,8},{4,12},{8,0},{12,4},{1,9},{5,13},{9,1},{13,5},{2,10},{6,14},... | collective-permute-start | bytes 688136 | tf_op jit(solution)/shard_map/ppermute | solution.py:378
  36.0 29.6 %collective-permute-start.22 = (bf16[224,2048]{1,0:T(8,128)(2,1)S(1)}, bf16[224,2048]{1,0:T(8,128)(2,1)S(1)}, u32[]{:S(2)}, u32[]{:S(2)}) collective-permute-start(bf16[224,2048]{1,0:T(8,128)(2,1)S(1)} %bitcast.51), channel_id=1, source_target_pairs={{0,16},{16,0},{32,48},{48,32},{1,17},{17,1},{33,49},{49,33},{2,18}... | collective-permute-start | bytes 2752520 | tf_op jit(solution)/shard_map/ppermute | solution.py:400
  37.0 13.2 %collective-permute-start.10 = (bf16[4,224,128]{2,1,0:T(8,128)(2,1)S(1)}, bf16[4,224,128]{2,1,0:T(8,128)(2,1)S(1)}, u32[]{:S(2)}, u32[]{:S(2)}) collective-permute-start(bf16[4,224,128]{2,1,0:T(8,128)(2,1)S(1)} %get-tuple-element.61), channel_id=1, source_target_pairs={{0,4},{4,8},{8,12},{12,0},{1,5},{5,9},{9,13},{13,1},{2,6},{6,10},{... | collective-permute-start | bytes 688136 | tf_op jit(solution)/shard_map/ppermute | solution.py:378
  40.8 9.4 %collective-permute-start.11 = (bf16[4,224,128]{2,1,0:T(8,128)(2,1)S(1)}, bf16[4,224,128]{2,1,0:T(8,128)(2,1)S(1)}, u32[]{:S(2)}, u32[]{:S(2)}) collective-permute-start(bf16[4,224,128]{2,1,0:T(8,128)(2,1)S(1)} %get-tuple-element.62), channel_id=1, source_target_pairs={{0,8},{4,12},{8,0},{12,4},{1,9},{5,13},{9,1},{13,5},{2,10},{6,14},... | collective-permute-start | bytes 688136 | tf_op jit(solution)/shard_map/ppermute | solution.py:378
  42.1 9.9 %collective-permute-start.12 = (bf16[4,224,128]{2,1,0:T(8,128)(2,1)S(1)}, bf16[4,224,128]{2,1,0:T(8,128)(2,1)S(1)}, u32[]{:S(2)}, u32[]{:S(2)}) collective-permute-start(bf16[4,224,128]{2,1,0:T(8,128)(2,1)S(1)} %get-tuple-element.63), channel_id=1, source_target_pairs={{0,12},{4,0},{8,4},{12,8},{1,13},{5,1},{9,5},{13,9},{2,14},{6,2},{... | collective-permute-start | bytes 688136 | tf_op jit(solution)/shard_map/ppermute | solution.py:378
  52.0 7.6 %collective-permute-start.13 = (bf16[4,224,128]{2,1,0:T(8,128)(2,1)S(1)}, bf16[4,224,128]{2,1,0:T(8,128)(2,1)S(1)}, u32[]{:S(2)}, u32[]{:S(2)}) collective-permute-start(bf16[4,224,128]{2,1,0:T(8,128)(2,1)S(1)} %get-tuple-element.65), channel_id=1, source_target_pairs={{0,4},{4,8},{8,12},{12,0},{1,5},{5,9},{9,13},{13,1},{2,6},{6,10},{... | collective-permute-start | bytes 688136 | tf_op jit(solution)/shard_map/ppermute | solution.py:378
  54.3 11.4 %collective-permute-start.14 = (bf16[4,224,128]{2,1,0:T(8,128)(2,1)S(1)}, bf16[4,224,128]{2,1,0:T(8,128)(2,1)S(1)}, u32[]{:S(2)}, u32[]{:S(2)}) collective-permute-start(bf16[4,224,128]{2,1,0:T(8,128)(2,1)S(1)} %get-tuple-element.66), channel_id=1, source_target_pairs={{0,8},{4,12},{8,0},{12,4},{1,9},{5,13},{9,1},{13,5},{2,10},{6,14},... | collective-permute-start | bytes 688136 | tf_op jit(solution)/shard_map/ppermute | solution.py:378
  56.7 8.9 %collective-permute-start.15 = (bf16[4,224,128]{2,1,0:T(8,128)(2,1)S(1)}, bf16[4,224,128]{2,1,0:T(8,128)(2,1)S(1)}, u32[]{:S(2)}, u32[]{:S(2)}) collective-permute-start(bf16[4,224,128]{2,1,0:T(8,128)(2,1)S(1)} %get-tuple-element.67), channel_id=1, source_target_pairs={{0,12},{4,0},{8,4},{12,8},{1,13},{5,1},{9,5},{13,9},{2,14},{6,2},{... | collective-permute-start | bytes 688136 | tf_op jit(solution)/shard_map/ppermute | solution.py:378
  56.8 17.0 %collective-permute-start.21 = (bf16[224,128]{1,0:T(8,128)(2,1)S(1)}, bf16[224,128]{1,0:T(8,128)(2,1)S(1)}, u32[]{:S(2)}, u32[]{:S(2)}) collective-permute-start(bf16[224,128]{1,0:T(8,128)(2,1)S(1)} %get-tuple-element.82), channel_id=1, source_target_pairs={{0,48},{16,0},{32,16},{48,32},{1,49},{17,1},{33,17},{49,33},{2,50}... | collective-permute-start | bytes 172040 | tf_op jit(solution)/shard_map/ppermute | solution.py:378
  59.6 14.3 %collective-permute-start.20 = (bf16[224,128]{1,0:T(8,128)(2,1)S(1)}, bf16[224,128]{1,0:T(8,128)(2,1)S(1)}, u32[]{:S(2)}, u32[]{:S(2)}) collective-permute-start(bf16[224,128]{1,0:T(8,128)(2,1)S(1)} %get-tuple-element.83), channel_id=1, source_target_pairs={{0,32},{16,48},{32,0},{48,16},{1,33},{17,49},{33,1},{49,17},{2,34}... | collective-permute-start | bytes 172040 | tf_op jit(solution)/shard_map/ppermute | solution.py:378
  65.6 8.6 %collective-permute-start.19 = (bf16[224,128]{1,0:T(8,128)(2,1)S(1)}, bf16[224,128]{1,0:T(8,128)(2,1)S(1)}, u32[]{:S(2)}, u32[]{:S(2)}) collective-permute-start(bf16[224,128]{1,0:T(8,128)(2,1)S(1)} %get-tuple-element.84), channel_id=1, source_target_pairs={{0,16},{16,32},{32,48},{48,0},{1,17},{17,33},{33,49},{49,1},{2,18}... | collective-permute-start | bytes 172040 | tf_op jit(solution)/shard_map/ppermute | solution.py:378
  65.7 35.8 %collective-permute-start.23 = (bf16[224,2048]{1,0:T(8,128)(2,1)S(1)}, bf16[224,2048]{1,0:T(8,128)(2,1)S(1)}, u32[]{:S(2)}, u32[]{:S(2)}) collective-permute-start(bf16[224,2048]{1,0:T(8,128)(2,1)S(1)} %collective-permute-done.22.hid1), channel_id=1, source_target_pairs={{0,64},{64,0},{1,65},{65,1},{2,66},{66,2},{3,67},{67,3},{4,68},{68... | collective-permute-start | bytes 2752520 | tf_op jit(solution)/shard_map/ppermute | solution.py:406
  70.3 4.8 %collective-permute-start.18 = (bf16[224,128]{1,0:T(8,128)(2,1)S(1)}, bf16[224,128]{1,0:T(8,128)(2,1)S(1)}, u32[]{:S(2)}, u32[]{:S(2)}) collective-permute-start(bf16[224,128]{1,0:T(8,128)(2,1)S(1)} %get-tuple-element.86), channel_id=1, source_target_pairs={{0,48},{16,0},{32,16},{48,32},{1,49},{17,1},{33,17},{49,33},{2,50}... | collective-permute-start | bytes 172040 | tf_op jit(solution)/shard_map/ppermute | solution.py:378
  73.8 6.6 %collective-permute-start.17 = (bf16[224,128]{1,0:T(8,128)(2,1)S(1)}, bf16[224,128]{1,0:T(8,128)(2,1)S(1)}, u32[]{:S(2)}, u32[]{:S(2)}) collective-permute-start(bf16[224,128]{1,0:T(8,128)(2,1)S(1)} %get-tuple-element.87), channel_id=1, source_target_pairs={{0,32},{16,48},{32,0},{48,16},{1,33},{17,49},{33,1},{49,17},{2,34}... | collective-permute-start | bytes 172040 | tf_op jit(solution)/shard_map/ppermute | solution.py:378
  73.8 6.6 %collective-permute-start.16 = (bf16[224,128]{1,0:T(8,128)(2,1)S(1)}, bf16[224,128]{1,0:T(8,128)(2,1)S(1)}, u32[]{:S(2)}, u32[]{:S(2)}) collective-permute-start(bf16[224,128]{1,0:T(8,128)(2,1)S(1)} %get-tuple-element.88), channel_id=1, source_target_pairs={{0,16},{16,32},{32,48},{48,0},{1,17},{17,33},{33,49},{49,1},{2,18}... | collective-permute-start | bytes 172040 | tf_op jit(solution)/shard_map/ppermute | solution.py:378
  81.8 3.0 %collective-permute-start.24 = (bf16[224,128]{1,0:T(8,128)(2,1)S(1)}, bf16[224,128]{1,0:T(8,128)(2,1)S(1)}, u32[]{:S(2)}, u32[]{:S(2)}) collective-permute-start(bf16[224,128]{1,0:T(8,128)(2,1)S(1)} %get-tuple-element.75), channel_id=1, source_target_pairs={{0,16},{16,0},{32,48},{48,32},{1,17},{17,1},{33,49},{49,33},{2,18}... | collective-permute-start | bytes 172040 | tf_op jit(solution)/shard_map/ppermute | solution.py:407
  84.8 4.5 %collective-permute-start.25 = (bf16[2,224,128]{2,1,0:T(8,128)(2,1)S(1)}, bf16[2,224,128]{2,1,0:T(8,128)(2,1)S(1)}, u32[]{:S(2)}, u32[]{:S(2)}) collective-permute-start(bf16[2,224,128]{2,1,0:T(8,128)(2,1)S(1)} %get-tuple-element.94), channel_id=1, source_target_pairs={{2,66},{3,67},{64,0},{65,1},{6,70},{7,71},{68,4},{69,5},{10,74},{1... | collective-permute-start | bytes 344072 | tf_op jit(solution)/shard_map/ppermute | solution.py:411
  89.4 3.3 %collective-permute-start.28 = (bf16[896,128]{1,0:T(8,128)(2,1)S(1)}, bf16[896,128]{1,0:T(8,128)(2,1)S(1)}, u32[]{:S(2)}, u32[]{:S(2)}) collective-permute-start(bf16[896,128]{1,0:T(8,128)(2,1)S(1)} %bitcast.53), channel_id=1, source_target_pairs={{0,3},{1,0},{66,65},{67,66},{4,7},{5,4},{70,69},{71,70},{8,11},{9,... | collective-permute-start | bytes 688136 | tf_op jit(solution)/shard_map/ppermute | solution.py:418
  90.0 8.9 %collective-permute-start.27 = (bf16[896,128]{1,0:T(8,128)(2,1)S(1)}, bf16[896,128]{1,0:T(8,128)(2,1)S(1)}, u32[]{:S(2)}, u32[]{:S(2)}) collective-permute-start(bf16[896,128]{1,0:T(8,128)(2,1)S(1)} %bitcast.54), channel_id=1, source_target_pairs={{0,2},{1,3},{66,64},{67,65},{4,6},{5,7},{70,68},{71,69},{8,10},{9,... | collective-permute-start | bytes 688136 | tf_op jit(solution)/shard_map/ppermute | solution.py:418
  91.3 10.2 %collective-permute-start.26 = (bf16[896,128]{1,0:T(8,128)(2,1)S(1)}, bf16[896,128]{1,0:T(8,128)(2,1)S(1)}, u32[]{:S(2)}, u32[]{:S(2)}) collective-permute-start(bf16[896,128]{1,0:T(8,128)(2,1)S(1)} %bitcast.55), channel_id=1, source_target_pairs={{0,1},{1,2},{66,67},{67,64},{4,5},{5,6},{70,71},{71,68},{8,9},{9,1... | collective-permute-start | bytes 688136 | tf_op jit(solution)/shard_map/ppermute | solution.py:418
  104.1 15.2 %collective-permute-start.29 = (bf16[2,2,16,2048]{3,2,1,0:T(8,128)(2,1)S(1)}, bf16[2,2,16,2048]{3,2,1,0:T(8,128)(2,1)S(1)}, u32[]{:S(2)}, u32[]{:S(2)}) collective-permute-start(bf16[2,2,16,2048]{3,2,1,0:T(8,128)(2,1)S(1)} %get-tuple-element.77), channel_id=1, source_target_pairs={{0,4},{4,8},{8,12},{12,0},{1,5},{5,9},{9,13},{13,1},{2,6},{6,10},{... | collective-permute-start | bytes 786440 | tf_op jit(solution)/shard_map/ppermute | solution.py:378
  104.2 15.1 %collective-permute-start.30 = (bf16[2,2,16,2048]{3,2,1,0:T(8,128)(2,1)S(1)}, bf16[2,2,16,2048]{3,2,1,0:T(8,128)(2,1)S(1)}, u32[]{:S(2)}, u32[]{:S(2)}) collective-permute-start(bf16[2,2,16,2048]{3,2,1,0:T(8,128)(2,1)S(1)} %get-tuple-element.78), channel_id=1, source_target_pairs={{0,8},{4,12},{8,0},{12,4},{1,9},{5,13},{9,1},{13,5},{2,10},{6,14},... | collective-permute-start | bytes 786440 | tf_op jit(solution)/shard_map/ppermute | solution.py:378
  104.3 15.4 %collective-permute-start.31 = (bf16[2,2,16,2048]{3,2,1,0:T(8,128)(2,1)S(1)}, bf16[2,2,16,2048]{3,2,1,0:T(8,128)(2,1)S(1)}, u32[]{:S(2)}, u32[]{:S(2)}) collective-permute-start(bf16[2,2,16,2048]{3,2,1,0:T(8,128)(2,1)S(1)} %get-tuple-element.79), channel_id=1, source_target_pairs={{0,12},{4,0},{8,4},{12,8},{1,13},{5,1},{9,5},{13,9},{2,14},{6,2},{... | collective-permute-start | bytes 786440 | tf_op jit(solution)/shard_map/ppermute | solution.py:378
  119.8 5.7 %collective-permute-start.32 = (bf16[16,2048]{1,0:T(8,128)(2,1)S(1)}, bf16[16,2048]{1,0:T(8,128)(2,1)S(1)}, u32[]{:S(2)}, u32[]{:S(2)}) collective-permute-start(bf16[16,2048]{1,0:T(8,128)(2,1)S(1)} %get-tuple-element.90), channel_id=1, source_target_pairs={{0,32},{32,0},{16,48},{48,16},{1,33},{33,1},{17,49},{49,17},{2,34}... | collective-permute-start | bytes 196616 | tf_op jit(solution)/shard_map/ppermute | solution.py:425
  120.9 5.4 %collective-permute-start.34 = (bf16[16,2048]{1,0:T(8,128)(2,1)S(1)}, bf16[16,2048]{1,0:T(8,128)(2,1)S(1)}, u32[]{:S(2)}, u32[]{:S(2)}) collective-permute-start(bf16[16,2048]{1,0:T(8,128)(2,1)S(1)} %get-tuple-element.91), channel_id=1, source_target_pairs={{0,160},{128,32},{32,128},{160,0},{16,176},{144,48},{48,144},{176,... | collective-permute-start | bytes 196616 | tf_op jit(solution)/shard_map/ppermute | solution.py:427
  123.2 7.4 %collective-permute-start.33 = (bf16[16,2048]{1,0:T(8,128)(2,1)S(1)}, bf16[16,2048]{1,0:T(8,128)(2,1)S(1)}, u32[]{:S(2)}, u32[]{:S(2)}) collective-permute-start(bf16[16,2048]{1,0:T(8,128)(2,1)S(1)} %get-tuple-element.92), channel_id=1, source_target_pairs={{0,128},{128,0},{1,129},{129,1},{2,130},{130,2},{3,131},{131,3},{4... | collective-permute-start | bytes 196616 | tf_op jit(solution)/shard_map/ppermute | solution.py:426

commit v11 on v10

--- a/solution.py
+++ b/solution.py
@@ -272,19 +272,18 @@
     )(*arrays)
 
 
-def columns_kernel(c0, c1, c2, c3, keys, values):
+def stack_kernel(c0, c1, c2, c3, out):
     for a, ref in enumerate((c0, c1, c2, c3)):
-        keys[a] = ref[:, 0:DH]
-        values[a] = ref[:, DH : 2 * DH]
-
-
-def columns_of(pieces):
-    vmem = pl.BlockSpec(memory_space=pltpu.VMEM)
-    return pl.pallas_call(
-        columns_kernel,
-        out_shape=SHARES[:2],
+        out[a] = ref[...]
+
+
+def stacked(pieces):
+    vmem = pl.BlockSpec(memory_space=pltpu.VMEM)
+    return pl.pallas_call(
+        stack_kernel,
+        out_shape=SHARES[0],
         in_specs=[vmem] * 4,
-        out_specs=(vmem,) * 2,
+        out_specs=vmem,
         compiler_params=pltpu.CompilerParams(vmem_limit_bytes=16 * 2**20),
     )(*pieces)
 
@@ -377,15 +376,14 @@
     def moved(value, axis, shift):
         return lax.ppermute(value, axis, ring(shift))
 
-    own = jnp.concatenate([keys_in[0], values_in[0]], axis=1)
-    pieces = [own] + [moved(own, "zl", a) for a in (1, 2, 3)]
+    ks, vs = (
+        [own] + [moved(own, "zl", a) for a in (1, 2, 3)] for own in (keys_in[0], values_in[0])
+    )
     rows_in = near(queries[0], out_grad[0])
-    hidden = hidden_in[0]
-    hidden = (hidden, lax.ppermute(hidden, "co", swap))
-    pieces, rows_in, hidden = lax.optimization_barrier((pieces, rows_in, hidden))
-    ks, vs = columns_of(pieces)
+    ks, vs, rows_in = lax.optimization_barrier((ks, vs, rows_in))
+    ks = stacked(ks)
     ks = [ks] + [moved(ks, "y", s) for s in (1, 2, 3)]
-    vs = after(vs, ks[1])
+    vs = after(stacked(vs), ks[1])
     vs = [vs] + [moved(vs if s != 2 else after(vs, *ks[2:]), "y", s) for s in (1, 2, 3)]
 
     def received(shares):
@@ -397,13 +395,14 @@
 
     stats, *dvs = forward(facts, *rows_in, ks)
     dvs = received(dvs)
-    beside = lax.ppermute(after(hidden[0], stats), "zl", neighbour)
+    hidden = hidden_in[0]
+    beside = lax.ppermute(after(hidden, stats), "zl", neighbour)
     dq, *dks = backward(facts, *rows_in, ks, vs, stats)
-    dks = received(after(dks, dvs))
+    dks = received(after(dks, dvs[1]))
     key_grads, value_grads, mine, sent = finish(facts, over_zl(dks), over_zl(dvs))
 
-    beside = after(beside, *dks)
-    hidden = (hidden[0], beside, hidden[1], lax.ppermute(beside, "co", swap))
+    hidden = after((hidden, beside), *dks)
+    hidden = (*hidden, *(lax.ppermute(h, "co", swap) for h in hidden))
     rows = jnp.stack([mine, lax.ppermute(sent, "zl", neighbour)])
     cross = [
         (x0 + 4 * c, x0 + 4 * (1 - c)) for c in range(2) for x0 in range(4) if x0 // 2 == 1 - c
@@ -422,9 +421,9 @@
     both = [(a + 4 * c, b + 4 * (1 - c)) for a, b in other_zl for c in range(2)]
     grad_weight = add_up(
         total[0, 0],
-        lax.ppermute(total[0, 1].astype(BF), "zl", other_zl),
         lax.ppermute(total[1, 0].astype(BF), "zh", swap),
         lax.ppermute(total[1, 1].astype(BF), ("zh", "zl"), both),
+        lax.ppermute(total[0, 1].astype(BF), "zl", other_zl),
     )
     return dq[None], key_grads[None], value_grads[None], grad_weight
 

time: 132 us -> 129 us (0.977)
  waiting for transfers between devices: 57.9 us -> 47.8 us
  starting transfers between devices: 54.8 us -> 63 us
    ppermute x24 -> x27, starting transfers between devices: 33.4 us -> 42.7 us  [moved(): return lax.ppermute(value, axis, ring(shift))]
    ppermute x24 -> x27, waiting for transfers between devices: 40 us -> 31.1 us  [moved(): return lax.ppermute(value, axis, ring(shift))]
    ppermute x3, starting transfers between devices: 8.85 us -> 3.56 us  [the longest x2 2.27 us: per_device(): hidden = (*hidden, *(lax.ppermute(h, 'co', swap) for h in hidden))]
    ppermute x1, waiting for transfers between devices: 0.01 us -> 3.65 us  [per_device(): lax.ppermute(total[0, 1].astype(BF), 'zl', other_zl)]
    ppermute x1, waiting for transfers between devices: 4.36 us -> 1.56 us  [per_device(): lax.ppermute(total[1, 0].astype(BF), 'zh', swap)]
    ppermute x1, starting transfers between devices: 3.57 us -> 6.36 us  [per_device(): lax.ppermute(rows, ('co', 'x'), cross)]
    ppermute x1, starting transfers between devices: 0.01 us -> 1.39 us  [per_device(): rows = jnp.stack([mine, lax.ppermute(sent, 'zl', neighbour)])]
    ppermute x1, waiting for transfers between devices: 3.03 us -> 1.64 us  [per_device(): rows = jnp.stack([mine, lax.ppermute(sent, 'zl', neighbour)])]
  transfers between devices with their start and end apart: 35 -> 38, of which waited for: 17 -> 19; matrix products, arithmetic and copies ran while one was open for 1% -> 0% of each run, Pallas kernels for 8% -> 8%
where the time goes in v11:
time: 129 us
  starting transfers between devices  63 us (49%)
  waiting for transfers between devices  47.8 us (37%)
  Pallas kernels  13.2 us (10%)
  local copies, waits for them, and re-layouts  2.82 us (2%)
    ppermute x27, starting transfers between devices, moved(): return lax.ppermute(value, axis, ring(shift))  42.7 us
    ppermute x27, waiting for transfers between devices, moved(): return lax.ppermute(value, axis, ring(shift))  31.1 us
    ppermute x3, waiting for transfers between devices, per_device(): lax.ppermute(rows, ('co', 'x'), along(j))  8.85 us
    ppermute x1, starting transfers between devices, per_device(): lax.ppermute(rows, ('co', 'x'), cross)  6.36 us
    pallas_call x1, Pallas kernels, backward(): pl.pallas_call(backward_kernel, out_shape=(jax.ShapeDtypeStruct((ROWS, HE...  5.57 us
    ppermute x1, waiting for transfers between devices, per_device(): lax.ppermute(total[0, 1].astype(BF), 'zl', other_zl)  3.65 us
    pallas_call x1, Pallas kernels, forward(): pl.pallas_call(forward_kernel, out_shape=(jax.ShapeDtypeStruct((2, 1, LAN...  3.64 us
    ppermute x3, starting transfers between devices, per_device(): lax.ppermute(rows, ('co', 'x'), along(j))  3.26 us
  transfers between devices with their start and end apart: 38, of which 19 were waited for; matrix products, arithmetic and copies ran while one was open for 0% of the time, Pallas kernels for 8%

profile of v11, /device:TPU:1, one launch (start us, length us, event | category | flops | bytes accessed | tf_op | source)
XLA Modules:
  0.0 128.8 jit_solution(8274884617614385844)
XLA Ops:
  0.6 5.2 %collective-permute-start.2 = (bf16[224,128]{1,0:T(8,128)(2,1)}, bf16[224,128]{1,0:T(8,128)(2,1)S(1)}, u32[]{:S(2)}, u32[]{:S(2)}) collective-permute-start(bf16[224,128]{1,0:T(8,128)(2,1)} %bitcast.59), channel_id=1, source_target_pairs={{0,48},{16,0},{32,16},{48,32},{1,49},{17,1},{33,17},{49,33},{2,50}... | collective-permute-start | bytes 172040 | tf_op jit(solution)/shard_map/ppermute | solution.py:377
  5.9 0.4 collective-permute-start
  6.3 2.9 %collective-permute-start.5 = (bf16[224,128]{1,0:T(8,128)(2,1)}, bf16[224,128]{1,0:T(8,128)(2,1)S(1)}, u32[]{:S(2)}, u32[]{:S(2)}) collective-permute-start(bf16[224,128]{1,0:T(8,128)(2,1)} %bitcast.63), channel_id=1, source_target_pairs={{0,48},{16,0},{32,16},{48,32},{1,49},{17,1},{33,17},{49,33},{2,50}... | collective-permute-start | bytes 172040 | tf_op jit(solution)/shard_map/ppermute | solution.py:377
  9.1 0.6 collective-permute-start.4
  9.7 1.0 copy-done.1
  10.7 1.0 copy-done.2
  11.8 0.1 collective-permute-done.1.c2
  11.9 0.7 collective-permute-done.5.c3
  12.6 4.2 %collective-permute-done.4.c2 = bf16[224,128]{1,0:T(8,128)(2,1)S(1)} collective-permute-done((bf16[224,128]{1,0:T(8,128)(2,1)}, bf16[224,128]{1,0:T(8,128)(2,1)S(1)}, u32[]{:S(2)}, u32[]{:S(2)}) %collective-permute-start.4) | collective-permute-done | bytes 57376 | tf_op jit(solution)/shard_map/ppermute | solution.py:377
  16.8 0.4 collective-permute-start.6
  17.2 2.3 %collective-permute-start.8 = (bf16[4,224,128]{2,1,0:T(8,128)(2,1)S(1)}, bf16[4,224,128]{2,1,0:T(8,128)(2,1)S(1)}, u32[]{:S(2)}, u32[]{:S(2)}) collective-permute-start(bf16[4,224,128]{2,1,0:T(8,128)(2,1)S(1)} %shard_map.103.k0), channel_id=1, source_target_pairs={{0,12},{4,0},{8,4},{12,8},{1,13},{5,1},{9,5},{13,9},{2,14},{6,2},{... | collective-permute-start | bytes 688136 | tf_op jit(solution)/shard_map/ppermute | solution.py:377
  19.6 0.7 collective-permute-start.7
  20.3 0.7 copy-done.5
  21.0 0.1 concatenate.3.facts
  21.1 2.9 %collective-permute-done.6.k1 = bf16[4,224,128]{2,1,0:T(8,128)(2,1)S(1)} collective-permute-done((bf16[4,224,128]{2,1,0:T(8,128)(2,1)S(1)}, bf16[4,224,128]{2,1,0:T(8,128)(2,1)S(1)}, u32[]{:S(2)}, u32[]{:S(2)}) %collective-permute-start.6) | collective-permute-done | bytes 229408 | tf_op jit(solution)/shard_map/ppermute | solution.py:377
  24.0 1.5 %collective-permute-start.9 = (bf16[4,224,128]{2,1,0:T(8,128)(2,1)S(1)}, bf16[4,224,128]{2,1,0:T(8,128)(2,1)S(1)}, u32[]{:S(2)}, u32[]{:S(2)}) collective-permute-start(bf16[4,224,128]{2,1,0:T(8,128)(2,1)S(1)} %shard_map.104.v0), channel_id=1, source_target_pairs={{0,4},{4,8},{8,12},{12,0},{1,5},{5,9},{9,13},{13,1},{2,6},{6,10},{... | collective-permute-start | bytes 688136 | tf_op jit(solution)/shard_map/ppermute | solution.py:377
  25.5 0.1 collective-permute-done.8.k3
  25.6 3.1 %collective-permute-done.7.k2 = bf16[4,224,128]{2,1,0:T(8,128)(2,1)S(1)} collective-permute-done((bf16[4,224,128]{2,1,0:T(8,128)(2,1)S(1)}, bf16[4,224,128]{2,1,0:T(8,128)(2,1)S(1)}, u32[]{:S(2)}, u32[]{:S(2)}) %collective-permute-start.7) | collective-permute-done | bytes 229408 | tf_op jit(solution)/shard_map/ppermute | solution.py:377
  28.7 0.7 collective-permute-start.10
  29.4 3.6 %shard_map.105 = (f32[2,1,896]{2,1,0:T(1,128)S(1)}, bf16[4,224,128]{2,1,0:T(8,128)(2,1)S(1)}, bf16[4,224,128]{2,1,0:T(8,128)(2,1)S(1)}, bf16[4,224,128]{2,1,0:T(8,128)(2,1)S(1)}, bf16[4,224,128]{2,1,0:T(8,128)(2,1)S(1)}) custom-call(s32[27]{0:T(128)S(1)} %concatenate.3.facts, bf16[224,1024]{1,0:T(8,128)(2,1)S(1)} %get-tuple-element.45.q_ref, ...), custom_call_target="tpu_custom_call" | custom-call | flops 3000000000 | bytes 4000000 | tf_op jit(solution)/shard_map/pallas_call | solution.py:211
  33.0 1.3 collective-permute-start.24
  34.3 0.6 collective-permute-start.12
  34.9 2.8 %collective-permute-done.10.v2 = bf16[4,224,128]{2,1,0:T(8,128)(2,1)S(1)} collective-permute-done((bf16[4,224,128]{2,1,0:T(8,128)(2,1)S(1)}, bf16[4,224,128]{2,1,0:T(8,128)(2,1)S(1)}, u32[]{:S(2)}, u32[]{:S(2)}) %collective-permute-start.10) | collective-permute-done | bytes 229408 | tf_op jit(solution)/shard_map/ppermute | solution.py:377
  37.7 2.8 %collective-permute-start.19 = (bf16[4,224,128]{2,1,0:T(8,128)(2,1)S(1)}, bf16[4,224,128]{2,1,0:T(8,128)(2,1)S(1)}, u32[]{:S(2)}, u32[]{:S(2)}) collective-permute-start(bf16[4,224,128]{2,1,0:T(8,128)(2,1)S(1)} %get-tuple-element.69), channel_id=1, source_target_pairs={{0,8},{4,12},{8,0},{12,4},{1,9},{5,13},{9,1},{13,5},{2,10},{6,14},... | collective-permute-start | bytes 688136 | tf_op jit(solution)/shard_map/ppermute | solution.py:377
  40.5 0.3 collective-permute-start.20
  40.8 5.6 %shard_map.106 = (bf16[224,1024]{1,0:T(8,128)(2,1)}, bf16[4,224,128]{2,1,0:T(8,128)(2,1)S(1)}, bf16[4,224,128]{2,1,0:T(8,128)(2,1)S(1)}, bf16[4,224,128]{2,1,0:T(8,128)(2,1)S(1)}, bf16[4,224,128]{2,1,0:T(8,128)(2,1)S(1)}) custom-call(s32[27]{0:T(128)S(1)} %concatenate.3.facts, bf16[224,1024]{1,0:T(8,128)(2,1)S(1)} %get-tuple-element.45.q_ref, ...), custom_call_target="tpu_custom_call" | custom-call | flops 5000000000 | bytes 5000000 | tf_op jit(solution)/shard_map/pallas_call | solution.py:230
  46.4 0.3 collective-permute-start.13
  46.8 3.4 %collective-permute-start.14 = (bf16[4,224,128]{2,1,0:T(8,128)(2,1)S(1)}, bf16[4,224,128]{2,1,0:T(8,128)(2,1)S(1)}, u32[]{:S(2)}, u32[]{:S(2)}) collective-permute-start(bf16[4,224,128]{2,1,0:T(8,128)(2,1)S(1)} %get-tuple-element.66), channel_id=1, source_target_pairs={{0,8},{4,12},{8,0},{12,4},{1,9},{5,13},{9,1},{13,5},{2,10},{6,14},... | collective-permute-start | bytes 688136 | tf_op jit(solution)/shard_map/ppermute | solution.py:377
  50.2 0.1 fusion.8
  50.3 5.2 %collective-permute-start.23 = (bf16[224,128]{1,0:T(8,128)(2,1)S(1)}, bf16[224,128]{1,0:T(8,128)(2,1)S(1)}, u32[]{:S(2)}, u32[]{:S(2)}) collective-permute-start(bf16[224,128]{1,0:T(8,128)(2,1)S(1)} %get-tuple-element.84), channel_id=1, source_target_pairs={{0,48},{16,0},{32,16},{48,32},{1,49},{17,1},{33,17},{49,33},{2,50}... | collective-permute-start | bytes 172040 | tf_op jit(solution)/shard_map/ppermute | solution.py:377
  55.6 0.4 collective-permute-start.22
  55.9 0.5 collective-permute-done.14
  56.5 8.7 %collective-permute-start.21 = (bf16[224,128]{1,0:T(8,128)(2,1)S(1)}, bf16[224,128]{1,0:T(8,128)(2,1)S(1)}, u32[]{:S(2)}, u32[]{:S(2)}) collective-permute-start(bf16[224,128]{1,0:T(8,128)(2,1)S(1)} %get-tuple-element.86), channel_id=1, source_target_pairs={{0,16},{16,32},{32,48},{48,0},{1,17},{17,33},{33,49},{49,1},{2,18}... | collective-permute-start | bytes 172040 | tf_op jit(solution)/shard_map/ppermute | solution.py:377
  65.1 2.2 %collective-permute-start.25 = (bf16[224,2048]{1,0:T(8,128)(2,1)S(1)}, bf16[224,2048]{1,0:T(8,128)(2,1)S(1)}, u32[]{:S(2)}, u32[]{:S(2)}) collective-permute-start(bf16[224,2048]{1,0:T(8,128)(2,1)S(1)} %bitcast.51), channel_id=1, source_target_pairs={{0,64},{64,0},{1,65},{65,1},{2,66},{66,2},{3,67},{67,3},{4,68},{68... | collective-permute-start | bytes 2752520 | tf_op jit(solution)/shard_map/ppermute | solution.py:405
  67.3 0.1 collective-permute-start.26
  67.4 0.1 fusion.5
  67.5 2.4 %collective-permute-start.18 = (bf16[224,128]{1,0:T(8,128)(2,1)S(1)}, bf16[224,128]{1,0:T(8,128)(2,1)S(1)}, u32[]{:S(2)}, u32[]{:S(2)}) collective-permute-start(bf16[224,128]{1,0:T(8,128)(2,1)S(1)} %get-tuple-element.88), channel_id=1, source_target_pairs={{0,48},{16,0},{32,16},{48,32},{1,49},{17,1},{33,17},{49,33},{2,50}... | collective-permute-start | bytes 172040 | tf_op jit(solution)/shard_map/ppermute | solution.py:377
  70.0 1.1 collective-permute-start.16
  71.1 0.1 collective-permute-done.18.refs_3_
  71.2 2.7 %collective-permute-done.17.refs_2_ = bf16[224,128]{1,0:T(8,128)(2,1)S(1)} collective-permute-done((bf16[224,128]{1,0:T(8,128)(2,1)S(1)}, bf16[224,128]{1,0:T(8,128)(2,1)S(1)}, u32[]{:S(2)}, u32[]{:S(2)}) %collective-permute-start.17) | collective-permute-done | bytes 57376 | tf_op jit(solution)/shard_map/ppermute | solution.py:377
  73.9 1.0 collective-permute-done.16.refs_1_
  74.9 1.3 %shard_map.107 = (bf16[224,128]{1,0:T(8,128)(2,1)}, bf16[224,128]{1,0:T(8,128)(2,1)}, bf16[224,128]{1,0:T(8,128)(2,1)S(1)}, bf16[224,128]{1,0:T(8,128)(2,1)S(1)}) custom-call(s32[27]{0:T(128)S(1)} %concatenate.3.facts, f32[224,128]{1,0:T(8,128)S(1)} %get-tuple-element.91.refs_0_, bf16[224,128]{1,0:T(8,128)(2,1)S(1)} %collective-permute-done.16.refs_1_, ...), custom_call_target="tpu_custom_call" | custom-call | tf_op jit(solution)/shard_map/pallas_call | solution.py:319
  76.3 1.4 %collective-permute-start.27 = (bf16[224,128]{1,0:T(8,128)(2,1)S(1)}, bf16[224,128]{1,0:T(8,128)(2,1)S(1)}, u32[]{:S(2)}, u32[]{:S(2)}) collective-permute-start(bf16[224,128]{1,0:T(8,128)(2,1)S(1)} %get-tuple-element.77), channel_id=1, source_target_pairs={{0,16},{16,0},{32,48},{48,32},{1,17},{17,1},{33,49},{49,33},{2,18}... | collective-permute-start | bytes 172040 | tf_op jit(solution)/shard_map/ppermute | solution.py:406
  77.6 1.6 %collective-permute-done.27 = bf16[224,128]{1,0:T(8,128)(2,1)S(1)} collective-permute-done((bf16[224,128]{1,0:T(8,128)(2,1)S(1)}, bf16[224,128]{1,0:T(8,128)(2,1)S(1)}, u32[]{:S(2)}, u32[]{:S(2)}) %collective-permute-start.27) | collective-permute-done | bytes 57376 | tf_op jit(solution)/shard_map/ppermute | solution.py:406
  79.3 6.4 %collective-permute-start.28 = (bf16[2,224,128]{2,1,0:T(8,128)(2,1)S(1)}, bf16[2,224,128]{2,1,0:T(8,128)(2,1)S(1)}, u32[]{:S(2)}, u32[]{:S(2)}) collective-permute-start(bf16[2,224,128]{2,1,0:T(8,128)(2,1)S(1)} %get-tuple-element.96), channel_id=1, source_target_pairs={{2,66},{3,67},{64,0},{65,1},{6,70},{7,71},{68,4},{69,5},{10,74},{1... | collective-permute-start | bytes 344072 | tf_op jit(solution)/shard_map/ppermute | solution.py:410
  85.7 0.9 collective-permute-done.28
  86.6 0.7 collective-permute-start.31
  87.3 1.3 %collective-permute-start.30 = (bf16[896,128]{1,0:T(8,128)(2,1)S(1)}, bf16[896,128]{1,0:T(8,128)(2,1)S(1)}, u32[]{:S(2)}, u32[]{:S(2)}) collective-permute-start(bf16[896,128]{1,0:T(8,128)(2,1)S(1)} %bitcast.54), channel_id=1, source_target_pairs={{0,2},{1,3},{66,64},{67,65},{4,6},{5,7},{70,68},{71,69},{8,10},{9,... | collective-permute-start | bytes 688136 | tf_op jit(solution)/shard_map/ppermute | solution.py:417
  88.6 1.3 %collective-permute-start.29 = (bf16[896,128]{1,0:T(8,128)(2,1)S(1)}, bf16[896,128]{1,0:T(8,128)(2,1)S(1)}, u32[]{:S(2)}, u32[]{:S(2)}) collective-permute-start(bf16[896,128]{1,0:T(8,128)(2,1)S(1)} %bitcast.55), channel_id=1, source_target_pairs={{0,1},{1,2},{66,67},{67,64},{4,5},{5,6},{70,71},{71,68},{8,9},{9,1... | collective-permute-start | bytes 688136 | tf_op jit(solution)/shard_map/ppermute | solution.py:417
  89.9 6.3 %collective-permute-done.30.row2 = bf16[896,128]{1,0:T(8,128)(2,1)S(1)} collective-permute-done((bf16[896,128]{1,0:T(8,128)(2,1)S(1)}, bf16[896,128]{1,0:T(8,128)(2,1)S(1)}, u32[]{:S(2)}, u32[]{:S(2)}) %collective-permute-start.30) | collective-permute-done | bytes 229408 | tf_op jit(solution)/shard_map/ppermute | solution.py:417
  96.2 2.5 %collective-permute-done.29.row1 = bf16[896,128]{1,0:T(8,128)(2,1)S(1)} collective-permute-done((bf16[896,128]{1,0:T(8,128)(2,1)S(1)}, bf16[896,128]{1,0:T(8,128)(2,1)S(1)}, u32[]{:S(2)}, u32[]{:S(2)}) %collective-permute-start.29) | collective-permute-done | bytes 229408 | tf_op jit(solution)/shard_map/ppermute | solution.py:417
  98.8 2.6 %shard_map.108 = (bf16[2,2,16,2048]{3,2,1,0:T(8,128)(2,1)S(1)}, bf16[2,2,16,2048]{3,2,1,0:T(8,128)(2,1)S(1)}, bf16[2,2,16,2048]{3,2,1,0:T(8,128)(2,1)S(1)}, bf16[2,2,16,2048]{3,2,1,0:T(8,128)(2,1)S(1)}) custom-call(s32[27]{0:T(128)S(1)} %concatenate.3.facts, bf16[224,2048]{1,0:T(8,128)(2,1)S(1)} %bitcast.52, ...), custom_call_target="tpu_custom_call" | custom-call | flops 1000000000 | bytes 4000000 | tf_op jit(solution)/shard_map/pallas_call | solution.py:354
  101.4 0.1 collective-permute-start.32
  101.5 0.9 collective-permute-start.33
  102.3 1.8 %collective-permute-start.34 = (bf16[2,2,16,2048]{3,2,1,0:T(8,128)(2,1)S(1)}, bf16[2,2,16,2048]{3,2,1,0:T(8,128)(2,1)S(1)}, u32[]{:S(2)}, u32[]{:S(2)}) collective-permute-start(bf16[2,2,16,2048]{3,2,1,0:T(8,128)(2,1)S(1)} %get-tuple-element.81), channel_id=1, source_target_pairs={{0,12},{4,0},{8,4},{12,8},{1,13},{5,1},{9,5},{13,9},{2,14},{6,2},{... | collective-permute-start | bytes 786440 | tf_op jit(solution)/shard_map/ppermute | solution.py:377
  104.1 12.4 %collective-permute-done.32 = bf16[2,2,16,2048]{3,2,1,0:T(8,128)(2,1)S(1)} collective-permute-done((bf16[2,2,16,2048]{3,2,1,0:T(8,128)(2,1)S(1)}, bf16[2,2,16,2048]{3,2,1,0:T(8,128)(2,1)S(1)}, u32[]{:S(2)}, u32[]{:S(2)}) %collective-permute-start.32) | collective-permute-done | bytes 262176 | tf_op jit(solution)/shard_map/ppermute | solution.py:377
  116.5 0.4 collective-permute-done.34
  117.0 0.1 fusion.10
  117.1 3.1 %collective-permute-start.35 = (bf16[16,2048]{1,0:T(8,128)(2,1)S(1)}, bf16[16,2048]{1,0:T(8,128)(2,1)S(1)}, u32[]{:S(2)}, u32[]{:S(2)}) collective-permute-start(bf16[16,2048]{1,0:T(8,128)(2,1)S(1)} %get-tuple-element.92), channel_id=1, source_target_pairs={{0,128},{128,0},{1,129},{129,1},{2,130},{130,2},{3,131},{131,3},{4... | collective-permute-start | bytes 196616 | tf_op jit(solution)/shard_map/ppermute | solution.py:424
  120.3 0.8 collective-permute-start.37
  121.1 1.8 %collective-permute-start.36 = (bf16[16,2048]{1,0:T(8,128)(2,1)S(1)}, bf16[16,2048]{1,0:T(8,128)(2,1)S(1)}, u32[]{:S(2)}, u32[]{:S(2)}) collective-permute-start(bf16[16,2048]{1,0:T(8,128)(2,1)S(1)} %get-tuple-element.94), channel_id=1, source_target_pairs={{0,160},{128,32},{32,128},{160,0},{16,176},{144,48},{48,144},{176,... | collective-permute-start | bytes 196616 | tf_op jit(solution)/shard_map/ppermute | solution.py:425
  122.9 1.6 %collective-permute-done.35 = bf16[16,2048]{1,0:T(8,128)(2,1)S(1)} collective-permute-done((bf16[16,2048]{1,0:T(8,128)(2,1)S(1)}, bf16[16,2048]{1,0:T(8,128)(2,1)S(1)}, u32[]{:S(2)}, u32[]{:S(2)}) %collective-permute-start.35) | collective-permute-done | bytes 65568 | tf_op jit(solution)/shard_map/ppermute | solution.py:424
  124.5 3.7 %collective-permute-done.37 = bf16[16,2048]{1,0:T(8,128)(2,1)S(1)} collective-permute-done((bf16[16,2048]{1,0:T(8,128)(2,1)S(1)}, bf16[16,2048]{1,0:T(8,128)(2,1)S(1)}, u32[]{:S(2)}, u32[]{:S(2)}) %collective-permute-start.37) | collective-permute-done | bytes 65568 | tf_op jit(solution)/shard_map/ppermute | solution.py:426
  128.1 0.7 fusion.2
  (41 shorter events, 0.2 us)
Async XLA Ops:
  0.6 9.1 %collective-permute-start.2 = (bf16[224,128]{1,0:T(8,128)(2,1)}, bf16[224,128]{1,0:T(8,128)(2,1)S(1)}, u32[]{:S(2)}, u32[]{:S(2)}) collective-permute-start(bf16[224,128]{1,0:T(8,128)(2,1)} %bitcast.59), channel_id=1, source_target_pairs={{0,48},{16,0},{32,16},{48,32},{1,49},{17,1},{33,17},{49,33},{2,50}... | collective-permute-start | bytes 172040 | tf_op jit(solution)/shard_map/ppermute | solution.py:377
  5.9 6.0 %collective-permute-start.1 = (bf16[224,128]{1,0:T(8,128)(2,1)}, bf16[224,128]{1,0:T(8,128)(2,1)S(1)}, u32[]{:S(2)}, u32[]{:S(2)}) collective-permute-start(bf16[224,128]{1,0:T(8,128)(2,1)} %bitcast.60), channel_id=1, source_target_pairs={{0,32},{16,48},{32,0},{48,16},{1,33},{17,49},{33,1},{49,17},{2,34}... | collective-permute-start | bytes 172040 | tf_op jit(solution)/shard_map/ppermute | solution.py:377
  5.9 6.0 %collective-permute-start = (bf16[224,128]{1,0:T(8,128)(2,1)}, bf16[224,128]{1,0:T(8,128)(2,1)S(1)}, u32[]{:S(2)}, u32[]{:S(2)}) collective-permute-start(bf16[224,128]{1,0:T(8,128)(2,1)} %bitcast.61), channel_id=1, source_target_pairs={{0,16},{16,32},{32,48},{48,0},{1,17},{17,33},{33,49},{49,1},{2,18}... | collective-permute-start | bytes 172040 | tf_op jit(solution)/shard_map/ppermute | solution.py:377
  6.3 6.3 %collective-permute-start.5 = (bf16[224,128]{1,0:T(8,128)(2,1)}, bf16[224,128]{1,0:T(8,128)(2,1)S(1)}, u32[]{:S(2)}, u32[]{:S(2)}) collective-permute-start(bf16[224,128]{1,0:T(8,128)(2,1)} %bitcast.63), channel_id=1, source_target_pairs={{0,48},{16,0},{32,16},{48,32},{1,49},{17,1},{33,17},{49,33},{2,50}... | collective-permute-start | bytes 172040 | tf_op jit(solution)/shard_map/ppermute | solution.py:377
  9.1 7.7 %collective-permute-start.4 = (bf16[224,128]{1,0:T(8,128)(2,1)}, bf16[224,128]{1,0:T(8,128)(2,1)S(1)}, u32[]{:S(2)}, u32[]{:S(2)}) collective-permute-start(bf16[224,128]{1,0:T(8,128)(2,1)} %bitcast.64), channel_id=1, source_target_pairs={{0,32},{16,48},{32,0},{48,16},{1,33},{17,49},{33,1},{49,17},{2,34}... | collective-permute-start | bytes 172040 | tf_op jit(solution)/shard_map/ppermute | solution.py:377
  9.7 7.1 %collective-permute-start.3 = (bf16[224,128]{1,0:T(8,128)(2,1)}, bf16[224,128]{1,0:T(8,128)(2,1)S(1)}, u32[]{:S(2)}, u32[]{:S(2)}) collective-permute-start(bf16[224,128]{1,0:T(8,128)(2,1)} %bitcast.65), channel_id=1, source_target_pairs={{0,16},{16,32},{32,48},{48,0},{1,17},{17,33},{33,49},{49,1},{2,18}... | collective-permute-start | bytes 172040 | tf_op jit(solution)/shard_map/ppermute | solution.py:377
  9.7 1.0 copy-start.1
  10.7 1.0 copy-start.2
  11.8 5.1 %copy-start.3 = (bf16[1,224,128]{2,1,0:T(8,128)(2,1)S(1)}, bf16[1,224,128]{2,1,0:T(8,128)(2,1)}, u32[]{:S(2)}) copy-start(bf16[1,224,128]{2,1,0:T(8,128)(2,1)} %param.9) | copy-start | bytes 172036
  16.8 4.3 %copy-start.4 = (bf16[1,224,128]{2,1,0:T(8,128)(2,1)S(1)}, bf16[1,224,128]{2,1,0:T(8,128)(2,1)}, u32[]{:S(2)}) copy-start(bf16[1,224,128]{2,1,0:T(8,128)(2,1)} %param.10) | copy-start | bytes 172036
  16.8 7.2 %collective-permute-start.6 = (bf16[4,224,128]{2,1,0:T(8,128)(2,1)S(1)}, bf16[4,224,128]{2,1,0:T(8,128)(2,1)S(1)}, u32[]{:S(2)}, u32[]{:S(2)}) collective-permute-start(bf16[4,224,128]{2,1,0:T(8,128)(2,1)S(1)} %shard_map.103.k0), channel_id=1, source_target_pairs={{0,4},{4,8},{8,12},{12,0},{1,5},{5,9},{9,13},{13,1},{2,6},{6,10},{... | collective-permute-start | bytes 688136 | tf_op jit(solution)/shard_map/ppermute | solution.py:377
  17.2 8.4 %collective-permute-start.8 = (bf16[4,224,128]{2,1,0:T(8,128)(2,1)S(1)}, bf16[4,224,128]{2,1,0:T(8,128)(2,1)S(1)}, u32[]{:S(2)}, u32[]{:S(2)}) collective-permute-start(bf16[4,224,128]{2,1,0:T(8,128)(2,1)S(1)} %shard_map.103.k0), channel_id=1, source_target_pairs={{0,12},{4,0},{8,4},{12,8},{1,13},{5,1},{9,5},{13,9},{2,14},{6,2},{... | collective-permute-start | bytes 688136 | tf_op jit(solution)/shard_map/ppermute | solution.py:377
  19.6 9.1 %collective-permute-start.7 = (bf16[4,224,128]{2,1,0:T(8,128)(2,1)S(1)}, bf16[4,224,128]{2,1,0:T(8,128)(2,1)S(1)}, u32[]{:S(2)}, u32[]{:S(2)}) collective-permute-start(bf16[4,224,128]{2,1,0:T(8,128)(2,1)S(1)} %shard_map.103.k0), channel_id=1, source_target_pairs={{0,8},{4,12},{8,0},{12,4},{1,9},{5,13},{9,1},{13,5},{2,10},{6,14},... | collective-permute-start | bytes 688136 | tf_op jit(solution)/shard_map/ppermute | solution.py:377
  20.3 0.7 copy-start.5
  20.3 0.7 copy-start.6
  21.1 11.9 %copy-start = (bf16[1,224,2048]{2,1,0:T(8,128)(2,1)S(1)}, bf16[1,224,2048]{2,1,0:T(8,128)(2,1)}, u32[]{:S(2)}) copy-start(bf16[1,224,2048]{2,1,0:T(8,128)(2,1)} %param.7) | copy-start | bytes 2752516
  24.0 16.5 %collective-permute-start.11 = (bf16[4,224,128]{2,1,0:T(8,128)(2,1)S(1)}, bf16[4,224,128]{2,1,0:T(8,128)(2,1)S(1)}, u32[]{:S(2)}, u32[]{:S(2)}) collective-permute-start(bf16[4,224,128]{2,1,0:T(8,128)(2,1)S(1)} %shard_map.104.v0), channel_id=1, source_target_pairs={{0,12},{4,0},{8,4},{12,8},{1,13},{5,1},{9,5},{13,9},{2,14},{6,2},{... | collective-permute-start | bytes 688136 | tf_op jit(solution)/shard_map/ppermute | solution.py:377
  24.0 16.8 %collective-permute-start.9 = (bf16[4,224,128]{2,1,0:T(8,128)(2,1)S(1)}, bf16[4,224,128]{2,1,0:T(8,128)(2,1)S(1)}, u32[]{:S(2)}, u32[]{:S(2)}) collective-permute-start(bf16[4,224,128]{2,1,0:T(8,128)(2,1)S(1)} %shard_map.104.v0), channel_id=1, source_target_pairs={{0,4},{4,8},{8,12},{12,0},{1,5},{5,9},{9,13},{13,1},{2,6},{6,10},{... | collective-permute-start | bytes 688136 | tf_op jit(solution)/shard_map/ppermute | solution.py:377
  28.7 9.0 %collective-permute-start.10 = (bf16[4,224,128]{2,1,0:T(8,128)(2,1)S(1)}, bf16[4,224,128]{2,1,0:T(8,128)(2,1)S(1)}, u32[]{:S(2)}, u32[]{:S(2)}) collective-permute-start(bf16[4,224,128]{2,1,0:T(8,128)(2,1)S(1)} %shard_map.104.v0), channel_id=1, source_target_pairs={{0,8},{4,12},{8,0},{12,4},{1,9},{5,13},{9,1},{13,5},{2,10},{6,14},... | collective-permute-start | bytes 688136 | tf_op jit(solution)/shard_map/ppermute | solution.py:377
  33.0 32.1 %collective-permute-start.24 = (bf16[224,2048]{1,0:T(8,128)(2,1)S(1)}, bf16[224,2048]{1,0:T(8,128)(2,1)S(1)}, u32[]{:S(2)}, u32[]{:S(2)}) collective-permute-start(bf16[224,2048]{1,0:T(8,128)(2,1)S(1)} %bitcast.50), channel_id=1, source_target_pairs={{0,16},{16,0},{32,48},{48,32},{1,17},{17,1},{33,49},{49,33},{2,18}... | collective-permute-start | bytes 2752520 | tf_op jit(solution)/shard_map/ppermute | solution.py:399
  34.3 12.1 %collective-permute-start.12 = (bf16[4,224,128]{2,1,0:T(8,128)(2,1)S(1)}, bf16[4,224,128]{2,1,0:T(8,128)(2,1)S(1)}, u32[]{:S(2)}, u32[]{:S(2)}) collective-permute-start(bf16[4,224,128]{2,1,0:T(8,128)(2,1)S(1)} %get-tuple-element.63), channel_id=1, source_target_pairs={{0,4},{4,8},{8,12},{12,0},{1,5},{5,9},{9,13},{13,1},{2,6},{6,10},{... | collective-permute-start | bytes 688136 | tf_op jit(solution)/shard_map/ppermute | solution.py:377
  37.7 12.5 %collective-permute-start.19 = (bf16[4,224,128]{2,1,0:T(8,128)(2,1)S(1)}, bf16[4,224,128]{2,1,0:T(8,128)(2,1)S(1)}, u32[]{:S(2)}, u32[]{:S(2)}) collective-permute-start(bf16[4,224,128]{2,1,0:T(8,128)(2,1)S(1)} %get-tuple-element.69), channel_id=1, source_target_pairs={{0,8},{4,12},{8,0},{12,4},{1,9},{5,13},{9,1},{13,5},{2,10},{6,14},... | collective-permute-start | bytes 688136 | tf_op jit(solution)/shard_map/ppermute | solution.py:377
  40.5 9.7 %collective-permute-start.20 = (bf16[4,224,128]{2,1,0:T(8,128)(2,1)S(1)}, bf16[4,224,128]{2,1,0:T(8,128)(2,1)S(1)}, u32[]{:S(2)}, u32[]{:S(2)}) collective-permute-start(bf16[4,224,128]{2,1,0:T(8,128)(2,1)S(1)} %get-tuple-element.70), channel_id=1, source_target_pairs={{0,12},{4,0},{8,4},{12,8},{1,13},{5,1},{9,5},{13,9},{2,14},{6,2},{... | collective-permute-start | bytes 688136 | tf_op jit(solution)/shard_map/ppermute | solution.py:377
  46.4 9.1 %collective-permute-start.13 = (bf16[4,224,128]{2,1,0:T(8,128)(2,1)S(1)}, bf16[4,224,128]{2,1,0:T(8,128)(2,1)S(1)}, u32[]{:S(2)}, u32[]{:S(2)}) collective-permute-start(bf16[4,224,128]{2,1,0:T(8,128)(2,1)S(1)} %get-tuple-element.65), channel_id=1, source_target_pairs={{0,4},{4,8},{8,12},{12,0},{1,5},{5,9},{9,13},{13,1},{2,6},{6,10},{... | collective-permute-start | bytes 688136 | tf_op jit(solution)/shard_map/ppermute | solution.py:377
  46.8 9.7 %collective-permute-start.14 = (bf16[4,224,128]{2,1,0:T(8,128)(2,1)S(1)}, bf16[4,224,128]{2,1,0:T(8,128)(2,1)S(1)}, u32[]{:S(2)}, u32[]{:S(2)}) collective-permute-start(bf16[4,224,128]{2,1,0:T(8,128)(2,1)S(1)} %get-tuple-element.66), channel_id=1, source_target_pairs={{0,8},{4,12},{8,0},{12,4},{1,9},{5,13},{9,1},{13,5},{2,10},{6,14},... | collective-permute-start | bytes 688136 | tf_op jit(solution)/shard_map/ppermute | solution.py:377
  50.2 15.0 %collective-permute-start.15 = (bf16[4,224,128]{2,1,0:T(8,128)(2,1)S(1)}, bf16[4,224,128]{2,1,0:T(8,128)(2,1)S(1)}, u32[]{:S(2)}, u32[]{:S(2)}) collective-permute-start(bf16[4,224,128]{2,1,0:T(8,128)(2,1)S(1)} %get-tuple-element.67), channel_id=1, source_target_pairs={{0,12},{4,0},{8,4},{12,8},{1,13},{5,1},{9,5},{13,9},{2,14},{6,2},{... | collective-permute-start | bytes 688136 | tf_op jit(solution)/shard_map/ppermute | solution.py:377
  50.3 17.2 %collective-permute-start.23 = (bf16[224,128]{1,0:T(8,128)(2,1)S(1)}, bf16[224,128]{1,0:T(8,128)(2,1)S(1)}, u32[]{:S(2)}, u32[]{:S(2)}) collective-permute-start(bf16[224,128]{1,0:T(8,128)(2,1)S(1)} %get-tuple-element.84), channel_id=1, source_target_pairs={{0,48},{16,0},{32,16},{48,32},{1,49},{17,1},{33,17},{49,33},{2,50}... | collective-permute-start | bytes 172040 | tf_op jit(solution)/shard_map/ppermute | solution.py:377
  55.6 14.4 %collective-permute-start.22 = (bf16[224,128]{1,0:T(8,128)(2,1)S(1)}, bf16[224,128]{1,0:T(8,128)(2,1)S(1)}, u32[]{:S(2)}, u32[]{:S(2)}) collective-permute-start(bf16[224,128]{1,0:T(8,128)(2,1)S(1)} %get-tuple-element.85), channel_id=1, source_target_pairs={{0,32},{16,48},{32,0},{48,16},{1,33},{17,49},{33,1},{49,17},{2,34}... | collective-permute-start | bytes 172040 | tf_op jit(solution)/shard_map/ppermute | solution.py:377
  56.5 13.5 %collective-permute-start.21 = (bf16[224,128]{1,0:T(8,128)(2,1)S(1)}, bf16[224,128]{1,0:T(8,128)(2,1)S(1)}, u32[]{:S(2)}, u32[]{:S(2)}) collective-permute-start(bf16[224,128]{1,0:T(8,128)(2,1)S(1)} %get-tuple-element.86), channel_id=1, source_target_pairs={{0,16},{16,32},{32,48},{48,0},{1,17},{17,33},{33,49},{49,1},{2,18}... | collective-permute-start | bytes 172040 | tf_op jit(solution)/shard_map/ppermute | solution.py:377
  65.1 33.6 %collective-permute-start.25 = (bf16[224,2048]{1,0:T(8,128)(2,1)S(1)}, bf16[224,2048]{1,0:T(8,128)(2,1)S(1)}, u32[]{:S(2)}, u32[]{:S(2)}) collective-permute-start(bf16[224,2048]{1,0:T(8,128)(2,1)S(1)} %bitcast.51), channel_id=1, source_target_pairs={{0,64},{64,0},{1,65},{65,1},{2,66},{66,2},{3,67},{67,3},{4,68},{68... | collective-permute-start | bytes 2752520 | tf_op jit(solution)/shard_map/ppermute | solution.py:405
  67.3 31.5 %collective-permute-start.26 = (bf16[224,2048]{1,0:T(8,128)(2,1)S(1)}, bf16[224,2048]{1,0:T(8,128)(2,1)S(1)}, u32[]{:S(2)}, u32[]{:S(2)}) collective-permute-start(bf16[224,2048]{1,0:T(8,128)(2,1)S(1)} %collective-permute-done.24.hid1), channel_id=1, source_target_pairs={{0,64},{64,0},{1,65},{65,1},{2,66},{66,2},{3,67},{67,3},{4,68},{68... | collective-permute-start | bytes 2752520 | tf_op jit(solution)/shard_map/ppermute | solution.py:405
  67.5 3.7 %collective-permute-start.18 = (bf16[224,128]{1,0:T(8,128)(2,1)S(1)}, bf16[224,128]{1,0:T(8,128)(2,1)S(1)}, u32[]{:S(2)}, u32[]{:S(2)}) collective-permute-start(bf16[224,128]{1,0:T(8,128)(2,1)S(1)} %get-tuple-element.88), channel_id=1, source_target_pairs={{0,48},{16,0},{32,16},{48,32},{1,49},{17,1},{33,17},{49,33},{2,50}... | collective-permute-start | bytes 172040 | tf_op jit(solution)/shard_map/ppermute | solution.py:377
  70.0 4.0 %collective-permute-start.17 = (bf16[224,128]{1,0:T(8,128)(2,1)S(1)}, bf16[224,128]{1,0:T(8,128)(2,1)S(1)}, u32[]{:S(2)}, u32[]{:S(2)}) collective-permute-start(bf16[224,128]{1,0:T(8,128)(2,1)S(1)} %get-tuple-element.89), channel_id=1, source_target_pairs={{0,32},{16,48},{32,0},{48,16},{1,33},{17,49},{33,1},{49,17},{2,34}... | collective-permute-start | bytes 172040 | tf_op jit(solution)/shard_map/ppermute | solution.py:377
  70.0 4.9 %collective-permute-start.16 = (bf16[224,128]{1,0:T(8,128)(2,1)S(1)}, bf16[224,128]{1,0:T(8,128)(2,1)S(1)}, u32[]{:S(2)}, u32[]{:S(2)}) collective-permute-start(bf16[224,128]{1,0:T(8,128)(2,1)S(1)} %get-tuple-element.90), channel_id=1, source_target_pairs={{0,16},{16,32},{32,48},{48,0},{1,17},{17,33},{33,49},{49,1},{2,18}... | collective-permute-start | bytes 172040 | tf_op jit(solution)/shard_map/ppermute | solution.py:377
  76.3 3.0 %collective-permute-start.27 = (bf16[224,128]{1,0:T(8,128)(2,1)S(1)}, bf16[224,128]{1,0:T(8,128)(2,1)S(1)}, u32[]{:S(2)}, u32[]{:S(2)}) collective-permute-start(bf16[224,128]{1,0:T(8,128)(2,1)S(1)} %get-tuple-element.77), channel_id=1, source_target_pairs={{0,16},{16,0},{32,48},{48,32},{1,17},{17,1},{33,49},{49,33},{2,18}... | collective-permute-start | bytes 172040 | tf_op jit(solution)/shard_map/ppermute | solution.py:406
  79.3 7.3 %collective-permute-start.28 = (bf16[2,224,128]{2,1,0:T(8,128)(2,1)S(1)}, bf16[2,224,128]{2,1,0:T(8,128)(2,1)S(1)}, u32[]{:S(2)}, u32[]{:S(2)}) collective-permute-start(bf16[2,224,128]{2,1,0:T(8,128)(2,1)S(1)} %get-tuple-element.96), channel_id=1, source_target_pairs={{2,66},{3,67},{64,0},{65,1},{6,70},{7,71},{68,4},{69,5},{10,74},{1... | collective-permute-start | bytes 344072 | tf_op jit(solution)/shard_map/ppermute | solution.py:410
  86.6 3.3 %collective-permute-start.31 = (bf16[896,128]{1,0:T(8,128)(2,1)S(1)}, bf16[896,128]{1,0:T(8,128)(2,1)S(1)}, u32[]{:S(2)}, u32[]{:S(2)}) collective-permute-start(bf16[896,128]{1,0:T(8,128)(2,1)S(1)} %bitcast.53), channel_id=1, source_target_pairs={{0,3},{1,0},{66,65},{67,66},{4,7},{5,4},{70,69},{71,70},{8,11},{9,... | collective-permute-start | bytes 688136 | tf_op jit(solution)/shard_map/ppermute | solution.py:417
  87.3 8.9 %collective-permute-start.30 = (bf16[896,128]{1,0:T(8,128)(2,1)S(1)}, bf16[896,128]{1,0:T(8,128)(2,1)S(1)}, u32[]{:S(2)}, u32[]{:S(2)}) collective-permute-start(bf16[896,128]{1,0:T(8,128)(2,1)S(1)} %bitcast.54), channel_id=1, source_target_pairs={{0,2},{1,3},{66,64},{67,65},{4,6},{5,7},{70,68},{71,69},{8,10},{9,... | collective-permute-start | bytes 688136 | tf_op jit(solution)/shard_map/ppermute | solution.py:417
  88.6 10.2 %collective-permute-start.29 = (bf16[896,128]{1,0:T(8,128)(2,1)S(1)}, bf16[896,128]{1,0:T(8,128)(2,1)S(1)}, u32[]{:S(2)}, u32[]{:S(2)}) collective-permute-start(bf16[896,128]{1,0:T(8,128)(2,1)S(1)} %bitcast.55), channel_id=1, source_target_pairs={{0,1},{1,2},{66,67},{67,64},{4,5},{5,6},{70,71},{71,68},{8,9},{9,1... | collective-permute-start | bytes 688136 | tf_op jit(solution)/shard_map/ppermute | solution.py:417
  101.4 15.2 %collective-permute-start.32 = (bf16[2,2,16,2048]{3,2,1,0:T(8,128)(2,1)S(1)}, bf16[2,2,16,2048]{3,2,1,0:T(8,128)(2,1)S(1)}, u32[]{:S(2)}, u32[]{:S(2)}) collective-permute-start(bf16[2,2,16,2048]{3,2,1,0:T(8,128)(2,1)S(1)} %get-tuple-element.79), channel_id=1, source_target_pairs={{0,4},{4,8},{8,12},{12,0},{1,5},{5,9},{9,13},{13,1},{2,6},{6,10},{... | collective-permute-start | bytes 786440 | tf_op jit(solution)/shard_map/ppermute | solution.py:377
  101.5 15.1 %collective-permute-start.33 = (bf16[2,2,16,2048]{3,2,1,0:T(8,128)(2,1)S(1)}, bf16[2,2,16,2048]{3,2,1,0:T(8,128)(2,1)S(1)}, u32[]{:S(2)}, u32[]{:S(2)}) collective-permute-start(bf16[2,2,16,2048]{3,2,1,0:T(8,128)(2,1)S(1)} %get-tuple-element.80), channel_id=1, source_target_pairs={{0,8},{4,12},{8,0},{12,4},{1,9},{5,13},{9,1},{13,5},{2,10},{6,14},... | collective-permute-start | bytes 786440 | tf_op jit(solution)/shard_map/ppermute | solution.py:377
  102.3 14.6 %collective-permute-start.34 = (bf16[2,2,16,2048]{3,2,1,0:T(8,128)(2,1)S(1)}, bf16[2,2,16,2048]{3,2,1,0:T(8,128)(2,1)S(1)}, u32[]{:S(2)}, u32[]{:S(2)}) collective-permute-start(bf16[2,2,16,2048]{3,2,1,0:T(8,128)(2,1)S(1)} %get-tuple-element.81), channel_id=1, source_target_pairs={{0,12},{4,0},{8,4},{12,8},{1,13},{5,1},{9,5},{13,9},{2,14},{6,2},{... | collective-permute-start | bytes 786440 | tf_op jit(solution)/shard_map/ppermute | solution.py:377
  117.1 7.3 %collective-permute-start.35 = (bf16[16,2048]{1,0:T(8,128)(2,1)S(1)}, bf16[16,2048]{1,0:T(8,128)(2,1)S(1)}, u32[]{:S(2)}, u32[]{:S(2)}) collective-permute-start(bf16[16,2048]{1,0:T(8,128)(2,1)S(1)} %get-tuple-element.92), channel_id=1, source_target_pairs={{0,128},{128,0},{1,129},{129,1},{2,130},{130,2},{3,131},{131,3},{4... | collective-permute-start | bytes 196616 | tf_op jit(solution)/shard_map/ppermute | solution.py:424
  120.3 7.9 %collective-permute-start.37 = (bf16[16,2048]{1,0:T(8,128)(2,1)S(1)}, bf16[16,2048]{1,0:T(8,128)(2,1)S(1)}, u32[]{:S(2)}, u32[]{:S(2)}) collective-permute-start(bf16[16,2048]{1,0:T(8,128)(2,1)S(1)} %get-tuple-element.93), channel_id=1, source_target_pairs={{0,32},{32,0},{16,48},{48,16},{1,33},{33,1},{17,49},{49,17},{2,34}... | collective-permute-start | bytes 196616 | tf_op jit(solution)/shard_map/ppermute | solution.py:426
  121.1 7.0 %collective-permute-start.36 = (bf16[16,2048]{1,0:T(8,128)(2,1)S(1)}, bf16[16,2048]{1,0:T(8,128)(2,1)S(1)}, u32[]{:S(2)}, u32[]{:S(2)}) collective-permute-start(bf16[16,2048]{1,0:T(8,128)(2,1)S(1)} %get-tuple-element.94), channel_id=1, source_target_pairs={{0,160},{128,32},{32,128},{160,0},{16,176},{144,48},{48,144},{176,... | collective-permute-start | bytes 196616 | tf_op jit(solution)/shard_map/ppermute | solution.py:425

commit v12 on v11

--- a/solution.py
+++ b/solution.py
@@ -326,7 +326,7 @@
 
 
 def product_kernel(
-    facts, hid0, hid1, hid2, hid3, row0, row1, row2, row3, out0, out1, out2, out3, acc
+    facts, hid0, hid1, hid2, hid3, row0, row2, row1, row3, out0, out1, out2, out3, acc
 ):
     my_zl, my_y, my_x, core, zh = (facts[DOCS + RANKS + i] for i in range(5))
     for j, row in enumerate((row0, row1, row2, row3)):
@@ -387,7 +387,7 @@
     vs = [vs] + [moved(vs if s != 2 else after(vs, *ks[2:]), "y", s) for s in (1, 2, 3)]
 
     def received(shares):
-        return [shares[0]] + [moved(shares[s], "y", s) for s in (1, 2, 3)]
+        return [shares[0]] + [moved(shares[s], "y", s) for s in (1, 3, 2)]
 
     def over_zl(got):
         parts = [add_up(*[g[a] for g in got]) for a in range(4)]
@@ -415,15 +415,15 @@
         ]
 
     rows = [rows] + [lax.ppermute(rows, ("co", "x"), along(j)) for j in (1, 2, 3)]
-    shares = received(weight_product(facts, *hidden, *rows))
+    shares = received(weight_product(facts, *hidden, rows[0], rows[2], rows[1], rows[3]))
     total = add_up(*shares)
     other_zl = [(0, 2), (2, 0), (1, 3), (3, 1)]
     both = [(a + 4 * c, b + 4 * (1 - c)) for a, b in other_zl for c in range(2)]
     grad_weight = add_up(
         total[0, 0],
+        lax.ppermute(total[0, 1].astype(BF), "zl", other_zl),
         lax.ppermute(total[1, 0].astype(BF), "zh", swap),
         lax.ppermute(total[1, 1].astype(BF), ("zh", "zl"), both),
-        lax.ppermute(total[0, 1].astype(BF), "zl", other_zl),
     )
     return dq[None], key_grads[None], value_grads[None], grad_weight
 

time: 129 us -> 132 us (1.023)
  starting transfers between devices: 63 us -> 65.6 us
    ppermute x1, waiting for transfers between devices: 0.01 us -> 4.72 us  [per_device(): lax.ppermute(total[1, 1].astype(BF), ('zh', 'zl'), both)]
    ppermute x27, waiting for transfers between devices: 31.1 us -> 26.9 us  [moved(): return lax.ppermute(value, axis, ring(shift))]
    ppermute x1, waiting for transfers between devices: 3.65 us -> 0.1 us  [per_device(): lax.ppermute(total[0, 1].astype(BF), 'zl', other_zl)]
    ppermute x1, starting transfers between devices: 1.28 us -> 4.81 us  [per_device(): beside = lax.ppermute(after(hidden, stats), 'zl', neighbour)]
    ppermute x1, starting transfers between devices: 3.11 us -> 0.5 us  [per_device(): lax.ppermute(total[1, 0].astype(BF), 'zh', swap)]
    ppermute x1, starting transfers between devices: 1.82 us -> 4.3 us  [per_device(): lax.ppermute(total[1, 1].astype(BF), ('zh', 'zl'), both)]
    ppermute x1, starting transfers between devices: 1.39 us -> 0.01 us  [per_device(): rows = jnp.stack([mine, lax.ppermute(sent, 'zl', neighbour)])]
    ppermute x1, waiting for transfers between devices: 1.64 us -> 3.03 us  [per_device(): rows = jnp.stack([mine, lax.ppermute(sent, 'zl', neighbour)])]
  transfers between devices with their start and end apart: 38 -> 38, of which waited for: 19 -> 18; matrix products, arithmetic and copies ran while one was open for 0% -> 0% of each run, Pallas kernels for 8% -> 8%
where the time goes in v12:
time: 132 us; the launch traced here: 131 us
  starting transfers between devices  65.6 us (50%)
  waiting for transfers between devices  47.6 us (36%)
  Pallas kernels  13.2 us (10%)
  local copies, waits for them, and re-layouts  2.82 us (2%)
    ppermute x27, starting transfers between devices, moved(): return lax.ppermute(value, axis, ring(shift))  43.6 us
    ppermute x27, waiting for transfers between devices, moved(): return lax.ppermute(value, axis, ring(shift))  26.9 us
    ppermute x3, waiting for transfers between devices, per_device(): lax.ppermute(rows, ('co', 'x'), along(j))  9.84 us
    ppermute x1, starting transfers between devices, per_device(): lax.ppermute(rows, ('co', 'x'), cross)  7.1 us
    pallas_call x1, Pallas kernels, backward(): pl.pallas_call(backward_kernel, out_shape=(jax.ShapeDtypeStruct((ROWS, HE...  5.6 us
    ppermute x1, starting transfers between devices, per_device(): beside = lax.ppermute(after(hidden, stats), 'zl', neighbour)  4.81 us
    ppermute x1, waiting for transfers between devices, per_device(): lax.ppermute(total[1, 1].astype(BF), ('zh', 'zl'), both)  4.72 us
    ppermute x1, starting transfers between devices, per_device(): lax.ppermute(total[1, 1].astype(BF), ('zh', 'zl'), both)  4.3 us
  transfers between devices with their start and end apart: 38, of which 18 were waited for; matrix products, arithmetic and copies ran while one was open for 0% of the time, Pallas kernels for 8%

profile of v12, /device:TPU:1, one launch (start us, length us, event | category | flops | bytes accessed | tf_op | source)
XLA Modules:
  0.0 131.2 jit_solution(264482235143035589)
XLA Ops:
  0.6 5.2 %collective-permute-start.2 = (bf16[224,128]{1,0:T(8,128)(2,1)}, bf16[224,128]{1,0:T(8,128)(2,1)S(1)}, u32[]{:S(2)}, u32[]{:S(2)}) collective-permute-start(bf16[224,128]{1,0:T(8,128)(2,1)} %bitcast.59), channel_id=1, source_target_pairs={{0,48},{16,0},{32,16},{48,32},{1,49},{17,1},{33,17},{49,33},{2,50}... | collective-permute-start | bytes 172040 | tf_op jit(solution)/shard_map/ppermute | solution.py:377
  5.9 0.4 collective-permute-start
  6.3 2.9 %collective-permute-start.5 = (bf16[224,128]{1,0:T(8,128)(2,1)}, bf16[224,128]{1,0:T(8,128)(2,1)S(1)}, u32[]{:S(2)}, u32[]{:S(2)}) collective-permute-start(bf16[224,128]{1,0:T(8,128)(2,1)} %bitcast.63), channel_id=1, source_target_pairs={{0,48},{16,0},{32,16},{48,32},{1,49},{17,1},{33,17},{49,33},{2,50}... | collective-permute-start | bytes 172040 | tf_op jit(solution)/shard_map/ppermute | solution.py:377
  9.1 0.6 collective-permute-start.4
  9.7 1.0 copy-done.1
  10.7 1.0 copy-done.2
  11.8 0.1 shard_map.102
  11.8 0.1 collective-permute-done.1.c2
  11.9 0.7 collective-permute-done.5.c3
  12.6 4.2 %collective-permute-done.4.c2 = bf16[224,128]{1,0:T(8,128)(2,1)S(1)} collective-permute-done((bf16[224,128]{1,0:T(8,128)(2,1)}, bf16[224,128]{1,0:T(8,128)(2,1)S(1)}, u32[]{:S(2)}, u32[]{:S(2)}) %collective-permute-start.4) | collective-permute-done | bytes 57376 | tf_op jit(solution)/shard_map/ppermute | solution.py:377
  16.8 0.4 collective-permute-start.6
  17.2 2.3 %collective-permute-start.8 = (bf16[4,224,128]{2,1,0:T(8,128)(2,1)S(1)}, bf16[4,224,128]{2,1,0:T(8,128)(2,1)S(1)}, u32[]{:S(2)}, u32[]{:S(2)}) collective-permute-start(bf16[4,224,128]{2,1,0:T(8,128)(2,1)S(1)} %shard_map.103.k0), channel_id=1, source_target_pairs={{0,12},{4,0},{8,4},{12,8},{1,13},{5,1},{9,5},{13,9},{2,14},{6,2},{... | collective-permute-start | bytes 688136 | tf_op jit(solution)/shard_map/ppermute | solution.py:377
  19.6 0.7 collective-permute-start.7
  20.3 0.7 copy-done.5
  21.0 0.0 copy-done.6
  21.0 0.1 concatenate.3.facts
  21.1 2.9 %collective-permute-done.6.k1 = bf16[4,224,128]{2,1,0:T(8,128)(2,1)S(1)} collective-permute-done((bf16[4,224,128]{2,1,0:T(8,128)(2,1)S(1)}, bf16[4,224,128]{2,1,0:T(8,128)(2,1)S(1)}, u32[]{:S(2)}, u32[]{:S(2)}) %collective-permute-start.6) | collective-permute-done | bytes 229408 | tf_op jit(solution)/shard_map/ppermute | solution.py:377
  24.0 1.5 %collective-permute-start.9 = (bf16[4,224,128]{2,1,0:T(8,128)(2,1)S(1)}, bf16[4,224,128]{2,1,0:T(8,128)(2,1)S(1)}, u32[]{:S(2)}, u32[]{:S(2)}) collective-permute-start(bf16[4,224,128]{2,1,0:T(8,128)(2,1)S(1)} %shard_map.104.v0), channel_id=1, source_target_pairs={{0,4},{4,8},{8,12},{12,0},{1,5},{5,9},{9,13},{13,1},{2,6},{6,10},{... | collective-permute-start | bytes 688136 | tf_op jit(solution)/shard_map/ppermute | solution.py:377
  25.5 0.1 collective-permute-done.8.k3
  25.6 3.1 %collective-permute-done.7.k2 = bf16[4,224,128]{2,1,0:T(8,128)(2,1)S(1)} collective-permute-done((bf16[4,224,128]{2,1,0:T(8,128)(2,1)S(1)}, bf16[4,224,128]{2,1,0:T(8,128)(2,1)S(1)}, u32[]{:S(2)}, u32[]{:S(2)}) %collective-permute-start.7) | collective-permute-done | bytes 229408 | tf_op jit(solution)/shard_map/ppermute | solution.py:377
  28.7 0.7 collective-permute-start.10
  29.4 3.6 %shard_map.105 = (f32[2,1,896]{2,1,0:T(1,128)S(1)}, bf16[4,224,128]{2,1,0:T(8,128)(2,1)S(1)}, bf16[4,224,128]{2,1,0:T(8,128)(2,1)S(1)}, bf16[4,224,128]{2,1,0:T(8,128)(2,1)S(1)}, bf16[4,224,128]{2,1,0:T(8,128)(2,1)S(1)}) custom-call(s32[27]{0:T(128)S(1)} %concatenate.3.facts, bf16[224,1024]{1,0:T(8,128)(2,1)S(1)} %get-tuple-element.45.q_ref, ...), custom_call_target="tpu_custom_call" | custom-call | flops 3000000000 | bytes 4000000 | tf_op jit(solution)/shard_map/pallas_call | solution.py:211
  33.0 4.8 %collective-permute-start.24 = (bf16[224,2048]{1,0:T(8,128)(2,1)S(1)}, bf16[224,2048]{1,0:T(8,128)(2,1)S(1)}, u32[]{:S(2)}, u32[]{:S(2)}) collective-permute-start(bf16[224,2048]{1,0:T(8,128)(2,1)S(1)} %bitcast.50), channel_id=1, source_target_pairs={{0,16},{16,0},{32,48},{48,32},{1,17},{17,1},{33,49},{49,33},{2,18}... | collective-permute-start | bytes 2752520 | tf_op jit(solution)/shard_map/ppermute | solution.py:399
  37.9 2.7 %collective-permute-start.19 = (bf16[4,224,128]{2,1,0:T(8,128)(2,1)S(1)}, bf16[4,224,128]{2,1,0:T(8,128)(2,1)S(1)}, u32[]{:S(2)}, u32[]{:S(2)}) collective-permute-start(bf16[4,224,128]{2,1,0:T(8,128)(2,1)S(1)} %get-tuple-element.69), channel_id=1, source_target_pairs={{0,12},{4,0},{8,4},{12,8},{1,13},{5,1},{9,5},{13,9},{2,14},{6,2},{... | collective-permute-start | bytes 688136 | tf_op jit(solution)/shard_map/ppermute | solution.py:377
  40.6 5.6 %shard_map.106 = (bf16[224,1024]{1,0:T(8,128)(2,1)}, bf16[4,224,128]{2,1,0:T(8,128)(2,1)S(1)}, bf16[4,224,128]{2,1,0:T(8,128)(2,1)S(1)}, bf16[4,224,128]{2,1,0:T(8,128)(2,1)S(1)}, bf16[4,224,128]{2,1,0:T(8,128)(2,1)S(1)}) custom-call(s32[27]{0:T(128)S(1)} %concatenate.3.facts, bf16[224,1024]{1,0:T(8,128)(2,1)S(1)} %get-tuple-element.45.q_ref, ...), custom_call_target="tpu_custom_call" | custom-call | flops 5000000000 | bytes 5000000 | tf_op jit(solution)/shard_map/pallas_call | solution.py:230
  46.2 0.0 collective-permute-start.13
  46.2 5.7 %collective-permute-start.14 = (bf16[4,224,128]{2,1,0:T(8,128)(2,1)S(1)}, bf16[4,224,128]{2,1,0:T(8,128)(2,1)S(1)}, u32[]{:S(2)}, u32[]{:S(2)}) collective-permute-start(bf16[4,224,128]{2,1,0:T(8,128)(2,1)S(1)} %get-tuple-element.66), channel_id=1, source_target_pairs={{0,12},{4,0},{8,4},{12,8},{1,13},{5,1},{9,5},{13,9},{2,14},{6,2},{... | collective-permute-start | bytes 688136 | tf_op jit(solution)/shard_map/ppermute | solution.py:377
  51.9 1.2 collective-permute-start.15
  53.0 0.1 fusion.8
  53.2 2.4 %collective-permute-start.23 = (bf16[224,128]{1,0:T(8,128)(2,1)S(1)}, bf16[224,128]{1,0:T(8,128)(2,1)S(1)}, u32[]{:S(2)}, u32[]{:S(2)}) collective-permute-start(bf16[224,128]{1,0:T(8,128)(2,1)S(1)} %get-tuple-element.84), channel_id=1, source_target_pairs={{0,48},{16,0},{32,16},{48,32},{1,49},{17,1},{33,17},{49,33},{2,50}... | collective-permute-start | bytes 172040 | tf_op jit(solution)/shard_map/ppermute | solution.py:377
  55.5 1.0 collective-permute-start.22
  56.5 0.0 collective-permute-done.14
  56.5 9.3 %collective-permute-start.21 = (bf16[224,128]{1,0:T(8,128)(2,1)S(1)}, bf16[224,128]{1,0:T(8,128)(2,1)S(1)}, u32[]{:S(2)}, u32[]{:S(2)}) collective-permute-start(bf16[224,128]{1,0:T(8,128)(2,1)S(1)} %get-tuple-element.86), channel_id=1, source_target_pairs={{0,16},{16,32},{32,48},{48,0},{1,17},{17,33},{33,49},{49,1},{2,18}... | collective-permute-start | bytes 172040 | tf_op jit(solution)/shard_map/ppermute | solution.py:377
  65.9 1.0 collective-permute-start.25
  66.8 0.1 collective-permute-start.26
  66.9 0.1 fusion.5
  67.1 2.3 %collective-permute-start.18 = (bf16[224,128]{1,0:T(8,128)(2,1)S(1)}, bf16[224,128]{1,0:T(8,128)(2,1)S(1)}, u32[]{:S(2)}, u32[]{:S(2)}) collective-permute-start(bf16[224,128]{1,0:T(8,128)(2,1)S(1)} %get-tuple-element.88), channel_id=1, source_target_pairs={{0,48},{16,0},{32,16},{48,32},{1,49},{17,1},{33,17},{49,33},{2,50}... | collective-permute-start | bytes 172040 | tf_op jit(solution)/shard_map/ppermute | solution.py:377
  69.3 0.7 collective-permute-start.17
  70.0 0.2 collective-permute-done.21.refs_5_
  70.3 1.0 collective-permute-start.16
  71.3 1.3 collective-permute-done.18.refs_3_
  72.5 1.9 %collective-permute-done.17.refs_2_ = bf16[224,128]{1,0:T(8,128)(2,1)S(1)} collective-permute-done((bf16[224,128]{1,0:T(8,128)(2,1)S(1)}, bf16[224,128]{1,0:T(8,128)(2,1)S(1)}, u32[]{:S(2)}, u32[]{:S(2)}) %collective-permute-start.17) | collective-permute-done | bytes 57376 | tf_op jit(solution)/shard_map/ppermute | solution.py:377
  74.4 0.7 collective-permute-done.16.refs_1_
  75.1 1.3 %shard_map.107 = (bf16[224,128]{1,0:T(8,128)(2,1)}, bf16[224,128]{1,0:T(8,128)(2,1)}, bf16[224,128]{1,0:T(8,128)(2,1)S(1)}, bf16[224,128]{1,0:T(8,128)(2,1)S(1)}) custom-call(s32[27]{0:T(128)S(1)} %concatenate.3.facts, f32[224,128]{1,0:T(8,128)S(1)} %get-tuple-element.91.refs_0_, bf16[224,128]{1,0:T(8,128)(2,1)S(1)} %collective-permute-done.16.refs_1_, ...), custom_call_target="tpu_custom_call" | custom-call | tf_op jit(solution)/shard_map/pallas_call | solution.py:319
  76.4 3.0 %collective-permute-done.27 = bf16[224,128]{1,0:T(8,128)(2,1)S(1)} collective-permute-done((bf16[224,128]{1,0:T(8,128)(2,1)S(1)}, bf16[224,128]{1,0:T(8,128)(2,1)S(1)}, u32[]{:S(2)}, u32[]{:S(2)}) %collective-permute-start.27) | collective-permute-done | bytes 57376 | tf_op jit(solution)/shard_map/ppermute | solution.py:406
  79.5 7.1 %collective-permute-start.28 = (bf16[2,224,128]{2,1,0:T(8,128)(2,1)S(1)}, bf16[2,224,128]{2,1,0:T(8,128)(2,1)S(1)}, u32[]{:S(2)}, u32[]{:S(2)}) collective-permute-start(bf16[2,224,128]{2,1,0:T(8,128)(2,1)S(1)} %get-tuple-element.96), channel_id=1, source_target_pairs={{2,66},{3,67},{64,0},{65,1},{6,70},{7,71},{68,4},{69,5},{10,74},{1... | collective-permute-start | bytes 344072 | tf_op jit(solution)/shard_map/ppermute | solution.py:410
  86.6 0.9 collective-permute-done.28
  87.5 0.7 collective-permute-start.31
  88.2 1.3 collective-permute-start.30
  89.5 1.3 collective-permute-start.29
  90.8 6.2 %collective-permute-done.30.row1 = bf16[896,128]{1,0:T(8,128)(2,1)S(1)} collective-permute-done((bf16[896,128]{1,0:T(8,128)(2,1)S(1)}, bf16[896,128]{1,0:T(8,128)(2,1)S(1)}, u32[]{:S(2)}, u32[]{:S(2)}) %collective-permute-start.30) | collective-permute-done | bytes 229408 | tf_op jit(solution)/shard_map/ppermute | solution.py:417
  97.1 3.6 %collective-permute-done.29.row2 = bf16[896,128]{1,0:T(8,128)(2,1)S(1)} collective-permute-done((bf16[896,128]{1,0:T(8,128)(2,1)S(1)}, bf16[896,128]{1,0:T(8,128)(2,1)S(1)}, u32[]{:S(2)}, u32[]{:S(2)}) %collective-permute-start.29) | collective-permute-done | bytes 229408 | tf_op jit(solution)/shard_map/ppermute | solution.py:417
  100.7 2.6 %shard_map.108 = (bf16[2,2,16,2048]{3,2,1,0:T(8,128)(2,1)S(1)}, bf16[2,2,16,2048]{3,2,1,0:T(8,128)(2,1)S(1)}, bf16[2,2,16,2048]{3,2,1,0:T(8,128)(2,1)S(1)}, bf16[2,2,16,2048]{3,2,1,0:T(8,128)(2,1)S(1)}) custom-call(s32[27]{0:T(128)S(1)} %concatenate.3.facts, bf16[224,2048]{1,0:T(8,128)(2,1)S(1)} %bitcast.52, ...), custom_call_target="tpu_custom_call" | custom-call | flops 1000000000 | bytes 4000000 | tf_op jit(solution)/shard_map/pallas_call | solution.py:354
  103.3 0.1 collective-permute-start.32
  103.4 2.7 %collective-permute-start.33 = (bf16[2,2,16,2048]{3,2,1,0:T(8,128)(2,1)S(1)}, bf16[2,2,16,2048]{3,2,1,0:T(8,128)(2,1)S(1)}, u32[]{:S(2)}, u32[]{:S(2)}) collective-permute-start(bf16[2,2,16,2048]{3,2,1,0:T(8,128)(2,1)S(1)} %get-tuple-element.80), channel_id=1, source_target_pairs={{0,12},{4,0},{8,4},{12,8},{1,13},{5,1},{9,5},{13,9},{2,14},{6,2},{... | collective-permute-start | bytes 786440 | tf_op jit(solution)/shard_map/ppermute | solution.py:377
  106.0 11.7 %collective-permute-done.32 = bf16[2,2,16,2048]{3,2,1,0:T(8,128)(2,1)S(1)} collective-permute-done((bf16[2,2,16,2048]{3,2,1,0:T(8,128)(2,1)S(1)}, bf16[2,2,16,2048]{3,2,1,0:T(8,128)(2,1)S(1)}, u32[]{:S(2)}, u32[]{:S(2)}) %collective-permute-start.32) | collective-permute-done | bytes 262176 | tf_op jit(solution)/shard_map/ppermute | solution.py:377
  117.7 0.1 fusion.10
  117.9 0.9 collective-permute-start.35
  118.8 4.3 %collective-permute-start.37 = (bf16[16,2048]{1,0:T(8,128)(2,1)S(1)}, bf16[16,2048]{1,0:T(8,128)(2,1)S(1)}, u32[]{:S(2)}, u32[]{:S(2)}) collective-permute-start(bf16[16,2048]{1,0:T(8,128)(2,1)S(1)} %get-tuple-element.93), channel_id=1, source_target_pairs={{0,160},{128,32},{32,128},{160,0},{16,176},{144,48},{48,144},{176,... | collective-permute-start | bytes 196616 | tf_op jit(solution)/shard_map/ppermute | solution.py:426
  123.1 0.5 collective-permute-start.36
  123.6 0.1 collective-permute-done.35
  123.7 4.7 %collective-permute-done.37 = bf16[16,2048]{1,0:T(8,128)(2,1)S(1)} collective-permute-done((bf16[16,2048]{1,0:T(8,128)(2,1)S(1)}, bf16[16,2048]{1,0:T(8,128)(2,1)S(1)}, u32[]{:S(2)}, u32[]{:S(2)}) %collective-permute-start.37) | collective-permute-done | bytes 65568 | tf_op jit(solution)/shard_map/ppermute | solution.py:426
  128.5 2.0 %collective-permute-done.36 = bf16[16,2048]{1,0:T(8,128)(2,1)S(1)} collective-permute-done((bf16[16,2048]{1,0:T(8,128)(2,1)S(1)}, bf16[16,2048]{1,0:T(8,128)(2,1)S(1)}, u32[]{:S(2)}, u32[]{:S(2)}) %collective-permute-start.36) | collective-permute-done | bytes 65568 | tf_op jit(solution)/shard_map/ppermute | solution.py:425
  130.5 0.7 fusion.2
  (41 shorter events, 0.2 us)
Async XLA Ops:
  0.6 9.1 %collective-permute-start.2 = (bf16[224,128]{1,0:T(8,128)(2,1)}, bf16[224,128]{1,0:T(8,128)(2,1)S(1)}, u32[]{:S(2)}, u32[]{:S(2)}) collective-permute-start(bf16[224,128]{1,0:T(8,128)(2,1)} %bitcast.59), channel_id=1, source_target_pairs={{0,48},{16,0},{32,16},{48,32},{1,49},{17,1},{33,17},{49,33},{2,50}... | collective-permute-start | bytes 172040 | tf_op jit(solution)/shard_map/ppermute | solution.py:377
  5.9 6.0 %collective-permute-start.1 = (bf16[224,128]{1,0:T(8,128)(2,1)}, bf16[224,128]{1,0:T(8,128)(2,1)S(1)}, u32[]{:S(2)}, u32[]{:S(2)}) collective-permute-start(bf16[224,128]{1,0:T(8,128)(2,1)} %bitcast.60), channel_id=1, source_target_pairs={{0,32},{16,48},{32,0},{48,16},{1,33},{17,49},{33,1},{49,17},{2,34}... | collective-permute-start | bytes 172040 | tf_op jit(solution)/shard_map/ppermute | solution.py:377
  5.9 6.0 %collective-permute-start = (bf16[224,128]{1,0:T(8,128)(2,1)}, bf16[224,128]{1,0:T(8,128)(2,1)S(1)}, u32[]{:S(2)}, u32[]{:S(2)}) collective-permute-start(bf16[224,128]{1,0:T(8,128)(2,1)} %bitcast.61), channel_id=1, source_target_pairs={{0,16},{16,32},{32,48},{48,0},{1,17},{17,33},{33,49},{49,1},{2,18}... | collective-permute-start | bytes 172040 | tf_op jit(solution)/shard_map/ppermute | solution.py:377
  6.3 6.3 %collective-permute-start.5 = (bf16[224,128]{1,0:T(8,128)(2,1)}, bf16[224,128]{1,0:T(8,128)(2,1)S(1)}, u32[]{:S(2)}, u32[]{:S(2)}) collective-permute-start(bf16[224,128]{1,0:T(8,128)(2,1)} %bitcast.63), channel_id=1, source_target_pairs={{0,48},{16,0},{32,16},{48,32},{1,49},{17,1},{33,17},{49,33},{2,50}... | collective-permute-start | bytes 172040 | tf_op jit(solution)/shard_map/ppermute | solution.py:377
  9.1 7.7 %collective-permute-start.4 = (bf16[224,128]{1,0:T(8,128)(2,1)}, bf16[224,128]{1,0:T(8,128)(2,1)S(1)}, u32[]{:S(2)}, u32[]{:S(2)}) collective-permute-start(bf16[224,128]{1,0:T(8,128)(2,1)} %bitcast.64), channel_id=1, source_target_pairs={{0,32},{16,48},{32,0},{48,16},{1,33},{17,49},{33,1},{49,17},{2,34}... | collective-permute-start | bytes 172040 | tf_op jit(solution)/shard_map/ppermute | solution.py:377
  9.7 7.1 %collective-permute-start.3 = (bf16[224,128]{1,0:T(8,128)(2,1)}, bf16[224,128]{1,0:T(8,128)(2,1)S(1)}, u32[]{:S(2)}, u32[]{:S(2)}) collective-permute-start(bf16[224,128]{1,0:T(8,128)(2,1)} %bitcast.65), channel_id=1, source_target_pairs={{0,16},{16,32},{32,48},{48,0},{1,17},{17,33},{33,49},{49,1},{2,18}... | collective-permute-start | bytes 172040 | tf_op jit(solution)/shard_map/ppermute | solution.py:377
  9.7 1.0 copy-start.1
  10.7 1.0 copy-start.2
  11.8 5.1 %copy-start.3 = (bf16[1,224,128]{2,1,0:T(8,128)(2,1)S(1)}, bf16[1,224,128]{2,1,0:T(8,128)(2,1)}, u32[]{:S(2)}) copy-start(bf16[1,224,128]{2,1,0:T(8,128)(2,1)} %param.9) | copy-start | bytes 172036
  16.8 4.3 %copy-start.4 = (bf16[1,224,128]{2,1,0:T(8,128)(2,1)S(1)}, bf16[1,224,128]{2,1,0:T(8,128)(2,1)}, u32[]{:S(2)}) copy-start(bf16[1,224,128]{2,1,0:T(8,128)(2,1)} %param.10) | copy-start | bytes 172036
  16.8 7.2 %collective-permute-start.6 = (bf16[4,224,128]{2,1,0:T(8,128)(2,1)S(1)}, bf16[4,224,128]{2,1,0:T(8,128)(2,1)S(1)}, u32[]{:S(2)}, u32[]{:S(2)}) collective-permute-start(bf16[4,224,128]{2,1,0:T(8,128)(2,1)S(1)} %shard_map.103.k0), channel_id=1, source_target_pairs={{0,4},{4,8},{8,12},{12,0},{1,5},{5,9},{9,13},{13,1},{2,6},{6,10},{... | collective-permute-start | bytes 688136 | tf_op jit(solution)/shard_map/ppermute | solution.py:377
  17.2 8.4 %collective-permute-start.8 = (bf16[4,224,128]{2,1,0:T(8,128)(2,1)S(1)}, bf16[4,224,128]{2,1,0:T(8,128)(2,1)S(1)}, u32[]{:S(2)}, u32[]{:S(2)}) collective-permute-start(bf16[4,224,128]{2,1,0:T(8,128)(2,1)S(1)} %shard_map.103.k0), channel_id=1, source_target_pairs={{0,12},{4,0},{8,4},{12,8},{1,13},{5,1},{9,5},{13,9},{2,14},{6,2},{... | collective-permute-start | bytes 688136 | tf_op jit(solution)/shard_map/ppermute | solution.py:377
  19.6 9.1 %collective-permute-start.7 = (bf16[4,224,128]{2,1,0:T(8,128)(2,1)S(1)}, bf16[4,224,128]{2,1,0:T(8,128)(2,1)S(1)}, u32[]{:S(2)}, u32[]{:S(2)}) collective-permute-start(bf16[4,224,128]{2,1,0:T(8,128)(2,1)S(1)} %shard_map.103.k0), channel_id=1, source_target_pairs={{0,8},{4,12},{8,0},{12,4},{1,9},{5,13},{9,1},{13,5},{2,10},{6,14},... | collective-permute-start | bytes 688136 | tf_op jit(solution)/shard_map/ppermute | solution.py:377
  20.3 0.7 copy-start.5
  20.3 0.7 copy-start.6
  21.1 11.9 %copy-start = (bf16[1,224,2048]{2,1,0:T(8,128)(2,1)S(1)}, bf16[1,224,2048]{2,1,0:T(8,128)(2,1)}, u32[]{:S(2)}) copy-start(bf16[1,224,2048]{2,1,0:T(8,128)(2,1)} %param.7) | copy-start | bytes 2752516
  24.0 16.5 %collective-permute-start.11 = (bf16[4,224,128]{2,1,0:T(8,128)(2,1)S(1)}, bf16[4,224,128]{2,1,0:T(8,128)(2,1)S(1)}, u32[]{:S(2)}, u32[]{:S(2)}) collective-permute-start(bf16[4,224,128]{2,1,0:T(8,128)(2,1)S(1)} %shard_map.104.v0), channel_id=1, source_target_pairs={{0,12},{4,0},{8,4},{12,8},{1,13},{5,1},{9,5},{13,9},{2,14},{6,2},{... | collective-permute-start | bytes 688136 | tf_op jit(solution)/shard_map/ppermute | solution.py:377
  24.0 16.5 %collective-permute-start.9 = (bf16[4,224,128]{2,1,0:T(8,128)(2,1)S(1)}, bf16[4,224,128]{2,1,0:T(8,128)(2,1)S(1)}, u32[]{:S(2)}, u32[]{:S(2)}) collective-permute-start(bf16[4,224,128]{2,1,0:T(8,128)(2,1)S(1)} %shard_map.104.v0), channel_id=1, source_target_pairs={{0,4},{4,8},{8,12},{12,0},{1,5},{5,9},{9,13},{13,1},{2,6},{6,10},{... | collective-permute-start | bytes 688136 | tf_op jit(solution)/shard_map/ppermute | solution.py:377
  28.7 9.1 %collective-permute-start.10 = (bf16[4,224,128]{2,1,0:T(8,128)(2,1)S(1)}, bf16[4,224,128]{2,1,0:T(8,128)(2,1)S(1)}, u32[]{:S(2)}, u32[]{:S(2)}) collective-permute-start(bf16[4,224,128]{2,1,0:T(8,128)(2,1)S(1)} %shard_map.104.v0), channel_id=1, source_target_pairs={{0,8},{4,12},{8,0},{12,4},{1,9},{5,13},{9,1},{13,5},{2,10},{6,14},... | collective-permute-start | bytes 688136 | tf_op jit(solution)/shard_map/ppermute | solution.py:377
  33.0 32.8 %collective-permute-start.24 = (bf16[224,2048]{1,0:T(8,128)(2,1)S(1)}, bf16[224,2048]{1,0:T(8,128)(2,1)S(1)}, u32[]{:S(2)}, u32[]{:S(2)}) collective-permute-start(bf16[224,2048]{1,0:T(8,128)(2,1)S(1)} %bitcast.50), channel_id=1, source_target_pairs={{0,16},{16,0},{32,48},{48,32},{1,17},{17,1},{33,49},{49,33},{2,18}... | collective-permute-start | bytes 2752520 | tf_op jit(solution)/shard_map/ppermute | solution.py:399
  37.9 8.3 %collective-permute-start.12 = (bf16[4,224,128]{2,1,0:T(8,128)(2,1)S(1)}, bf16[4,224,128]{2,1,0:T(8,128)(2,1)S(1)}, u32[]{:S(2)}, u32[]{:S(2)}) collective-permute-start(bf16[4,224,128]{2,1,0:T(8,128)(2,1)S(1)} %get-tuple-element.63), channel_id=1, source_target_pairs={{0,4},{4,8},{8,12},{12,0},{1,5},{5,9},{9,13},{13,1},{2,6},{6,10},{... | collective-permute-start | bytes 688136 | tf_op jit(solution)/shard_map/ppermute | solution.py:377
  37.9 14.0 %collective-permute-start.19 = (bf16[4,224,128]{2,1,0:T(8,128)(2,1)S(1)}, bf16[4,224,128]{2,1,0:T(8,128)(2,1)S(1)}, u32[]{:S(2)}, u32[]{:S(2)}) collective-permute-start(bf16[4,224,128]{2,1,0:T(8,128)(2,1)S(1)} %get-tuple-element.69), channel_id=1, source_target_pairs={{0,12},{4,0},{8,4},{12,8},{1,13},{5,1},{9,5},{13,9},{2,14},{6,2},{... | collective-permute-start | bytes 688136 | tf_op jit(solution)/shard_map/ppermute | solution.py:377
  40.5 12.5 %collective-permute-start.20 = (bf16[4,224,128]{2,1,0:T(8,128)(2,1)S(1)}, bf16[4,224,128]{2,1,0:T(8,128)(2,1)S(1)}, u32[]{:S(2)}, u32[]{:S(2)}) collective-permute-start(bf16[4,224,128]{2,1,0:T(8,128)(2,1)S(1)} %get-tuple-element.70), channel_id=1, source_target_pairs={{0,8},{4,12},{8,0},{12,4},{1,9},{5,13},{9,1},{13,5},{2,10},{6,14},... | collective-permute-start | bytes 688136 | tf_op jit(solution)/shard_map/ppermute | solution.py:377
  46.2 9.4 %collective-permute-start.13 = (bf16[4,224,128]{2,1,0:T(8,128)(2,1)S(1)}, bf16[4,224,128]{2,1,0:T(8,128)(2,1)S(1)}, u32[]{:S(2)}, u32[]{:S(2)}) collective-permute-start(bf16[4,224,128]{2,1,0:T(8,128)(2,1)S(1)} %get-tuple-element.65), channel_id=1, source_target_pairs={{0,4},{4,8},{8,12},{12,0},{1,5},{5,9},{9,13},{13,1},{2,6},{6,10},{... | collective-permute-start | bytes 688136 | tf_op jit(solution)/shard_map/ppermute | solution.py:377
  46.2 10.3 %collective-permute-start.14 = (bf16[4,224,128]{2,1,0:T(8,128)(2,1)S(1)}, bf16[4,224,128]{2,1,0:T(8,128)(2,1)S(1)}, u32[]{:S(2)}, u32[]{:S(2)}) collective-permute-start(bf16[4,224,128]{2,1,0:T(8,128)(2,1)S(1)} %get-tuple-element.66), channel_id=1, source_target_pairs={{0,12},{4,0},{8,4},{12,8},{1,13},{5,1},{9,5},{13,9},{2,14},{6,2},{... | collective-permute-start | bytes 688136 | tf_op jit(solution)/shard_map/ppermute | solution.py:377
  51.9 14.0 %collective-permute-start.15 = (bf16[4,224,128]{2,1,0:T(8,128)(2,1)S(1)}, bf16[4,224,128]{2,1,0:T(8,128)(2,1)S(1)}, u32[]{:S(2)}, u32[]{:S(2)}) collective-permute-start(bf16[4,224,128]{2,1,0:T(8,128)(2,1)S(1)} %get-tuple-element.67), channel_id=1, source_target_pairs={{0,8},{4,12},{8,0},{12,4},{1,9},{5,13},{9,1},{13,5},{2,10},{6,14},... | collective-permute-start | bytes 688136 | tf_op jit(solution)/shard_map/ppermute | solution.py:377
  53.2 13.9 %collective-permute-start.23 = (bf16[224,128]{1,0:T(8,128)(2,1)S(1)}, bf16[224,128]{1,0:T(8,128)(2,1)S(1)}, u32[]{:S(2)}, u32[]{:S(2)}) collective-permute-start(bf16[224,128]{1,0:T(8,128)(2,1)S(1)} %get-tuple-element.84), channel_id=1, source_target_pairs={{0,48},{16,0},{32,16},{48,32},{1,49},{17,1},{33,17},{49,33},{2,50}... | collective-permute-start | bytes 172040 | tf_op jit(solution)/shard_map/ppermute | solution.py:377
  55.5 13.8 %collective-permute-start.22 = (bf16[224,128]{1,0:T(8,128)(2,1)S(1)}, bf16[224,128]{1,0:T(8,128)(2,1)S(1)}, u32[]{:S(2)}, u32[]{:S(2)}) collective-permute-start(bf16[224,128]{1,0:T(8,128)(2,1)S(1)} %get-tuple-element.85), channel_id=1, source_target_pairs={{0,32},{16,48},{32,0},{48,16},{1,33},{17,49},{33,1},{49,17},{2,34}... | collective-permute-start | bytes 172040 | tf_op jit(solution)/shard_map/ppermute | solution.py:377
  56.5 13.7 %collective-permute-start.21 = (bf16[224,128]{1,0:T(8,128)(2,1)S(1)}, bf16[224,128]{1,0:T(8,128)(2,1)S(1)}, u32[]{:S(2)}, u32[]{:S(2)}) collective-permute-start(bf16[224,128]{1,0:T(8,128)(2,1)S(1)} %get-tuple-element.86), channel_id=1, source_target_pairs={{0,16},{16,32},{32,48},{48,0},{1,17},{17,33},{33,49},{49,1},{2,18}... | collective-permute-start | bytes 172040 | tf_op jit(solution)/shard_map/ppermute | solution.py:377
  65.9 34.8 %collective-permute-start.25 = (bf16[224,2048]{1,0:T(8,128)(2,1)S(1)}, bf16[224,2048]{1,0:T(8,128)(2,1)S(1)}, u32[]{:S(2)}, u32[]{:S(2)}) collective-permute-start(bf16[224,2048]{1,0:T(8,128)(2,1)S(1)} %bitcast.51), channel_id=1, source_target_pairs={{0,64},{64,0},{1,65},{65,1},{2,66},{66,2},{3,67},{67,3},{4,68},{68... | collective-permute-start | bytes 2752520 | tf_op jit(solution)/shard_map/ppermute | solution.py:405
  66.8 33.9 %collective-permute-start.26 = (bf16[224,2048]{1,0:T(8,128)(2,1)S(1)}, bf16[224,2048]{1,0:T(8,128)(2,1)S(1)}, u32[]{:S(2)}, u32[]{:S(2)}) collective-permute-start(bf16[224,2048]{1,0:T(8,128)(2,1)S(1)} %collective-permute-done.24.hid1), channel_id=1, source_target_pairs={{0,64},{64,0},{1,65},{65,1},{2,66},{66,2},{3,67},{67,3},{4,68},{68... | collective-permute-start | bytes 2752520 | tf_op jit(solution)/shard_map/ppermute | solution.py:405
  67.1 5.4 %collective-permute-start.18 = (bf16[224,128]{1,0:T(8,128)(2,1)S(1)}, bf16[224,128]{1,0:T(8,128)(2,1)S(1)}, u32[]{:S(2)}, u32[]{:S(2)}) collective-permute-start(bf16[224,128]{1,0:T(8,128)(2,1)S(1)} %get-tuple-element.88), channel_id=1, source_target_pairs={{0,48},{16,0},{32,16},{48,32},{1,49},{17,1},{33,17},{49,33},{2,50}... | collective-permute-start | bytes 172040 | tf_op jit(solution)/shard_map/ppermute | solution.py:377
  69.3 5.1 %collective-permute-start.17 = (bf16[224,128]{1,0:T(8,128)(2,1)S(1)}, bf16[224,128]{1,0:T(8,128)(2,1)S(1)}, u32[]{:S(2)}, u32[]{:S(2)}) collective-permute-start(bf16[224,128]{1,0:T(8,128)(2,1)S(1)} %get-tuple-element.89), channel_id=1, source_target_pairs={{0,32},{16,48},{32,0},{48,16},{1,33},{17,49},{33,1},{49,17},{2,34}... | collective-permute-start | bytes 172040 | tf_op jit(solution)/shard_map/ppermute | solution.py:377
  70.3 4.8 %collective-permute-start.16 = (bf16[224,128]{1,0:T(8,128)(2,1)S(1)}, bf16[224,128]{1,0:T(8,128)(2,1)S(1)}, u32[]{:S(2)}, u32[]{:S(2)}) collective-permute-start(bf16[224,128]{1,0:T(8,128)(2,1)S(1)} %get-tuple-element.90), channel_id=1, source_target_pairs={{0,16},{16,32},{32,48},{48,0},{1,17},{17,33},{33,49},{49,1},{2,18}... | collective-permute-start | bytes 172040 | tf_op jit(solution)/shard_map/ppermute | solution.py:377
  76.4 3.0 %collective-permute-start.27 = (bf16[224,128]{1,0:T(8,128)(2,1)S(1)}, bf16[224,128]{1,0:T(8,128)(2,1)S(1)}, u32[]{:S(2)}, u32[]{:S(2)}) collective-permute-start(bf16[224,128]{1,0:T(8,128)(2,1)S(1)} %get-tuple-element.77), channel_id=1, source_target_pairs={{0,16},{16,0},{32,48},{48,32},{1,17},{17,1},{33,49},{49,33},{2,18}... | collective-permute-start | bytes 172040 | tf_op jit(solution)/shard_map/ppermute | solution.py:406
  79.5 8.1 %collective-permute-start.28 = (bf16[2,224,128]{2,1,0:T(8,128)(2,1)S(1)}, bf16[2,224,128]{2,1,0:T(8,128)(2,1)S(1)}, u32[]{:S(2)}, u32[]{:S(2)}) collective-permute-start(bf16[2,224,128]{2,1,0:T(8,128)(2,1)S(1)} %get-tuple-element.96), channel_id=1, source_target_pairs={{2,66},{3,67},{64,0},{65,1},{6,70},{7,71},{68,4},{69,5},{10,74},{1... | collective-permute-start | bytes 344072 | tf_op jit(solution)/shard_map/ppermute | solution.py:410
  87.5 3.3 %collective-permute-start.31 = (bf16[896,128]{1,0:T(8,128)(2,1)S(1)}, bf16[896,128]{1,0:T(8,128)(2,1)S(1)}, u32[]{:S(2)}, u32[]{:S(2)}) collective-permute-start(bf16[896,128]{1,0:T(8,128)(2,1)S(1)} %bitcast.53), channel_id=1, source_target_pairs={{0,3},{1,0},{66,65},{67,66},{4,7},{5,4},{70,69},{71,70},{8,11},{9,... | collective-permute-start | bytes 688136 | tf_op jit(solution)/shard_map/ppermute | solution.py:417
  88.2 8.8 %collective-permute-start.30 = (bf16[896,128]{1,0:T(8,128)(2,1)S(1)}, bf16[896,128]{1,0:T(8,128)(2,1)S(1)}, u32[]{:S(2)}, u32[]{:S(2)}) collective-permute-start(bf16[896,128]{1,0:T(8,128)(2,1)S(1)} %bitcast.54), channel_id=1, source_target_pairs={{0,1},{1,2},{66,67},{67,64},{4,5},{5,6},{70,71},{71,68},{8,9},{9,1... | collective-permute-start | bytes 688136 | tf_op jit(solution)/shard_map/ppermute | solution.py:417
  89.5 11.2 %collective-permute-start.29 = (bf16[896,128]{1,0:T(8,128)(2,1)S(1)}, bf16[896,128]{1,0:T(8,128)(2,1)S(1)}, u32[]{:S(2)}, u32[]{:S(2)}) collective-permute-start(bf16[896,128]{1,0:T(8,128)(2,1)S(1)} %bitcast.55), channel_id=1, source_target_pairs={{0,2},{1,3},{66,64},{67,65},{4,6},{5,7},{70,68},{71,69},{8,10},{9,... | collective-permute-start | bytes 688136 | tf_op jit(solution)/shard_map/ppermute | solution.py:417
  103.3 14.5 %collective-permute-start.32 = (bf16[2,2,16,2048]{3,2,1,0:T(8,128)(2,1)S(1)}, bf16[2,2,16,2048]{3,2,1,0:T(8,128)(2,1)S(1)}, u32[]{:S(2)}, u32[]{:S(2)}) collective-permute-start(bf16[2,2,16,2048]{3,2,1,0:T(8,128)(2,1)S(1)} %get-tuple-element.79), channel_id=1, source_target_pairs={{0,4},{4,8},{8,12},{12,0},{1,5},{5,9},{9,13},{13,1},{2,6},{6,10},{... | collective-permute-start | bytes 786440 | tf_op jit(solution)/shard_map/ppermute | solution.py:377
  103.4 14.4 %collective-permute-start.33 = (bf16[2,2,16,2048]{3,2,1,0:T(8,128)(2,1)S(1)}, bf16[2,2,16,2048]{3,2,1,0:T(8,128)(2,1)S(1)}, u32[]{:S(2)}, u32[]{:S(2)}) collective-permute-start(bf16[2,2,16,2048]{3,2,1,0:T(8,128)(2,1)S(1)} %get-tuple-element.80), channel_id=1, source_target_pairs={{0,12},{4,0},{8,4},{12,8},{1,13},{5,1},{9,5},{13,9},{2,14},{6,2},{... | collective-permute-start | bytes 786440 | tf_op jit(solution)/shard_map/ppermute | solution.py:377
  106.0 11.7 %collective-permute-start.34 = (bf16[2,2,16,2048]{3,2,1,0:T(8,128)(2,1)S(1)}, bf16[2,2,16,2048]{3,2,1,0:T(8,128)(2,1)S(1)}, u32[]{:S(2)}, u32[]{:S(2)}) collective-permute-start(bf16[2,2,16,2048]{3,2,1,0:T(8,128)(2,1)S(1)} %get-tuple-element.81), channel_id=1, source_target_pairs={{0,8},{4,12},{8,0},{12,4},{1,9},{5,13},{9,1},{13,5},{2,10},{6,14},... | collective-permute-start | bytes 786440 | tf_op jit(solution)/shard_map/ppermute | solution.py:377
  117.9 5.8 %collective-permute-start.35 = (bf16[16,2048]{1,0:T(8,128)(2,1)S(1)}, bf16[16,2048]{1,0:T(8,128)(2,1)S(1)}, u32[]{:S(2)}, u32[]{:S(2)}) collective-permute-start(bf16[16,2048]{1,0:T(8,128)(2,1)S(1)} %get-tuple-element.92), channel_id=1, source_target_pairs={{0,32},{32,0},{16,48},{48,16},{1,33},{33,1},{17,49},{49,17},{2,34}... | collective-permute-start | bytes 196616 | tf_op jit(solution)/shard_map/ppermute | solution.py:424
  118.8 9.6 %collective-permute-start.37 = (bf16[16,2048]{1,0:T(8,128)(2,1)S(1)}, bf16[16,2048]{1,0:T(8,128)(2,1)S(1)}, u32[]{:S(2)}, u32[]{:S(2)}) collective-permute-start(bf16[16,2048]{1,0:T(8,128)(2,1)S(1)} %get-tuple-element.93), channel_id=1, source_target_pairs={{0,160},{128,32},{32,128},{160,0},{16,176},{144,48},{48,144},{176,... | collective-permute-start | bytes 196616 | tf_op jit(solution)/shard_map/ppermute | solution.py:426
  123.1 7.3 %collective-permute-start.36 = (bf16[16,2048]{1,0:T(8,128)(2,1)S(1)}, bf16[16,2048]{1,0:T(8,128)(2,1)S(1)}, u32[]{:S(2)}, u32[]{:S(2)}) collective-permute-start(bf16[16,2048]{1,0:T(8,128)(2,1)S(1)} %get-tuple-element.94), channel_id=1, source_target_pairs={{0,128},{128,0},{1,129},{129,1},{2,130},{130,2},{3,131},{131,3},{4... | collective-permute-start | bytes 196616 | tf_op jit(solution)/shard_map/ppermute | solution.py:425

commit v13 on v12

--- a/solution.py
+++ b/solution.py
@@ -421,9 +421,9 @@
     both = [(a + 4 * c, b + 4 * (1 - c)) for a, b in other_zl for c in range(2)]
     grad_weight = add_up(
         total[0, 0],
-        lax.ppermute(total[0, 1].astype(BF), "zl", other_zl),
         lax.ppermute(total[1, 0].astype(BF), "zh", swap),
         lax.ppermute(total[1, 1].astype(BF), ("zh", "zl"), both),
+        lax.ppermute(total[0, 1].astype(BF), "zl", other_zl),
     )
     return dq[None], key_grads[None], value_grads[None], grad_weight
 

time: 132 us -> 132 us (level); the launches traced: 131 us -> 133 us
  waiting for transfers between devices: 47.6 us -> 49.4 us
    ppermute x1, starting transfers between devices: 0.5 us -> 10.2 us  [per_device(): lax.ppermute(total[1, 0].astype(BF), 'zh', swap)]
    ppermute x27, starting transfers between devices: 43.6 us -> 37.5 us  [moved(): return lax.ppermute(value, axis, ring(shift))]
    ppermute x1, waiting for transfers between devices: 4.72 us -> 0.01 us  [per_device(): lax.ppermute(total[1, 1].astype(BF), ('zh', 'zl'), both)]
    ppermute x2, starting transfers between devices: 1.06 us -> 5.72 us  [per_device(): hidden = (*hidden, *(lax.ppermute(h, 'co', swap) for h in hidden))]
    ppermute x1, waiting for transfers between devices: 0.1 us -> 4.17 us  [per_device(): lax.ppermute(total[0, 1].astype(BF), 'zl', other_zl)]
    ppermute x1, starting transfers between devices: 4.3 us -> 0.38 us  [per_device(): lax.ppermute(total[1, 1].astype(BF), ('zh', 'zl'), both)]
    ppermute x1, starting transfers between devices: 7.1 us -> 4.58 us  [per_device(): lax.ppermute(rows, ('co', 'x'), cross)]
    ppermute x27, waiting for transfers between devices: 26.9 us -> 28.6 us  [moved(): return lax.ppermute(value, axis, ring(shift))]
  transfers between devices with their start and end apart: 38 -> 38, of which waited for: 18 -> 18; matrix products, arithmetic and copies ran while one was open for 0% -> 0% of each run, Pallas kernels for 8% -> 9%
where the time goes in v13:
time: 132 us; the launch traced here: 133 us
  starting transfers between devices  64.8 us (49%)
  waiting for transfers between devices  49.4 us (37%)
  Pallas kernels  14.5 us (11%)
  local copies, waits for them, and re-layouts  2.82 us (2%)
    ppermute x27, starting transfers between devices, moved(): return lax.ppermute(value, axis, ring(shift))  37.5 us
    ppermute x27, waiting for transfers between devices, moved(): return lax.ppermute(value, axis, ring(shift))  28.6 us
    ppermute x3, waiting for transfers between devices, per_device(): lax.ppermute(rows, ('co', 'x'), along(j))  10.7 us
    ppermute x1, starting transfers between devices, per_device(): lax.ppermute(total[1, 0].astype(BF), 'zh', swap)  10.2 us
    pallas_call x1, Pallas kernels, backward(): pl.pallas_call(backward_kernel, out_shape=(jax.ShapeDtypeStruct((ROWS, HE...  6.33 us
    ppermute x2, starting transfers between devices, per_device(): hidden = (*hidden, *(lax.ppermute(h, 'co', swap) for h in hidden))  5.72 us
    ppermute x1, starting transfers between devices, per_device(): lax.ppermute(rows, ('co', 'x'), cross)  4.58 us
    pallas_call x1, Pallas kernels, forward(): pl.pallas_call(forward_kernel, out_shape=(jax.ShapeDtypeStruct((2, 1, LAN...  4.22 us
  transfers between devices with their start and end apart: 38, of which 18 were waited for; matrix products, arithmetic and copies ran while one was open for 0% of the time, Pallas kernels for 9%

profile of v13, /device:TPU:1, one launch (start us, length us, event | category | flops | bytes accessed | tf_op | source)
XLA Modules:
  0.0 133.4 jit_solution(2338911146184838767)
XLA Ops:
  0.6 5.2 %collective-permute-start.2 = (bf16[224,128]{1,0:T(8,128)(2,1)}, bf16[224,128]{1,0:T(8,128)(2,1)S(1)}, u32[]{:S(2)}, u32[]{:S(2)}) collective-permute-start(bf16[224,128]{1,0:T(8,128)(2,1)} %bitcast.59), channel_id=1, source_target_pairs={{0,48},{16,0},{32,16},{48,32},{1,49},{17,1},{33,17},{49,33},{2,50}... | collective-permute-start | bytes 172040 | tf_op jit(solution)/shard_map/ppermute | solution.py:377
  5.9 0.4 collective-permute-start
  6.3 2.9 %collective-permute-start.5 = (bf16[224,128]{1,0:T(8,128)(2,1)}, bf16[224,128]{1,0:T(8,128)(2,1)S(1)}, u32[]{:S(2)}, u32[]{:S(2)}) collective-permute-start(bf16[224,128]{1,0:T(8,128)(2,1)} %bitcast.63), channel_id=1, source_target_pairs={{0,48},{16,0},{32,16},{48,32},{1,49},{17,1},{33,17},{49,33},{2,50}... | collective-permute-start | bytes 172040 | tf_op jit(solution)/shard_map/ppermute | solution.py:377
  9.1 0.6 collective-permute-start.4
  9.7 0.0 collective-permute-start.3
  9.7 1.0 copy-done.1
  10.7 1.0 copy-done.2
  11.8 0.1 shard_map.102
  11.8 0.1 collective-permute-done.1.c2
  11.9 0.7 collective-permute-done.5.c3
  12.6 4.2 %collective-permute-done.4.c2 = bf16[224,128]{1,0:T(8,128)(2,1)S(1)} collective-permute-done((bf16[224,128]{1,0:T(8,128)(2,1)}, bf16[224,128]{1,0:T(8,128)(2,1)S(1)}, u32[]{:S(2)}, u32[]{:S(2)}) %collective-permute-start.4) | collective-permute-done | bytes 57376 | tf_op jit(solution)/shard_map/ppermute | solution.py:377
  16.8 0.4 collective-permute-start.6
  17.2 2.3 %collective-permute-start.8 = (bf16[4,224,128]{2,1,0:T(8,128)(2,1)S(1)}, bf16[4,224,128]{2,1,0:T(8,128)(2,1)S(1)}, u32[]{:S(2)}, u32[]{:S(2)}) collective-permute-start(bf16[4,224,128]{2,1,0:T(8,128)(2,1)S(1)} %shard_map.103.k0), channel_id=1, source_target_pairs={{0,12},{4,0},{8,4},{12,8},{1,13},{5,1},{9,5},{13,9},{2,14},{6,2},{... | collective-permute-start | bytes 688136 | tf_op jit(solution)/shard_map/ppermute | solution.py:377
  19.6 0.7 collective-permute-start.7
  20.3 0.7 copy-done.5
  21.0 0.0 copy-done.6
  21.0 0.1 concatenate.3.facts
  21.1 0.0 copy-start
  21.1 2.9 %collective-permute-done.6.k1 = bf16[4,224,128]{2,1,0:T(8,128)(2,1)S(1)} collective-permute-done((bf16[4,224,128]{2,1,0:T(8,128)(2,1)S(1)}, bf16[4,224,128]{2,1,0:T(8,128)(2,1)S(1)}, u32[]{:S(2)}, u32[]{:S(2)}) %collective-permute-start.6) | collective-permute-done | bytes 229408 | tf_op jit(solution)/shard_map/ppermute | solution.py:377
  24.0 1.5 %collective-permute-start.9 = (bf16[4,224,128]{2,1,0:T(8,128)(2,1)S(1)}, bf16[4,224,128]{2,1,0:T(8,128)(2,1)S(1)}, u32[]{:S(2)}, u32[]{:S(2)}) collective-permute-start(bf16[4,224,128]{2,1,0:T(8,128)(2,1)S(1)} %shard_map.104.v0), channel_id=1, source_target_pairs={{0,4},{4,8},{8,12},{12,0},{1,5},{5,9},{9,13},{13,1},{2,6},{6,10},{... | collective-permute-start | bytes 688136 | tf_op jit(solution)/shard_map/ppermute | solution.py:377
  25.5 0.1 collective-permute-done.8.k3
  25.6 3.1 %collective-permute-done.7.k2 = bf16[4,224,128]{2,1,0:T(8,128)(2,1)S(1)} collective-permute-done((bf16[4,224,128]{2,1,0:T(8,128)(2,1)S(1)}, bf16[4,224,128]{2,1,0:T(8,128)(2,1)S(1)}, u32[]{:S(2)}, u32[]{:S(2)}) %collective-permute-start.7) | collective-permute-done | bytes 229408 | tf_op jit(solution)/shard_map/ppermute | solution.py:377
  28.7 0.7 collective-permute-start.10
  29.4 4.2 %shard_map.105 = (f32[2,1,896]{2,1,0:T(1,128)S(1)}, bf16[4,224,128]{2,1,0:T(8,128)(2,1)S(1)}, bf16[4,224,128]{2,1,0:T(8,128)(2,1)S(1)}, bf16[4,224,128]{2,1,0:T(8,128)(2,1)S(1)}, bf16[4,224,128]{2,1,0:T(8,128)(2,1)S(1)}) custom-call(s32[27]{0:T(128)S(1)} %concatenate.3.facts, bf16[224,1024]{1,0:T(8,128)(2,1)S(1)} %get-tuple-element.45.q_ref, ...), custom_call_target="tpu_custom_call" | custom-call | flops 3000000000 | bytes 4000000 | tf_op jit(solution)/shard_map/pallas_call | solution.py:211
  33.6 3.1 %collective-permute-start.24 = (bf16[224,2048]{1,0:T(8,128)(2,1)S(1)}, bf16[224,2048]{1,0:T(8,128)(2,1)S(1)}, u32[]{:S(2)}, u32[]{:S(2)}) collective-permute-start(bf16[224,2048]{1,0:T(8,128)(2,1)S(1)} %bitcast.50), channel_id=1, source_target_pairs={{0,16},{16,0},{32,48},{48,32},{1,17},{17,1},{33,49},{49,33},{2,18}... | collective-permute-start | bytes 2752520 | tf_op jit(solution)/shard_map/ppermute | solution.py:399
  36.8 0.9 collective-permute-done.10.v2
  37.7 1.8 %collective-permute-start.19 = (bf16[4,224,128]{2,1,0:T(8,128)(2,1)S(1)}, bf16[4,224,128]{2,1,0:T(8,128)(2,1)S(1)}, u32[]{:S(2)}, u32[]{:S(2)}) collective-permute-start(bf16[4,224,128]{2,1,0:T(8,128)(2,1)S(1)} %get-tuple-element.69), channel_id=1, source_target_pairs={{0,12},{4,0},{8,4},{12,8},{1,13},{5,1},{9,5},{13,9},{2,14},{6,2},{... | collective-permute-start | bytes 688136 | tf_op jit(solution)/shard_map/ppermute | solution.py:377
  39.5 0.8 collective-permute-start.20
  40.2 6.3 %shard_map.106 = (bf16[224,1024]{1,0:T(8,128)(2,1)}, bf16[4,224,128]{2,1,0:T(8,128)(2,1)S(1)}, bf16[4,224,128]{2,1,0:T(8,128)(2,1)S(1)}, bf16[4,224,128]{2,1,0:T(8,128)(2,1)S(1)}, bf16[4,224,128]{2,1,0:T(8,128)(2,1)S(1)}) custom-call(s32[27]{0:T(128)S(1)} %concatenate.3.facts, bf16[224,1024]{1,0:T(8,128)(2,1)S(1)} %get-tuple-element.45.q_ref, ...), custom_call_target="tpu_custom_call" | custom-call | flops 5000000000 | bytes 5000000 | tf_op jit(solution)/shard_map/pallas_call | solution.py:230
  46.6 3.7 %collective-permute-start.14 = (bf16[4,224,128]{2,1,0:T(8,128)(2,1)S(1)}, bf16[4,224,128]{2,1,0:T(8,128)(2,1)S(1)}, u32[]{:S(2)}, u32[]{:S(2)}) collective-permute-start(bf16[4,224,128]{2,1,0:T(8,128)(2,1)S(1)} %get-tuple-element.66), channel_id=1, source_target_pairs={{0,12},{4,0},{8,4},{12,8},{1,13},{5,1},{9,5},{13,9},{2,14},{6,2},{... | collective-permute-start | bytes 688136 | tf_op jit(solution)/shard_map/ppermute | solution.py:377
  50.3 1.2 collective-permute-start.15
  51.5 0.1 fusion.8
  51.6 2.2 %collective-permute-start.23 = (bf16[224,128]{1,0:T(8,128)(2,1)S(1)}, bf16[224,128]{1,0:T(8,128)(2,1)S(1)}, u32[]{:S(2)}, u32[]{:S(2)}) collective-permute-start(bf16[224,128]{1,0:T(8,128)(2,1)S(1)} %get-tuple-element.84), channel_id=1, source_target_pairs={{0,48},{16,0},{32,16},{48,32},{1,49},{17,1},{33,17},{49,33},{2,50}... | collective-permute-start | bytes 172040 | tf_op jit(solution)/shard_map/ppermute | solution.py:377
  53.8 5.7 %collective-permute-start.22 = (bf16[224,128]{1,0:T(8,128)(2,1)S(1)}, bf16[224,128]{1,0:T(8,128)(2,1)S(1)}, u32[]{:S(2)}, u32[]{:S(2)}) collective-permute-start(bf16[224,128]{1,0:T(8,128)(2,1)S(1)} %get-tuple-element.85), channel_id=1, source_target_pairs={{0,32},{16,48},{32,0},{48,16},{1,33},{17,49},{33,1},{49,17},{2,34}... | collective-permute-start | bytes 172040 | tf_op jit(solution)/shard_map/ppermute | solution.py:377
  59.4 0.8 collective-permute-start.21
  60.3 5.6 %collective-permute-start.25 = (bf16[224,2048]{1,0:T(8,128)(2,1)S(1)}, bf16[224,2048]{1,0:T(8,128)(2,1)S(1)}, u32[]{:S(2)}, u32[]{:S(2)}) collective-permute-start(bf16[224,2048]{1,0:T(8,128)(2,1)S(1)} %bitcast.51), channel_id=1, source_target_pairs={{0,64},{64,0},{1,65},{65,1},{2,66},{66,2},{3,67},{67,3},{4,68},{68... | collective-permute-start | bytes 2752520 | tf_op jit(solution)/shard_map/ppermute | solution.py:405
  65.9 0.1 collective-permute-start.26
  66.0 0.1 fusion.5
  66.1 2.6 %collective-permute-start.18 = (bf16[224,128]{1,0:T(8,128)(2,1)S(1)}, bf16[224,128]{1,0:T(8,128)(2,1)S(1)}, u32[]{:S(2)}, u32[]{:S(2)}) collective-permute-start(bf16[224,128]{1,0:T(8,128)(2,1)S(1)} %get-tuple-element.88), channel_id=1, source_target_pairs={{0,48},{16,0},{32,16},{48,32},{1,49},{17,1},{33,17},{49,33},{2,50}... | collective-permute-start | bytes 172040 | tf_op jit(solution)/shard_map/ppermute | solution.py:377
  68.7 0.6 collective-permute-start.16
  69.3 0.7 collective-permute-done.18.refs_3_
  70.0 4.2 %collective-permute-done.17.refs_2_ = bf16[224,128]{1,0:T(8,128)(2,1)S(1)} collective-permute-done((bf16[224,128]{1,0:T(8,128)(2,1)S(1)}, bf16[224,128]{1,0:T(8,128)(2,1)S(1)}, u32[]{:S(2)}, u32[]{:S(2)}) %collective-permute-start.17) | collective-permute-done | bytes 57376 | tf_op jit(solution)/shard_map/ppermute | solution.py:377
  74.2 1.3 shard_map.107
  75.5 3.0 %collective-permute-done.27 = bf16[224,128]{1,0:T(8,128)(2,1)S(1)} collective-permute-done((bf16[224,128]{1,0:T(8,128)(2,1)S(1)}, bf16[224,128]{1,0:T(8,128)(2,1)S(1)}, u32[]{:S(2)}, u32[]{:S(2)}) %collective-permute-start.27) | collective-permute-done | bytes 57376 | tf_op jit(solution)/shard_map/ppermute | solution.py:406
  78.5 4.6 %collective-permute-start.28 = (bf16[2,224,128]{2,1,0:T(8,128)(2,1)S(1)}, bf16[2,224,128]{2,1,0:T(8,128)(2,1)S(1)}, u32[]{:S(2)}, u32[]{:S(2)}) collective-permute-start(bf16[2,224,128]{2,1,0:T(8,128)(2,1)S(1)} %get-tuple-element.96), channel_id=1, source_target_pairs={{2,66},{3,67},{64,0},{65,1},{6,70},{7,71},{68,4},{69,5},{10,74},{1... | collective-permute-start | bytes 344072 | tf_op jit(solution)/shard_map/ppermute | solution.py:410
  83.1 0.9 collective-permute-done.28
  84.1 0.7 collective-permute-start.31
  84.8 1.3 collective-permute-start.30
  86.1 1.3 collective-permute-start.29
  87.4 7.1 %collective-permute-done.30.row1 = bf16[896,128]{1,0:T(8,128)(2,1)S(1)} collective-permute-done((bf16[896,128]{1,0:T(8,128)(2,1)S(1)}, bf16[896,128]{1,0:T(8,128)(2,1)S(1)}, u32[]{:S(2)}, u32[]{:S(2)}) %collective-permute-start.30) | collective-permute-done | bytes 229408 | tf_op jit(solution)/shard_map/ppermute | solution.py:417
  94.4 3.6 %collective-permute-done.29.row2 = bf16[896,128]{1,0:T(8,128)(2,1)S(1)} collective-permute-done((bf16[896,128]{1,0:T(8,128)(2,1)S(1)}, bf16[896,128]{1,0:T(8,128)(2,1)S(1)}, u32[]{:S(2)}, u32[]{:S(2)}) %collective-permute-start.29) | collective-permute-done | bytes 229408 | tf_op jit(solution)/shard_map/ppermute | solution.py:417
  98.1 2.6 %shard_map.108 = (bf16[2,2,16,2048]{3,2,1,0:T(8,128)(2,1)S(1)}, bf16[2,2,16,2048]{3,2,1,0:T(8,128)(2,1)S(1)}, bf16[2,2,16,2048]{3,2,1,0:T(8,128)(2,1)S(1)}, bf16[2,2,16,2048]{3,2,1,0:T(8,128)(2,1)S(1)}) custom-call(s32[27]{0:T(128)S(1)} %concatenate.3.facts, bf16[224,2048]{1,0:T(8,128)(2,1)S(1)} %bitcast.52, ...), custom_call_target="tpu_custom_call" | custom-call | flops 1000000000 | bytes 4000000 | tf_op jit(solution)/shard_map/pallas_call | solution.py:354
  100.7 0.1 collective-permute-start.32
  100.7 2.7 %collective-permute-start.33 = (bf16[2,2,16,2048]{3,2,1,0:T(8,128)(2,1)S(1)}, bf16[2,2,16,2048]{3,2,1,0:T(8,128)(2,1)S(1)}, u32[]{:S(2)}, u32[]{:S(2)}) collective-permute-start(bf16[2,2,16,2048]{3,2,1,0:T(8,128)(2,1)S(1)} %get-tuple-element.80), channel_id=1, source_target_pairs={{0,12},{4,0},{8,4},{12,8},{1,13},{5,1},{9,5},{13,9},{2,14},{6,2},{... | collective-permute-start | bytes 786440 | tf_op jit(solution)/shard_map/ppermute | solution.py:377
  103.4 0.8 collective-permute-start.34
  104.2 4.6 %collective-permute-done.32 = bf16[2,2,16,2048]{3,2,1,0:T(8,128)(2,1)S(1)} collective-permute-done((bf16[2,2,16,2048]{3,2,1,0:T(8,128)(2,1)S(1)}, bf16[2,2,16,2048]{3,2,1,0:T(8,128)(2,1)S(1)}, u32[]{:S(2)}, u32[]{:S(2)}) %collective-permute-start.32) | collective-permute-done | bytes 262176 | tf_op jit(solution)/shard_map/ppermute | solution.py:377
  108.8 5.5 %collective-permute-done.33 = bf16[2,2,16,2048]{3,2,1,0:T(8,128)(2,1)S(1)} collective-permute-done((bf16[2,2,16,2048]{3,2,1,0:T(8,128)(2,1)S(1)}, bf16[2,2,16,2048]{3,2,1,0:T(8,128)(2,1)S(1)}, u32[]{:S(2)}, u32[]{:S(2)}) %collective-permute-start.33) | collective-permute-done | bytes 262176 | tf_op jit(solution)/shard_map/ppermute | solution.py:377
  114.4 1.5 %collective-permute-done.34 = bf16[2,2,16,2048]{3,2,1,0:T(8,128)(2,1)S(1)} collective-permute-done((bf16[2,2,16,2048]{3,2,1,0:T(8,128)(2,1)S(1)}, bf16[2,2,16,2048]{3,2,1,0:T(8,128)(2,1)S(1)}, u32[]{:S(2)}, u32[]{:S(2)}) %collective-permute-start.34) | collective-permute-done | bytes 262176 | tf_op jit(solution)/shard_map/ppermute | solution.py:377
  115.9 0.1 fusion.10
  116.1 10.2 %collective-permute-start.35 = (bf16[16,2048]{1,0:T(8,128)(2,1)S(1)}, bf16[16,2048]{1,0:T(8,128)(2,1)S(1)}, u32[]{:S(2)}, u32[]{:S(2)}) collective-permute-start(bf16[16,2048]{1,0:T(8,128)(2,1)S(1)} %get-tuple-element.92), channel_id=1, source_target_pairs={{0,128},{128,0},{1,129},{129,1},{2,130},{130,2},{3,131},{131,3},{4... | collective-permute-start | bytes 196616 | tf_op jit(solution)/shard_map/ppermute | solution.py:424
  126.2 0.4 collective-permute-start.36
  126.6 1.9 %collective-permute-done.35 = bf16[16,2048]{1,0:T(8,128)(2,1)S(1)} collective-permute-done((bf16[16,2048]{1,0:T(8,128)(2,1)S(1)}, bf16[16,2048]{1,0:T(8,128)(2,1)S(1)}, u32[]{:S(2)}, u32[]{:S(2)}) %collective-permute-start.35) | collective-permute-done | bytes 65568 | tf_op jit(solution)/shard_map/ppermute | solution.py:424
  128.5 4.2 %collective-permute-done.37 = bf16[16,2048]{1,0:T(8,128)(2,1)S(1)} collective-permute-done((bf16[16,2048]{1,0:T(8,128)(2,1)S(1)}, bf16[16,2048]{1,0:T(8,128)(2,1)S(1)}, u32[]{:S(2)}, u32[]{:S(2)}) %collective-permute-start.37) | collective-permute-done | bytes 65568 | tf_op jit(solution)/shard_map/ppermute | solution.py:426
  132.7 0.7 fusion.2
  (41 shorter events, 0.2 us)
Async XLA Ops:
  0.6 9.1 %collective-permute-start.2 = (bf16[224,128]{1,0:T(8,128)(2,1)}, bf16[224,128]{1,0:T(8,128)(2,1)S(1)}, u32[]{:S(2)}, u32[]{:S(2)}) collective-permute-start(bf16[224,128]{1,0:T(8,128)(2,1)} %bitcast.59), channel_id=1, source_target_pairs={{0,48},{16,0},{32,16},{48,32},{1,49},{17,1},{33,17},{49,33},{2,50}... | collective-permute-start | bytes 172040 | tf_op jit(solution)/shard_map/ppermute | solution.py:377
  5.9 6.0 %collective-permute-start.1 = (bf16[224,128]{1,0:T(8,128)(2,1)}, bf16[224,128]{1,0:T(8,128)(2,1)S(1)}, u32[]{:S(2)}, u32[]{:S(2)}) collective-permute-start(bf16[224,128]{1,0:T(8,128)(2,1)} %bitcast.60), channel_id=1, source_target_pairs={{0,32},{16,48},{32,0},{48,16},{1,33},{17,49},{33,1},{49,17},{2,34}... | collective-permute-start | bytes 172040 | tf_op jit(solution)/shard_map/ppermute | solution.py:377
  5.9 6.0 %collective-permute-start = (bf16[224,128]{1,0:T(8,128)(2,1)}, bf16[224,128]{1,0:T(8,128)(2,1)S(1)}, u32[]{:S(2)}, u32[]{:S(2)}) collective-permute-start(bf16[224,128]{1,0:T(8,128)(2,1)} %bitcast.61), channel_id=1, source_target_pairs={{0,16},{16,32},{32,48},{48,0},{1,17},{17,33},{33,49},{49,1},{2,18}... | collective-permute-start | bytes 172040 | tf_op jit(solution)/shard_map/ppermute | solution.py:377
  6.3 6.3 %collective-permute-start.5 = (bf16[224,128]{1,0:T(8,128)(2,1)}, bf16[224,128]{1,0:T(8,128)(2,1)S(1)}, u32[]{:S(2)}, u32[]{:S(2)}) collective-permute-start(bf16[224,128]{1,0:T(8,128)(2,1)} %bitcast.63), channel_id=1, source_target_pairs={{0,48},{16,0},{32,16},{48,32},{1,49},{17,1},{33,17},{49,33},{2,50}... | collective-permute-start | bytes 172040 | tf_op jit(solution)/shard_map/ppermute | solution.py:377
  9.1 7.7 %collective-permute-start.4 = (bf16[224,128]{1,0:T(8,128)(2,1)}, bf16[224,128]{1,0:T(8,128)(2,1)S(1)}, u32[]{:S(2)}, u32[]{:S(2)}) collective-permute-start(bf16[224,128]{1,0:T(8,128)(2,1)} %bitcast.64), channel_id=1, source_target_pairs={{0,32},{16,48},{32,0},{48,16},{1,33},{17,49},{33,1},{49,17},{2,34}... | collective-permute-start | bytes 172040 | tf_op jit(solution)/shard_map/ppermute | solution.py:377
  9.7 7.1 %collective-permute-start.3 = (bf16[224,128]{1,0:T(8,128)(2,1)}, bf16[224,128]{1,0:T(8,128)(2,1)S(1)}, u32[]{:S(2)}, u32[]{:S(2)}) collective-permute-start(bf16[224,128]{1,0:T(8,128)(2,1)} %bitcast.65), channel_id=1, source_target_pairs={{0,16},{16,32},{32,48},{48,0},{1,17},{17,33},{33,49},{49,1},{2,18}... | collective-permute-start | bytes 172040 | tf_op jit(solution)/shard_map/ppermute | solution.py:377
  9.7 1.0 copy-start.1
  10.7 1.0 copy-start.2
  11.8 5.1 %copy-start.3 = (bf16[1,224,128]{2,1,0:T(8,128)(2,1)S(1)}, bf16[1,224,128]{2,1,0:T(8,128)(2,1)}, u32[]{:S(2)}) copy-start(bf16[1,224,128]{2,1,0:T(8,128)(2,1)} %param.9) | copy-start | bytes 172036
  16.8 4.3 %copy-start.4 = (bf16[1,224,128]{2,1,0:T(8,128)(2,1)S(1)}, bf16[1,224,128]{2,1,0:T(8,128)(2,1)}, u32[]{:S(2)}) copy-start(bf16[1,224,128]{2,1,0:T(8,128)(2,1)} %param.10) | copy-start | bytes 172036
  16.8 7.2 %collective-permute-start.6 = (bf16[4,224,128]{2,1,0:T(8,128)(2,1)S(1)}, bf16[4,224,128]{2,1,0:T(8,128)(2,1)S(1)}, u32[]{:S(2)}, u32[]{:S(2)}) collective-permute-start(bf16[4,224,128]{2,1,0:T(8,128)(2,1)S(1)} %shard_map.103.k0), channel_id=1, source_target_pairs={{0,4},{4,8},{8,12},{12,0},{1,5},{5,9},{9,13},{13,1},{2,6},{6,10},{... | collective-permute-start | bytes 688136 | tf_op jit(solution)/shard_map/ppermute | solution.py:377
  17.2 8.4 %collective-permute-start.8 = (bf16[4,224,128]{2,1,0:T(8,128)(2,1)S(1)}, bf16[4,224,128]{2,1,0:T(8,128)(2,1)S(1)}, u32[]{:S(2)}, u32[]{:S(2)}) collective-permute-start(bf16[4,224,128]{2,1,0:T(8,128)(2,1)S(1)} %shard_map.103.k0), channel_id=1, source_target_pairs={{0,12},{4,0},{8,4},{12,8},{1,13},{5,1},{9,5},{13,9},{2,14},{6,2},{... | collective-permute-start | bytes 688136 | tf_op jit(solution)/shard_map/ppermute | solution.py:377
  19.6 9.1 %collective-permute-start.7 = (bf16[4,224,128]{2,1,0:T(8,128)(2,1)S(1)}, bf16[4,224,128]{2,1,0:T(8,128)(2,1)S(1)}, u32[]{:S(2)}, u32[]{:S(2)}) collective-permute-start(bf16[4,224,128]{2,1,0:T(8,128)(2,1)S(1)} %shard_map.103.k0), channel_id=1, source_target_pairs={{0,8},{4,12},{8,0},{12,4},{1,9},{5,13},{9,1},{13,5},{2,10},{6,14},... | collective-permute-start | bytes 688136 | tf_op jit(solution)/shard_map/ppermute | solution.py:377
  20.3 0.7 copy-start.5
  20.3 0.7 copy-start.6
  21.1 12.5 %copy-start = (bf16[1,224,2048]{2,1,0:T(8,128)(2,1)S(1)}, bf16[1,224,2048]{2,1,0:T(8,128)(2,1)}, u32[]{:S(2)}) copy-start(bf16[1,224,2048]{2,1,0:T(8,128)(2,1)} %param.7) | copy-start | bytes 2752516
  24.0 15.4 %collective-permute-start.11 = (bf16[4,224,128]{2,1,0:T(8,128)(2,1)S(1)}, bf16[4,224,128]{2,1,0:T(8,128)(2,1)S(1)}, u32[]{:S(2)}, u32[]{:S(2)}) collective-permute-start(bf16[4,224,128]{2,1,0:T(8,128)(2,1)S(1)} %shard_map.104.v0), channel_id=1, source_target_pairs={{0,12},{4,0},{8,4},{12,8},{1,13},{5,1},{9,5},{13,9},{2,14},{6,2},{... | collective-permute-start | bytes 688136 | tf_op jit(solution)/shard_map/ppermute | solution.py:377
  24.0 16.2 %collective-permute-start.9 = (bf16[4,224,128]{2,1,0:T(8,128)(2,1)S(1)}, bf16[4,224,128]{2,1,0:T(8,128)(2,1)S(1)}, u32[]{:S(2)}, u32[]{:S(2)}) collective-permute-start(bf16[4,224,128]{2,1,0:T(8,128)(2,1)S(1)} %shard_map.104.v0), channel_id=1, source_target_pairs={{0,4},{4,8},{8,12},{12,0},{1,5},{5,9},{9,13},{13,1},{2,6},{6,10},{... | collective-permute-start | bytes 688136 | tf_op jit(solution)/shard_map/ppermute | solution.py:377
  28.7 9.0 %collective-permute-start.10 = (bf16[4,224,128]{2,1,0:T(8,128)(2,1)S(1)}, bf16[4,224,128]{2,1,0:T(8,128)(2,1)S(1)}, u32[]{:S(2)}, u32[]{:S(2)}) collective-permute-start(bf16[4,224,128]{2,1,0:T(8,128)(2,1)S(1)} %shard_map.104.v0), channel_id=1, source_target_pairs={{0,8},{4,12},{8,0},{12,4},{1,9},{5,13},{9,1},{13,5},{2,10},{6,14},... | collective-permute-start | bytes 688136 | tf_op jit(solution)/shard_map/ppermute | solution.py:377
  33.6 26.6 %collective-permute-start.24 = (bf16[224,2048]{1,0:T(8,128)(2,1)S(1)}, bf16[224,2048]{1,0:T(8,128)(2,1)S(1)}, u32[]{:S(2)}, u32[]{:S(2)}) collective-permute-start(bf16[224,2048]{1,0:T(8,128)(2,1)S(1)} %bitcast.50), channel_id=1, source_target_pairs={{0,16},{16,0},{32,48},{48,32},{1,17},{17,1},{33,49},{49,33},{2,18}... | collective-permute-start | bytes 2752520 | tf_op jit(solution)/shard_map/ppermute | solution.py:399
  36.8 9.8 %collective-permute-start.12 = (bf16[4,224,128]{2,1,0:T(8,128)(2,1)S(1)}, bf16[4,224,128]{2,1,0:T(8,128)(2,1)S(1)}, u32[]{:S(2)}, u32[]{:S(2)}) collective-permute-start(bf16[4,224,128]{2,1,0:T(8,128)(2,1)S(1)} %get-tuple-element.63), channel_id=1, source_target_pairs={{0,4},{4,8},{8,12},{12,0},{1,5},{5,9},{9,13},{13,1},{2,6},{6,10},{... | collective-permute-start | bytes 688136 | tf_op jit(solution)/shard_map/ppermute | solution.py:377
  37.7 12.6 %collective-permute-start.19 = (bf16[4,224,128]{2,1,0:T(8,128)(2,1)S(1)}, bf16[4,224,128]{2,1,0:T(8,128)(2,1)S(1)}, u32[]{:S(2)}, u32[]{:S(2)}) collective-permute-start(bf16[4,224,128]{2,1,0:T(8,128)(2,1)S(1)} %get-tuple-element.69), channel_id=1, source_target_pairs={{0,12},{4,0},{8,4},{12,8},{1,13},{5,1},{9,5},{13,9},{2,14},{6,2},{... | collective-permute-start | bytes 688136 | tf_op jit(solution)/shard_map/ppermute | solution.py:377
  39.5 12.0 %collective-permute-start.20 = (bf16[4,224,128]{2,1,0:T(8,128)(2,1)S(1)}, bf16[4,224,128]{2,1,0:T(8,128)(2,1)S(1)}, u32[]{:S(2)}, u32[]{:S(2)}) collective-permute-start(bf16[4,224,128]{2,1,0:T(8,128)(2,1)S(1)} %get-tuple-element.70), channel_id=1, source_target_pairs={{0,8},{4,12},{8,0},{12,4},{1,9},{5,13},{9,1},{13,5},{2,10},{6,14},... | collective-permute-start | bytes 688136 | tf_op jit(solution)/shard_map/ppermute | solution.py:377
  46.6 7.2 %collective-permute-start.13 = (bf16[4,224,128]{2,1,0:T(8,128)(2,1)S(1)}, bf16[4,224,128]{2,1,0:T(8,128)(2,1)S(1)}, u32[]{:S(2)}, u32[]{:S(2)}) collective-permute-start(bf16[4,224,128]{2,1,0:T(8,128)(2,1)S(1)} %get-tuple-element.65), channel_id=1, source_target_pairs={{0,4},{4,8},{8,12},{12,0},{1,5},{5,9},{9,13},{13,1},{2,6},{6,10},{... | collective-permute-start | bytes 688136 | tf_op jit(solution)/shard_map/ppermute | solution.py:377
  46.6 12.9 %collective-permute-start.14 = (bf16[4,224,128]{2,1,0:T(8,128)(2,1)S(1)}, bf16[4,224,128]{2,1,0:T(8,128)(2,1)S(1)}, u32[]{:S(2)}, u32[]{:S(2)}) collective-permute-start(bf16[4,224,128]{2,1,0:T(8,128)(2,1)S(1)} %get-tuple-element.66), channel_id=1, source_target_pairs={{0,12},{4,0},{8,4},{12,8},{1,13},{5,1},{9,5},{13,9},{2,14},{6,2},{... | collective-permute-start | bytes 688136 | tf_op jit(solution)/shard_map/ppermute | solution.py:377
  50.3 10.0 %collective-permute-start.15 = (bf16[4,224,128]{2,1,0:T(8,128)(2,1)S(1)}, bf16[4,224,128]{2,1,0:T(8,128)(2,1)S(1)}, u32[]{:S(2)}, u32[]{:S(2)}) collective-permute-start(bf16[4,224,128]{2,1,0:T(8,128)(2,1)S(1)} %get-tuple-element.67), channel_id=1, source_target_pairs={{0,8},{4,12},{8,0},{12,4},{1,9},{5,13},{9,1},{13,5},{2,10},{6,14},... | collective-permute-start | bytes 688136 | tf_op jit(solution)/shard_map/ppermute | solution.py:377
  51.6 14.5 %collective-permute-start.23 = (bf16[224,128]{1,0:T(8,128)(2,1)S(1)}, bf16[224,128]{1,0:T(8,128)(2,1)S(1)}, u32[]{:S(2)}, u32[]{:S(2)}) collective-permute-start(bf16[224,128]{1,0:T(8,128)(2,1)S(1)} %get-tuple-element.84), channel_id=1, source_target_pairs={{0,48},{16,0},{32,16},{48,32},{1,49},{17,1},{33,17},{49,33},{2,50}... | collective-permute-start | bytes 172040 | tf_op jit(solution)/shard_map/ppermute | solution.py:377
  53.8 14.9 %collective-permute-start.22 = (bf16[224,128]{1,0:T(8,128)(2,1)S(1)}, bf16[224,128]{1,0:T(8,128)(2,1)S(1)}, u32[]{:S(2)}, u32[]{:S(2)}) collective-permute-start(bf16[224,128]{1,0:T(8,128)(2,1)S(1)} %get-tuple-element.85), channel_id=1, source_target_pairs={{0,32},{16,48},{32,0},{48,16},{1,33},{17,49},{33,1},{49,17},{2,34}... | collective-permute-start | bytes 172040 | tf_op jit(solution)/shard_map/ppermute | solution.py:377
  59.4 9.3 %collective-permute-start.21 = (bf16[224,128]{1,0:T(8,128)(2,1)S(1)}, bf16[224,128]{1,0:T(8,128)(2,1)S(1)}, u32[]{:S(2)}, u32[]{:S(2)}) collective-permute-start(bf16[224,128]{1,0:T(8,128)(2,1)S(1)} %get-tuple-element.86), channel_id=1, source_target_pairs={{0,16},{16,32},{32,48},{48,0},{1,17},{17,33},{33,49},{49,1},{2,18}... | collective-permute-start | bytes 172040 | tf_op jit(solution)/shard_map/ppermute | solution.py:377
  60.3 37.8 %collective-permute-start.25 = (bf16[224,2048]{1,0:T(8,128)(2,1)S(1)}, bf16[224,2048]{1,0:T(8,128)(2,1)S(1)}, u32[]{:S(2)}, u32[]{:S(2)}) collective-permute-start(bf16[224,2048]{1,0:T(8,128)(2,1)S(1)} %bitcast.51), channel_id=1, source_target_pairs={{0,64},{64,0},{1,65},{65,1},{2,66},{66,2},{3,67},{67,3},{4,68},{68... | collective-permute-start | bytes 2752520 | tf_op jit(solution)/shard_map/ppermute | solution.py:405
  65.9 32.2 %collective-permute-start.26 = (bf16[224,2048]{1,0:T(8,128)(2,1)S(1)}, bf16[224,2048]{1,0:T(8,128)(2,1)S(1)}, u32[]{:S(2)}, u32[]{:S(2)}) collective-permute-start(bf16[224,2048]{1,0:T(8,128)(2,1)S(1)} %collective-permute-done.24.hid1), channel_id=1, source_target_pairs={{0,64},{64,0},{1,65},{65,1},{2,66},{66,2},{3,67},{67,3},{4,68},{68... | collective-permute-start | bytes 2752520 | tf_op jit(solution)/shard_map/ppermute | solution.py:405
  66.1 3.8 %collective-permute-start.18 = (bf16[224,128]{1,0:T(8,128)(2,1)S(1)}, bf16[224,128]{1,0:T(8,128)(2,1)S(1)}, u32[]{:S(2)}, u32[]{:S(2)}) collective-permute-start(bf16[224,128]{1,0:T(8,128)(2,1)S(1)} %get-tuple-element.88), channel_id=1, source_target_pairs={{0,48},{16,0},{32,16},{48,32},{1,49},{17,1},{33,17},{49,33},{2,50}... | collective-permute-start | bytes 172040 | tf_op jit(solution)/shard_map/ppermute | solution.py:377
  68.7 5.5 %collective-permute-start.17 = (bf16[224,128]{1,0:T(8,128)(2,1)S(1)}, bf16[224,128]{1,0:T(8,128)(2,1)S(1)}, u32[]{:S(2)}, u32[]{:S(2)}) collective-permute-start(bf16[224,128]{1,0:T(8,128)(2,1)S(1)} %get-tuple-element.89), channel_id=1, source_target_pairs={{0,32},{16,48},{32,0},{48,16},{1,33},{17,49},{33,1},{49,17},{2,34}... | collective-permute-start | bytes 172040 | tf_op jit(solution)/shard_map/ppermute | solution.py:377
  68.7 5.4 %collective-permute-start.16 = (bf16[224,128]{1,0:T(8,128)(2,1)S(1)}, bf16[224,128]{1,0:T(8,128)(2,1)S(1)}, u32[]{:S(2)}, u32[]{:S(2)}) collective-permute-start(bf16[224,128]{1,0:T(8,128)(2,1)S(1)} %get-tuple-element.90), channel_id=1, source_target_pairs={{0,16},{16,32},{32,48},{48,0},{1,17},{17,33},{33,49},{49,1},{2,18}... | collective-permute-start | bytes 172040 | tf_op jit(solution)/shard_map/ppermute | solution.py:377
  75.5 3.0 %collective-permute-start.27 = (bf16[224,128]{1,0:T(8,128)(2,1)S(1)}, bf16[224,128]{1,0:T(8,128)(2,1)S(1)}, u32[]{:S(2)}, u32[]{:S(2)}) collective-permute-start(bf16[224,128]{1,0:T(8,128)(2,1)S(1)} %get-tuple-element.77), channel_id=1, source_target_pairs={{0,16},{16,0},{32,48},{48,32},{1,17},{17,1},{33,49},{49,33},{2,18}... | collective-permute-start | bytes 172040 | tf_op jit(solution)/shard_map/ppermute | solution.py:406
  78.5 5.5 %collective-permute-start.28 = (bf16[2,224,128]{2,1,0:T(8,128)(2,1)S(1)}, bf16[2,224,128]{2,1,0:T(8,128)(2,1)S(1)}, u32[]{:S(2)}, u32[]{:S(2)}) collective-permute-start(bf16[2,224,128]{2,1,0:T(8,128)(2,1)S(1)} %get-tuple-element.96), channel_id=1, source_target_pairs={{2,66},{3,67},{64,0},{65,1},{6,70},{7,71},{68,4},{69,5},{10,74},{1... | collective-permute-start | bytes 344072 | tf_op jit(solution)/shard_map/ppermute | solution.py:410
  84.1 3.3 %collective-permute-start.31 = (bf16[896,128]{1,0:T(8,128)(2,1)S(1)}, bf16[896,128]{1,0:T(8,128)(2,1)S(1)}, u32[]{:S(2)}, u32[]{:S(2)}) collective-permute-start(bf16[896,128]{1,0:T(8,128)(2,1)S(1)} %bitcast.53), channel_id=1, source_target_pairs={{0,3},{1,0},{66,65},{67,66},{4,7},{5,4},{70,69},{71,70},{8,11},{9,... | collective-permute-start | bytes 688136 | tf_op jit(solution)/shard_map/ppermute | solution.py:417
  84.8 9.7 %collective-permute-start.30 = (bf16[896,128]{1,0:T(8,128)(2,1)S(1)}, bf16[896,128]{1,0:T(8,128)(2,1)S(1)}, u32[]{:S(2)}, u32[]{:S(2)}) collective-permute-start(bf16[896,128]{1,0:T(8,128)(2,1)S(1)} %bitcast.54), channel_id=1, source_target_pairs={{0,1},{1,2},{66,67},{67,64},{4,5},{5,6},{70,71},{71,68},{8,9},{9,1... | collective-permute-start | bytes 688136 | tf_op jit(solution)/shard_map/ppermute | solution.py:417
  86.1 12.0 %collective-permute-start.29 = (bf16[896,128]{1,0:T(8,128)(2,1)S(1)}, bf16[896,128]{1,0:T(8,128)(2,1)S(1)}, u32[]{:S(2)}, u32[]{:S(2)}) collective-permute-start(bf16[896,128]{1,0:T(8,128)(2,1)S(1)} %bitcast.55), channel_id=1, source_target_pairs={{0,2},{1,3},{66,64},{67,65},{4,6},{5,7},{70,68},{71,69},{8,10},{9,... | collective-permute-start | bytes 688136 | tf_op jit(solution)/shard_map/ppermute | solution.py:417
  100.7 8.2 %collective-permute-start.32 = (bf16[2,2,16,2048]{3,2,1,0:T(8,128)(2,1)S(1)}, bf16[2,2,16,2048]{3,2,1,0:T(8,128)(2,1)S(1)}, u32[]{:S(2)}, u32[]{:S(2)}) collective-permute-start(bf16[2,2,16,2048]{3,2,1,0:T(8,128)(2,1)S(1)} %get-tuple-element.79), channel_id=1, source_target_pairs={{0,4},{4,8},{8,12},{12,0},{1,5},{5,9},{9,13},{13,1},{2,6},{6,10},{... | collective-permute-start | bytes 786440 | tf_op jit(solution)/shard_map/ppermute | solution.py:377
  100.7 13.7 %collective-permute-start.33 = (bf16[2,2,16,2048]{3,2,1,0:T(8,128)(2,1)S(1)}, bf16[2,2,16,2048]{3,2,1,0:T(8,128)(2,1)S(1)}, u32[]{:S(2)}, u32[]{:S(2)}) collective-permute-start(bf16[2,2,16,2048]{3,2,1,0:T(8,128)(2,1)S(1)} %get-tuple-element.80), channel_id=1, source_target_pairs={{0,12},{4,0},{8,4},{12,8},{1,13},{5,1},{9,5},{13,9},{2,14},{6,2},{... | collective-permute-start | bytes 786440 | tf_op jit(solution)/shard_map/ppermute | solution.py:377
  103.4 12.5 %collective-permute-start.34 = (bf16[2,2,16,2048]{3,2,1,0:T(8,128)(2,1)S(1)}, bf16[2,2,16,2048]{3,2,1,0:T(8,128)(2,1)S(1)}, u32[]{:S(2)}, u32[]{:S(2)}) collective-permute-start(bf16[2,2,16,2048]{3,2,1,0:T(8,128)(2,1)S(1)} %get-tuple-element.81), channel_id=1, source_target_pairs={{0,8},{4,12},{8,0},{12,4},{1,9},{5,13},{9,1},{13,5},{2,10},{6,14},... | collective-permute-start | bytes 786440 | tf_op jit(solution)/shard_map/ppermute | solution.py:377
  116.1 12.5 %collective-permute-start.35 = (bf16[16,2048]{1,0:T(8,128)(2,1)S(1)}, bf16[16,2048]{1,0:T(8,128)(2,1)S(1)}, u32[]{:S(2)}, u32[]{:S(2)}) collective-permute-start(bf16[16,2048]{1,0:T(8,128)(2,1)S(1)} %get-tuple-element.92), channel_id=1, source_target_pairs={{0,128},{128,0},{1,129},{129,1},{2,130},{130,2},{3,131},{131,3},{4... | collective-permute-start | bytes 196616 | tf_op jit(solution)/shard_map/ppermute | solution.py:424
  126.2 6.5 %collective-permute-start.37 = (bf16[16,2048]{1,0:T(8,128)(2,1)S(1)}, bf16[16,2048]{1,0:T(8,128)(2,1)S(1)}, u32[]{:S(2)}, u32[]{:S(2)}) collective-permute-start(bf16[16,2048]{1,0:T(8,128)(2,1)S(1)} %get-tuple-element.93), channel_id=1, source_target_pairs={{0,32},{32,0},{16,48},{48,16},{1,33},{33,1},{17,49},{49,17},{2,34}... | collective-permute-start | bytes 196616 | tf_op jit(solution)/shard_map/ppermute | solution.py:426
  126.2 6.5 %collective-permute-start.36 = (bf16[16,2048]{1,0:T(8,128)(2,1)S(1)}, bf16[16,2048]{1,0:T(8,128)(2,1)S(1)}, u32[]{:S(2)}, u32[]{:S(2)}) collective-permute-start(bf16[16,2048]{1,0:T(8,128)(2,1)S(1)} %get-tuple-element.94), channel_id=1, source_target_pairs={{0,160},{128,32},{32,128},{160,0},{16,176},{144,48},{48,144},{176,... | collective-permute-start | bytes 196616 | tf_op jit(solution)/shard_map/ppermute | solution.py:425

commit v14 on v13

--- a/solution.py
+++ b/solution.py
@@ -272,7 +272,7 @@
     )(*arrays)
 
 
-def stack_kernel(c0, c1, c2, c3, out):
+def stack_kernel(c0, c2, c1, c3, out):
     for a, ref in enumerate((c0, c1, c2, c3)):
         out[a] = ref[...]
 
@@ -285,7 +285,7 @@
         in_specs=[vmem] * 4,
         out_specs=vmem,
         compiler_params=pltpu.CompilerParams(vmem_limit_bytes=16 * 2**20),
-    )(*pieces)
+    )(pieces[0], pieces[2], pieces[1], pieces[3])
 
 
 def finish_kernel(facts, *refs):
@@ -391,7 +391,7 @@
 
     def over_zl(got):
         parts = [add_up(*[g[a] for g in got]) for a in range(4)]
-        return [parts[0]] + [moved(parts[a].astype(BF), "zl", a) for a in (1, 2, 3)]
+        return [parts[0]] + [moved(parts[a].astype(BF), "zl", a) for a in (2, 1, 3)]
 
     stats, *dvs = forward(facts, *rows_in, ks)
     dvs = received(dvs)

time: 132 us -> 129 us (0.977); the launches traced: 133 us -> 129 us
  starting transfers between devices: 64.8 us -> 62.4 us
  waiting for transfers between devices: 49.4 us -> 47.2 us
    ppermute x1, starting transfers between devices: 10.2 us -> 3.71 us  [per_device(): lax.ppermute(total[1, 0].astype(BF), 'zh', swap)]
    ppermute x1, starting transfers between devices: 3.14 us -> 1.21 us  [per_device(): beside = lax.ppermute(after(hidden, stats), 'zl', neighbour)]
    ppermute x1, starting transfers between devices: 4.58 us -> 6.18 us  [per_device(): lax.ppermute(rows, ('co', 'x'), cross)]
  transfers between devices with their start and end apart: 38 -> 38, of which waited for: 18 -> 16; matrix products, arithmetic and copies ran while one was open for 0% -> 0% of each run, Pallas kernels for 9% -> 9%
where the time goes in v14:
time: 129 us
  starting transfers between devices  62.4 us (48%)
  waiting for transfers between devices  47.2 us (37%)
  Pallas kernels  14.7 us (11%)
  local copies, waits for them, and re-layouts  2.82 us (2%)
    ppermute x27, starting transfers between devices, moved(): return lax.ppermute(value, axis, ring(shift))  38.3 us
    ppermute x27, waiting for transfers between devices, moved(): return lax.ppermute(value, axis, ring(shift))  28.8 us
    ppermute x3, waiting for transfers between devices, per_device(): lax.ppermute(rows, ('co', 'x'), along(j))  9.83 us
    ppermute x2, starting transfers between devices, per_device(): hidden = (*hidden, *(lax.ppermute(h, 'co', swap) for h in hidden))  6.71 us
    pallas_call x1, Pallas kernels, backward(): pl.pallas_call(backward_kernel, out_shape=(jax.ShapeDtypeStruct((ROWS, HE...  6.38 us
    ppermute x1, starting transfers between devices, per_device(): lax.ppermute(rows, ('co', 'x'), cross)  6.18 us
    pallas_call x1, Pallas kernels, forward(): pl.pallas_call(forward_kernel, out_shape=(jax.ShapeDtypeStruct((2, 1, LAN...  4.29 us
    ppermute x1, waiting for transfers between devices, per_device(): lax.ppermute(total[0, 1].astype(BF), 'zl', other_zl)  4.19 us
  transfers between devices with their start and end apart: 38, of which 16 were waited for; matrix products, arithmetic and copies ran while one was open for 0% of the time, Pallas kernels for 9%

profile of v14, /device:TPU:1, one launch (start us, length us, event | category | flops | bytes accessed | tf_op | source)
XLA Modules:
  0.0 129.0 jit_solution(16010408882314987102)
XLA Ops:
  0.6 5.2 %collective-permute-start.2 = (bf16[224,128]{1,0:T(8,128)(2,1)}, bf16[224,128]{1,0:T(8,128)(2,1)S(1)}, u32[]{:S(2)}, u32[]{:S(2)}) collective-permute-start(bf16[224,128]{1,0:T(8,128)(2,1)} %bitcast.59), channel_id=1, source_target_pairs={{0,48},{16,0},{32,16},{48,32},{1,49},{17,1},{33,17},{49,33},{2,50}... | collective-permute-start | bytes 172040 | tf_op jit(solution)/shard_map/ppermute | solution.py:377
  5.9 0.4 collective-permute-start
  6.3 2.9 %collective-permute-start.5 = (bf16[224,128]{1,0:T(8,128)(2,1)}, bf16[224,128]{1,0:T(8,128)(2,1)S(1)}, u32[]{:S(2)}, u32[]{:S(2)}) collective-permute-start(bf16[224,128]{1,0:T(8,128)(2,1)} %bitcast.63), channel_id=1, source_target_pairs={{0,48},{16,0},{32,16},{48,32},{1,49},{17,1},{33,17},{49,33},{2,50}... | collective-permute-start | bytes 172040 | tf_op jit(solution)/shard_map/ppermute | solution.py:377
  9.1 0.6 collective-permute-start.4
  9.7 0.0 collective-permute-start.3
  9.7 1.0 copy-done.1
  10.7 1.0 copy-done.2
  11.8 0.1 shard_map.102
  11.8 0.1 collective-permute-done.1.c2
  11.9 0.7 collective-permute-done.5.c3
  12.6 4.2 %collective-permute-done.4.c2 = bf16[224,128]{1,0:T(8,128)(2,1)S(1)} collective-permute-done((bf16[224,128]{1,0:T(8,128)(2,1)}, bf16[224,128]{1,0:T(8,128)(2,1)S(1)}, u32[]{:S(2)}, u32[]{:S(2)}) %collective-permute-start.4) | collective-permute-done | bytes 57376 | tf_op jit(solution)/shard_map/ppermute | solution.py:377
  16.8 0.4 collective-permute-start.6
  17.2 2.3 %collective-permute-start.8 = (bf16[4,224,128]{2,1,0:T(8,128)(2,1)S(1)}, bf16[4,224,128]{2,1,0:T(8,128)(2,1)S(1)}, u32[]{:S(2)}, u32[]{:S(2)}) collective-permute-start(bf16[4,224,128]{2,1,0:T(8,128)(2,1)S(1)} %shard_map.103.k0), channel_id=1, source_target_pairs={{0,12},{4,0},{8,4},{12,8},{1,13},{5,1},{9,5},{13,9},{2,14},{6,2},{... | collective-permute-start | bytes 688136 | tf_op jit(solution)/shard_map/ppermute | solution.py:377
  19.6 0.7 collective-permute-start.7
  20.3 0.7 copy-done.5
  21.0 0.0 copy-done.6
  21.0 0.1 concatenate.3.facts
  21.1 0.0 copy-start
  21.1 2.9 %collective-permute-done.6.k1 = bf16[4,224,128]{2,1,0:T(8,128)(2,1)S(1)} collective-permute-done((bf16[4,224,128]{2,1,0:T(8,128)(2,1)S(1)}, bf16[4,224,128]{2,1,0:T(8,128)(2,1)S(1)}, u32[]{:S(2)}, u32[]{:S(2)}) %collective-permute-start.6) | collective-permute-done | bytes 229408 | tf_op jit(solution)/shard_map/ppermute | solution.py:377
  24.0 1.5 %collective-permute-start.9 = (bf16[4,224,128]{2,1,0:T(8,128)(2,1)S(1)}, bf16[4,224,128]{2,1,0:T(8,128)(2,1)S(1)}, u32[]{:S(2)}, u32[]{:S(2)}) collective-permute-start(bf16[4,224,128]{2,1,0:T(8,128)(2,1)S(1)} %shard_map.104.v0), channel_id=1, source_target_pairs={{0,4},{4,8},{8,12},{12,0},{1,5},{5,9},{9,13},{13,1},{2,6},{6,10},{... | collective-permute-start | bytes 688136 | tf_op jit(solution)/shard_map/ppermute | solution.py:377
  25.5 0.1 collective-permute-done.8.k3
  25.6 3.1 %collective-permute-done.7.k2 = bf16[4,224,128]{2,1,0:T(8,128)(2,1)S(1)} collective-permute-done((bf16[4,224,128]{2,1,0:T(8,128)(2,1)S(1)}, bf16[4,224,128]{2,1,0:T(8,128)(2,1)S(1)}, u32[]{:S(2)}, u32[]{:S(2)}) %collective-permute-start.7) | collective-permute-done | bytes 229408 | tf_op jit(solution)/shard_map/ppermute | solution.py:377
  28.7 0.7 collective-permute-start.10
  29.4 4.3 %shard_map.105 = (f32[2,1,896]{2,1,0:T(1,128)S(1)}, bf16[4,224,128]{2,1,0:T(8,128)(2,1)S(1)}, bf16[4,224,128]{2,1,0:T(8,128)(2,1)S(1)}, bf16[4,224,128]{2,1,0:T(8,128)(2,1)S(1)}, bf16[4,224,128]{2,1,0:T(8,128)(2,1)S(1)}) custom-call(s32[27]{0:T(128)S(1)} %concatenate.3.facts, bf16[224,1024]{1,0:T(8,128)(2,1)S(1)} %get-tuple-element.45.q_ref, ...), custom_call_target="tpu_custom_call" | custom-call | flops 3000000000 | bytes 4000000 | tf_op jit(solution)/shard_map/pallas_call | solution.py:211
  33.7 1.2 collective-permute-start.24
  34.9 1.3 %collective-permute-start.12 = (bf16[4,224,128]{2,1,0:T(8,128)(2,1)S(1)}, bf16[4,224,128]{2,1,0:T(8,128)(2,1)S(1)}, u32[]{:S(2)}, u32[]{:S(2)}) collective-permute-start(bf16[4,224,128]{2,1,0:T(8,128)(2,1)S(1)} %get-tuple-element.63), channel_id=1, source_target_pairs={{0,4},{4,8},{8,12},{12,0},{1,5},{5,9},{9,13},{13,1},{2,6},{6,10},{... | collective-permute-start | bytes 688136 | tf_op jit(solution)/shard_map/ppermute | solution.py:377
  36.2 1.5 %collective-permute-done.10.v2 = bf16[4,224,128]{2,1,0:T(8,128)(2,1)S(1)} collective-permute-done((bf16[4,224,128]{2,1,0:T(8,128)(2,1)S(1)}, bf16[4,224,128]{2,1,0:T(8,128)(2,1)S(1)}, u32[]{:S(2)}, u32[]{:S(2)}) %collective-permute-start.10) | collective-permute-done | bytes 229408 | tf_op jit(solution)/shard_map/ppermute | solution.py:377
  37.7 1.1 collective-permute-start.19
  38.8 1.4 %collective-permute-start.20 = (bf16[4,224,128]{2,1,0:T(8,128)(2,1)S(1)}, bf16[4,224,128]{2,1,0:T(8,128)(2,1)S(1)}, u32[]{:S(2)}, u32[]{:S(2)}) collective-permute-start(bf16[4,224,128]{2,1,0:T(8,128)(2,1)S(1)} %get-tuple-element.70), channel_id=1, source_target_pairs={{0,8},{4,12},{8,0},{12,4},{1,9},{5,13},{9,1},{13,5},{2,10},{6,14},... | collective-permute-start | bytes 688136 | tf_op jit(solution)/shard_map/ppermute | solution.py:377
  40.2 6.4 %shard_map.106 = (bf16[224,1024]{1,0:T(8,128)(2,1)}, bf16[4,224,128]{2,1,0:T(8,128)(2,1)S(1)}, bf16[4,224,128]{2,1,0:T(8,128)(2,1)S(1)}, bf16[4,224,128]{2,1,0:T(8,128)(2,1)S(1)}, bf16[4,224,128]{2,1,0:T(8,128)(2,1)S(1)}) custom-call(s32[27]{0:T(128)S(1)} %concatenate.3.facts, bf16[224,1024]{1,0:T(8,128)(2,1)S(1)} %get-tuple-element.45.q_ref, ...), custom_call_target="tpu_custom_call" | custom-call | flops 5000000000 | bytes 5000000 | tf_op jit(solution)/shard_map/pallas_call | solution.py:230
  46.6 3.6 %collective-permute-start.14 = (bf16[4,224,128]{2,1,0:T(8,128)(2,1)S(1)}, bf16[4,224,128]{2,1,0:T(8,128)(2,1)S(1)}, u32[]{:S(2)}, u32[]{:S(2)}) collective-permute-start(bf16[4,224,128]{2,1,0:T(8,128)(2,1)S(1)} %get-tuple-element.66), channel_id=1, source_target_pairs={{0,12},{4,0},{8,4},{12,8},{1,13},{5,1},{9,5},{13,9},{2,14},{6,2},{... | collective-permute-start | bytes 688136 | tf_op jit(solution)/shard_map/ppermute | solution.py:377
  50.2 1.6 %collective-permute-start.15 = (bf16[4,224,128]{2,1,0:T(8,128)(2,1)S(1)}, bf16[4,224,128]{2,1,0:T(8,128)(2,1)S(1)}, u32[]{:S(2)}, u32[]{:S(2)}) collective-permute-start(bf16[4,224,128]{2,1,0:T(8,128)(2,1)S(1)} %get-tuple-element.67), channel_id=1, source_target_pairs={{0,8},{4,12},{8,0},{12,4},{1,9},{5,13},{9,1},{13,5},{2,10},{6,14},... | collective-permute-start | bytes 688136 | tf_op jit(solution)/shard_map/ppermute | solution.py:377
  51.8 0.1 fusion.8
  52.0 2.4 %collective-permute-start.23 = (bf16[224,128]{1,0:T(8,128)(2,1)S(1)}, bf16[224,128]{1,0:T(8,128)(2,1)S(1)}, u32[]{:S(2)}, u32[]{:S(2)}) collective-permute-start(bf16[224,128]{1,0:T(8,128)(2,1)S(1)} %get-tuple-element.84), channel_id=1, source_target_pairs={{0,48},{16,0},{32,16},{48,32},{1,49},{17,1},{33,17},{49,33},{2,50}... | collective-permute-start | bytes 172040 | tf_op jit(solution)/shard_map/ppermute | solution.py:377
  54.4 0.6 collective-permute-start.22
  55.0 5.6 %collective-permute-start.21 = (bf16[224,128]{1,0:T(8,128)(2,1)S(1)}, bf16[224,128]{1,0:T(8,128)(2,1)S(1)}, u32[]{:S(2)}, u32[]{:S(2)}) collective-permute-start(bf16[224,128]{1,0:T(8,128)(2,1)S(1)} %get-tuple-element.86), channel_id=1, source_target_pairs={{0,32},{16,48},{32,0},{48,16},{1,33},{17,49},{33,1},{49,17},{2,34}... | collective-permute-start | bytes 172040 | tf_op jit(solution)/shard_map/ppermute | solution.py:377
  60.7 6.6 %collective-permute-start.25 = (bf16[224,2048]{1,0:T(8,128)(2,1)S(1)}, bf16[224,2048]{1,0:T(8,128)(2,1)S(1)}, u32[]{:S(2)}, u32[]{:S(2)}) collective-permute-start(bf16[224,2048]{1,0:T(8,128)(2,1)S(1)} %bitcast.51), channel_id=1, source_target_pairs={{0,64},{64,0},{1,65},{65,1},{2,66},{66,2},{3,67},{67,3},{4,68},{68... | collective-permute-start | bytes 2752520 | tf_op jit(solution)/shard_map/ppermute | solution.py:405
  67.3 0.1 collective-permute-start.26
  67.4 0.1 fusion.5
  67.5 2.7 %collective-permute-start.18 = (bf16[224,128]{1,0:T(8,128)(2,1)S(1)}, bf16[224,128]{1,0:T(8,128)(2,1)S(1)}, u32[]{:S(2)}, u32[]{:S(2)}) collective-permute-start(bf16[224,128]{1,0:T(8,128)(2,1)S(1)} %get-tuple-element.88), channel_id=1, source_target_pairs={{0,48},{16,0},{32,16},{48,32},{1,49},{17,1},{33,17},{49,33},{2,50}... | collective-permute-start | bytes 172040 | tf_op jit(solution)/shard_map/ppermute | solution.py:377
  70.2 0.4 collective-permute-start.16
  70.6 0.9 collective-permute-done.18.refs_3_
  71.5 3.6 %collective-permute-done.17.refs_2_ = bf16[224,128]{1,0:T(8,128)(2,1)S(1)} collective-permute-done((bf16[224,128]{1,0:T(8,128)(2,1)S(1)}, bf16[224,128]{1,0:T(8,128)(2,1)S(1)}, u32[]{:S(2)}, u32[]{:S(2)}) %collective-permute-start.17) | collective-permute-done | bytes 57376 | tf_op jit(solution)/shard_map/ppermute | solution.py:377
  75.1 1.3 %shard_map.107 = (bf16[224,128]{1,0:T(8,128)(2,1)}, bf16[224,128]{1,0:T(8,128)(2,1)}, bf16[224,128]{1,0:T(8,128)(2,1)S(1)}, bf16[224,128]{1,0:T(8,128)(2,1)S(1)}) custom-call(s32[27]{0:T(128)S(1)} %concatenate.3.facts, f32[224,128]{1,0:T(8,128)S(1)} %get-tuple-element.91.refs_0_, bf16[224,128]{1,0:T(8,128)(2,1)S(1)} %collective-permute-done.16.refs_1_, ...), custom_call_target="tpu_custom_call" | custom-call | tf_op jit(solution)/shard_map/pallas_call | solution.py:319
  76.4 1.0 collective-permute-start.27
  77.4 2.0 %collective-permute-done.27 = bf16[224,128]{1,0:T(8,128)(2,1)S(1)} collective-permute-done((bf16[224,128]{1,0:T(8,128)(2,1)S(1)}, bf16[224,128]{1,0:T(8,128)(2,1)S(1)}, u32[]{:S(2)}, u32[]{:S(2)}) %collective-permute-start.27) | collective-permute-done | bytes 57376 | tf_op jit(solution)/shard_map/ppermute | solution.py:406
  79.5 6.2 %collective-permute-start.28 = (bf16[2,224,128]{2,1,0:T(8,128)(2,1)S(1)}, bf16[2,224,128]{2,1,0:T(8,128)(2,1)S(1)}, u32[]{:S(2)}, u32[]{:S(2)}) collective-permute-start(bf16[2,224,128]{2,1,0:T(8,128)(2,1)S(1)} %get-tuple-element.96), channel_id=1, source_target_pairs={{2,66},{3,67},{64,0},{65,1},{6,70},{7,71},{68,4},{69,5},{10,74},{1... | collective-permute-start | bytes 344072 | tf_op jit(solution)/shard_map/ppermute | solution.py:410
  85.7 0.9 collective-permute-done.28
  86.6 0.7 collective-permute-start.31
  87.3 1.3 %collective-permute-start.30 = (bf16[896,128]{1,0:T(8,128)(2,1)S(1)}, bf16[896,128]{1,0:T(8,128)(2,1)S(1)}, u32[]{:S(2)}, u32[]{:S(2)}) collective-permute-start(bf16[896,128]{1,0:T(8,128)(2,1)S(1)} %bitcast.54), channel_id=1, source_target_pairs={{0,1},{1,2},{66,67},{67,64},{4,5},{5,6},{70,71},{71,68},{8,9},{9,1... | collective-permute-start | bytes 688136 | tf_op jit(solution)/shard_map/ppermute | solution.py:417
  88.6 1.3 %collective-permute-start.29 = (bf16[896,128]{1,0:T(8,128)(2,1)S(1)}, bf16[896,128]{1,0:T(8,128)(2,1)S(1)}, u32[]{:S(2)}, u32[]{:S(2)}) collective-permute-start(bf16[896,128]{1,0:T(8,128)(2,1)S(1)} %bitcast.55), channel_id=1, source_target_pairs={{0,2},{1,3},{66,64},{67,65},{4,6},{5,7},{70,68},{71,69},{8,10},{9,... | collective-permute-start | bytes 688136 | tf_op jit(solution)/shard_map/ppermute | solution.py:417
  89.9 6.2 %collective-permute-done.30.row1 = bf16[896,128]{1,0:T(8,128)(2,1)S(1)} collective-permute-done((bf16[896,128]{1,0:T(8,128)(2,1)S(1)}, bf16[896,128]{1,0:T(8,128)(2,1)S(1)}, u32[]{:S(2)}, u32[]{:S(2)}) %collective-permute-start.30) | collective-permute-done | bytes 229408 | tf_op jit(solution)/shard_map/ppermute | solution.py:417
  96.1 3.6 %collective-permute-done.29.row2 = bf16[896,128]{1,0:T(8,128)(2,1)S(1)} collective-permute-done((bf16[896,128]{1,0:T(8,128)(2,1)S(1)}, bf16[896,128]{1,0:T(8,128)(2,1)S(1)}, u32[]{:S(2)}, u32[]{:S(2)}) %collective-permute-start.29) | collective-permute-done | bytes 229408 | tf_op jit(solution)/shard_map/ppermute | solution.py:417
  99.7 2.6 %shard_map.108 = (bf16[2,2,16,2048]{3,2,1,0:T(8,128)(2,1)S(1)}, bf16[2,2,16,2048]{3,2,1,0:T(8,128)(2,1)S(1)}, bf16[2,2,16,2048]{3,2,1,0:T(8,128)(2,1)S(1)}, bf16[2,2,16,2048]{3,2,1,0:T(8,128)(2,1)S(1)}) custom-call(s32[27]{0:T(128)S(1)} %concatenate.3.facts, bf16[224,2048]{1,0:T(8,128)(2,1)S(1)} %bitcast.52, ...), custom_call_target="tpu_custom_call" | custom-call | flops 1000000000 | bytes 4000000 | tf_op jit(solution)/shard_map/pallas_call | solution.py:354
  102.3 0.1 collective-permute-start.32
  102.4 2.7 %collective-permute-start.33 = (bf16[2,2,16,2048]{3,2,1,0:T(8,128)(2,1)S(1)}, bf16[2,2,16,2048]{3,2,1,0:T(8,128)(2,1)S(1)}, u32[]{:S(2)}, u32[]{:S(2)}) collective-permute-start(bf16[2,2,16,2048]{3,2,1,0:T(8,128)(2,1)S(1)} %get-tuple-element.80), channel_id=1, source_target_pairs={{0,12},{4,0},{8,4},{12,8},{1,13},{5,1},{9,5},{13,9},{2,14},{6,2},{... | collective-permute-start | bytes 786440 | tf_op jit(solution)/shard_map/ppermute | solution.py:377
  105.1 11.7 %collective-permute-done.32 = bf16[2,2,16,2048]{3,2,1,0:T(8,128)(2,1)S(1)} collective-permute-done((bf16[2,2,16,2048]{3,2,1,0:T(8,128)(2,1)S(1)}, bf16[2,2,16,2048]{3,2,1,0:T(8,128)(2,1)S(1)}, u32[]{:S(2)}, u32[]{:S(2)}) %collective-permute-start.32) | collective-permute-done | bytes 262176 | tf_op jit(solution)/shard_map/ppermute | solution.py:377
  116.8 0.1 fusion.10
  117.0 3.7 %collective-permute-start.35 = (bf16[16,2048]{1,0:T(8,128)(2,1)S(1)}, bf16[16,2048]{1,0:T(8,128)(2,1)S(1)}, u32[]{:S(2)}, u32[]{:S(2)}) collective-permute-start(bf16[16,2048]{1,0:T(8,128)(2,1)S(1)} %get-tuple-element.92), channel_id=1, source_target_pairs={{0,128},{128,0},{1,129},{129,1},{2,130},{130,2},{3,131},{131,3},{4... | collective-permute-start | bytes 196616 | tf_op jit(solution)/shard_map/ppermute | solution.py:424
  120.7 1.1 collective-permute-start.37
  121.7 1.0 collective-permute-start.36
  122.7 1.4 %collective-permute-done.35 = bf16[16,2048]{1,0:T(8,128)(2,1)S(1)} collective-permute-done((bf16[16,2048]{1,0:T(8,128)(2,1)S(1)}, bf16[16,2048]{1,0:T(8,128)(2,1)S(1)}, u32[]{:S(2)}, u32[]{:S(2)}) %collective-permute-start.35) | collective-permute-done | bytes 65568 | tf_op jit(solution)/shard_map/ppermute | solution.py:424
  124.1 4.2 %collective-permute-done.37 = bf16[16,2048]{1,0:T(8,128)(2,1)S(1)} collective-permute-done((bf16[16,2048]{1,0:T(8,128)(2,1)S(1)}, bf16[16,2048]{1,0:T(8,128)(2,1)S(1)}, u32[]{:S(2)}, u32[]{:S(2)}) %collective-permute-start.37) | collective-permute-done | bytes 65568 | tf_op jit(solution)/shard_map/ppermute | solution.py:426
  128.3 0.7 fusion.2
  (41 shorter events, 0.2 us)
Async XLA Ops:
  0.6 9.1 %collective-permute-start.2 = (bf16[224,128]{1,0:T(8,128)(2,1)}, bf16[224,128]{1,0:T(8,128)(2,1)S(1)}, u32[]{:S(2)}, u32[]{:S(2)}) collective-permute-start(bf16[224,128]{1,0:T(8,128)(2,1)} %bitcast.59), channel_id=1, source_target_pairs={{0,48},{16,0},{32,16},{48,32},{1,49},{17,1},{33,17},{49,33},{2,50}... | collective-permute-start | bytes 172040 | tf_op jit(solution)/shard_map/ppermute | solution.py:377
  5.9 6.0 %collective-permute-start.1 = (bf16[224,128]{1,0:T(8,128)(2,1)}, bf16[224,128]{1,0:T(8,128)(2,1)S(1)}, u32[]{:S(2)}, u32[]{:S(2)}) collective-permute-start(bf16[224,128]{1,0:T(8,128)(2,1)} %bitcast.60), channel_id=1, source_target_pairs={{0,32},{16,48},{32,0},{48,16},{1,33},{17,49},{33,1},{49,17},{2,34}... | collective-permute-start | bytes 172040 | tf_op jit(solution)/shard_map/ppermute | solution.py:377
  5.9 6.0 %collective-permute-start = (bf16[224,128]{1,0:T(8,128)(2,1)}, bf16[224,128]{1,0:T(8,128)(2,1)S(1)}, u32[]{:S(2)}, u32[]{:S(2)}) collective-permute-start(bf16[224,128]{1,0:T(8,128)(2,1)} %bitcast.61), channel_id=1, source_target_pairs={{0,16},{16,32},{32,48},{48,0},{1,17},{17,33},{33,49},{49,1},{2,18}... | collective-permute-start | bytes 172040 | tf_op jit(solution)/shard_map/ppermute | solution.py:377
  6.3 6.3 %collective-permute-start.5 = (bf16[224,128]{1,0:T(8,128)(2,1)}, bf16[224,128]{1,0:T(8,128)(2,1)S(1)}, u32[]{:S(2)}, u32[]{:S(2)}) collective-permute-start(bf16[224,128]{1,0:T(8,128)(2,1)} %bitcast.63), channel_id=1, source_target_pairs={{0,48},{16,0},{32,16},{48,32},{1,49},{17,1},{33,17},{49,33},{2,50}... | collective-permute-start | bytes 172040 | tf_op jit(solution)/shard_map/ppermute | solution.py:377
  9.1 7.7 %collective-permute-start.4 = (bf16[224,128]{1,0:T(8,128)(2,1)}, bf16[224,128]{1,0:T(8,128)(2,1)S(1)}, u32[]{:S(2)}, u32[]{:S(2)}) collective-permute-start(bf16[224,128]{1,0:T(8,128)(2,1)} %bitcast.64), channel_id=1, source_target_pairs={{0,32},{16,48},{32,0},{48,16},{1,33},{17,49},{33,1},{49,17},{2,34}... | collective-permute-start | bytes 172040 | tf_op jit(solution)/shard_map/ppermute | solution.py:377
  9.7 7.1 %collective-permute-start.3 = (bf16[224,128]{1,0:T(8,128)(2,1)}, bf16[224,128]{1,0:T(8,128)(2,1)S(1)}, u32[]{:S(2)}, u32[]{:S(2)}) collective-permute-start(bf16[224,128]{1,0:T(8,128)(2,1)} %bitcast.65), channel_id=1, source_target_pairs={{0,16},{16,32},{32,48},{48,0},{1,17},{17,33},{33,49},{49,1},{2,18}... | collective-permute-start | bytes 172040 | tf_op jit(solution)/shard_map/ppermute | solution.py:377
  9.7 1.0 copy-start.1
  10.7 1.0 copy-start.2
  11.8 5.1 %copy-start.3 = (bf16[1,224,128]{2,1,0:T(8,128)(2,1)S(1)}, bf16[1,224,128]{2,1,0:T(8,128)(2,1)}, u32[]{:S(2)}) copy-start(bf16[1,224,128]{2,1,0:T(8,128)(2,1)} %param.9) | copy-start | bytes 172036
  16.8 4.3 %copy-start.4 = (bf16[1,224,128]{2,1,0:T(8,128)(2,1)S(1)}, bf16[1,224,128]{2,1,0:T(8,128)(2,1)}, u32[]{:S(2)}) copy-start(bf16[1,224,128]{2,1,0:T(8,128)(2,1)} %param.10) | copy-start | bytes 172036
  16.8 7.2 %collective-permute-start.6 = (bf16[4,224,128]{2,1,0:T(8,128)(2,1)S(1)}, bf16[4,224,128]{2,1,0:T(8,128)(2,1)S(1)}, u32[]{:S(2)}, u32[]{:S(2)}) collective-permute-start(bf16[4,224,128]{2,1,0:T(8,128)(2,1)S(1)} %shard_map.103.k0), channel_id=1, source_target_pairs={{0,4},{4,8},{8,12},{12,0},{1,5},{5,9},{9,13},{13,1},{2,6},{6,10},{... | collective-permute-start | bytes 688136 | tf_op jit(solution)/shard_map/ppermute | solution.py:377
  17.2 8.4 %collective-permute-start.8 = (bf16[4,224,128]{2,1,0:T(8,128)(2,1)S(1)}, bf16[4,224,128]{2,1,0:T(8,128)(2,1)S(1)}, u32[]{:S(2)}, u32[]{:S(2)}) collective-permute-start(bf16[4,224,128]{2,1,0:T(8,128)(2,1)S(1)} %shard_map.103.k0), channel_id=1, source_target_pairs={{0,12},{4,0},{8,4},{12,8},{1,13},{5,1},{9,5},{13,9},{2,14},{6,2},{... | collective-permute-start | bytes 688136 | tf_op jit(solution)/shard_map/ppermute | solution.py:377
  19.6 9.1 %collective-permute-start.7 = (bf16[4,224,128]{2,1,0:T(8,128)(2,1)S(1)}, bf16[4,224,128]{2,1,0:T(8,128)(2,1)S(1)}, u32[]{:S(2)}, u32[]{:S(2)}) collective-permute-start(bf16[4,224,128]{2,1,0:T(8,128)(2,1)S(1)} %shard_map.103.k0), channel_id=1, source_target_pairs={{0,8},{4,12},{8,0},{12,4},{1,9},{5,13},{9,1},{13,5},{2,10},{6,14},... | collective-permute-start | bytes 688136 | tf_op jit(solution)/shard_map/ppermute | solution.py:377
  20.3 0.7 copy-start.5
  20.3 0.7 copy-start.6
  21.1 12.6 %copy-start = (bf16[1,224,2048]{2,1,0:T(8,128)(2,1)S(1)}, bf16[1,224,2048]{2,1,0:T(8,128)(2,1)}, u32[]{:S(2)}) copy-start(bf16[1,224,2048]{2,1,0:T(8,128)(2,1)} %param.7) | copy-start | bytes 2752516
  24.0 14.8 %collective-permute-start.11 = (bf16[4,224,128]{2,1,0:T(8,128)(2,1)S(1)}, bf16[4,224,128]{2,1,0:T(8,128)(2,1)S(1)}, u32[]{:S(2)}, u32[]{:S(2)}) collective-permute-start(bf16[4,224,128]{2,1,0:T(8,128)(2,1)S(1)} %shard_map.104.v0), channel_id=1, source_target_pairs={{0,12},{4,0},{8,4},{12,8},{1,13},{5,1},{9,5},{13,9},{2,14},{6,2},{... | collective-permute-start | bytes 688136 | tf_op jit(solution)/shard_map/ppermute | solution.py:377
  24.0 16.2 %collective-permute-start.9 = (bf16[4,224,128]{2,1,0:T(8,128)(2,1)S(1)}, bf16[4,224,128]{2,1,0:T(8,128)(2,1)S(1)}, u32[]{:S(2)}, u32[]{:S(2)}) collective-permute-start(bf16[4,224,128]{2,1,0:T(8,128)(2,1)S(1)} %shard_map.104.v0), channel_id=1, source_target_pairs={{0,4},{4,8},{8,12},{12,0},{1,5},{5,9},{9,13},{13,1},{2,6},{6,10},{... | collective-permute-start | bytes 688136 | tf_op jit(solution)/shard_map/ppermute | solution.py:377
  28.7 9.0 %collective-permute-start.10 = (bf16[4,224,128]{2,1,0:T(8,128)(2,1)S(1)}, bf16[4,224,128]{2,1,0:T(8,128)(2,1)S(1)}, u32[]{:S(2)}, u32[]{:S(2)}) collective-permute-start(bf16[4,224,128]{2,1,0:T(8,128)(2,1)S(1)} %shard_map.104.v0), channel_id=1, source_target_pairs={{0,8},{4,12},{8,0},{12,4},{1,9},{5,13},{9,1},{13,5},{2,10},{6,14},... | collective-permute-start | bytes 688136 | tf_op jit(solution)/shard_map/ppermute | solution.py:377
  33.7 27.0 %collective-permute-start.24 = (bf16[224,2048]{1,0:T(8,128)(2,1)S(1)}, bf16[224,2048]{1,0:T(8,128)(2,1)S(1)}, u32[]{:S(2)}, u32[]{:S(2)}) collective-permute-start(bf16[224,2048]{1,0:T(8,128)(2,1)S(1)} %bitcast.50), channel_id=1, source_target_pairs={{0,16},{16,0},{32,48},{48,32},{1,17},{17,1},{33,49},{49,33},{2,18}... | collective-permute-start | bytes 2752520 | tf_op jit(solution)/shard_map/ppermute | solution.py:399
  34.9 11.7 %collective-permute-start.12 = (bf16[4,224,128]{2,1,0:T(8,128)(2,1)S(1)}, bf16[4,224,128]{2,1,0:T(8,128)(2,1)S(1)}, u32[]{:S(2)}, u32[]{:S(2)}) collective-permute-start(bf16[4,224,128]{2,1,0:T(8,128)(2,1)S(1)} %get-tuple-element.63), channel_id=1, source_target_pairs={{0,4},{4,8},{8,12},{12,0},{1,5},{5,9},{9,13},{13,1},{2,6},{6,10},{... | collective-permute-start | bytes 688136 | tf_op jit(solution)/shard_map/ppermute | solution.py:377
  37.7 12.6 %collective-permute-start.19 = (bf16[4,224,128]{2,1,0:T(8,128)(2,1)S(1)}, bf16[4,224,128]{2,1,0:T(8,128)(2,1)S(1)}, u32[]{:S(2)}, u32[]{:S(2)}) collective-permute-start(bf16[4,224,128]{2,1,0:T(8,128)(2,1)S(1)} %get-tuple-element.69), channel_id=1, source_target_pairs={{0,12},{4,0},{8,4},{12,8},{1,13},{5,1},{9,5},{13,9},{2,14},{6,2},{... | collective-permute-start | bytes 688136 | tf_op jit(solution)/shard_map/ppermute | solution.py:377
  38.8 13.1 %collective-permute-start.20 = (bf16[4,224,128]{2,1,0:T(8,128)(2,1)S(1)}, bf16[4,224,128]{2,1,0:T(8,128)(2,1)S(1)}, u32[]{:S(2)}, u32[]{:S(2)}) collective-permute-start(bf16[4,224,128]{2,1,0:T(8,128)(2,1)S(1)} %get-tuple-element.70), channel_id=1, source_target_pairs={{0,8},{4,12},{8,0},{12,4},{1,9},{5,13},{9,1},{13,5},{2,10},{6,14},... | collective-permute-start | bytes 688136 | tf_op jit(solution)/shard_map/ppermute | solution.py:377
  46.6 7.8 %collective-permute-start.13 = (bf16[4,224,128]{2,1,0:T(8,128)(2,1)S(1)}, bf16[4,224,128]{2,1,0:T(8,128)(2,1)S(1)}, u32[]{:S(2)}, u32[]{:S(2)}) collective-permute-start(bf16[4,224,128]{2,1,0:T(8,128)(2,1)S(1)} %get-tuple-element.65), channel_id=1, source_target_pairs={{0,4},{4,8},{8,12},{12,0},{1,5},{5,9},{9,13},{13,1},{2,6},{6,10},{... | collective-permute-start | bytes 688136 | tf_op jit(solution)/shard_map/ppermute | solution.py:377
  46.6 8.4 %collective-permute-start.14 = (bf16[4,224,128]{2,1,0:T(8,128)(2,1)S(1)}, bf16[4,224,128]{2,1,0:T(8,128)(2,1)S(1)}, u32[]{:S(2)}, u32[]{:S(2)}) collective-permute-start(bf16[4,224,128]{2,1,0:T(8,128)(2,1)S(1)} %get-tuple-element.66), channel_id=1, source_target_pairs={{0,12},{4,0},{8,4},{12,8},{1,13},{5,1},{9,5},{13,9},{2,14},{6,2},{... | collective-permute-start | bytes 688136 | tf_op jit(solution)/shard_map/ppermute | solution.py:377
  50.2 10.4 %collective-permute-start.15 = (bf16[4,224,128]{2,1,0:T(8,128)(2,1)S(1)}, bf16[4,224,128]{2,1,0:T(8,128)(2,1)S(1)}, u32[]{:S(2)}, u32[]{:S(2)}) collective-permute-start(bf16[4,224,128]{2,1,0:T(8,128)(2,1)S(1)} %get-tuple-element.67), channel_id=1, source_target_pairs={{0,8},{4,12},{8,0},{12,4},{1,9},{5,13},{9,1},{13,5},{2,10},{6,14},... | collective-permute-start | bytes 688136 | tf_op jit(solution)/shard_map/ppermute | solution.py:377
  52.0 15.5 %collective-permute-start.23 = (bf16[224,128]{1,0:T(8,128)(2,1)S(1)}, bf16[224,128]{1,0:T(8,128)(2,1)S(1)}, u32[]{:S(2)}, u32[]{:S(2)}) collective-permute-start(bf16[224,128]{1,0:T(8,128)(2,1)S(1)} %get-tuple-element.84), channel_id=1, source_target_pairs={{0,48},{16,0},{32,16},{48,32},{1,49},{17,1},{33,17},{49,33},{2,50}... | collective-permute-start | bytes 172040 | tf_op jit(solution)/shard_map/ppermute | solution.py:377
  54.4 15.8 %collective-permute-start.22 = (bf16[224,128]{1,0:T(8,128)(2,1)S(1)}, bf16[224,128]{1,0:T(8,128)(2,1)S(1)}, u32[]{:S(2)}, u32[]{:S(2)}) collective-permute-start(bf16[224,128]{1,0:T(8,128)(2,1)S(1)} %get-tuple-element.85), channel_id=1, source_target_pairs={{0,16},{16,32},{32,48},{48,0},{1,17},{17,33},{33,49},{49,1},{2,18}... | collective-permute-start | bytes 172040 | tf_op jit(solution)/shard_map/ppermute | solution.py:377
  55.0 15.2 %collective-permute-start.21 = (bf16[224,128]{1,0:T(8,128)(2,1)S(1)}, bf16[224,128]{1,0:T(8,128)(2,1)S(1)}, u32[]{:S(2)}, u32[]{:S(2)}) collective-permute-start(bf16[224,128]{1,0:T(8,128)(2,1)S(1)} %get-tuple-element.86), channel_id=1, source_target_pairs={{0,32},{16,48},{32,0},{48,16},{1,33},{17,49},{33,1},{49,17},{2,34}... | collective-permute-start | bytes 172040 | tf_op jit(solution)/shard_map/ppermute | solution.py:377
  60.7 39.1 %collective-permute-start.25 = (bf16[224,2048]{1,0:T(8,128)(2,1)S(1)}, bf16[224,2048]{1,0:T(8,128)(2,1)S(1)}, u32[]{:S(2)}, u32[]{:S(2)}) collective-permute-start(bf16[224,2048]{1,0:T(8,128)(2,1)S(1)} %bitcast.51), channel_id=1, source_target_pairs={{0,64},{64,0},{1,65},{65,1},{2,66},{66,2},{3,67},{67,3},{4,68},{68... | collective-permute-start | bytes 2752520 | tf_op jit(solution)/shard_map/ppermute | solution.py:405
  67.3 32.5 %collective-permute-start.26 = (bf16[224,2048]{1,0:T(8,128)(2,1)S(1)}, bf16[224,2048]{1,0:T(8,128)(2,1)S(1)}, u32[]{:S(2)}, u32[]{:S(2)}) collective-permute-start(bf16[224,2048]{1,0:T(8,128)(2,1)S(1)} %collective-permute-done.24.hid1), channel_id=1, source_target_pairs={{0,64},{64,0},{1,65},{65,1},{2,66},{66,2},{3,67},{67,3},{4,68},{68... | collective-permute-start | bytes 2752520 | tf_op jit(solution)/shard_map/ppermute | solution.py:405
  67.5 4.0 %collective-permute-start.18 = (bf16[224,128]{1,0:T(8,128)(2,1)S(1)}, bf16[224,128]{1,0:T(8,128)(2,1)S(1)}, u32[]{:S(2)}, u32[]{:S(2)}) collective-permute-start(bf16[224,128]{1,0:T(8,128)(2,1)S(1)} %get-tuple-element.88), channel_id=1, source_target_pairs={{0,48},{16,0},{32,16},{48,32},{1,49},{17,1},{33,17},{49,33},{2,50}... | collective-permute-start | bytes 172040 | tf_op jit(solution)/shard_map/ppermute | solution.py:377
  70.2 4.9 %collective-permute-start.17 = (bf16[224,128]{1,0:T(8,128)(2,1)S(1)}, bf16[224,128]{1,0:T(8,128)(2,1)S(1)}, u32[]{:S(2)}, u32[]{:S(2)}) collective-permute-start(bf16[224,128]{1,0:T(8,128)(2,1)S(1)} %get-tuple-element.89), channel_id=1, source_target_pairs={{0,16},{16,32},{32,48},{48,0},{1,17},{17,33},{33,49},{49,1},{2,18}... | collective-permute-start | bytes 172040 | tf_op jit(solution)/shard_map/ppermute | solution.py:377
  70.2 4.8 %collective-permute-start.16 = (bf16[224,128]{1,0:T(8,128)(2,1)S(1)}, bf16[224,128]{1,0:T(8,128)(2,1)S(1)}, u32[]{:S(2)}, u32[]{:S(2)}) collective-permute-start(bf16[224,128]{1,0:T(8,128)(2,1)S(1)} %get-tuple-element.90), channel_id=1, source_target_pairs={{0,32},{16,48},{32,0},{48,16},{1,33},{17,49},{33,1},{49,17},{2,34}... | collective-permute-start | bytes 172040 | tf_op jit(solution)/shard_map/ppermute | solution.py:377
  76.4 3.0 %collective-permute-start.27 = (bf16[224,128]{1,0:T(8,128)(2,1)S(1)}, bf16[224,128]{1,0:T(8,128)(2,1)S(1)}, u32[]{:S(2)}, u32[]{:S(2)}) collective-permute-start(bf16[224,128]{1,0:T(8,128)(2,1)S(1)} %get-tuple-element.77), channel_id=1, source_target_pairs={{0,16},{16,0},{32,48},{48,32},{1,17},{17,1},{33,49},{49,33},{2,18}... | collective-permute-start | bytes 172040 | tf_op jit(solution)/shard_map/ppermute | solution.py:406
  79.5 7.1 %collective-permute-start.28 = (bf16[2,224,128]{2,1,0:T(8,128)(2,1)S(1)}, bf16[2,224,128]{2,1,0:T(8,128)(2,1)S(1)}, u32[]{:S(2)}, u32[]{:S(2)}) collective-permute-start(bf16[2,224,128]{2,1,0:T(8,128)(2,1)S(1)} %get-tuple-element.96), channel_id=1, source_target_pairs={{2,66},{3,67},{64,0},{65,1},{6,70},{7,71},{68,4},{69,5},{10,74},{1... | collective-permute-start | bytes 344072 | tf_op jit(solution)/shard_map/ppermute | solution.py:410
  86.6 3.3 %collective-permute-start.31 = (bf16[896,128]{1,0:T(8,128)(2,1)S(1)}, bf16[896,128]{1,0:T(8,128)(2,1)S(1)}, u32[]{:S(2)}, u32[]{:S(2)}) collective-permute-start(bf16[896,128]{1,0:T(8,128)(2,1)S(1)} %bitcast.53), channel_id=1, source_target_pairs={{0,3},{1,0},{66,65},{67,66},{4,7},{5,4},{70,69},{71,70},{8,11},{9,... | collective-permute-start | bytes 688136 | tf_op jit(solution)/shard_map/ppermute | solution.py:417
  87.3 8.8 %collective-permute-start.30 = (bf16[896,128]{1,0:T(8,128)(2,1)S(1)}, bf16[896,128]{1,0:T(8,128)(2,1)S(1)}, u32[]{:S(2)}, u32[]{:S(2)}) collective-permute-start(bf16[896,128]{1,0:T(8,128)(2,1)S(1)} %bitcast.54), channel_id=1, source_target_pairs={{0,1},{1,2},{66,67},{67,64},{4,5},{5,6},{70,71},{71,68},{8,9},{9,1... | collective-permute-start | bytes 688136 | tf_op jit(solution)/shard_map/ppermute | solution.py:417
  88.6 11.1 %collective-permute-start.29 = (bf16[896,128]{1,0:T(8,128)(2,1)S(1)}, bf16[896,128]{1,0:T(8,128)(2,1)S(1)}, u32[]{:S(2)}, u32[]{:S(2)}) collective-permute-start(bf16[896,128]{1,0:T(8,128)(2,1)S(1)} %bitcast.55), channel_id=1, source_target_pairs={{0,2},{1,3},{66,64},{67,65},{4,6},{5,7},{70,68},{71,69},{8,10},{9,... | collective-permute-start | bytes 688136 | tf_op jit(solution)/shard_map/ppermute | solution.py:417
  102.3 14.5 %collective-permute-start.32 = (bf16[2,2,16,2048]{3,2,1,0:T(8,128)(2,1)S(1)}, bf16[2,2,16,2048]{3,2,1,0:T(8,128)(2,1)S(1)}, u32[]{:S(2)}, u32[]{:S(2)}) collective-permute-start(bf16[2,2,16,2048]{3,2,1,0:T(8,128)(2,1)S(1)} %get-tuple-element.79), channel_id=1, source_target_pairs={{0,4},{4,8},{8,12},{12,0},{1,5},{5,9},{9,13},{13,1},{2,6},{6,10},{... | collective-permute-start | bytes 786440 | tf_op jit(solution)/shard_map/ppermute | solution.py:377
  102.4 14.4 %collective-permute-start.33 = (bf16[2,2,16,2048]{3,2,1,0:T(8,128)(2,1)S(1)}, bf16[2,2,16,2048]{3,2,1,0:T(8,128)(2,1)S(1)}, u32[]{:S(2)}, u32[]{:S(2)}) collective-permute-start(bf16[2,2,16,2048]{3,2,1,0:T(8,128)(2,1)S(1)} %get-tuple-element.80), channel_id=1, source_target_pairs={{0,12},{4,0},{8,4},{12,8},{1,13},{5,1},{9,5},{13,9},{2,14},{6,2},{... | collective-permute-start | bytes 786440 | tf_op jit(solution)/shard_map/ppermute | solution.py:377
  105.1 11.7 %collective-permute-start.34 = (bf16[2,2,16,2048]{3,2,1,0:T(8,128)(2,1)S(1)}, bf16[2,2,16,2048]{3,2,1,0:T(8,128)(2,1)S(1)}, u32[]{:S(2)}, u32[]{:S(2)}) collective-permute-start(bf16[2,2,16,2048]{3,2,1,0:T(8,128)(2,1)S(1)} %get-tuple-element.81), channel_id=1, source_target_pairs={{0,8},{4,12},{8,0},{12,4},{1,9},{5,13},{9,1},{13,5},{2,10},{6,14},... | collective-permute-start | bytes 786440 | tf_op jit(solution)/shard_map/ppermute | solution.py:377
  117.0 7.2 %collective-permute-start.35 = (bf16[16,2048]{1,0:T(8,128)(2,1)S(1)}, bf16[16,2048]{1,0:T(8,128)(2,1)S(1)}, u32[]{:S(2)}, u32[]{:S(2)}) collective-permute-start(bf16[16,2048]{1,0:T(8,128)(2,1)S(1)} %get-tuple-element.92), channel_id=1, source_target_pairs={{0,128},{128,0},{1,129},{129,1},{2,130},{130,2},{3,131},{131,3},{4... | collective-permute-start | bytes 196616 | tf_op jit(solution)/shard_map/ppermute | solution.py:424
  120.7 7.6 %collective-permute-start.37 = (bf16[16,2048]{1,0:T(8,128)(2,1)S(1)}, bf16[16,2048]{1,0:T(8,128)(2,1)S(1)}, u32[]{:S(2)}, u32[]{:S(2)}) collective-permute-start(bf16[16,2048]{1,0:T(8,128)(2,1)S(1)} %get-tuple-element.93), channel_id=1, source_target_pairs={{0,32},{32,0},{16,48},{48,16},{1,33},{33,1},{17,49},{49,17},{2,34}... | collective-permute-start | bytes 196616 | tf_op jit(solution)/shard_map/ppermute | solution.py:426
  121.7 6.6 %collective-permute-start.36 = (bf16[16,2048]{1,0:T(8,128)(2,1)S(1)}, bf16[16,2048]{1,0:T(8,128)(2,1)S(1)}, u32[]{:S(2)}, u32[]{:S(2)}) collective-permute-start(bf16[16,2048]{1,0:T(8,128)(2,1)S(1)} %get-tuple-element.94), channel_id=1, source_target_pairs={{0,160},{128,32},{32,128},{160,0},{16,176},{144,48},{48,144},{176,... | collective-permute-start | bytes 196616 | tf_op jit(solution)/shard_map/ppermute | solution.py:425
